TPU v7x, 32 devices: a whole 2x2x4 slice. The times are simulated.
32 devices in a mesh: row: 4 (over y, x), seq: 4 (over z), tp: 2 (over core).
Axes of the slice: x: 2, y: 2, z: 4, core: 2. Of those that a mesh axis runs over, the one named last changes fastest.
Arguments:
- block_input: bfloat16 [4, 1024, 2048], P('row', 'seq'), may hold values from -6 to 6
- grad_out: bfloat16 [4, 1024, 2048], P('row', 'seq'), may hold values from -6 to 6
- doc_lengths: int32 [4, 8], P('row'), may hold values from 1 to 896, as said below
- attn_gain: float32 [2048], replicated, may hold values from 0.5 to 1.5
- mlp_gain: float32 [2048], replicated, may hold values from 0.5 to 1.5
- out_gain: float32 [128], replicated, may hold values from 0.5 to 1.5
- conv_weight: float32 [3, 4, 2048], P(None, None, 'tp'), may hold values from -3 to 3
- qkv_weight: bfloat16 [3, 2048, 2048], P(None, ('row', 'seq'), 'tp'), may hold values from -0.125 to 0.125
- beta_weight: bfloat16 [2048, 16], P(('row', 'seq'), 'tp'), may hold values from -0.125 to 0.125
- o_weight: bfloat16 [2048, 2048], P('tp', ('row', 'seq')), may hold values from -0.125 to 0.125
- gate_up_weight: bfloat16 [2, 2048, 5632], P(None, ('row', 'seq'), 'tp'), may hold values from -0.125 to 0.125
- down_weight: bfloat16 [5632, 2048], P('tp', ('row', 'seq')), may hold values from -0.078125 to 0.078125
Outputs:
- block_output: bfloat16 [4, 1024, 2048], P('row', 'seq')
- input_grad: bfloat16 [4, 1024, 2048], P('row', 'seq')
- attn_gain_grad: float32 [2048], replicated
- mlp_gain_grad: float32 [2048], replicated
- out_gain_grad: float32 [128], replicated
- conv_grad: float32 [3, 4, 2048], replicated
- qkv_grad: float32 [3, 2048, 2048], P(None, ('row', 'seq'), 'tp')
- beta_grad: float32 [2048, 16], P(('row', 'seq'), 'tp')
- o_grad: float32 [2048, 2048], P('tp', ('row', 'seq'))
- gate_up_grad: float32 [2, 2048, 5632], P(None, ('row', 'seq'), 'tp')
- down_grad: float32 [5632, 2048], P('tp', ('row', 'seq'))
Inputs may be any that keep to these rules, and one draw needn't show every extreme that they name: `doc_lengths`: the 8 documents of each row lie one after another from position 0 and sum to less than 1024; the positions after them are padding; one document of each row has exactly 896 positions.
All inputs are finite; a program needn't handle non-finite values.
Results may differ from a plain program's by a relative error of at most 0.023.
Values may be sent and summed in bfloat16 or wider, within the bound.
A program may use at most 256 MiB of HBM per device.

v0:
```python
import jax
import jax.numpy as jnp
from jax import lax
from jax.sharding import PartitionSpec as P

DK = 128
KW = 4
GROUP = 64
DOCS = 8


eps = 1e-06
mix_floor = 0.01
precise = lax.Precision.HIGHEST


def from_behind(shard, axis, by):
    devices = lax.axis_size(axis)
    pairs = [(i, i + by) for i in range(devices) if 0 <= i + by < devices]
    return lax.ppermute(shard, axis, pairs)


def prefix(shard, axis, combine, identity, reverse):
    devices, place = (lax.axis_size(axis), lax.axis_index(axis))
    everything = jax.tree.map(
        lambda part, kind: lax.all_gather(part.astype(kind), axis),
        shard,
        (jnp.bfloat16, jnp.bfloat16),
    )
    start = jax.tree.map(
        lambda part, zero: jnp.broadcast_to(jnp.asarray(zero, part.dtype), part.shape),
        shard,
        identity,
    )

    def step(k, before):
        at = devices - 1 - k if reverse else k
        reached = at > place if reverse else at < place
        new = combine(
            before, jax.tree.map(lambda part, own: part[at].astype(own.dtype), everything, shard)
        )
        return jax.tree.map(lambda a, b: jnp.where(reached, a, b), new, before)

    return lax.fori_loop(0, devices, step, start)


def norm_scale(values):
    return lax.rsqrt(jnp.mean(values * values, axis=-1, keepdims=True) + eps)


def norm_back(values, scale, gain, grad):
    weighted = gain * grad
    return scale * weighted - values * scale**3 * jnp.mean(
        weighted * values, axis=-1, keepdims=True
    )


def batch_mul(left, right):
    return jnp.einsum("hij,hjk->hik", left, right, precision=precise)


def batch_mul_t(left, right):
    return jnp.einsum("hji,hjk->hik", left, right, precision=precise)


def compose(earlier, later):
    return (batch_mul(later[0], earlier[0]), batch_mul(later[0], earlier[1]) + later[1])


def over_heads(function, shared):
    return jax.vmap(jax.vmap(function), in_axes=shared)


def tp_total(term):
    return lax.psum(term.astype(jnp.bfloat16), "tp").astype(jnp.float32)


def group_parts(key_rows, value_rows, rates, same_doc, carry_mask):
    size = key_rows.shape[0]
    strict = jnp.tril(jnp.ones((size, size), jnp.float32), -1) * same_doc
    inner = jnp.dot(key_rows, key_rows.T, precision=precise)
    system = jnp.eye(size, dtype=jnp.float32) + rates[:, None] * inner * strict
    right_side = jnp.concatenate(
        [rates[:, None] * value_rows, (rates * carry_mask)[:, None] * key_rows], axis=1
    )
    solved = jax.scipy.linalg.solve_triangular(system, right_side, lower=True)
    base_rows = solved[:, : value_rows.shape[1]]
    wy_rows = solved[:, value_rows.shape[1] :]
    tail_keys = same_doc[size - 1][:, None] * key_rows
    identity_mat = jnp.eye(key_rows.shape[1], dtype=jnp.float32)
    transition = carry_mask[size - 1] * identity_mat - jnp.dot(
        tail_keys.T, wy_rows, precision=precise
    )
    contribution = jnp.dot(tail_keys.T, base_rows, precision=precise)
    return (transition, contribution, base_rows, wy_rows)


def group_output(queries, key_rows, same_doc, carry_mask, base_rows, wy_rows, state_in):
    size = key_rows.shape[0]
    lower = jnp.tril(jnp.ones((size, size), jnp.float32)) * same_doc
    written = base_rows - jnp.dot(wy_rows, state_in, precision=precise)
    scores = jnp.dot(queries, key_rows.T, precision=precise) * lower
    carried = carry_mask[:, None] * jnp.dot(queries, state_in, precision=precise)
    return carried + jnp.dot(scores, written, precision=precise)


def group_full(queries, key_rows, value_rows, rates, same_doc, carry_mask, state_in):
    transition, contribution, base_rows, wy_rows = group_parts(
        key_rows, value_rows, rates, same_doc, carry_mask
    )
    outputs = group_output(queries, key_rows, same_doc, carry_mask, base_rows, wy_rows, state_in)
    return (outputs, jnp.dot(transition, state_in, precision=precise) + contribution)


def state_pull(queries, key_rows, same_doc, carry_mask, wy_rows, grad_rows):
    size = key_rows.shape[0]
    lower = jnp.tril(jnp.ones((size, size), jnp.float32)) * same_doc
    scores = jnp.dot(queries, key_rows.T, precision=precise) * lower
    pulled = jnp.dot(scores.T, grad_rows, precision=precise)
    direct = jnp.dot((carry_mask[:, None] * queries).T, grad_rows, precision=precise)
    return direct - jnp.dot(wy_rows.T, pulled, precision=precise)


def group_grads(
    queries, key_rows, value_rows, rates, same_doc, carry_mask, state_in, grad_rows, grad_end
):

    def group_local(query_in, key_in, value_in, rate_in):
        return group_full(query_in, key_in, value_in, rate_in, same_doc, carry_mask, state_in)

    outputs, pullback = jax.vjp(group_local, queries, key_rows, value_rows, rates)
    return pullback((grad_rows, grad_end))


def local(
    block_input,
    grad_out,
    doc_lengths,
    attn_gain,
    mlp_gain,
    out_gain,
    conv_weight,
    qkv_weight,
    beta_weight,
    o_weight,
    gate_up_weight,
    down_weight,
):
    tok_rows = block_input.shape[1]
    model_width = block_input.shape[2]
    blocks = tok_rows // GROUP
    unit_floor = DK / 16.0
    x_rows = block_input[0].astype(jnp.float32)
    grad_rows_out = grad_out[0]
    qkv_full, beta_full, o_full, gate_up_full, down_full = (
        lax.all_gather(qkv_weight, ("row", "seq"), axis=1, tiled=True),
        lax.all_gather(beta_weight, ("row", "seq"), axis=0, tiled=True),
        lax.all_gather(o_weight, ("row", "seq"), axis=1, tiled=True),
        lax.all_gather(gate_up_weight, ("row", "seq"), axis=1, tiled=True),
        lax.all_gather(down_weight, ("row", "seq"), axis=1, tiled=True),
    )
    local_width = qkv_full.shape[2]
    head_count = local_width // DK
    lead_mask = (lax.axis_index("tp") == 0).astype(jnp.float32)
    ends = jnp.cumsum(doc_lengths[0])
    places = (
        lax.axis_index("seq") * tok_rows + jnp.arange(tok_rows + KW - 1, dtype=jnp.int32) - (KW - 1)
    )
    doc_ids = jnp.sum((places[:, None] >= ends[None, :]).astype(jnp.int32), axis=1)
    doc_ids = jnp.where(places < 0, -1, doc_ids)
    own_docs = doc_ids[KW - 1 :]
    prior_docs = doc_ids[KW - 2 : KW - 2 + tok_rows]
    valid = (own_docs < DOCS).astype(jnp.float32)
    fresh = (own_docs != prior_docs).astype(jnp.int32)
    tap_masks = [
        (doc_ids[KW - 1 - tap : KW - 1 - tap + tok_rows] == own_docs).astype(jnp.float32)
        for tap in range(KW)
    ]
    own_blocks = own_docs.reshape(blocks, GROUP)
    same_doc = (own_blocks[:, :, None] == own_blocks[:, None, :]).astype(jnp.float32)
    carry_mask = (jnp.cumsum(fresh.reshape(blocks, GROUP), axis=1) == 0).astype(jnp.float32)

    def to_blocks(array):
        return array.reshape(blocks, GROUP, head_count, -1).transpose(2, 0, 1, 3)

    def from_blocks(array):
        return array.transpose(1, 2, 0, 3).reshape(tok_rows, head_count, -1)

    scale_one = norm_scale(x_rows)
    normed_one = (x_rows * scale_one * attn_gain).astype(jnp.bfloat16)
    proj_low = jnp.einsum(
        "td,cde->cte", normed_one, qkv_full, preferred_element_type=jnp.float32
    ).astype(jnp.bfloat16)
    logit = jnp.dot(normed_one, beta_full, preferred_element_type=jnp.float32)
    rim_rows = from_behind(proj_low[:, tok_rows - (KW - 1) :, :], "seq", 1)
    extended = jnp.concatenate([rim_rows, proj_low], axis=1).astype(jnp.float32)
    conv_out = jnp.zeros((3, tok_rows, local_width), jnp.float32)
    for tap in range(KW):
        window = extended[:, KW - 1 - tap : KW - 1 - tap + tok_rows]
        conv_out = (
            conv_out + conv_weight[:, tap][:, None, :] * window * tap_masks[tap][None, :, None]
        )
    conv_sig = jax.nn.sigmoid(conv_out)
    activated = conv_out * conv_sig
    query_raw = activated[0].reshape(tok_rows, head_count, DK)
    key_raw = activated[1].reshape(tok_rows, head_count, DK)
    query_sq = jnp.sum(query_raw * query_raw, axis=-1, keepdims=True)
    key_sq = jnp.sum(key_raw * key_raw, axis=-1, keepdims=True)
    query_scale = lax.rsqrt(jnp.maximum(query_sq, unit_floor))
    key_scale = lax.rsqrt(jnp.maximum(key_sq, unit_floor))
    query_live = (query_sq > unit_floor).astype(jnp.float32)
    key_live = (key_sq > unit_floor).astype(jnp.float32)
    query_blocks = to_blocks(query_raw * query_scale)
    key_blocks = to_blocks(key_raw * key_scale)
    value_blocks = to_blocks(activated[2].reshape(tok_rows, head_count, DK))
    rate_sig = jax.nn.sigmoid(logit)
    rate_blocks = (rate_sig * valid[:, None]).reshape(blocks, GROUP, head_count).transpose(2, 0, 1)
    transition, contribution, base_rows, wy_rows = over_heads(group_parts, (0, 0, 0, None, None))(
        key_blocks, value_blocks, rate_blocks, same_doc, carry_mask
    )
    identity_mat = jnp.broadcast_to(jnp.eye(DK, dtype=jnp.float32), (head_count, DK, DK))
    zero_state = jnp.zeros((head_count, DK, DK), jnp.float32)
    transition_steps = jnp.moveaxis(transition, 1, 0)

    def chain(running, pair):
        product, partial_state = running
        step_trans, step_contrib = pair
        advanced = (
            batch_mul(step_trans, product),
            batch_mul(step_trans, partial_state) + step_contrib,
        )
        return (advanced, (product, partial_state))

    (dev_trans, dev_state), (products, partials) = lax.scan(
        chain, (identity_mat, zero_state), (transition_steps, jnp.moveaxis(contribution, 1, 0))
    )
    incoming = prefix((dev_trans, dev_state), "seq", compose, (identity_mat, zero_state), False)[1]
    group_starts = partials + jnp.einsum("nhij,hjk->nhik", products, incoming, precision=precise)
    start_blocks = jnp.moveaxis(group_starts, 0, 1)
    mix_blocks = over_heads(group_output, (0, 0, None, None, 0, 0, 0))(
        query_blocks, key_blocks, same_doc, carry_mask, base_rows, wy_rows, start_blocks
    )
    mixed = from_blocks(mix_blocks) * valid[:, None, None]
    mix_sq = jnp.mean(mixed * mixed, axis=-1, keepdims=True)
    mix_scale = lax.rsqrt(jnp.maximum(mix_sq, mix_floor))
    mix_live = (mix_sq > mix_floor).astype(jnp.float32)
    normed_mix = (mixed * mix_scale * out_gain).astype(jnp.bfloat16).reshape(tok_rows, local_width)
    o_term = jnp.dot(normed_mix, o_full, preferred_element_type=jnp.float32)
    resid = x_rows + tp_total(o_term)
    scale_two = norm_scale(resid)
    normed_local = (resid * scale_two * mlp_gain).astype(jnp.bfloat16)
    gate_up = jnp.einsum(
        "td,cdf->ctf", normed_local, gate_up_full, preferred_element_type=jnp.float32
    )
    gate_sig = jax.nn.sigmoid(gate_up[0])
    gate_act = gate_up[0] * gate_sig
    hidden = (gate_act * gate_up[1]).astype(jnp.bfloat16)
    down_term = jnp.dot(hidden, down_full, preferred_element_type=jnp.float32)
    mlp_out = tp_total(down_term)
    result = (resid + mlp_out).astype(jnp.bfloat16)
    grad_hidden = jnp.einsum(
        "td,fd->tf", grad_rows_out, down_full, preferred_element_type=jnp.float32
    )
    grad_gate = grad_hidden * gate_up[1] * gate_sig * (1.0 + gate_up[0] * (1.0 - gate_sig))
    grad_up = grad_hidden * gate_act
    grad_gate_up = jnp.stack([grad_gate, grad_up]).astype(jnp.bfloat16)
    down_part = jnp.einsum("tf,td->fd", hidden, grad_rows_out, preferred_element_type=jnp.float32)
    gate_up_part = jnp.einsum(
        "td,ctf->cdf", normed_local, grad_gate_up, preferred_element_type=jnp.float32
    )
    two_term = jnp.einsum(
        "ctf,cdf->td", grad_gate_up, gate_up_full, preferred_element_type=jnp.float32
    )
    grad_two = tp_total(two_term)
    mlp_gain_part = jnp.sum(grad_two * resid * scale_two, axis=0)
    grad_resid = grad_rows_out.astype(jnp.float32) + norm_back(resid, scale_two, mlp_gain, grad_two)
    grad_attn_local = grad_resid.astype(jnp.bfloat16)
    o_part = jnp.einsum(
        "te,td->ed", normed_mix, grad_attn_local, preferred_element_type=jnp.float32
    )
    grad_normed = jnp.einsum(
        "td,ed->te", grad_attn_local, o_full, preferred_element_type=jnp.float32
    ).reshape(tok_rows, head_count, DK)
    out_gain_part = jnp.sum(grad_normed * mixed * mix_scale, axis=(0, 1))
    weighted_mix = out_gain * grad_normed
    grad_mixed = (
        mix_scale * weighted_mix
        - mixed * mix_scale**3 * mix_live * jnp.mean(weighted_mix * mixed, axis=-1, keepdims=True)
    ) * valid[:, None, None]
    grad_blocks = to_blocks(grad_mixed)
    pulls = over_heads(state_pull, (0, 0, None, None, 0, 0))(
        query_blocks, key_blocks, same_doc, carry_mask, wy_rows, grad_blocks
    )

    def back_chain(running, pair):
        grad_end, product = running
        step_trans, step_pull = pair
        advanced = (step_pull + batch_mul_t(step_trans, grad_end), batch_mul_t(step_trans, product))
        return (advanced, (grad_end, product))

    (dev_pull, dev_back), (grad_ends, back_products) = lax.scan(
        back_chain,
        (zero_state, identity_mat),
        (transition_steps, jnp.moveaxis(pulls, 1, 0)),
        reverse=True,
    )
    outgoing = prefix((dev_back, dev_pull), "seq", compose, (identity_mat, zero_state), True)[1]
    end_grads = grad_ends + jnp.einsum("nhij,hjk->nhik", back_products, outgoing, precision=precise)
    grad_query, grad_key, grad_value, grad_rate = over_heads(
        group_grads, (0, 0, 0, 0, None, None, 0, 0, 0)
    )(
        query_blocks,
        key_blocks,
        value_blocks,
        rate_blocks,
        same_doc,
        carry_mask,
        start_blocks,
        grad_blocks,
        jnp.moveaxis(end_grads, 0, 1),
    )
    grad_query = from_blocks(grad_query)
    grad_key = from_blocks(grad_key)
    grad_query_raw = query_scale * grad_query - query_raw * query_scale**3 * query_live * jnp.sum(
        query_raw * grad_query, axis=-1, keepdims=True
    )
    grad_key_raw = key_scale * grad_key - key_raw * key_scale**3 * key_live * jnp.sum(
        key_raw * grad_key, axis=-1, keepdims=True
    )
    grad_activated = jnp.stack(
        [
            grad_query_raw.reshape(tok_rows, local_width),
            grad_key_raw.reshape(tok_rows, local_width),
            from_blocks(grad_value).reshape(tok_rows, local_width),
        ]
    )
    grad_conv = grad_activated * conv_sig * (1.0 + conv_out * (1.0 - conv_sig))
    grad_extended = jnp.zeros((3, tok_rows + KW - 1, local_width), jnp.float32)
    tap_grads = []
    for tap in range(KW):
        masked = grad_conv * tap_masks[tap][None, :, None]
        window = extended[:, KW - 1 - tap : KW - 1 - tap + tok_rows]
        tap_grads.append(jnp.sum(masked * window, axis=1))
        grad_extended = grad_extended + jnp.pad(
            conv_weight[:, tap][:, None, :] * masked, ((0, 0), (KW - 1 - tap, tap), (0, 0))
        )
    conv_part = jnp.stack(tap_grads, axis=1)
    rim_back = from_behind(grad_extended[:, : KW - 1], "seq", -1)
    grad_proj = jnp.concatenate(
        [grad_extended[:, KW - 1 : tok_rows], grad_extended[:, tok_rows:] + rim_back], axis=1
    ).astype(jnp.bfloat16)
    rate_grad = grad_rate.transpose(1, 2, 0).reshape(tok_rows, head_count)
    grad_logit = (rate_grad * valid[:, None] * rate_sig * (1.0 - rate_sig)).astype(jnp.bfloat16)
    qkv_part = jnp.einsum("td,cte->cde", normed_one, grad_proj, preferred_element_type=jnp.float32)
    beta_part = jnp.einsum("td,th->dh", normed_one, grad_logit, preferred_element_type=jnp.float32)
    grad_one_part = jnp.einsum(
        "cte,cde->td", grad_proj, qkv_full, preferred_element_type=jnp.float32
    ) + jnp.einsum("th,dh->td", grad_logit, beta_full, preferred_element_type=jnp.float32)
    grad_one = tp_total(grad_one_part)
    attn_gain_part = jnp.sum(grad_one * x_rows * scale_one, axis=0)
    input_local = (grad_resid + norm_back(x_rows, scale_one, attn_gain, grad_one)).astype(
        jnp.bfloat16
    )
    conv_whole = lax.dynamic_update_slice(
        jnp.zeros((3, KW, model_width), jnp.float32),
        conv_part,
        (0, 0, lax.axis_index("tp") * local_width),
    )
    attn_gain_grad, mlp_gain_grad, out_gain_grad, conv_grad = lax.psum(
        (attn_gain_part * lead_mask, mlp_gain_part * lead_mask, out_gain_part, conv_whole),
        ("row", "seq", "tp"),
    )
    qkv_sum, beta_sum, o_sum, gate_up_sum, down_sum = (
        lax.psum_scatter(
            qkv_part.astype(jnp.bfloat16), ("row", "seq"), scatter_dimension=1, tiled=True
        ).astype(jnp.float32),
        lax.psum_scatter(
            beta_part.astype(jnp.bfloat16), ("row", "seq"), scatter_dimension=0, tiled=True
        ).astype(jnp.float32),
        lax.psum_scatter(
            o_part.astype(jnp.bfloat16), ("row", "seq"), scatter_dimension=1, tiled=True
        ).astype(jnp.float32),
        lax.psum_scatter(
            gate_up_part.astype(jnp.bfloat16), ("row", "seq"), scatter_dimension=1, tiled=True
        ).astype(jnp.float32),
        lax.psum_scatter(
            down_part.astype(jnp.bfloat16), ("row", "seq"), scatter_dimension=1, tiled=True
        ).astype(jnp.float32),
    )
    return (
        result[None],
        input_local[None],
        attn_gain_grad,
        mlp_gain_grad,
        out_gain_grad,
        conv_grad,
        qkv_sum,
        beta_sum,
        o_sum,
        gate_up_sum,
        down_sum,
    )


def solution(mesh):
    in_specs = (
        P("row", "seq", None),
        P("row", "seq", None),
        P("row", None),
        P(),
        P(),
        P(),
        P(None, None, "tp"),
        P(None, ("row", "seq"), "tp"),
        P(("row", "seq"), "tp"),
        P("tp", ("row", "seq")),
        P(None, ("row", "seq"), "tp"),
        P("tp", ("row", "seq")),
    )
    out_specs = (
        P("row", "seq", None),
        P("row", "seq", None),
        P(),
        P(),
        P(),
        P(),
        P(None, ("row", "seq"), "tp"),
        P(("row", "seq"), "tp"),
        P("tp", ("row", "seq")),
        P(None, ("row", "seq"), "tp"),
        P("tp", ("row", "seq")),
    )
    return jax.shard_map(local, mesh=mesh, in_specs=in_specs, out_specs=out_specs, check_vma=False)
```

profile of v0, /device:TPU:8, one launch (start us, length us, event | category | flops | bytes accessed | tf_op | source)
XLA Modules:
  0.0 2571.5 jit_solution(17202493832168915003)
XLA Ops:
  9.4 37.2 %all_gather.40 = bf16[2048,8]{0,1:T(8,128)(2,1)S(1)} all-gather(bf16[128,8]{0,1:T(8,128)(2,1)} %param.30), channel_id=1, replica_groups=mesh['row'=4,'seq'=4,'tp'=2] {'row','seq'}, dimensions={0}, use_global_device_ids=true | all-gather | bytes 34816 | tf_op jit(solution)/shard_map/all_gather | solution.py:157
  52.3 110.2 %all-gather.13.cloned.1.call-done = bf16[3,2048,1024]{2,1,0:T(8,128)(2,1)} async-done(((bf16[3,128,1024]{2,1,0:T(8,128)(2,1)}), bf16[3,2048,1024]{2,1,0:T(8,128)(2,1)}) %all-gather.13.cloned.1.call-update) | async-done | bytes 12582928 | tf_op jit(solution)/shard_map/all_gather | solution.py:156
  162.4 8.1 fusion.95
  170.6 4.3 collective-permute-start
  177.0 3.6 fusion.41
  192.1 158.9 %custom-call.15 = f32[8,4,1,64,64]{3,4,2,1,0:T(8,128)} custom-call(f32[8,4,1,64,64]{4,3,2,1,0:T(8,128)} %select_bitcast_fusion.2), custom_call_target="InvertDiagBlocksLowerTriangular" | custom-call | tf_op jit(solution)/shard_map/vmap(vmap(jit(_solve_triangular)))/triangular_solve/custom-call.1 | solution.py:86
  351.0 3.8 fusion.70
  354.8 5.2 convolution_bitcast_fusion.3
  360.0 5.2 subtract_bitcast_fusion.1
  369.1 36.8 %while.68 = (s32[]{:T(128)}, f32[8,128,128]{2,1,0:T(8,128)}, f32[8,128,128]{2,1,0:T(8,128)}, f32[4,8,128,128]{3,2,0,1:T(8,128)}, f32[4,8,128,128]{2,3,0,1:T(8,12...) while((s32[]{:T(128)}, f32[8,128,128]{2,1,0:T(8,128)}, ...), condition=%wide.region_7.9_spmd.clone, body=%wide.region_6.8_spmd.clone.sunk | while | flops 403046400 | bytes 9963131 | solution.py:234
  410.2 10.5 all-reduce.13.cloned.1.call-start
  424.2 4.3 convolution_multiply_fusion.1
  428.6 7.1 all-gather.21.cloned.1.call-done
  435.7 29.6 %all-gather.23.cloned.1.call-done = bf16[32,128,128]{2,1,0:T(8,128)(2,1)} async-done(((bf16[8,128,128]{2,1,0:T(8,128)(2,1)}), bf16[32,128,128]{2,1,0:T(8,128)(2,1)}) %all-gather.23.cloned.1.call-update) | async-done | bytes 1048592 | tf_op jit(solution)/shard_map/all_gather | solution.py:26
  465.3 6.3 while.69
  471.6 4.4 bitcast_add_fusion.1
  476.1 4.2 fusion.109
  480.3 4.1 fusion.106
  490.4 64.3 %all-gather.15.cloned.1.call-done = bf16[1024,2048]{1,0:T(8,128)(2,1)} async-done(((bf16[1024,128]{1,0:T(8,128)(2,1)}), bf16[1024,2048]{1,0:T(8,128)(2,1)}) %all-gather.15.cloned.1.call-update) | async-done | bytes 4194320 | tf_op jit(solution)/shard_map/all_gather | solution.py:158
  554.8 4.4 convolution_convert_fusion.3
  561.0 18.3 all-reduce.13.cloned.1.call-done
  581.0 251.8 %all-gather.17.cloned.1.call-done = bf16[2,2048,2816]{2,1,0:T(8,128)(2,1)} async-done(((bf16[2,128,2816]{2,1,0:T(8,128)(2,1)}), bf16[2,2048,2816]{2,1,0:T(8,128)(2,1)}) %all-gather.17.cloned.1.call-update) | async-done | bytes 23068688 | tf_op jit(solution)/shard_map/all_gather | solution.py:159
  832.8 12.8 convolution_bitcast_fusion
  845.5 171.1 %all-gather.19.cloned.1.call-done = bf16[2816,2048]{1,0:T(8,128)(2,1)} async-done(((bf16[2816,128]{1,0:T(8,128)(2,1)}), bf16[2816,2048]{1,0:T(8,128)(2,1)}) %all-gather.19.cloned.1.call-update) | async-done | bytes 11534352 | tf_op jit(solution)/shard_map/all_gather | solution.py:160
  1016.6 11.6 fusion.99
  1028.2 12.4 fusion.50
  1040.7 20.0 all-reduce.15.cloned.1.call-done
  1063.7 5.9 fusion.132
  1073.8 3.4 fusion.135
  1077.3 3.8 fusion.137
  1081.1 4.9 subtract_bitcast_fusion
  1089.9 36.1 %while.70 = (s32[]{:T(128)}, f32[8,128,128]{2,1,0:T(8,128)}, f32[8,128,128]{2,1,0:T(8,128)}, f32[4,8,128,128]{2,3,0,1:T(8,128)}, f32[4,8,128,128]{3,2,0,1:T(8,12...) while((s32[]{:T(128)}, f32[8,128,128]{2,1,0:T(8,128)}, ...), condition=%wide.region_19.21_spmd.clone, body=%wide.region_18.20_spmd.clone.sunk | while | flops 403046400 | bytes 12060331 | solution.py:301
  1100.2 3.1 convolution_add_fusion.12
  1145.4 10.4 convolution_convert_fusion.2
  1175.0 4.2 fusion.80
  1179.3 7.3 all-gather.27.cloned.1.call-done
  1186.6 17.9 while.71
  1204.5 4.5 bitcast_add_fusion
  1209.0 4.4 fusion.115
  1213.4 3.7 fusion.76
  1224.6 3.2 fusion.93
  1233.3 6.2 fusion.121
  1248.9 21.8 fusion.38
  1277.1 5.7 multiply_subtract_fusion.1
  1283.3 3.3 multiply_reduce_fusion.3
  1296.3 6.3 pad_add_fusion
  1305.3 6.5 convolution_bitcast_fusion.1
  1313.6 5.0 convolution_convert_fusion.1
  1318.6 6.4 copy.259
  1325.1 10.5 convolution_convert_fusion
  1335.6 15.3 copy.263
  1351.0 8.1 convert_bitcast_fusion.1
  1359.1 27.5 %copy.255 = bf16[3,2048,1024]{2,0,1:T(4,128)(2,1)} copy(bf16[3,2048,1024]{1,2,0:T(8,128)(2,1)} %convert_bitcast_fusion.1) | data formatting | bytes 25165824
  1386.6 16.6 copy.317
  1403.5 12.8 convert_bitcast_fusion
  1416.3 56.7 %copy.261 = bf16[2,2048,2816]{2,0,1:T(2,128)(2,1)} copy(bf16[2,2048,2816]{1,2,0:T(8,128)(2,1)} %convert_bitcast_fusion) | data formatting | bytes 46137344
  1473.0 24.3 copy.318
  1502.4 4.2 fusion.129
  1506.5 44.9 %all-reduce.6 = (f32[2048]{0:T(1024)}, f32[2048]{0:T(1024)}, f32[128]{0:T(128)}) all-reduce(f32[2048]{0:T(1024)S(1)} %broadcast_multiply_fusion.4, f32[2048]{0:T(1024)S(1)} %broadcast_multiply_fusion.3, f32[128]{0:T(128)S(1)} %bitcast_reduce_fusion), channel_id=1, replica_groups=mesh['row'=4,'seq'=4,'tp'=2] {'row','seq','tp'}, use_global_device_ids=true, to_apply=%region_29.31 | all-reduce | flops 4224 | bytes 33792 | tf_op jit(solution)/shard_map/psum | solution.py:369
  1553.4 190.6 %reduce-scatter.24.cloned.1.call-done = bf16[128,2816]{1,0:T(8,128)(2,1)} async-done(((bf16[2048,2816]{1,0:T(8,128)(2,1)}), bf16[128,2816]{1,0:T(8,128)(2,1)}) %reduce-scatter.24.cloned.1.call-update) | async-done | bytes 720912
  1746.7 209.8 %reduce-scatter.16.cloned.1.call-done = bf16[128,3072]{1,0:T(8,128)(2,1)} async-done(((bf16[2048,3072]{1,0:T(8,128)(2,1)}), bf16[128,3072]{1,0:T(8,128)(2,1)}) %reduce-scatter.16.cloned.1.call-update) | async-done | bytes 786448
  1961.5 469.9 %reduce-scatter.22.cloned.1.call-done = bf16[128,5632]{1,0:T(8,128)(2,1)} async-done(((bf16[2048,5632]{1,0:T(8,128)(2,1)}), bf16[128,5632]{1,0:T(8,128)(2,1)}) %reduce-scatter.22.cloned.1.call-update) | async-done | bytes 1441808
  2431.4 3.4 reshape.431
  2438.7 124.6 %all-reduce.17.cloned.1.call-done = f32[3,4,2048]{2,1,0:T(4,128)} async-done(((f32[3,4,2048]{2,1,0:T(4,128)}), f32[3,4,2048]{2,1,0:T(4,128)}) %all-reduce.17.cloned.1.call-update) | async-done | bytes 98320 | tf_op jit(solution)/shard_map/psum | solution.py:369
  (478 shorter events, 248.5 us)
Async XLA Ops:
  7.2 44.7 %copy-start.79 = (f32[3,4,1024]{2,1,0:T(4,128)S(1)}, f32[3,4,1024]{2,1,0:T(4,128)}, u32[]{:S(2)}) copy-start(f32[3,4,1024]{2,1,0:T(4,128)} %param.28) | copy-start | bytes 147460
  7.2 155.3 %all-gather.13.cloned.1.call-start = ((), (), s32[]{:S(2)}) async-start(), calls=%async_computation.5 | async-start | bytes 13369344 | tf_op jit(solution)/shard_map/all_gather | solution.py:156
  7.9 427.8 %all-gather.21.cloned.1.call-start = ((), (), s32[]{:S(2)}) async-start(), calls=%async_computation.12 | async-start | bytes 1310720 | tf_op jit(solution)/shard_map/all_gather | solution.py:26
  9.2 153.3 %copy-start.4 = (bf16[1,256,2048]{2,1,0:T(8,128)(2,1)S(1)}, bf16[1,256,2048]{2,1,0:T(8,128)(2,1)}, u32[]{:S(2)}) copy-start(bf16[1,256,2048]{2,1,0:T(8,128)(2,1)} %param.22) | copy-start | bytes 3145732
  9.2 153.3 %copy-start.83 = (f32[2048]{0:T(1024)S(1)}, f32[2048]{0:T(1024)}, u32[]{:S(2)}) copy-start(f32[2048]{0:T(1024)} %param.25) | copy-start | bytes 24580
  46.6 5.5 copy-start.73
  49.0 121.5 %copy-start.93 = (f32[256]{0:T(256)}, f32[256]{0:T(256)S(1)}, u32[]{:S(2)}) copy-start(f32[256]{0:T(256)S(1)} %get-tuple-element.717) | copy-start | bytes 3076
  49.1 127.9 %copy-start.85 = (f32[256]{0:T(256)}, f32[256]{0:T(256)S(1)}, u32[]{:S(2)}) copy-start(f32[256]{0:T(256)S(1)} %get-tuple-element.708) | copy-start | bytes 3076
  49.1 127.9 %copy-start.87 = (f32[256]{0:T(256)}, f32[256]{0:T(256)S(1)}, u32[]{:S(2)}) copy-start(f32[256]{0:T(256)S(1)} %get-tuple-element.710) | copy-start | bytes 3076
  49.1 127.9 %copy-start.89 = (f32[256]{0:T(256)}, f32[256]{0:T(256)S(1)}, u32[]{:S(2)}) copy-start(f32[256]{0:T(256)S(1)} %get-tuple-element.711) | copy-start | bytes 3076
  49.1 1020.5 %copy-start.91 = (f32[256]{0:T(256)}, f32[256]{0:T(256)S(1)}, u32[]{:S(2)}) copy-start(f32[256]{0:T(256)S(1)} %get-tuple-element.709) | copy-start | bytes 3076
  51.8 134.8 %copy-start.63 = (f32[8,4,64]{2,1,0:T(4,128)}, f32[8,4,64]{2,1,0:T(4,128)S(1)}, u32[]{:S(2)}) copy-start(f32[8,4,64]{2,1,0:T(4,128)S(1)} %broadcast_multiply_fusion.2) | copy-start | bytes 24580
  51.9 125.1 %copy-start.65 = (f32[3,1024]{1,0:T(4,128)}, f32[3,1024]{1,0:T(4,128)S(1)}, u32[]{:S(2)}) copy-start(f32[3,1024]{1,0:T(4,128)S(1)} %get-tuple-element.728) | copy-start | bytes 36868
  51.9 125.1 %copy-start.67 = (f32[3,1024]{1,0:T(4,128)}, f32[3,1024]{1,0:T(4,128)S(1)}, u32[]{:S(2)}) copy-start(f32[3,1024]{1,0:T(4,128)S(1)} %get-tuple-element.729) | copy-start | bytes 36868
  52.0 125.0 %copy-start.69 = (f32[3,1024]{1,0:T(4,128)}, f32[3,1024]{1,0:T(4,128)S(1)}, u32[]{:S(2)}) copy-start(f32[3,1024]{1,0:T(4,128)S(1)} %get-tuple-element.730) | copy-start | bytes 36868
  52.0 125.0 %copy-start.71 = (f32[3,1024]{1,0:T(4,128)}, f32[3,1024]{1,0:T(4,128)S(1)}, u32[]{:S(2)}) copy-start(f32[3,1024]{1,0:T(4,128)S(1)} %get-tuple-element.731) | copy-start | bytes 36868
  52.3 138.5 %copy-start.57 = (f32[4,64,64]{2,1,0:T(8,128)}, f32[4,64,64]{2,1,0:T(8,128)S(1)}, u32[]{:S(2)}) copy-start(f32[4,64,64]{2,1,0:T(8,128)S(1)} %get-tuple-element.707) | copy-start | bytes 196612
  170.6 5.9 collective-permute-start
  175.0 15.8 copy-start.75
  354.8 5.2 copy-start.6
  405.9 14.8 copy-start.96
  407.8 57.6 %all-gather.23.cloned.1.call-start = ((), (), s32[]{:S(2)}) async-start(), calls=%async_computation.13 | async-start | bytes 1310720 | tf_op jit(solution)/shard_map/all_gather | solution.py:26
  409.6 145.2 %all-gather.15.cloned.1.call-start = ((), (), s32[]{:S(2)}) async-start(), calls=%async_computation.6 | async-start | bytes 4456448 | tf_op jit(solution)/shard_map/all_gather | solution.py:158
  410.2 169.1 %all-reduce.13.cloned.1.call-start = ((), (), s32[]{:S(2)}) async-start(), calls=%async_computation.7 | async-start | bytes 2097152 | tf_op jit(solution)/shard_map/psum | solution.py:75
  490.4 68.8 %copy-start.60 = (bf16[256,1024]{1,0:T(8,128)(2,1)}, bf16[256,1024]{1,0:T(8,128)(2,1)S(1)}, u32[]{:S(2)}) copy-start(bf16[256,1024]{1,0:T(8,128)(2,1)S(1)} %fusion.131) | copy-start | bytes 1572868
  559.2 273.6 %copy-start.62 = (f32[2048]{0:T(1024)S(1)}, f32[2048]{0:T(1024)}, u32[]{:S(2)}) copy-start(f32[2048]{0:T(1024)} %param.26) | copy-start | bytes 24580
  559.2 273.5 %all-gather.17.cloned.1.call-start = ((), (), s32[]{:S(2)}) async-start(), calls=%async_computation.8 | async-start | bytes 24510464 | tf_op jit(solution)/shard_map/all_gather | solution.py:159
  559.8 456.8 %all-gather.19.cloned.1.call-start = ((), (), s32[]{:S(2)}) async-start(), calls=%async_computation.9 | async-start | bytes 12255232 | tf_op jit(solution)/shard_map/all_gather | solution.py:160
  560.6 500.1 %all-reduce.15.cloned.1.call-start = ((), (), s32[]{:S(2)}) async-start(), calls=%async_computation.10 | async-start | bytes 2097152 | tf_op jit(solution)/shard_map/psum | solution.py:75
  580.9 482.7 %copy-start.77 = (f32[256]{0:T(256)}, f32[256]{0:T(256)S(1)}, u32[]{:S(2)}) copy-start(f32[256]{0:T(256)S(1)} %get-tuple-element.719) | copy-start | bytes 3076
  580.9 482.7 %copy-start.98 = (f32[256]{0:T(256)}, f32[256]{0:T(256)S(1)}, u32[]{:S(2)}) copy-start(f32[256]{0:T(256)S(1)} %get-tuple-element.718) | copy-start | bytes 3076
  1040.6 138.6 %all-gather.25.cloned.1.call-start = ((), (), s32[]{:S(2)}) async-start(), calls=%async_computation.14 | async-start | bytes 1310720 | tf_op jit(solution)/shard_map/all_gather | solution.py:26
  1063.6 5.9 copy-start.100
  1063.7 5.9 copy-start.29
  1073.8 84.3 %copy-start.21 = (f32[4,64,8,128]{3,1,0,2:T(8,128)}, f32[4,64,8,128]{3,1,0,2:T(8,128)S(1)}, u32[]{:S(2)}) copy-start(f32[4,64,8,128]{3,1,0,2:T(8,128)S(1)} %fusion.163) | copy-start | bytes 3145732
  1127.9 58.7 %all-gather.27.cloned.1.call-start = ((), (), s32[]{:S(2)}) async-start(), calls=%async_computation.15 | async-start | bytes 1310720 | tf_op jit(solution)/shard_map/all_gather | solution.py:26
  1145.4 12.7 copy-start.46
  1157.6 341.2 %reduce-scatter.18.cloned.1.call-start = ((), (), s32[]{:S(2)}) async-start(), calls=%async_computation.17 | async-start | bytes 557056
  1233.3 6.2 copy-start.15
  1233.3 6.2 copy-start.32
  1233.3 6.2 copy-start.35
  1233.3 6.2 copy-start.64
  1248.8 22.9 copy-start.42
  1271.8 5.3 copy-start.25
  1277.1 5.8 copy-start.1
  1277.1 5.9 copy-start.33
  1277.1 6.2 copy-start.48
  1277.1 6.2 copy-start.86
  1277.1 6.2 copy-start.88
  1277.1 6.1 copy-start.90
  1288.8 7.0 copy-start.92
  1288.8 7.0 copy-start.95
  1288.8 7.0 copy-start.5
  1288.8 7.0 copy-start.84
  1288.8 7.0 copy-start.94
  1293.2 11.0 collective-permute-start.1
  1304.2 196.1 %all-reduce.19.cloned.1.call-start = ((), (), s32[]{:S(2)}) async-start(), calls=%async_computation.21 | async-start | bytes 4194304 | tf_op jit(solution)/shard_map/psum | solution.py:75
  1305.3 6.5 copy-start.74
  1313.3 238.1 %reduce-scatter.20.cloned.1.call-start = ((), (), s32[]{:S(2)}) async-start(), calls=%async_computation.18 | async-start | bytes 4456448
  1325.1 418.9 %reduce-scatter.24.cloned.1.call-start = ((), (), s32[]{:S(2)}) async-start(), calls=%async_computation.20 | async-start | bytes 12255232
  1351.0 605.5 %reduce-scatter.16.cloned.1.call-start = ((), (), s32[]{:S(2)}) async-start(), calls=%async_computation.16 | async-start | bytes 13369344
  1403.2 1028.2 %reduce-scatter.22.cloned.1.call-start = ((), (), s32[]{:S(2)}) async-start(), calls=%async_computation.19 | async-start | bytes 24510464
  1497.4 5.0 copy-start.97
  1497.4 1065.9 %all-reduce.17.cloned.1.call-start = ((), (), s32[]{:S(2)}) async-start(), calls=%async_computation.11 | async-start | bytes 196608 | tf_op jit(solution)/shard_map/psum | solution.py:369
  (61 other events, 166.1 us)
Sparse Core Ops, SparseCore 0:
  10.8 151.5 all-gather.12
  407.9 27.7 all-gather.20
  437.9 27.4 all-gather.22
  467.9 86.8 all-gather.14
  559.3 19.8 all-reduce.12
  582.3 250.3 all-gather.16
  835.8 180.7 all-gather.18
  1040.8 19.8 all-reduce.14
  1128.0 28.7 all-gather.24
  1158.2 28.2 all-gather.26
  1304.3 72.7 reduce-scatter.17
  1380.1 22.4 all-reduce.18
  1404.9 94.3 reduce-scatter.19
  1501.4 242.5 reduce-scatter.23
  1749.5 206.8 reduce-scatter.15
  1958.7 472.5 reduce-scatter.21
  2438.3 124.8 all-reduce.16
where the time goes:
time: 2580 us; the launch traced here: 2570 us
  waiting for transfers between devices  1680 us (65%)
  matrix products  269 us (10%)
  local copies, waits for them, and re-layouts  265 us (10%)
  other arithmetic  241 us (9%)
  blocking collectives  82.1 us (3%)
    unnamed x22, waiting for transfers between devices  873 us
    all_gather x1, waiting for transfers between devices, local(): lax.all_gather(gate_up_weight, ('row', 'seq'), axis=1, tiled=True)  252 us
    unnamed x228, local copies, waits for them, and re-layouts  182 us
    all_gather x1, waiting for transfers between devices, local(): lax.all_gather(down_weight, ('row', 'seq'), axis=1, tiled=True)  171 us
    another operation x3, other arithmetic, group_parts(): solved = jax.scipy.linalg.solve_triangular(system, right_side, lower=True)  160 us
    psum x1, waiting for transfers between devices, local(): lax.psum((attn_gain_part * lead_mask, mlp_gain_part * lead_mask, out_gain...  125 us
    all_gather x1, waiting for transfers between devices, local(): lax.all_gather(qkv_weight, ('row', 'seq'), axis=1, tiled=True)  110 us
    all_gather x1, waiting for transfers between devices, local(): lax.all_gather(o_weight, ('row', 'seq'), axis=1, tiled=True)  64.3 us
  transfers between devices with their start and end apart: 19, of which 14 were waited for; matrix products, arithmetic and copies ran while one was open for 13% of the time, Pallas kernels for 0%

commit v1 on v0

--- a/solution.py
+++ b/solution.py
@@ -132,7 +132,7 @@
     return pullback((grad_rows, grad_end))
 
 
-def local(
+def local_pieces(
     block_input,
     grad_out,
     doc_lengths,
@@ -402,6 +402,375 @@
     )
 
 
+CHUNK = 128
+
+
+def lower_inverse(strict_part):
+    size = strict_part.shape[-1]
+    at = jnp.arange(size, dtype=jnp.int32)
+
+    def joins(half):
+        outer = (at[:, None] // (2 * half)) == (at[None, :] // (2 * half))
+        return jnp.where(outer & (at[:, None] // half != at[None, :] // half), strict_part, 0.0)
+
+    inverse = jnp.eye(size, dtype=jnp.float32) - joins(1)
+    half = 2
+    while half < size:
+        inverse = inverse - wide_mul(inverse, wide_mul(joins(half), inverse))
+        half *= 2
+    return inverse
+
+
+def wide_mul(left, right):
+    return jnp.einsum("...ij,...jk->...ik", left, right, precision=precise)
+
+
+def wide_mul_nt(left, right):
+    return jnp.einsum("...ij,...kj->...ik", left, right, precision=precise)
+
+
+def wide_mul_tn(left, right):
+    return jnp.einsum("...ji,...jk->...ik", left, right, precision=precise)
+
+
+def row_masks(doc_ids):
+    chunks = doc_ids.reshape(-1, CHUNK)
+    same = chunks[:, :, None] == chunks[:, None, :]
+    at = jnp.arange(CHUNK, dtype=jnp.int32)
+    lower = at[:, None] >= at[None, :]
+    strict = at[:, None] > at[None, :]
+    prior = jnp.concatenate([jnp.full((1,), -1, jnp.int32), chunks[:-1, -1]])
+    return (
+        (same & lower).astype(jnp.float32),
+        (same & strict).astype(jnp.float32),
+        same[:, -1, :].astype(jnp.float32),
+        (chunks == prior[:, None]).astype(jnp.float32),
+    )
+
+
+def mixer_forward(queries, key_rows, value_rows, rates, masks):
+    lower, strict, tail, carry = masks
+    system = rates[..., None] * wide_mul_nt(key_rows, key_rows) * strict
+    inverse = lower_inverse(system)
+    base = wide_mul(inverse, rates[..., None] * value_rows)
+    read = wide_mul(inverse, (rates * carry)[..., None] * key_rows)
+    scores = wide_mul_nt(queries, key_rows) * lower
+    tail_keys = tail[:, :, None] * key_rows
+
+    def step(state, parts):
+        base_n, read_n, tail_n, carry_n = parts
+        written = base_n - wide_mul(read_n, state)
+        after = carry_n * state + wide_mul_tn(tail_n, written)
+        return after, (state, written)
+
+    heads = queries.shape[0]
+    start = jnp.zeros((heads, DK, DK), jnp.float32)
+    _, (states, written) = lax.scan(
+        step,
+        start,
+        (
+            jnp.moveaxis(base, 1, 0),
+            jnp.moveaxis(read, 1, 0),
+            jnp.moveaxis(tail_keys, 1, 0),
+            carry[:, -1],
+        ),
+    )
+    states, written = jnp.moveaxis(states, 0, 1), jnp.moveaxis(written, 0, 1)
+    mixed = carry[:, :, None] * wide_mul(queries, states) + wide_mul(scores, written)
+    return mixed, (inverse, states, written)
+
+
+def mixer_backward(queries, key_rows, value_rows, rates, masks, saved, grads):
+    lower, strict, tail, carry = masks
+    inverse, states, written = saved
+    rate_col = rates[..., None]
+    carry_col = carry[:, :, None]
+    scores = wide_mul_nt(queries, key_rows) * lower
+    pulled = wide_mul_tn(scores, grads)
+    tail_keys = tail[:, :, None] * key_rows
+    direct = wide_mul_tn(carry_col * queries, grads)
+    carried_keys = rate_col * carry_col * key_rows
+
+    def step(grad_state, parts):
+        pulled_n, tail_n, inverse_n, carried_n, direct_n, carry_n = parts
+        grad_solved = wide_mul_tn(inverse_n, pulled_n + wide_mul(tail_n, grad_state))
+        before = carry_n * grad_state + direct_n - wide_mul_tn(carried_n, grad_solved)
+        return before, (grad_state, grad_solved)
+
+    heads = queries.shape[0]
+    _, (grad_states, grad_solved) = lax.scan(
+        step,
+        jnp.zeros((heads, DK, DK), jnp.float32),
+        (
+            jnp.moveaxis(pulled, 1, 0),
+            jnp.moveaxis(tail_keys, 1, 0),
+            jnp.moveaxis(inverse, 1, 0),
+            jnp.moveaxis(carried_keys, 1, 0),
+            jnp.moveaxis(direct, 1, 0),
+            carry[:, -1],
+        ),
+        reverse=True,
+    )
+    grad_states, grad_solved = jnp.moveaxis(grad_states, 0, 1), jnp.moveaxis(grad_solved, 0, 1)
+    grad_scores = wide_mul_nt(grads, written) * lower
+    grad_query = carry_col * wide_mul_nt(grads, states) + wide_mul(grad_scores, key_rows)
+    grad_key = wide_mul_tn(grad_scores, queries) + tail[:, :, None] * wide_mul_nt(
+        written, grad_states
+    )
+    guess_error = value_rows - carry_col * wide_mul(key_rows, states)
+    grad_value = rate_col * grad_solved
+    gram = wide_mul_nt(key_rows, key_rows) * strict
+    grad_system = -wide_mul_nt(grad_solved, written) * strict
+    grad_rate = jnp.sum(grad_solved * guess_error, axis=-1) + jnp.sum(
+        grad_system * gram, axis=-1
+    )
+    grad_gram = rate_col * grad_system
+    grad_key = (
+        grad_key
+        - rate_col * carry_col * wide_mul_nt(grad_solved, states)
+        + wide_mul(grad_gram, key_rows)
+        + wide_mul_tn(grad_gram, key_rows)
+    )
+    return grad_query, grad_key, grad_value, grad_rate
+
+
+def spread(shard, pieces, axis):
+    rows, width = shard.shape
+    parts = shard.reshape(rows, pieces, width // pieces).transpose(1, 0, 2)
+    return lax.all_to_all(parts, axis, 0, 0, tiled=True)
+
+
+def gathered(shard):
+    pieces = lax.axis_size("seq")
+    parts = spread(shard, pieces, "seq")
+    whole = lax.all_gather(parts, "row", axis=0, tiled=True)
+    return whole.reshape(-1, whole.shape[-1])
+
+
+def returned(part):
+    pieces = lax.axis_size("seq")
+    rows = part.shape[0] // (pieces * lax.axis_size("row"))
+    own = lax.psum_scatter(part, "row", scatter_dimension=0, tiled=True)
+    own = own.reshape(pieces, rows, -1)
+    return lax.all_to_all(own, "seq", 0, 0, tiled=True)
+
+
+def token_gather(own):
+    return lax.all_gather(own, ("seq", "tp"), axis=0, tiled=True)
+
+
+def token_sum(term):
+    return lax.psum_scatter(
+        term.astype(jnp.bfloat16), ("seq", "tp"), scatter_dimension=0, tiled=True
+    ).astype(jnp.float32)
+
+
+def both_cores(own):
+    cores = lax.axis_size("tp")
+    if cores == 1:
+        return own
+    other = lax.ppermute(own, "tp", [(0, 1), (1, 0)])
+    first = lax.axis_index("tp") == 0
+    return jnp.concatenate([jnp.where(first, own, other), jnp.where(first, other, own)], axis=0)
+
+
+def shifted(rows, by):
+    if by == 0:
+        return rows
+    pad = jnp.zeros((abs(by),) + rows.shape[1:], rows.dtype)
+    if by > 0:
+        return jnp.concatenate([pad, rows[:-by]], axis=0)
+    return jnp.concatenate([rows[-by:], pad], axis=0)
+
+
+def local_heads(
+    block_input,
+    grad_out,
+    doc_lengths,
+    attn_gain,
+    mlp_gain,
+    out_gain,
+    conv_weight,
+    qkv_weight,
+    beta_weight,
+    o_weight,
+    gate_up_weight,
+    down_weight,
+):
+    tok_rows, model_width = block_input.shape[1:]
+    pieces, cores = lax.axis_size("seq"), lax.axis_size("tp")
+    piece, core = lax.axis_index("seq"), lax.axis_index("tp")
+    row_len = pieces * tok_rows
+    own_rows = tok_rows // cores
+    unit_floor = DK / 16.0
+    shard_rows = qkv_weight.shape[1]
+    half_width = qkv_weight.shape[2]
+    width = half_width // pieces
+    heads = width // DK
+    units = gate_up_weight.shape[2] // pieces
+    chunks = row_len // CHUNK
+    f32, b16 = jnp.float32, jnp.bfloat16
+
+    qkv_parts = qkv_weight.reshape(3, shard_rows, pieces, width).transpose(1, 2, 0, 3)
+    qkv_full = gathered(qkv_parts.reshape(shard_rows, -1))
+    beta_full = lax.all_gather(beta_weight, ("row", "seq"), axis=0, tiled=True)
+    beta_full = lax.dynamic_slice_in_dim(beta_full, piece * heads, heads, axis=1)
+    o_full = gathered(o_weight.T)
+    gate_up_parts = gate_up_weight.reshape(2, shard_rows, pieces, units).transpose(1, 2, 0, 3)
+    gate_up_full = gathered(gate_up_parts.reshape(shard_rows, -1))
+    down_full = gathered(down_weight.T)
+
+    ends = jnp.cumsum(doc_lengths[0])
+    places = jnp.arange(row_len, dtype=jnp.int32)
+    docs = jnp.sum((places[:, None] >= ends[None, :]).astype(jnp.int32), axis=1)
+    padded_docs = jnp.concatenate([jnp.full((KW - 1,), -1, jnp.int32), docs])
+    valid = (docs < DOCS).astype(f32)
+    tap_masks = [
+        (padded_docs[KW - 1 - tap : KW - 1 - tap + row_len] == docs).astype(f32)[:, None]
+        for tap in range(KW)
+    ]
+    masks = row_masks(docs)
+    taps = lax.dynamic_slice_in_dim(conv_weight, piece * width, width, axis=2)
+    taps = taps.transpose(1, 0, 2).reshape(KW, 3 * width)
+
+    def to_chunks(array):
+        return array.reshape(chunks, CHUNK, heads, -1).transpose(2, 0, 1, 3)
+
+    def from_chunks(array):
+        return array.transpose(1, 2, 0, 3).reshape(row_len, heads, -1)
+
+    x_rows = lax.dynamic_slice_in_dim(block_input[0], core * own_rows, own_rows, axis=0)
+    x_rows = x_rows.astype(f32)
+    g_rows = lax.dynamic_slice_in_dim(grad_out[0], core * own_rows, own_rows, axis=0)
+    scale_one = norm_scale(x_rows)
+    normed_one = token_gather((x_rows * scale_one * attn_gain).astype(b16))
+    g_full = token_gather(g_rows)
+    proj = jnp.dot(normed_one, qkv_full, preferred_element_type=f32).astype(b16).astype(f32)
+    logit = jnp.dot(normed_one, beta_full, preferred_element_type=f32)
+    conv_out = sum(taps[tap] * shifted(proj, tap) * tap_masks[tap] for tap in range(KW))
+    conv_sig = jax.nn.sigmoid(conv_out)
+    activated = (conv_out * conv_sig).reshape(row_len, 3, heads, DK)
+    query_raw, key_raw = activated[:, 0], activated[:, 1]
+    query_sq = jnp.sum(query_raw * query_raw, axis=-1, keepdims=True)
+    key_sq = jnp.sum(key_raw * key_raw, axis=-1, keepdims=True)
+    query_scale = lax.rsqrt(jnp.maximum(query_sq, unit_floor))
+    key_scale = lax.rsqrt(jnp.maximum(key_sq, unit_floor))
+    query_live = (query_sq > unit_floor).astype(f32)
+    key_live = (key_sq > unit_floor).astype(f32)
+    query_chunks = to_chunks(query_raw * query_scale)
+    key_chunks = to_chunks(key_raw * key_scale)
+    value_chunks = to_chunks(activated[:, 2])
+    rate_sig = jax.nn.sigmoid(logit)
+    rate_chunks = (rate_sig * valid[:, None]).T.reshape(heads, chunks, CHUNK)
+    mix_chunks, saved = mixer_forward(query_chunks, key_chunks, value_chunks, rate_chunks, masks)
+    mixed = from_chunks(mix_chunks) * valid[:, None, None]
+    mix_sq = jnp.mean(mixed * mixed, axis=-1, keepdims=True)
+    mix_scale = lax.rsqrt(jnp.maximum(mix_sq, mix_floor))
+    mix_live = (mix_sq > mix_floor).astype(f32)
+    normed_mix = (mixed * mix_scale * out_gain).astype(b16).reshape(row_len, width)
+    o_term = jnp.einsum("te,de->td", normed_mix, o_full, preferred_element_type=f32)
+    resid = x_rows + token_sum(o_term)
+    scale_two = norm_scale(resid)
+    normed_two = token_gather((resid * scale_two * mlp_gain).astype(b16))
+    gate_up = jnp.dot(normed_two, gate_up_full, preferred_element_type=f32)
+    gate, up = gate_up[:, :units], gate_up[:, units:]
+    gate_sig = jax.nn.sigmoid(gate)
+    gate_act = gate * gate_sig
+    hidden = (gate_act * up).astype(b16)
+    grad_hidden = jnp.dot(g_full, down_full, preferred_element_type=f32)
+    grad_gate = grad_hidden * up * gate_sig * (1.0 + gate * (1.0 - gate_sig))
+    grad_up = grad_hidden * gate_act
+    grad_gate_up = jnp.concatenate([grad_gate, grad_up], axis=1).astype(b16)
+    two_term = jnp.einsum("tf,df->td", grad_gate_up, gate_up_full, preferred_element_type=f32)
+    grad_two = token_sum(two_term)
+    mlp_gain_part = jnp.sum(grad_two * resid * scale_two, axis=0)
+    grad_resid = g_rows.astype(f32) + norm_back(resid, scale_two, mlp_gain, grad_two)
+    grad_attn = token_gather(grad_resid.astype(b16))
+    down_term = jnp.einsum("tf,df->td", hidden, down_full, preferred_element_type=f32)
+    result = both_cores((resid + token_sum(down_term)).astype(b16))
+    down_part = jnp.einsum("td,tf->df", g_full, hidden, preferred_element_type=f32)
+    gate_up_part = jnp.einsum("td,tf->df", normed_two, grad_gate_up, preferred_element_type=f32)
+    o_part = jnp.einsum("td,te->de", grad_attn, normed_mix, preferred_element_type=f32)
+    grad_normed = jnp.dot(grad_attn, o_full, preferred_element_type=f32)
+    grad_normed = grad_normed.reshape(row_len, heads, DK)
+    out_gain_part = jnp.sum(grad_normed * mixed * mix_scale, axis=(0, 1))
+    weighted_mix = out_gain * grad_normed
+    grad_mixed = (
+        mix_scale * weighted_mix
+        - mixed * mix_scale**3 * mix_live * jnp.mean(weighted_mix * mixed, axis=-1, keepdims=True)
+    ) * valid[:, None, None]
+    grad_query, grad_key, grad_value, grad_rate = mixer_backward(
+        query_chunks, key_chunks, value_chunks, rate_chunks, masks, saved, to_chunks(grad_mixed)
+    )
+    grad_query, grad_key = from_chunks(grad_query), from_chunks(grad_key)
+    grad_query_raw = query_scale * grad_query - query_raw * query_scale**3 * query_live * jnp.sum(
+        query_raw * grad_query, axis=-1, keepdims=True
+    )
+    grad_key_raw = key_scale * grad_key - key_raw * key_scale**3 * key_live * jnp.sum(
+        key_raw * grad_key, axis=-1, keepdims=True
+    )
+    grad_activated = jnp.stack([grad_query_raw, grad_key_raw, from_chunks(grad_value)], axis=1)
+    grad_conv = grad_activated.reshape(row_len, -1) * conv_sig * (1.0 + conv_out * (1.0 - conv_sig))
+    grad_proj = jnp.zeros_like(proj)
+    tap_grads = []
+    for tap in range(KW):
+        masked = grad_conv * tap_masks[tap]
+        tap_grads.append(jnp.sum(masked * shifted(proj, tap), axis=0))
+        grad_proj = grad_proj + taps[tap] * shifted(masked, -tap)
+    grad_proj = grad_proj.astype(b16)
+    conv_part = jnp.stack(tap_grads).reshape(KW, 3, width).transpose(1, 0, 2)
+    rate_grad = grad_rate.reshape(heads, row_len).T
+    grad_logit = (rate_grad * valid[:, None] * rate_sig * (1.0 - rate_sig)).astype(b16)
+    one_term = jnp.einsum("te,de->td", grad_proj, qkv_full, preferred_element_type=f32)
+    one_term = one_term + jnp.einsum("th,dh->td", grad_logit, beta_full, preferred_element_type=f32)
+    grad_one = token_sum(one_term)
+    attn_gain_part = jnp.sum(grad_one * x_rows * scale_one, axis=0)
+    input_grad = both_cores(
+        (grad_resid + norm_back(x_rows, scale_one, attn_gain, grad_one)).astype(b16)
+    )
+    qkv_part = jnp.einsum("td,te->de", normed_one, grad_proj, preferred_element_type=f32)
+    beta_part = jnp.einsum("td,th->dh", normed_one, grad_logit, preferred_element_type=f32)
+    beta_part = lax.dynamic_update_slice(
+        jnp.zeros((model_width, pieces * heads), f32), beta_part, (0, piece * heads)
+    )
+    conv_whole = lax.dynamic_update_slice(
+        jnp.zeros((3, KW, model_width), f32),
+        conv_part,
+        (0, 0, core * half_width + piece * width),
+    )
+    attn_gain_grad, mlp_gain_grad, out_gain_grad, conv_grad = lax.psum(
+        (attn_gain_part, mlp_gain_part, out_gain_part, conv_whole), ("row", "seq", "tp")
+    )
+    down_sum = returned(down_part.astype(b16))
+    gate_up_sum = returned(gate_up_part.astype(b16)).reshape(pieces, shard_rows, 2, units)
+    o_sum = returned(o_part.astype(b16))
+    qkv_sum = returned(qkv_part.astype(b16)).reshape(pieces, shard_rows, 3, width)
+    beta_sum = lax.psum_scatter(
+        beta_part.astype(b16), ("row", "seq"), scatter_dimension=0, tiled=True
+    ).astype(f32)
+    return (
+        result[None],
+        input_grad[None],
+        attn_gain_grad,
+        mlp_gain_grad,
+        out_gain_grad,
+        conv_grad,
+        qkv_sum.transpose(2, 1, 0, 3).reshape(3, shard_rows, -1).astype(f32),
+        beta_sum,
+        o_sum.transpose(0, 2, 1).reshape(-1, shard_rows).astype(f32),
+        gate_up_sum.transpose(2, 1, 0, 3).reshape(2, shard_rows, -1).astype(f32),
+        down_sum.transpose(0, 2, 1).reshape(-1, shard_rows).astype(f32),
+    )
+
+
+def splits_heads(mesh, heads=16, units=5632):
+    return (
+        mesh.shape["tp"] == 2
+        and heads % (mesh.shape["seq"] * 2) == 0
+        and units % (mesh.shape["seq"] * 2) == 0
+    )
+
+
 def solution(mesh):
     in_specs = (
         P("row", "seq", None),
@@ -430,4 +799,5 @@
         P(None, ("row", "seq"), "tp"),
         P("tp", ("row", "seq")),
     )
+    local = local_heads if splits_heads(mesh) else local_pieces
     return jax.shard_map(local, mesh=mesh, in_specs=in_specs, out_specs=out_specs, check_vma=False)

time: 2580 us -> 1190 us (0.46)
  waiting for transfers between devices: 1680 us -> 474 us
  other arithmetic: 241 us -> 67.1 us
  local copies, waits for them, and re-layouts: 265 us -> 91.5 us
  blocking collectives: 82.1 us -> 249 us
    unnamed x22 -> x19, waiting for transfers between devices: 873 us -> 24 us
    all_gather x8, waiting for transfers between devices: 641 us -> 206 us  [the longest x4 118 us: token_gather(): return lax.all_gather(own, ('seq', 'tp'), axis=0, tiled=True)]
    all_to_all x0 -> x4, blocking collectives: none -> 170 us  [the longest x3 128 us: spread(): return lax.all_to_all(parts, axis, 0, 0, tiled=True)]
    another operation x7 -> x2, other arithmetic: 162 us -> 2.1 us  [the longest x1 1.92 us: local_heads(): jnp.stack([grad_query_raw, grad_key_raw, from_chunks(grad_value)], axis=1)]
    unnamed x228 -> x149, local copies, waits for them, and re-layouts: 182 us -> 28.5 us
    reduce_scatter x0 -> x8, waiting for transfers between devices: none -> 152 us  [the longest x4 152 us: token_sum(): lax.psum_scatter(term.astype(jnp.bfloat16), ('seq', 'tp'), scatter_dimens...]
    psum x4 -> x1, waiting for transfers between devices: 163 us -> 76.9 us  [local_heads(): lax.psum((attn_gain_part, mlp_gain_part, out_gain_part, conv_whole), ('ro...]
    mul x13 -> x7, other arithmetic: 34.7 us -> 8.74 us  [the longest x1 4.93 us: local_heads(): activated = (conv_out * conv_sig).reshape(row_len, 3, heads, DK)]
  transfers between devices with their start and end apart: 19 -> 24, of which waited for: 14 -> 13; matrix products, arithmetic and copies ran while one was open for 13% -> 32% of each run, Pallas kernels for 0% -> 0%
where the time goes in v1:
time: 1190 us; the launch traced here: 1180 us
  waiting for transfers between devices  474 us (40%)
  matrix products  256 us (22%)
  blocking collectives  249 us (21%)
  local copies, waits for them, and re-layouts  91.5 us (8%)
  other arithmetic  67.1 us (6%)
  starting transfers between devices  25.4 us (2%)
  between operations  15.7 us (1%)
    reduce_scatter x4, waiting for transfers between devices, token_sum(): lax.psum_scatter(term.astype(jnp.bfloat16), ('seq', 'tp'), scatter_dimens...  152 us
    all_to_all x3, blocking collectives, spread(): return lax.all_to_all(parts, axis, 0, 0, tiled=True)  128 us
    all_gather x4, waiting for transfers between devices, token_gather(): return lax.all_gather(own, ('seq', 'tp'), axis=0, tiled=True)  118 us
    all_gather x4, waiting for transfers between devices, gathered(): whole = lax.all_gather(parts, 'row', axis=0, tiled=True)  88.5 us
    dot_general x35, matrix products, wide_mul(): return jnp.einsum('...ij,...jk->...ik', left, right, precision=precise)  80.1 us
    psum x1, waiting for transfers between devices, local_heads(): lax.psum((attn_gain_part, mlp_gain_part, out_gain_part, conv_whole), ('ro...  76.9 us
    dot_general x28, matrix products, wide_mul_tn(): return jnp.einsum('...ji,...jk->...ik', left, right, precision=precise)  58.2 us
    all_to_all x1, blocking collectives, returned(): return lax.all_to_all(own, 'seq', 0, 0, tiled=True)  42.8 us
  transfers between devices with their start and end apart: 24, of which 13 were waited for; matrix products, arithmetic and copies ran while one was open for 32% of the time, Pallas kernels for 0%

profile of v1, /device:TPU:8, one launch (start us, length us, event | category | flops | bytes accessed | tf_op | source)
XLA Modules:
  0.0 1179.6 jit_solution(16371512294969991190)
XLA Ops:
  12.7 42.2 %all_to_all.40 = bf16[4,128,768]{1,2,0:T(8,128)(2,1)S(1)} all-to-all(bf16[4,128,768]{1,2,0:T(8,128)(2,1)S(1)} %bitcast.561), channel_id=1, replica_groups=mesh['row'=4,'seq'=4,'tp'=2] {'seq'}, dimensions={0} | all-to-all | bytes 1572864 | tf_op jit(solution)/shard_map/all_to_all | solution.py:540
  56.1 6.5 all-to-all-start.1
  67.1 36.4 %all_gather.29 = bf16[2048,8]{0,1:T(8,128)(2,1)S(1)} all-gather(bf16[128,8]{0,1:T(8,128)(2,1)S(1)} %copy-done.57), channel_id=1, replica_groups=mesh['row'=4,'seq'=4,'tp'=2] {'row','seq'}, dimensions={0}, use_global_device_ids=true | all-gather | bytes 34816 | tf_op jit(solution)/shard_map/all_gather | solution.py:616
  104.7 3.8 fusion.58
  108.6 15.5 %all-gather.12.cloned.1.call-done = bf16[16,128,768]{2,1,0:T(8,128)(2,1)} async-done(((bf16[4,128,768]{2,1,0:T(8,128)(2,1)}), bf16[16,128,768]{2,1,0:T(8,128)(2,1)}) %all-gather.12.cloned.1.call-update) | async-done | bytes 3145744 | tf_op jit(solution)/shard_map/all_gather | solution.py:546
  124.1 6.2 fusion.40
  130.4 4.9 fusion.35
  137.1 2.6 copy.656
  146.6 5.2 multiply_multiply_fusion
  157.6 2.9 fusion.168
  162.6 2.9 fusion.207
  167.4 2.9 fusion.208
  172.1 3.2 fusion.209
  177.8 2.6 copy.530
  180.4 3.9 fusion.98
  184.4 5.6 bitcast_subtract_fusion
  190.0 3.4 convolution_bitcast_fusion.5
  193.4 2.9 convolution_bitcast_fusion.6
  200.3 41.1 %while.34 = (s32[]{:T(128)}, f32[2,128,128]{2,1,0:T(8,128)S(1)}, f32[8,2,128,128]{3,2,1,0:T(8,128)}, f32[8,2,128,128]{3,2,1,0:T(8,128)}, f32[8]{0:T(128)S(1)}, /...) while((s32[]{:T(128)}, f32[2,128,128]{2,1,0:T(8,128)S(1)}, ...), condition=%wide.region_6.7_spmd.clone, body=%wide.region_5.6_spmd.clone.sunk | while | flops 100859904 | bytes 1444477 | solution.py:468
  244.1 3.5 convolution_multiply_fusion.5
  249.9 2.9 multiply_reduce_fusion.8
  259.9 4.8 convolution_convert_fusion.3
  268.8 62.4 %all_to_all.41 = bf16[4,128,1408]{1,2,0:T(8,128)(2,1)} all-to-all(bf16[4,128,1408]{1,2,0:T(8,128)(2,1)S(1)} %bitcast.553), channel_id=1, replica_groups=mesh['row'=4,'seq'=4,'tp'=2] {'seq'}, dimensions={0} | all-to-all | bytes 2883584 | tf_op jit(solution)/shard_map/all_to_all | solution.py:540
  333.7 9.2 reduce-scatter.12.cloned.1.call-done
  346.7 23.0 %all_to_all.42 = bf16[4,128,704]{1,2,0:T(8,128)(2,1)} all-to-all(bf16[4,128,704]{1,2,0:T(8,128)(2,1)} %bitcast.568), channel_id=1, replica_groups=mesh['row'=4,'seq'=4,'tp'=2] {'seq'}, dimensions={0} | all-to-all | bytes 1441792 | tf_op jit(solution)/shard_map/all_to_all | solution.py:540
  371.8 41.0 %all-gather.18.cloned.1.call-done = bf16[16,128,1408]{2,1,0:T(8,128)(2,1)} async-done(((bf16[4,128,1408]{2,1,0:T(8,128)(2,1)}), bf16[16,128,1408]{2,1,0:T(8,128)(2,1)}) %all-gather.18.cloned.1.call-update) | async-done | bytes 5767184 | tf_op jit(solution)/shard_map/all_gather | solution.py:546
  412.8 47.7 %all-gather.16.cloned.1.call-done = bf16[1024,2048]{1,0:T(8,128)(2,1)} async-done(((bf16[128,2048]{1,0:T(8,128)(2,1)}), bf16[1024,2048]{1,0:T(8,128)(2,1)}) %all-gather.16.cloned.1.call-update) | async-done | bytes 4194320 | tf_op jit(solution)/shard_map/all_gather | solution.py:559
  460.5 12.0 %fusion.210 = f32[1024,1408]{1,0:T(8,128)} fusion(bf16[1024,2048]{1,0:T(8,128)(2,1)} %all-gather.16.cloned.1.call-done, bf16[2048,1408]{1,0:T(8,128)(2,1)} %bitcast.584), kind=kOutput, calls=%fused_computation.390 | convolution fusion | flops 5905580032 | bytes 15728640 | tf_op jit(solution)/shard_map/dot_general | solution.py:675
  472.5 31.9 %all-gather.20.cloned.1.call-done = bf16[16,128,704]{1,2,0:T(8,128)(2,1)} async-done(((bf16[4,128,704]{1,2,0:T(8,128)(2,1)}), bf16[16,128,704]{1,2,0:T(8,128)(2,1)}) %all-gather.20.cloned.1.call-update) | async-done | bytes 2883600 | tf_op jit(solution)/shard_map/all_gather | solution.py:546
  504.4 47.8 %all-gather.24.cloned.1.call-done = bf16[1,1024,2048]{2,1,0:T(8,128)(2,1)} async-done(((bf16[1,128,2048]{2,1,0:T(8,128)(2,1)}), bf16[1,1024,2048]{2,1,0:T(8,128)(2,1)}) %all-gather.24.cloned.1.call-update) | async-done | bytes 4194320 | tf_op jit(solution)/shard_map/all_gather | solution.py:559
  552.3 10.3 multiply_convert_fusion.1
  564.2 8.3 convolution_convert_fusion.1
  572.6 46.5 %reduce-scatter.16.cloned.1.call-done = bf16[128,2048]{1,0:T(8,128)(2,1)} async-done(((bf16[1024,2048]{1,0:T(8,128)(2,1)}), bf16[128,2048]{1,0:T(8,128)(2,1)}) %reduce-scatter.16.cloned.1.call-update) | async-done | bytes 524304 | tf_op jit(solution)/shard_map/reduce_scatter | solution.py:563
  620.8 2.8 fusion.204
  623.6 7.5 fusion.30
  636.9 12.1 %convolution_convert_fusion = bf16[2048,1408]{1,0:T(8,128)(2,1)} fusion(bf16[1024,2048]{1,0:T(8,128)(2,1)} %all-gather.16.cloned.1.call-done, bf16[1024,704]{1,0:T(8,128)(2,1)S(1)} %copy-done.67, bf16[1024,704]{1,0:T(8,128)(2,1)S(1)} %copy-done.65), kind=kOutput, calls=%fused_computation.34 | convolution fusion | flops 5914230784 | bytes 12845056 | tf_op jit(solution)/shard_map/td,tf->df/dot_general | solution.py:692
  649.1 22.3 %all-gather.22.cloned.1.call-done = bf16[1024,2048]{1,0:T(8,128)(2,1)} async-done(((bf16[128,2048]{1,0:T(8,128)(2,1)}), bf16[1024,2048]{1,0:T(8,128)(2,1)}) %all-gather.22.cloned.1.call-update) | async-done | bytes 4194320 | tf_op jit(solution)/shard_map/all_gather | solution.py:559
  671.4 4.3 multiply_reduce_fusion.4
  684.4 3.1 fusion.49
  687.5 2.6 copy.560
  690.0 4.4 convolution_bitcast_fusion.3
  696.6 51.8 %while.35 = (s32[]{:T(128)}, f32[2,128,128]{2,1,0:T(8,128)S(1)}, f32[8,2,128,128]{3,2,1,0:T(8,128)}, f32[8,2,128,128]{3,2,1,0:T(8,128)}, f32[8]{0:T(128)S(1)}, /...) while((s32[]{:T(128)}, f32[2,128,128]{2,1,0:T(8,128)S(1)}, ...), condition=%wide.region_16.17_spmd.clone, body=%wide.region_15.16_spmd.clone.sunk | while | flops 151224320 | bytes 1970851 | solution.py:501
  753.0 3.6 fusion.92
  772.7 3.6 copy.588
  776.3 4.7 convolution_convert_fusion.5
  781.0 4.3 multiply_reduce_fusion.3
  785.4 4.1 multiply_reduce_fusion.2
  794.5 4.9 convolution_convert_fusion.4
  802.0 3.9 fusion.55
  807.6 7.6 fusion.211
  815.3 6.7 add_convert_fusion
  823.9 6.4 convolution_convert_fusion.2
  832.4 5.0 all-to-all-start.7
  839.2 14.3 %all-to-all-done.7 = bf16[4,128,704]{1,2,0:T(8,128)(2,1)S(1)} async-done(((bf16[4,128,704]{1,2,0:T(8,128)(2,1)}), bf16[4,128,704]{1,2,0:T(8,128)(2,1)S(1)}, u32[]{:S(2)}, u32[]{:S(2)}) %all-to-all-start.7) | async-done | bytes 720928 | tf_op jit(solution)/shard_map/all_to_all | solution.py:555
  853.5 42.8 %all_to_all.43 = bf16[4,128,1408]{1,2,0:T(8,128)(2,1)} all-to-all(bf16[4,128,1408]{1,2,0:T(8,128)(2,1)S(1)} %copy.595), channel_id=1, replica_groups=mesh['row'=4,'seq'=4,'tp'=2] {'seq'}, dimensions={0} | all-to-all | bytes 2883584 | tf_op jit(solution)/shard_map/all_to_all | solution.py:555
  896.2 5.3 all-to-all-start.5
  905.4 3.4 copy.599
  911.3 5.1 all-to-all-start.4
  917.4 23.7 %reduce-scatter.28.cloned.1.call-done = bf16[128,8]{1,0:T(8,128)(2,1)} async-done(((bf16[2048,8]{1,0:T(8,128)(2,1)}), bf16[128,8]{1,0:T(8,128)(2,1)}) %reduce-scatter.28.cloned.1.call-update) | async-done | bytes 2064
  942.5 47.7 %reduce-scatter.18.cloned.1.call-done = bf16[128,2048]{1,0:T(8,128)(2,1)} async-done(((bf16[1024,2048]{1,0:T(8,128)(2,1)}), bf16[128,2048]{1,0:T(8,128)(2,1)}) %reduce-scatter.18.cloned.1.call-update) | async-done | bytes 524304 | tf_op jit(solution)/shard_map/reduce_scatter | solution.py:563
  991.6 49.0 %reduce-scatter.14.cloned.1.call-done = bf16[128,2048]{1,0:T(8,128)(2,1)} async-done(((bf16[1024,2048]{1,0:T(8,128)(2,1)}), bf16[128,2048]{1,0:T(8,128)(2,1)}) %reduce-scatter.14.cloned.1.call-update) | async-done | bytes 524304 | tf_op jit(solution)/shard_map/reduce_scatter | solution.py:563
  1040.6 3.1 fusion.61
  1048.8 41.8 %all-reduce.7 = (f32[2048]{0:T(1024)}, f32[2048]{0:T(1024)}, f32[128]{0:T(128)}) all-reduce(f32[2048]{0:T(1024)S(1)} %get-tuple-element.484, f32[2048]{0:T(1024)S(1)} %get-tuple-element.482, f32[128]{0:T(128)S(1)} %get-tuple-element.480), channel_id=1, replica_groups=mesh['row'=4,'seq'=4,'tp'=2] {'row','seq','tp'}, use_global_device_ids=true, to_apply=%region_23.24 | all-reduce | flops 4224 | bytes 33792 | tf_op jit(solution)/shard_map/psum | solution.py:741
  1094.1 76.9 %all-reduce.10.cloned.1.call-done = f32[3,4,2048]{2,1,0:T(4,128)} async-done(((f32[3,4,2048]{2,1,0:T(4,128)}), f32[3,4,2048]{2,1,0:T(4,128)}) %all-reduce.10.cloned.1.call-update) | async-done | bytes 98320 | tf_op jit(solution)/shard_map/psum | solution.py:741
  (393 shorter events, 231.1 us)
Async XLA Ops:
  7.2 57.5 %copy-start = (f32[3,4,1024]{2,1,0:T(4,128)S(1)}, f32[3,4,1024]{2,1,0:T(4,128)}, u32[]{:S(2)}) copy-start(f32[3,4,1024]{2,1,0:T(4,128)} %param.22) | copy-start | bytes 147460
  7.2 97.5 %all-gather.10.cloned.1.call-start = ((), (), s32[]{:S(2)}) async-start(), calls=%async_computation.17 | async-start | bytes 4718592 | tf_op jit(solution)/shard_map/all_gather | solution.py:559
  9.0 3.6 copy-start.55
  11.1 113.1 %all-gather.12.cloned.1.call-start = ((), (), s32[]{:S(2)}) async-start(), calls=%async_computation.18 | async-start | bytes 3932160 | tf_op jit(solution)/shard_map/all_gather | solution.py:546
  12.6 50.0 %copy-start.63 = (s32[1,8]{1,0:T(1,128)S(1)}, s32[1,8]{1,0:T(1,128)}, u32[]{:S(2)}) copy-start(s32[1,8]{1,0:T(1,128)} %param.18) | copy-start | bytes 100
  54.9 12.2 %copy-start.57 = (bf16[128,8]{0,1:T(8,128)(2,1)S(1)}, bf16[128,8]{0,1:T(8,128)(2,1)}, u32[]{:S(2)}) copy-start(bf16[128,8]{0,1:T(8,128)(2,1)} %param.24) | copy-start | bytes 6148
  56.1 47.7 %all-to-all-start.1 = ((bf16[4,128,256]{1,2,0:T(8,128)(2,1)}), bf16[4,128,256]{1,2,0:T(8,128)(2,1)S(1)}, u32[]{:S(2)}, u32[]{:S(2)}) async-start(bf16[4,128,256]{1,2,0:T(8,128)(2,1)} %bitcast.32), calls=%async_computation.1 | async-start | bytes 524288 | tf_op jit(solution)/shard_map/all_to_all | solution.py:540
  62.7 197.3 %all-gather.14.cloned.1.call-start = ((), (), s32[]{:S(2)}) async-start(), calls=%async_computation.19 | async-start | bytes 1310720 | tf_op jit(solution)/shard_map/all_gather | solution.py:546
  103.5 5.0 copy-start.49
  104.6 238.3 %reduce-scatter.12.cloned.1.call-start = ((), (), s32[]{:S(2)}) async-start(), calls=%async_computation.20 | async-start | bytes 4718592 | tf_op jit(solution)/shard_map/reduce_scatter | solution.py:563
  108.5 21.8 %copy-start.46 = (f32[1024,2]{0,1:T(2,128)}, f32[1024,2]{0,1:T(2,128)S(1)}, u32[]{:S(2)}) copy-start(f32[1024,2]{0,1:T(2,128)S(1)} %fusion.58) | copy-start | bytes 24580
  151.8 18.4 %copy-start.7 = (f32[2,8,128,128]{2,3,1,0:T(8,128)}, f32[2,8,128,128]{2,3,1,0:T(8,128)S(1)}, u32[]{:S(2)}) copy-start(f32[2,8,128,128]{2,3,1,0:T(8,128)S(1)} %get-tuple-element.592) | copy-start | bytes 3145732
  155.6 4.9 copy-start.22
  177.8 6.5 copy-start.53
  180.4 4.0 copy-start.20
  180.4 4.0 copy-start.23
  180.4 4.0 copy-start.28
  184.4 5.6 copy-start.2
  196.3 4.1 copy-start.60
  244.0 3.5 copy-start.11
  244.0 3.6 copy-start.37
  244.0 5.9 copy-start.17
  244.1 5.9 copy-start.54
  249.9 5.4 copy-start.58
  264.7 148.1 %all-gather.18.cloned.1.call-start = ((), (), s32[]{:S(2)}) async-start(), calls=%async_computation.22 | async-start | bytes 7208960 | tf_op jit(solution)/shard_map/all_gather | solution.py:546
  331.1 13.3 %copy-start.45 = (f32[2048]{0:T(1024)S(1)}, f32[2048]{0:T(1024)}, u32[]{:S(2)}) copy-start(f32[2048]{0:T(1024)} %param.20) | copy-start | bytes 24580
  333.7 126.8 %all-gather.16.cloned.1.call-start = ((), (), s32[]{:S(2)}) async-start(), calls=%async_computation.21 | async-start | bytes 4718592 | tf_op jit(solution)/shard_map/all_gather | solution.py:559
  346.7 157.8 %all-gather.20.cloned.1.call-start = ((), (), s32[]{:S(2)}) async-start(), calls=%async_computation.23 | async-start | bytes 3604480 | tf_op jit(solution)/shard_map/all_gather | solution.py:546
  369.8 182.5 %all-gather.24.cloned.1.call-start = ((), (), s32[]{:S(2)}) async-start(), calls=%async_computation.33 | async-start | bytes 4718592 | tf_op jit(solution)/shard_map/all_gather | solution.py:559
  371.7 247.3 %reduce-scatter.16.cloned.1.call-start = ((), (), s32[]{:S(2)}) async-start(), calls=%async_computation.25 | async-start | bytes 4718592 | tf_op jit(solution)/shard_map/reduce_scatter | solution.py:563
  552.3 11.9 %copy-start.61 = (bf16[16,128,1408]{2,1,0:T(8,128)(2,1)S(1)}, bf16[16,128,1408]{2,1,0:T(8,128)(2,1)}, u32[]{:S(2)}) copy-start(bf16[16,128,1408]{2,1,0:T(8,128)(2,1)} %all-gather.18.cloned.1.call-done) | copy-start | bytes 17301508
  572.5 98.9 %all-gather.22.cloned.1.call-start = ((), (), s32[]{:S(2)}) async-start(), calls=%async_computation.26 | async-start | bytes 4718592 | tf_op jit(solution)/shard_map/all_gather | solution.py:559
  623.6 206.7 %reduce-scatter.26.cloned.1.call-start = ((), (), s32[]{:S(2)}) async-start(), calls=%async_computation.32 | async-start | bytes 3604480 | tf_op jit(solution)/shard_map/reduce_scatter | solution.py:553
  631.1 206.3 %reduce-scatter.24.cloned.1.call-start = ((), (), s32[]{:S(2)}) async-start(), calls=%async_computation.31 | async-start | bytes 7208960 | tf_op jit(solution)/shard_map/reduce_scatter | solution.py:553
  649.0 247.2 %reduce-scatter.22.cloned.1.call-start = ((), (), s32[]{:S(2)}) async-start(), calls=%async_computation.30 | async-start | bytes 1310720 | tf_op jit(solution)/shard_map/reduce_scatter | solution.py:553
  671.4 4.4 copy-start.33
  675.8 4.0 copy-start.18
  675.8 4.0 copy-start.38
  677.4 4.7 copy-start.13
  677.4 4.7 copy-start.12
  679.8 4.6 copy-start.4
  750.9 5.7 copy-start.19
  750.9 5.7 copy-start.40
  753.0 6.0 copy-start.15
  753.0 6.0 copy-start.34
  781.0 127.9 %reduce-scatter.20.cloned.1.call-start = ((), (), s32[]{:S(2)}) async-start(), calls=%async_computation.29 | async-start | bytes 3932160 | tf_op jit(solution)/shard_map/reduce_scatter | solution.py:553
  799.4 6.5 copy-start.47
  799.4 141.6 %reduce-scatter.28.cloned.1.call-start = ((), (), s32[]{:S(2)}) async-start(), calls=%async_computation.34 | async-start | bytes 557056
  802.0 4.0 copy-start.9
  815.3 174.9 %reduce-scatter.18.cloned.1.call-start = ((), (), s32[]{:S(2)}) async-start(), calls=%async_computation.27 | async-start | bytes 4718592 | tf_op jit(solution)/shard_map/reduce_scatter | solution.py:563
  822.1 218.5 %reduce-scatter.14.cloned.1.call-start = ((), (), s32[]{:S(2)}) async-start(), calls=%async_computation.24 | async-start | bytes 4718592 | tf_op jit(solution)/shard_map/reduce_scatter | solution.py:563
  832.4 21.0 %all-to-all-start.7 = ((bf16[4,128,704]{1,2,0:T(8,128)(2,1)}), bf16[4,128,704]{1,2,0:T(8,128)(2,1)S(1)}, u32[]{:S(2)}, u32[]{:S(2)}) async-start(bf16[4,128,704]{1,2,0:T(8,128)(2,1)} %copy_bitcast_fusion), calls=%async_computation.15 | async-start | bytes 1441792 | tf_op jit(solution)/shard_map/all_to_all | solution.py:555
  896.2 15.1 %all-to-all-start.5 = ((bf16[4,128,256]{2,1,0:T(8,128)(2,1)}), bf16[4,128,256]{2,1,0:T(8,128)(2,1)S(1)}, u32[]{:S(2)}, u32[]{:S(2)}) async-start(bf16[4,128,256]{2,1,0:T(8,128)(2,1)} %bitcast.570), calls=%async_computation.11 | async-start | bytes 524288 | tf_op jit(solution)/shard_map/all_to_all | solution.py:555
  908.8 81.4 %copy-start.21 = (bf16[1,256,2048]{2,1,0:T(8,128)(2,1)S(1)}, bf16[1,256,2048]{2,1,0:T(8,128)(2,1)}, u32[]{:S(2)}) copy-start(bf16[1,256,2048]{2,1,0:T(8,128)(2,1)} %param.16) | copy-start | bytes 3145732
  908.8 81.4 %copy-start.48 = (f32[2048]{0:T(1024)S(1)}, f32[2048]{0:T(1024)}, u32[]{:S(2)}) copy-start(f32[2048]{0:T(1024)} %param.19) | copy-start | bytes 24580
  908.8 81.4 %copy-start.56 = (f32[128]{0:T(128)S(1)}, f32[128]{0:T(128)}, u32[]{:S(2)}) copy-start(f32[128]{0:T(128)} %copy-done.55) | copy-start | bytes 1540
  908.8 131.8 %copy-start.26 = (bf16[128,2048]{1,0:T(8,128)(2,1)S(1)}, bf16[128,2048]{1,0:T(8,128)(2,1)}, u32[]{:S(2)}) copy-start(bf16[128,2048]{1,0:T(8,128)(2,1)} %reduce-scatter.12.cloned.1.call-done) | copy-start | bytes 1572868
  908.8 131.8 %copy-start.39 = (bf16[128,2048]{1,0:T(8,128)(2,1)S(1)}, bf16[128,2048]{1,0:T(8,128)(2,1)}, u32[]{:S(2)}) copy-start(bf16[128,2048]{1,0:T(8,128)(2,1)} %reduce-scatter.16.cloned.1.call-done) | copy-start | bytes 1572868
  908.8 131.8 %copy-start.59 = (f32[128]{0:T(128)S(1)}, f32[128]{0:T(128)}, u32[]{:S(2)}) copy-start(f32[128]{0:T(128)} %get-tuple-element.581) | copy-start | bytes 1540
  911.3 135.7 %all-to-all-start.4 = ((bf16[4,128,768]{1,2,0:T(8,128)(2,1)}), bf16[4,128,768]{1,2,0:T(8,128)(2,1)S(1)}, u32[]{:S(2)}, u32[]{:S(2)}) async-start(bf16[4,128,768]{1,2,0:T(8,128)(2,1)} %copy.590), calls=%async_computation.9 | async-start | bytes 1572864 | tf_op jit(solution)/shard_map/all_to_all | solution.py:555
  916.4 254.5 %all-reduce.10.cloned.1.call-start = ((), (), s32[]{:S(2)}) async-start(), calls=%async_computation.28 | async-start | bytes 196608 | tf_op jit(solution)/shard_map/psum | solution.py:741
  1043.7 46.9 %collective-permute-start.1 = (bf16[128,2048]{1,0:T(8,128)(2,1)}, bf16[128,2048]{1,0:T(8,128)(2,1)}, u32[]{:S(2)}, u32[]{:S(2)}) collective-permute-start(bf16[128,2048]{1,0:T(8,128)(2,1)} %get-tuple-element.553), channel_id=1, source_target_pairs={{0,1},{1,0},{2,3},{3,2},{4,5},{5,4},{6,7},{7,6},{8,9},{9,8},{10,11... | collective-permute-start | bytes 1572872 | tf_op jit(solution)/shard_map/ppermute | solution.py:572
  1048.8 44.1 %collective-permute-start = (bf16[128,2048]{1,0:T(8,128)(2,1)S(1)}, bf16[128,2048]{1,0:T(8,128)(2,1)S(1)}, u32[]{:S(2)}, u32[]{:S(2)}) collective-permute-start(bf16[128,2048]{1,0:T(8,128)(2,1)S(1)} %copy-done.41), channel_id=1, source_target_pairs={{0,1},{1,0},{2,3},{3,2},{4,5},{5,4},{6,7},{7,6},{8,9},{9,8},{10,11... | collective-permute-start | bytes 1572872 | tf_op jit(solution)/shard_map/ppermute | solution.py:572
  1091.9 80.6 %copy-start.1 = (f32[3,4,1024]{2,1,0:T(4,128)S(1)}, f32[3,4,1024]{2,1,0:T(4,128)}, u32[]{:S(2)}) copy-start(f32[3,4,1024]{2,1,0:T(4,128)} %param.22) | copy-start | bytes 147460
  (28 other events, 59.8 us)
Sparse Core Ops, SparseCore 0:
  11.2 63.0 all-gather.9
  76.7 47.4 all-gather.11
  126.0 26.6 all-gather.13
  264.8 78.0 reduce-scatter.11
  345.2 67.5 all-gather.17
  414.9 45.5 all-gather.15
  462.3 42.0 all-gather.19
  506.6 45.5 all-gather.23
  572.7 46.3 reduce-scatter.15
  623.7 47.6 all-gather.21
  675.0 42.1 reduce-scatter.25
  720.0 65.8 reduce-scatter.23
  789.3 27.6 reduce-scatter.21
  820.2 43.9 reduce-scatter.19
  866.9 74.0 reduce-scatter.27
  943.2 46.9 reduce-scatter.17
  992.3 48.2 reduce-scatter.13
  1046.6 124.3 all-reduce.9

commit v2 on v0

--- a/solution.py
+++ b/solution.py
@@ -1,6 +1,10 @@
+import functools
+
 import jax
 import jax.numpy as jnp
 from jax import lax
+from jax.experimental import pallas as pl
+from jax.experimental.pallas import tpu as pltpu
 from jax.sharding import PartitionSpec as P
 
 DK = 128
@@ -132,7 +136,7 @@
     return pullback((grad_rows, grad_end))
 
 
-def local(
+def local_pieces(
     block_input,
     grad_out,
     doc_lengths,
@@ -402,6 +406,661 @@
     )
 
 
+CHUNK = 128
+PAD = 8
+
+
+def mul(left, right, dims, precision=None):
+    return lax.dot_general(
+        left, right, ((dims[:1], dims[1:]), ((), ())), precision=precision, preferred_element_type=jnp.float32
+    )
+
+
+def fine(left, right, dims=(1, 0)):
+    return mul(left, right, dims, precise)
+
+
+def plain(left, right, dims=(1, 0)):
+    return mul(left.astype(jnp.bfloat16), right.astype(jnp.bfloat16), dims)
+
+
+def chunk_masks(doc_col, doc_row):
+    same = doc_col == doc_row
+    down = lax.broadcasted_iota(jnp.int32, (CHUNK, CHUNK), 0)
+    along = lax.broadcasted_iota(jnp.int32, (CHUNK, CHUNK), 1)
+    lower = jnp.where(same & (down >= along), 1.0, 0.0)
+    strict = jnp.where(same & (down > along), 1.0, 0.0)
+    return lower, strict, down, along
+
+
+def lower_inverse(systems, down, along):
+    at_one = (down // 2 == along // 2) & (down != along)
+    unit = jnp.where(down == along, 1.0, 0.0)
+    inverses = [unit - jnp.where(at_one, system, 0.0) for system in systems]
+    half = 2
+    while half < CHUNK:
+        joins = (down // (2 * half) == along // (2 * half)) & (down // half != along // half)
+        inner = [
+            fine(jnp.where(joins, system, 0.0), inverse)
+            for system, inverse in zip(systems, inverses)
+        ]
+        inverses = [inverse - fine(inverse, part) for inverse, part in zip(inverses, inner)]
+        half *= 2
+    return inverses
+
+
+def tap_mask(aux, tap):
+    return 1.0 if tap == 0 else aux[:, 3 + tap : 4 + tap]
+
+
+def convolved(window, taps, aux):
+    total = 0.0
+    for tap in range(KW):
+        total = total + (
+            taps[tap : tap + 1] * window[PAD - tap : PAD - tap + CHUNK] * tap_mask(aux, tap)
+        )
+    return total
+
+
+def sigmoid(values):
+    return 1.0 / (1.0 + jnp.exp(-values))
+
+
+def unit_scale(values):
+    total = jnp.sum(values * values, axis=1, keepdims=True)
+    floor = DK / 16.0
+    return lax.rsqrt(jnp.maximum(total, floor)), jnp.where(total > floor, 1.0, 0.0)
+
+
+def mix_norm(mixed):
+    mean = jnp.mean(mixed * mixed, axis=1, keepdims=True)
+    return lax.rsqrt(jnp.maximum(mean, mix_floor)), jnp.where(mean > mix_floor, 1.0, 0.0)
+
+
+def forward_kernel(
+    heads,
+    n1_ref,
+    qkv_ref,
+    beta_ref,
+    taps_ref,
+    aux_ref,
+    docs_ref,
+    gain_ref,
+    proj_ref,
+    logit_ref,
+    mixed_ref,
+    normed_ref,
+    inverse_ref,
+    states_ref,
+    written_ref,
+    window_ref,
+    state_ref,
+):
+    width = heads * DK
+    window_ref[0:PAD] = jnp.zeros((PAD, 3 * width), jnp.float32)
+    state_ref[...] = jnp.zeros_like(state_ref)
+
+    def chunk(n, _):
+        rows = pl.ds(pl.multiple_of(n * CHUNK, CHUNK), CHUNK)
+        n1 = n1_ref[rows]
+        proj = mul(n1, qkv_ref[...], (1, 0)).astype(jnp.bfloat16)
+        proj_ref[rows] = proj
+        window_ref[PAD : PAD + CHUNK] = proj.astype(jnp.float32)
+        logit = mul(n1, beta_ref[...], (1, 1))
+        logit_ref[rows] = logit
+        aux = aux_ref[rows]
+        conv = convolved(window_ref[...], taps_ref[...], aux)
+        act = conv * sigmoid(conv)
+        window_ref[0:PAD] = window_ref[CHUNK : CHUNK + PAD]
+        valid, carry, tail = aux[:, 1:2], aux[:, 2:3], aux[:, 3:4]
+        carry_last = carry[CHUNK - 1 :]
+        lower, strict, down, along = chunk_masks(aux[:, 0:1], docs_ref[pl.ds(n, 1)])
+        rate_all = sigmoid(logit) * valid
+        parts = []
+        for h in range(heads):
+            query = act[:, h * DK : (h + 1) * DK]
+            key = act[:, width + h * DK : width + (h + 1) * DK]
+            value = act[:, 2 * width + h * DK : 2 * width + (h + 1) * DK]
+            query = query * unit_scale(query)[0]
+            key = key * unit_scale(key)[0]
+            rate = rate_all[:, h : h + 1]
+            system = rate * fine(key, key, (1, 1)) * strict
+            parts.append((query, key, value, rate, system))
+        inverses = lower_inverse([part[4] for part in parts], down, along)
+        for h, (query, key, value, rate, _) in enumerate(parts):
+            inverse = inverses[h]
+            state = state_ref[h]
+            carried_key = carry * key
+            right = rate * (value - fine(carried_key, state))
+            written = fine(inverse, right)
+            scores = plain(query, key, (1, 1)) * lower
+            mixed = carry * plain(query, state) + plain(scores, written)
+            mixed = mixed * valid
+            states_ref[h, n] = state
+            written_ref[h, n] = written
+            inverse_ref[h, n] = inverse
+            state_ref[h] = carry_last * state + fine(tail * key, written, (0, 0))
+            columns = pl.ds(h * DK, DK)
+            mixed_ref[rows, columns] = mixed
+            normed_ref[rows, columns] = (
+                mixed * mix_norm(mixed)[0] * gain_ref[...]
+            ).astype(jnp.bfloat16)
+        return 0
+
+    lax.fori_loop(0, n1_ref.shape[0] // CHUNK, chunk, 0)
+
+
+def backward_kernel(
+    heads,
+    grad_ref,
+    o_ref,
+    proj_ref,
+    logit_ref,
+    mixed_ref,
+    inverse_ref,
+    states_ref,
+    written_ref,
+    taps_ref,
+    aux_ref,
+    docs_ref,
+    gain_ref,
+    grad_proj_ref,
+    grad_logit_ref,
+    conv_grad_ref,
+    gain_grad_ref,
+    window_ref,
+    masked_ref,
+    state_ref,
+):
+    width = heads * DK
+    chunks = grad_ref.shape[0] // CHUNK
+    state_ref[...] = jnp.zeros_like(state_ref)
+    masked_ref[...] = jnp.zeros_like(masked_ref)
+    conv_grad_ref[...] = jnp.zeros_like(conv_grad_ref)
+    gain_grad_ref[...] = jnp.zeros_like(gain_grad_ref)
+
+    def chunk(step, _):
+        n = chunks - 1 - step
+        rows = pl.ds(pl.multiple_of(n * CHUNK, CHUNK), CHUNK)
+        before = jnp.maximum(n - 1, 0)
+        aux = aux_ref[rows]
+        grad_normed = mul(grad_ref[rows], o_ref[...], (1, 0))
+        prior = proj_ref[pl.ds(pl.multiple_of(before * CHUNK + CHUNK - 16, 16), 16)]
+        window_ref[0:PAD] = prior.astype(jnp.float32)[16 - PAD :]
+        window_ref[PAD : PAD + CHUNK] = proj_ref[rows].astype(jnp.float32)
+        window = window_ref[...]
+        taps = taps_ref[...]
+        conv = convolved(window, taps, aux)
+        conv_sig = sigmoid(conv)
+        act = conv * conv_sig
+        valid, carry, tail = aux[:, 1:2], aux[:, 2:3], aux[:, 3:4]
+        carry_last = carry[CHUNK - 1 :]
+        lower, strict, down, along = chunk_masks(aux[:, 0:1], docs_ref[pl.ds(n, 1)])
+        rate_sig = sigmoid(logit_ref[rows])
+        rate_all = rate_sig * valid
+        lanes = lax.broadcasted_iota(jnp.int32, rate_all.shape, 1)
+        grad_rates = jnp.zeros_like(rate_all)
+        grads = [[], [], []]
+        for h in range(heads):
+            columns = pl.ds(h * DK, DK)
+            mixed = mixed_ref[rows, columns]
+            mix_scale, mix_live = mix_norm(mixed)
+            grad_out = grad_normed[:, h * DK : (h + 1) * DK]
+            scaled = mixed * mix_scale
+            gain_grad_ref[...] += jnp.sum(grad_out * scaled, axis=0, keepdims=True)
+            weighted = gain_ref[...] * grad_out
+            grad_mix = (
+                mix_scale * weighted
+                - scaled
+                * (mix_scale * mix_scale * mix_live)
+                * jnp.mean(weighted * mixed, axis=1, keepdims=True)
+            ) * valid
+            query_raw = act[:, h * DK : (h + 1) * DK]
+            key_raw = act[:, width + h * DK : width + (h + 1) * DK]
+            value = act[:, 2 * width + h * DK : 2 * width + (h + 1) * DK]
+            query_scale, query_live = unit_scale(query_raw)
+            key_scale, key_live = unit_scale(key_raw)
+            query = query_raw * query_scale
+            key = key_raw * key_scale
+            rate = rate_all[:, h : h + 1]
+            inverse = inverse_ref[h, n]
+            state = states_ref[h, n]
+            written = written_ref[h, n]
+            grad_state = state_ref[h]
+            tail_key = tail * key
+            carried_key = carry * key
+            scores = plain(query, key, (1, 1)) * lower
+            pulled = plain(scores, grad_mix, (0, 0)) + fine(tail_key, grad_state)
+            solved = fine(inverse, pulled, (0, 0))
+            state_ref[h] = (
+                carry_last * grad_state
+                + plain(carry * query, grad_mix, (0, 0))
+                - fine(rate * carried_key, solved, (0, 0))
+            )
+            grad_scores = plain(grad_mix, written, (1, 1)) * lower
+            grad_query = carry * plain(grad_mix, state, (1, 1)) + plain(grad_scores, key)
+            guess_error = value - plain(carried_key, state)
+            gram = plain(key, key, (1, 1)) * strict
+            grad_system = plain(solved, written, (1, 1)) * strict
+            grad_rate = jnp.sum(solved * guess_error, axis=1, keepdims=True) - jnp.sum(
+                grad_system * gram, axis=1, keepdims=True
+            )
+            grad_gram = rate * grad_system
+            grad_key = (
+                plain(grad_scores, query, (0, 0))
+                + tail * plain(written, grad_state, (1, 1))
+                - rate * carry * plain(solved, state, (1, 1))
+                - plain(grad_gram, key)
+                - plain(grad_gram, key, (0, 0))
+            )
+            grads[0].append(
+                query_scale
+                * (
+                    grad_query
+                    - query
+                    * query_live
+                    * jnp.sum(query * grad_query, axis=1, keepdims=True)
+                )
+            )
+            grads[1].append(
+                key_scale
+                * (grad_key - key * key_live * jnp.sum(key * grad_key, axis=1, keepdims=True))
+            )
+            grads[2].append(rate * solved)
+            grad_rates = grad_rates + jnp.where(lanes == h, grad_rate, 0.0)
+        grad_act = jnp.concatenate(grads[0] + grads[1] + grads[2], axis=1)
+        grad_conv = grad_act * conv_sig * (1.0 + conv * (1.0 - conv_sig))
+        grad_proj = taps[0:1] * grad_conv
+        conv_grad_ref[0:1] += jnp.sum(
+            grad_conv * window[PAD : PAD + CHUNK], axis=0, keepdims=True
+        )
+        for tap in range(1, KW):
+            masked = grad_conv * tap_mask(aux, tap)
+            conv_grad_ref[tap : tap + 1] += jnp.sum(
+                masked * window[PAD - tap : PAD - tap + CHUNK], axis=0, keepdims=True
+            )
+            masked_ref[tap - 1, CHUNK : CHUNK + PAD] = masked_ref[tap - 1, 0:PAD]
+            masked_ref[tap - 1, 0:CHUNK] = masked
+            grad_proj = grad_proj + taps[tap : tap + 1] * masked_ref[tap - 1, tap : tap + CHUNK]
+        grad_proj_ref[rows] = grad_proj.astype(jnp.bfloat16)
+        grad_logit_ref[rows] = (grad_rates * rate_sig * (1.0 - rate_sig) * valid).astype(
+            jnp.bfloat16
+        )
+        return 0
+
+    lax.fori_loop(0, chunks, chunk, 0)
+
+
+def in_vmem(count):
+    return [pl.BlockSpec(memory_space=pltpu.VMEM)] * count
+
+
+def run_forward(n1, qkv, beta, taps, aux, docs, gain):
+    row_len, heads = n1.shape[0], qkv.shape[1] // (3 * DK)
+    chunks, width, f32 = row_len // CHUNK, heads * DK, jnp.float32
+    shapes = (
+        ((row_len, 3 * width), jnp.bfloat16),
+        ((row_len, beta.shape[0]), f32),
+        ((row_len, width), f32),
+        ((row_len, width), jnp.bfloat16),
+        ((heads, chunks, CHUNK, CHUNK), f32),
+        ((heads, chunks, DK, DK), f32),
+        ((heads, chunks, CHUNK, DK), f32),
+    )
+    return pl.pallas_call(
+        functools.partial(forward_kernel, heads),
+        out_shape=[jax.ShapeDtypeStruct(*shape) for shape in shapes],
+        in_specs=in_vmem(7),
+        out_specs=in_vmem(len(shapes)),
+        scratch_shapes=[
+            pltpu.VMEM((PAD + CHUNK, 3 * width), f32),
+            pltpu.VMEM((heads, DK, DK), f32),
+        ],
+        compiler_params=pltpu.CompilerParams(vmem_limit_bytes=48 * 1024 * 1024),
+        name="mixer_forward",
+    )(n1, qkv, beta, taps, aux, docs, gain)
+
+
+def run_backward(grad, o_full, saved, taps, aux, docs, gain):
+    row_len, heads = grad.shape[0], o_full.shape[1] // DK
+    width, f32 = heads * DK, jnp.float32
+    logit = saved[1]
+    shapes = (
+        ((row_len, 3 * width), jnp.bfloat16),
+        (logit.shape, jnp.bfloat16),
+        ((KW, 3 * width), f32),
+        ((1, DK), f32),
+    )
+    return pl.pallas_call(
+        functools.partial(backward_kernel, heads),
+        out_shape=[jax.ShapeDtypeStruct(*shape) for shape in shapes],
+        in_specs=in_vmem(12),
+        out_specs=in_vmem(len(shapes)),
+        scratch_shapes=[
+            pltpu.VMEM((PAD + CHUNK, 3 * width), f32),
+            pltpu.VMEM((KW - 1, CHUNK + PAD, 3 * width), f32),
+            pltpu.VMEM((heads, DK, DK), f32),
+        ],
+        compiler_params=pltpu.CompilerParams(vmem_limit_bytes=48 * 1024 * 1024),
+        name="mixer_backward",
+    )(grad, o_full, *saved, taps, aux, docs, gain)
+
+
+def row_aux(docs):
+    f32 = jnp.float32
+    chunks = docs.reshape(-1, CHUNK)
+    prior = jnp.concatenate([jnp.full((1,), -1, jnp.int32), chunks[:-1, -1]])
+    padded = jnp.concatenate([jnp.full((KW - 1,), -1, jnp.int32), docs])
+    columns = [
+        docs,
+        docs < DOCS,
+        (chunks == prior[:, None]).reshape(-1),
+        (chunks == chunks[:, -1:]).reshape(-1),
+    ] + [padded[KW - 1 - tap : KW - 1 - tap + docs.shape[0]] == docs for tap in range(1, KW)]
+    columns = [column.astype(f32) for column in columns]
+    columns += [jnp.zeros_like(columns[0])] * (8 - len(columns))
+    return jnp.stack(columns, axis=1), chunks.astype(f32)
+
+
+def swap_copy(source, target, send, recv, where):
+    return pltpu.make_async_remote_copy(
+        src_ref=source,
+        dst_ref=target,
+        send_sem=send,
+        recv_sem=recv,
+        device_id=where,
+        device_id_type=pl.DeviceIdType.MESH,
+    )
+
+
+def greet(partners):
+    barrier = pltpu.get_barrier_semaphore()
+    for partner in partners:
+        pl.semaphore_signal(
+            barrier, inc=1, device_id=partner, device_id_type=pl.DeviceIdType.MESH
+        )
+    pl.semaphore_wait(barrier, len(partners))
+
+
+def around(axis):
+    count, place = lax.axis_size(axis), lax.axis_index(axis)
+    return [lax.rem(place + by, count) for by in range(1, count)]
+
+
+def small_sums_kernel(
+    part_ref, out_ref, rows_ref, all_ref, send_row, recv_row, send_seq, recv_seq, send_tp, recv_tp
+):
+    row, seq, tp = (lax.axis_index(axis) for axis in ("row", "seq", "tp"))
+    row_others, seq_others, tp_others = around("row"), around("seq"), around("tp")
+    greet(
+        [{"row": other} for other in row_others]
+        + [{"seq": other} for other in seq_others]
+        + [{"tp": other} for other in tp_others]
+    )
+    rows_ref[row] = part_ref[...]
+    copies = [
+        swap_copy(part_ref, rows_ref.at[row], send_row.at[i], recv_row.at[i], {"row": other})
+        for i, other in enumerate(row_others)
+    ]
+    for copy in copies:
+        copy.start()
+    for copy in copies:
+        copy.wait()
+    total = rows_ref[0]
+    for i in range(1, rows_ref.shape[0]):
+        total = total + rows_ref[i]
+    all_ref[tp, seq] = total
+    copies = [
+        swap_copy(
+            all_ref.at[tp, seq], all_ref.at[tp, seq], send_seq.at[i], recv_seq.at[i], {"seq": other}
+        )
+        for i, other in enumerate(seq_others)
+    ]
+    for copy in copies:
+        copy.start()
+    for copy in copies:
+        copy.wait()
+    copies = [
+        swap_copy(all_ref.at[tp], all_ref.at[tp], send_tp.at[i], recv_tp.at[i], {"tp": other})
+        for i, other in enumerate(tp_others)
+    ]
+    for copy in copies:
+        copy.start()
+    for copy in copies:
+        copy.wait()
+    out_ref[...] = all_ref[...]
+
+
+def run_small_sums(part):
+    rows, seqs, tps = (lax.axis_size(axis) for axis in ("row", "seq", "tp"))
+    dma = pltpu.SemaphoreType.DMA
+    shape = (tps, seqs) + part.shape
+    return pl.pallas_call(
+        small_sums_kernel,
+        out_shape=jax.ShapeDtypeStruct(shape, part.dtype),
+        in_specs=in_vmem(1),
+        out_specs=pl.BlockSpec(memory_space=pltpu.VMEM),
+        scratch_shapes=[
+            pltpu.VMEM((rows,) + part.shape, part.dtype),
+            pltpu.VMEM(shape, part.dtype),
+            dma((rows - 1,)),
+            dma((rows - 1,)),
+            dma((seqs - 1,)),
+            dma((seqs - 1,)),
+            dma((tps - 1,)),
+            dma((tps - 1,)),
+        ],
+        compiler_params=pltpu.CompilerParams(collective_id=0, has_side_effects=True),
+        name="small_sums",
+    )(part)
+
+
+def exchanged(parts, axis):
+    count, place = lax.axis_size(axis), lax.axis_index(axis)
+    came = [lax.dynamic_index_in_dim(parts, place, 0, keepdims=False)]
+    for by in range(1, count):
+        part = lax.dynamic_index_in_dim(parts, (place + by) % count, 0, keepdims=False)
+        came.append(lax.ppermute(part, axis, [(i, (i + by) % count) for i in range(count)]))
+    came = jnp.stack(came)
+    order = (place - jnp.arange(count)) % count
+    return jnp.concatenate(
+        [lax.dynamic_slice_in_dim(came, order[j], 1, axis=0) for j in range(count)], axis=0
+    )
+
+
+def spread(shard, pieces, axis):
+    rows, width = shard.shape
+    return exchanged(shard.reshape(rows, pieces, width // pieces).transpose(1, 0, 2), axis)
+
+
+def gathered(shard):
+    pieces = lax.axis_size("seq")
+    parts = spread(shard, pieces, "seq")
+    whole = lax.all_gather(parts, "row", axis=0, tiled=True)
+    return whole.reshape(-1, whole.shape[-1])
+
+
+def returned(part):
+    pieces = lax.axis_size("seq")
+    rows = part.shape[0] // (pieces * lax.axis_size("row"))
+    own = lax.psum_scatter(part, "row", scatter_dimension=0, tiled=True)
+    return exchanged(own.reshape(pieces, rows, -1), "seq")
+
+
+def token_gather(own):
+    return lax.all_gather(own, ("seq", "tp"), axis=0, tiled=True)
+
+
+def token_sum(term):
+    return lax.psum_scatter(
+        term.astype(jnp.bfloat16), ("seq", "tp"), scatter_dimension=0, tiled=True
+    ).astype(jnp.float32)
+
+
+def both_cores(own):
+    cores = lax.axis_size("tp")
+    if cores == 1:
+        return own
+    other = lax.ppermute(own, "tp", [(0, 1), (1, 0)])
+    first = lax.axis_index("tp") == 0
+    return jnp.concatenate([jnp.where(first, own, other), jnp.where(first, other, own)], axis=0)
+
+
+def shifted(rows, by):
+    if by == 0:
+        return rows
+    pad = jnp.zeros((abs(by),) + rows.shape[1:], rows.dtype)
+    if by > 0:
+        return jnp.concatenate([pad, rows[:-by]], axis=0)
+    return jnp.concatenate([rows[-by:], pad], axis=0)
+
+
+def local_heads(
+    block_input,
+    grad_out,
+    doc_lengths,
+    attn_gain,
+    mlp_gain,
+    out_gain,
+    conv_weight,
+    qkv_weight,
+    beta_weight,
+    o_weight,
+    gate_up_weight,
+    down_weight,
+):
+    tok_rows, model_width = block_input.shape[1:]
+    pieces, cores = lax.axis_size("seq"), lax.axis_size("tp")
+    piece, core = lax.axis_index("seq"), lax.axis_index("tp")
+    row_len = pieces * tok_rows
+    own_rows = tok_rows // cores
+    shard_rows = qkv_weight.shape[1]
+    half_width = qkv_weight.shape[2]
+    width = half_width // pieces
+    heads = width // DK
+    units = gate_up_weight.shape[2] // pieces
+    f32, b16 = jnp.float32, jnp.bfloat16
+
+    qkv_parts = qkv_weight.reshape(3, shard_rows, pieces, width).transpose(1, 2, 0, 3)
+    qkv_full = gathered(qkv_parts.reshape(shard_rows, -1))
+    beta_full = lax.all_gather(beta_weight.T, ("row", "seq"), axis=1, tiled=True)
+    beta_full = lax.dynamic_slice_in_dim(beta_full, piece * heads, heads, axis=0)
+    beta_full = jnp.pad(beta_full, ((0, 16 - heads), (0, 0)))
+    o_full = gathered(o_weight.T)
+    gate_up_parts = gate_up_weight.reshape(2, shard_rows, pieces, units).transpose(1, 2, 0, 3)
+    gate_up_full = gathered(gate_up_parts.reshape(shard_rows, -1))
+    down_full = gathered(down_weight.T)
+
+    ends = jnp.cumsum(doc_lengths[0])
+    places = jnp.arange(row_len, dtype=jnp.int32)
+    docs = jnp.sum((places[:, None] >= ends[None, :]).astype(jnp.int32), axis=1)
+    aux, doc_rows = row_aux(docs)
+    gain_row = out_gain[None]
+    taps = lax.dynamic_slice_in_dim(conv_weight, piece * width, width, axis=2)
+    taps = taps.transpose(1, 0, 2).reshape(KW, 3 * width)
+
+    x_rows = lax.dynamic_slice_in_dim(block_input[0], core * own_rows, own_rows, axis=0)
+    x_rows = x_rows.astype(f32)
+    g_rows = lax.dynamic_slice_in_dim(grad_out[0], core * own_rows, own_rows, axis=0)
+    scale_one = norm_scale(x_rows)
+    normed_one = token_gather((x_rows * scale_one * attn_gain).astype(b16))
+    g_full = token_gather(g_rows)
+    proj, logit, mixed, normed_mix, inverse, states, written = run_forward(
+        normed_one, qkv_full, beta_full, taps, aux, doc_rows, gain_row
+    )
+    o_term = jnp.einsum("te,de->td", normed_mix, o_full, preferred_element_type=f32)
+    resid = x_rows + token_sum(o_term)
+    scale_two = norm_scale(resid)
+    normed_two = token_gather((resid * scale_two * mlp_gain).astype(b16))
+    gate_up = jnp.dot(normed_two, gate_up_full, preferred_element_type=f32)
+    gate, up = gate_up[:, :units], gate_up[:, units:]
+    gate_sig = jax.nn.sigmoid(gate)
+    gate_act = gate * gate_sig
+    hidden = (gate_act * up).astype(b16)
+    grad_hidden = jnp.dot(g_full, down_full, preferred_element_type=f32)
+    grad_gate = grad_hidden * up * gate_sig * (1.0 + gate * (1.0 - gate_sig))
+    grad_up = grad_hidden * gate_act
+    grad_gate_up = jnp.concatenate([grad_gate, grad_up], axis=1).astype(b16)
+    two_term = jnp.einsum("tf,df->td", grad_gate_up, gate_up_full, preferred_element_type=f32)
+    grad_two = token_sum(two_term)
+    mlp_gain_part = jnp.sum(grad_two * resid * scale_two, axis=0)
+    grad_resid = g_rows.astype(f32) + norm_back(resid, scale_two, mlp_gain, grad_two)
+    grad_attn = token_gather(grad_resid.astype(b16))
+    down_term = jnp.einsum("tf,df->td", hidden, down_full, preferred_element_type=f32)
+    result = both_cores((resid + token_sum(down_term)).astype(b16))
+    down_part = jnp.einsum("td,tf->df", g_full, hidden, preferred_element_type=f32)
+    gate_up_part = jnp.einsum("td,tf->df", normed_two, grad_gate_up, preferred_element_type=f32)
+    o_part = jnp.einsum("td,te->de", grad_attn, normed_mix, preferred_element_type=f32)
+    grad_proj, grad_logit, conv_part, out_gain_part = run_backward(
+        grad_attn,
+        o_full,
+        (proj, logit, mixed, inverse, states, written),
+        taps,
+        aux,
+        doc_rows,
+        gain_row,
+    )
+    one_term = jnp.einsum("te,de->td", grad_proj, qkv_full, preferred_element_type=f32)
+    one_term = one_term + jnp.einsum("th,hd->td", grad_logit, beta_full, preferred_element_type=f32)
+    grad_one = token_sum(one_term)
+    attn_gain_part = jnp.sum(grad_one * x_rows * scale_one, axis=0)
+    input_grad = both_cores(
+        (grad_resid + norm_back(x_rows, scale_one, attn_gain, grad_one)).astype(b16)
+    )
+    qkv_part = jnp.einsum("td,te->de", normed_one, grad_proj, preferred_element_type=f32)
+    beta_part = jnp.einsum("td,th->hd", normed_one, grad_logit, preferred_element_type=f32)
+    packed = jnp.concatenate(
+        [
+            conv_part.reshape(-1, 128),
+            attn_gain_part.reshape(-1, 128),
+            mlp_gain_part.reshape(-1, 128),
+            beta_part[:heads].reshape(-1, 128),
+            jnp.pad(out_gain_part, ((0, 7), (0, 0))),
+        ],
+        axis=0,
+    )
+    small = run_small_sums(packed)
+    at = KW * 3 * width // 128
+    span = model_width // 128
+    conv_grad = small[:, :, :at].reshape(cores, pieces, KW, 3, width)
+    conv_grad = conv_grad.transpose(3, 2, 0, 1, 4).reshape(3, KW, model_width)
+    sums = jnp.sum(small[:, :, at:], axis=(0, 1))
+    attn_gain_grad = sums[:span].reshape(-1)
+    mlp_gain_grad = sums[span : 2 * span].reshape(-1)
+    out_gain_grad = sums[(2 + heads) * span]
+    beta_sum = lax.dynamic_index_in_dim(small, core, 0, keepdims=False)
+    beta_sum = beta_sum[:, at + 2 * span : at + (2 + heads) * span]
+    beta_sum = beta_sum.reshape(pieces * heads, model_width)
+    beta_sum = lax.dynamic_slice_in_dim(
+        beta_sum, (lax.axis_index("row") * pieces + piece) * shard_rows, shard_rows, axis=1
+    ).T
+    down_sum = returned(down_part.astype(b16))
+    gate_up_sum = returned(gate_up_part.astype(b16)).reshape(pieces, shard_rows, 2, units)
+    o_sum = returned(o_part.astype(b16))
+    qkv_sum = returned(qkv_part.astype(b16)).reshape(pieces, shard_rows, 3, width)
+    return (
+        result[None],
+        input_grad[None],
+        attn_gain_grad,
+        mlp_gain_grad,
+        out_gain_grad,
+        conv_grad,
+        qkv_sum.transpose(2, 1, 0, 3).reshape(3, shard_rows, -1).astype(f32),
+        beta_sum,
+        o_sum.transpose(0, 2, 1).reshape(-1, shard_rows).astype(f32),
+        gate_up_sum.transpose(2, 1, 0, 3).reshape(2, shard_rows, -1).astype(f32),
+        down_sum.transpose(0, 2, 1).reshape(-1, shard_rows).astype(f32),
+    )
+
+
+def splits_heads(mesh, heads=16, units=5632):
+    return (
+        mesh.shape["tp"] == 2
+        and heads % (mesh.shape["seq"] * 2) == 0
+        and units % (mesh.shape["seq"] * 2) == 0
+    )
+
+
 def solution(mesh):
     in_specs = (
         P("row", "seq", None),
@@ -430,4 +1089,5 @@
         P(None, ("row", "seq"), "tp"),
         P("tp", ("row", "seq")),
     )
+    local = local_heads if splits_heads(mesh) else local_pieces
     return jax.shard_map(local, mesh=mesh, in_specs=in_specs, out_specs=out_specs, check_vma=False)

time: 2580 us -> 915 us (0.35)
  waiting for transfers between devices: 1680 us -> 552 us
  other arithmetic: 241 us -> 26 us
  local copies, waits for them, and re-layouts: 265 us -> 50.3 us
  matrix products: 269 us -> 83.7 us
  Pallas kernels: 0 us -> 88.7 us
  blocking collectives: 82.1 us -> 36.9 us
    unnamed x22 -> x16, waiting for transfers between devices: 873 us -> 0.26 us
    all_gather x8, waiting for transfers between devices: 641 us -> 244 us  [the longest x4 166 us: token_gather(): return lax.all_gather(own, ('seq', 'tp'), axis=0, tiled=True)]
    dot_general x64 -> x12, matrix products: 261 us -> 83.7 us  [the longest x1 11.7 us: local_heads(): gate_up = jnp.dot(normed_two, gate_up_full, preferred_element_type=f32)]
    reduce_scatter x0 -> x8, waiting for transfers between devices: none -> 173 us  [the longest x4 105 us: token_sum(): lax.psum_scatter(term.astype(jnp.bfloat16), ('seq', 'tp'), scatter_dimens...]
    psum x4 -> x0, waiting for transfers between devices: 163 us -> none  [the longest x1 125 us: local(): lax.psum((attn_gain_part * lead_mask, mlp_gain_part * lead_mask, out_gain...]
    unnamed x228 -> x76, local copies, waits for them, and re-layouts: 182 us -> 23.7 us
    another operation x7 -> x10, other arithmetic: 162 us -> 4.39 us  [the longest x8 4.13 us: exchanged(): came = jnp.stack(came)]
    ppermute x2 -> x26, waiting for transfers between devices: 1.46 us -> 135 us  [the longest x24 135 us: exchanged(): lax.ppermute(part, axis, [(i, (i + by) % count) for i in range(count)])]
  transfers between devices with their start and end apart: 19 -> 42, of which waited for: 14 -> 30; matrix products, arithmetic and copies ran while one was open for 13% -> 13% of each run, Pallas kernels for 0% -> 10%
where the time goes in v2:
time: 915 us; the launch traced here: 903 us
  waiting for transfers between devices  552 us (60%)
  Pallas kernels  88.7 us (10%)
  matrix products  83.7 us (9%)
  local copies, waits for them, and re-layouts  50.3 us (5%)
  starting transfers between devices  42.4 us (5%)
  blocking collectives  36.9 us (4%)
  other arithmetic  26 us (3%)
  between operations  23.1 us (3%)
    all_gather x4, waiting for transfers between devices, token_gather(): return lax.all_gather(own, ('seq', 'tp'), axis=0, tiled=True)  166 us
    ppermute x24, waiting for transfers between devices, exchanged(): lax.ppermute(part, axis, [(i, (i + by) % count) for i in range(count)])  135 us
    reduce_scatter x4, waiting for transfers between devices, token_sum(): lax.psum_scatter(term.astype(jnp.bfloat16), ('seq', 'tp'), scatter_dimens...  105 us
    all_gather x4, waiting for transfers between devices, gathered(): whole = lax.all_gather(parts, 'row', axis=0, tiled=True)  77.5 us
    reduce_scatter x4, waiting for transfers between devices, returned(): own = lax.psum_scatter(part, 'row', scatter_dimension=0, tiled=True)  67.4 us
    pallas_call x1, Pallas kernels, run_forward(): pl.pallas_call(functools.partial(forward_kernel, heads), out_shape=[jax.S...  43.5 us
    ppermute x24, starting transfers between devices, exchanged(): lax.ppermute(part, axis, [(i, (i + by) % count) for i in range(count)])  37.3 us
    all_gather x1, blocking collectives, local_heads(): lax.all_gather(beta_weight.T, ('row', 'seq'), axis=1, tiled=True)  36.9 us
  transfers between devices with their start and end apart: 42, of which 30 were waited for; matrix products, arithmetic and copies ran while one was open for 13% of the time, Pallas kernels for 10%

profile of v2, /device:TPU:8, one launch (start us, length us, event | category | flops | bytes accessed | tf_op | source)
XLA Modules:
  0.0 902.9 jit_solution(3601981190862061871)
XLA Ops:
  9.1 1.6 collective-permute-start
  12.1 2.1 collective-permute-start.2
  22.8 1.6 collective-permute-done
  24.5 3.1 collective-permute-done.1
  27.5 1.8 collective-permute-done.2
  32.2 2.1 collective-permute-start.3
  34.4 3.5 collective-permute-start.4
  38.5 2.2 collective-permute-done.4
  42.8 36.9 %all_gather.29 = bf16[8,2048]{1,0:T(8,128)(2,1)S(1)} all-gather(bf16[8,128]{1,0:T(8,128)(2,1)S(1)} %bitcast.274), channel_id=1, replica_groups=mesh['row'=4,'seq'=4,'tp'=2] {'row','seq'}, dimensions={1}, use_global_device_ids=true | all-gather | bytes 34816 | tf_op jit(solution)/shard_map/all_gather | solution.py:946
  79.7 43.1 %all-gather.10.cloned.1.call-done.n1_ref = bf16[1024,2048]{1,0:T(8,128)(2,1)} async-done(((bf16[128,2048]{1,0:T(8,128)(2,1)}), bf16[1024,2048]{1,0:T(8,128)(2,1)}) %all-gather.10.cloned.1.call-update) | async-done | bytes 4194320 | tf_op jit(solution)/shard_map/all_gather | solution.py:891
  122.8 43.5 %mixer_forward.1 = (bf16[1024,768]{1,0:T(8,128)(2,1)}, f32[1024,16]{1,0:T(8,128)S(1)}, f32[1024,256]{1,0:T(8,128)S(1)}, bf16[1024,256]{1,0:T(8,128)(2,1)S(1)}, f...) custom-call(bf16[1024,2048]{1,0:T(8,128)(2,1)} %all-gather.10.cloned.1.call-done.n1_ref, ...), custom_call_target="tpu_custom_call" | custom-call | tf_op jit(solution)/shard_map/mixer_forward/pallas_call | solution.py:710
  169.1 5.0 convolution_convert_fusion.3
  174.2 2.5 copy.166
  179.0 1.9 copy.169
  180.9 1.7 collective-permute-start.6
  183.5 2.8 collective-permute-start.7
  186.8 13.5 %collective-permute-done.6 = bf16[128,1408]{1,0:T(8,128)(2,1)} collective-permute-done((bf16[128,1408]{1,0:T(8,128)(2,1)}, bf16[128,1408]{1,0:T(8,128)(2,1)}, u32[]{:S(2)}, u32[]{:S(2)}) %collective-permute-start.6) | collective-permute-done | bytes 360480 | tf_op jit(solution)/shard_map/ppermute | solution.py:863
  200.3 38.5 %collective-permute-done.7 = bf16[128,1408]{1,0:T(8,128)(2,1)} collective-permute-done((bf16[128,1408]{1,0:T(8,128)(2,1)}, bf16[128,1408]{1,0:T(8,128)(2,1)}, u32[]{:S(2)}, u32[]{:S(2)}) %collective-permute-start.7) | collective-permute-done | bytes 360480 | tf_op jit(solution)/shard_map/ppermute | solution.py:863
  238.7 2.4 collective-permute-done.8
  244.1 9.3 %reduce-scatter.9.cloned.1.call-done = bf16[128,2048]{1,0:T(8,128)(2,1)} async-done(((bf16[1024,2048]{1,0:T(8,128)(2,1)}), bf16[128,2048]{1,0:T(8,128)(2,1)}) %reduce-scatter.9.cloned.1.call-update) | async-done | bytes 524304 | tf_op jit(solution)/shard_map/reduce_scatter | solution.py:895
  254.8 2.0 multiply_convert_fusion.3
  258.2 4.3 collective-permute-start.10
  262.6 11.5 %collective-permute-done.11 = bf16[128,704]{0,1:T(8,128)(2,1)S(1)} collective-permute-done((bf16[128,704]{0,1:T(8,128)(2,1)S(1)}, bf16[128,704]{0,1:T(8,128)(2,1)S(1)}, u32[]{:S(2)}, u32[]{:S(2)}) %collective-permute-start.11) | collective-permute-done | bytes 180256 | tf_op jit(solution)/shard_map/ppermute | solution.py:863
  275.8 1.9 constant_dynamic-slice_fusion.30
  278.2 44.7 %all-gather.18.cloned.1.call-done = bf16[16,128,1408]{2,1,0:T(8,128)(2,1)} async-done(((bf16[4,128,1408]{2,1,0:T(8,128)(2,1)}), bf16[16,128,1408]{2,1,0:T(8,128)(2,1)}) %all-gather.18.cloned.1.call-update) | async-done | bytes 5767184 | tf_op jit(solution)/shard_map/all_gather | solution.py:879
  322.9 47.7 %all-gather.16.cloned.1.call-done = bf16[1024,2048]{1,0:T(8,128)(2,1)} async-done(((bf16[128,2048]{1,0:T(8,128)(2,1)}), bf16[1024,2048]{1,0:T(8,128)(2,1)}) %all-gather.16.cloned.1.call-update) | async-done | bytes 4194320 | tf_op jit(solution)/shard_map/all_gather | solution.py:891
  370.6 11.7 %fusion.46 = f32[1024,1408]{1,0:T(8,128)} fusion(bf16[1024,2048]{1,0:T(8,128)(2,1)} %all-gather.16.cloned.1.call-done, bf16[2048,1408]{1,0:T(8,128)(2,1)} %bitcast.276), kind=kOutput, calls=%fused_computation.195 | convolution fusion | flops 5905580032 | bytes 15728640 | tf_op jit(solution)/shard_map/dot_general | solution.py:975
  382.3 32.8 %all-gather.20.cloned.1.call-done = bf16[16,128,704]{1,2,0:T(8,128)(2,1)} async-done(((bf16[4,128,704]{1,2,0:T(8,128)(2,1)}), bf16[16,128,704]{1,2,0:T(8,128)(2,1)}) %all-gather.20.cloned.1.call-update) | async-done | bytes 2883600 | tf_op jit(solution)/shard_map/all_gather | solution.py:879
  415.1 47.2 %all-gather.24.cloned.1.call-done = bf16[1,1024,2048]{2,1,0:T(8,128)(2,1)} async-done(((bf16[1,128,2048]{2,1,0:T(8,128)(2,1)}), bf16[1,1024,2048]{2,1,0:T(8,128)(2,1)}) %all-gather.24.cloned.1.call-update) | async-done | bytes 4194320 | tf_op jit(solution)/shard_map/all_gather | solution.py:891
  462.3 10.3 %multiply_convert_fusion.1 = (bf16[1024,704]{1,0:T(8,128)(2,1)S(1)}, bf16[1024,704]{1,0:T(8,128)(2,1)S(1)}, bf16[1024,704]{1,0:T(8,128)(2,1)}) fusion(f32[1024,1408]{1,0:T(8,128)} %fusion.46, bf16[1,1024,2048]{2,1,0:T(8,128)(2,1)} %all-gather.24.cloned.1.call-done, bf16[16,128,704]{1,2,0:T(8,128)(2,1)} %all-gather.20.cloned.1.call-done), kind=kOutput, calls=%fused_computation.12 | convolution fusion | flops 2963603456 | bytes 17170432 | tf_op jit(solution)/shard_map/dot_general | solution.py:980
  474.3 8.3 convolution_convert_fusion.1
  482.7 46.6 %reduce-scatter.13.cloned.1.call-done = bf16[128,2048]{1,0:T(8,128)(2,1)} async-done(((bf16[1024,2048]{1,0:T(8,128)(2,1)}), bf16[128,2048]{1,0:T(8,128)(2,1)}) %reduce-scatter.13.cloned.1.call-update) | async-done | bytes 524304 | tf_op jit(solution)/shard_map/reduce_scatter | solution.py:895
  530.8 2.6 fusion.44
  533.7 7.5 fusion.4
  541.2 11.6 %convolution_convert_fusion = bf16[2048,1408]{1,0:T(8,128)(2,1)} fusion(bf16[1024,2048]{1,0:T(8,128)(2,1)} %all-gather.16.cloned.1.call-done, bf16[1024,704]{1,0:T(8,128)(2,1)} %copy-done.28, bf16[1024,704]{1,0:T(8,128)(2,1)} %copy-done.27), kind=kOutput, calls=%fused_computation.1 | convolution fusion | flops 5914230784 | bytes 12845056 | tf_op jit(solution)/shard_map/td,tf->df/dot_general | solution.py:992
  552.9 28.3 %all-gather.22.cloned.1.call-done.grad_ref = bf16[1024,2048]{1,0:T(8,128)(2,1)} async-done(((bf16[128,2048]{1,0:T(8,128)(2,1)}), bf16[1024,2048]{1,0:T(8,128)(2,1)}) %all-gather.22.cloned.1.call-update) | async-done | bytes 4194320 | tf_op jit(solution)/shard_map/all_gather | solution.py:891
  581.2 4.5 convolution_convert_fusion.5
  589.5 26.0 %mixer_backward.1 = (bf16[1024,768]{1,0:T(8,128)(2,1)}, bf16[1024,16]{1,0:T(8,128)(2,1)S(1)}, f32[4,768]{1,0:T(4,128)S(1)}, f32[1,128]{1,0:T(1,128)S(1)}) custom-call(bf16[1024,2048]{1,0:T(8,128)(2,1)} %all-gather.22.cloned.1.call-done.grad_ref, bf16[2048,256]{1,0:T(8,128)(2,1)S(1)} %bitcast.207, bf16[1024,768]{1,0:T(8,128)(2,1)} %get-tuple-element.23.proj_ref, ...), custom_call_target="tpu_custom_call" | custom-call | tf_op jit(solution)/shard_map/mixer_backward/pallas_call | solution.py:734
  615.5 6.6 convolution_convert_fusion.4
  623.6 5.4 fusion.47
  628.9 3.3 add_convert_fusion
  633.6 6.7 convolution_convert_fusion.2
  640.4 1.7 reshape.283
  645.8 1.6 collective-permute-start.25
  648.0 2.8 collective-permute-start.24
  650.8 44.7 %reduce-scatter.21.cloned.1.call-done = bf16[512,1408]{1,0:T(8,128)(2,1)} async-done(((bf16[2048,1408]{1,0:T(8,128)(2,1)}), bf16[512,1408]{1,0:T(8,128)(2,1)}) %reduce-scatter.21.cloned.1.call-update) | async-done | bytes 1441808 | tf_op jit(solution)/shard_map/reduce_scatter | solution.py:886
  704.9 18.6 %collective-permute-done.20 = bf16[128,1408]{0,1:T(8,128)(2,1)S(1)} collective-permute-done((bf16[128,1408]{0,1:T(8,128)(2,1)S(1)}, bf16[128,1408]{0,1:T(8,128)(2,1)S(1)}, u32[]{:S(2)}, u32[]{:S(2)}) %collective-permute-start.20) | collective-permute-done | bytes 360480 | tf_op jit(solution)/shard_map/ppermute | solution.py:863
  723.5 6.6 collective-permute-done.21
  730.0 2.0 collective-permute-done.22
  733.7 1.7 copy.187
  735.4 3.8 copy.193
  739.3 2.9 fusion.30
  744.3 2.8 collective-permute-start.17
  747.1 3.0 collective-permute-done.19
  750.7 22.6 %reduce-scatter.17.cloned.1.call-done = bf16[512,768]{1,0:T(8,128)(2,1)} async-done(((bf16[2048,768]{1,0:T(8,128)(2,1)}), bf16[512,768]{1,0:T(8,128)(2,1)}) %reduce-scatter.17.cloned.1.call-update) | async-done | bytes 786448 | tf_op jit(solution)/shard_map/reduce_scatter | solution.py:886
  780.8 5.7 collective-permute-done.14
  786.5 16.0 %collective-permute-done.15 = bf16[128,768]{0,1:T(8,128)(2,1)S(1)} collective-permute-done((bf16[128,768]{0,1:T(8,128)(2,1)S(1)}, bf16[128,768]{0,1:T(8,128)(2,1)S(1)}, u32[]{:S(2)}, u32[]{:S(2)}) %collective-permute-start.15) | collective-permute-done | bytes 196640 | tf_op jit(solution)/shard_map/ppermute | solution.py:863
  802.5 6.9 collective-permute-done.16
  810.0 1.6 copy.192
  811.6 22.4 %reduce-scatter.15.cloned.1.call-done = bf16[128,2048]{1,0:T(8,128)(2,1)} async-done(((bf16[1024,2048]{1,0:T(8,128)(2,1)}), bf16[128,2048]{1,0:T(8,128)(2,1)}) %reduce-scatter.15.cloned.1.call-update) | async-done | bytes 524304 | tf_op jit(solution)/shard_map/reduce_scatter | solution.py:895
  836.0 19.3 %small_sums.1 = f32[2,4,96,128]{3,2,1,0:T(8,128)} custom-call(f32[96,128]{1,0:T(8,128)} %copy-done.20), custom_call_target="tpu_custom_call" | custom-call | tf_op jit(solution)/shard_map/small_sums/pallas_call | solution.py:838
  859.1 27.0 %reduce-scatter.11.cloned.1.call-done = bf16[128,2048]{1,0:T(8,128)(2,1)} async-done(((bf16[1024,2048]{1,0:T(8,128)(2,1)}), bf16[128,2048]{1,0:T(8,128)(2,1)}) %reduce-scatter.11.cloned.1.call-update) | async-done | bytes 524304 | tf_op jit(solution)/shard_map/reduce_scatter | solution.py:895
  886.1 2.1 fusion.17
  888.2 3.5 collective-permute-start.13
  (232 shorter events, 69.9 us)
Async XLA Ops:
  7.2 72.5 %copy-start = (f32[3,4,1024]{2,1,0:T(4,128)S(1)}, f32[3,4,1024]{2,1,0:T(4,128)}, u32[]{:S(2)}) copy-start(f32[3,4,1024]{2,1,0:T(4,128)} %param.18) | copy-start | bytes 147460
  7.2 72.5 %all-gather.12.cloned.1.call-start = ((), (), s32[]{:S(2)}) async-start(), calls=%async_computation.9 | async-start | bytes 3932160 | tf_op jit(solution)/shard_map/all_gather | solution.py:879
  9.1 15.4 %collective-permute-start = (bf16[128,768]{1,0:T(8,128)(2,1)S(1)}, bf16[128,768]{1,0:T(8,128)(2,1)S(1)}, u32[]{:S(2)}, u32[]{:S(2)}) collective-permute-start(bf16[128,768]{1,0:T(8,128)(2,1)S(1)} %bitcast.251), channel_id=1, source_target_pairs={{0,2},{2,4},{4,6},{6,0},{1,3},{3,5},{5,7},{7,1},{8,10},{10,12},{12... | collective-permute-start | bytes 589832 | tf_op jit(solution)/shard_map/ppermute | solution.py:863
  10.9 16.6 %collective-permute-start.1 = (bf16[128,768]{1,0:T(8,128)(2,1)S(1)}, bf16[128,768]{1,0:T(8,128)(2,1)S(1)}, u32[]{:S(2)}, u32[]{:S(2)}) collective-permute-start(bf16[128,768]{1,0:T(8,128)(2,1)S(1)} %bitcast.252), channel_id=1, source_target_pairs={{0,4},{2,6},{4,0},{6,2},{1,5},{3,7},{5,1},{7,3},{8,12},{10,14},{12... | collective-permute-start | bytes 589832 | tf_op jit(solution)/shard_map/ppermute | solution.py:863
  12.1 17.2 %collective-permute-start.2 = (bf16[128,768]{1,0:T(8,128)(2,1)S(1)}, bf16[128,768]{1,0:T(8,128)(2,1)S(1)}, u32[]{:S(2)}, u32[]{:S(2)}) collective-permute-start(bf16[128,768]{1,0:T(8,128)(2,1)S(1)} %bitcast.253), channel_id=1, source_target_pairs={{0,6},{2,0},{4,2},{6,4},{1,7},{3,1},{5,3},{7,5},{8,14},{10,8},{12,... | collective-permute-start | bytes 589832 | tf_op jit(solution)/shard_map/ppermute | solution.py:863
  20.0 10.6 %copy-start.11 = (bf16[1,256,2048]{2,1,0:T(8,128)(2,1)S(1)}, bf16[1,256,2048]{2,1,0:T(8,128)(2,1)}, u32[]{:S(2)}) copy-start(bf16[1,256,2048]{2,1,0:T(8,128)(2,1)} %param.12) | copy-start | bytes 3145732
  29.3 1.5 copy-start.21
  29.4 2.5 copy-start.18
  30.5 11.1 %copy-start.25 = (s32[1,8]{1,0:T(1,128)S(1)}, s32[1,8]{1,0:T(1,128)}, u32[]{:S(2)}) copy-start(s32[1,8]{1,0:T(1,128)} %param.14) | copy-start | bytes 100
  30.5 92.3 %all-gather.10.cloned.1.call-start = ((), (), s32[]{:S(2)}) async-start(), calls=%async_computation.8 | async-start | bytes 4718592 | tf_op jit(solution)/shard_map/all_gather | solution.py:891
  30.5 12.2 %copy-start.22 = (bf16[128,8]{0,1:T(8,128)(2,1)S(1)}, bf16[128,8]{0,1:T(8,128)(2,1)}, u32[]{:S(2)}) copy-start(bf16[128,8]{0,1:T(8,128)(2,1)} %param.20) | copy-start | bytes 6148
  30.6 92.3 %copy-start.10 = (f32[128]{0:T(128)S(1)}, f32[128]{0:T(128)}, u32[]{:S(2)}) copy-start(f32[128]{0:T(128)} %param.17) | copy-start | bytes 1540
  31.8 137.3 %all-gather.14.cloned.1.call-start = ((), (), s32[]{:S(2)}) async-start(), calls=%async_computation.10 | async-start | bytes 1310720 | tf_op jit(solution)/shard_map/all_gather | solution.py:879
  32.0 6.0 collective-permute-start.5
  32.2 6.3 collective-permute-start.3
  34.4 6.3 collective-permute-start.4
  41.5 212.0 %reduce-scatter.9.cloned.1.call-start = ((), (), s32[]{:S(2)}) async-start(), calls=%async_computation.11 | async-start | bytes 4718592 | tf_op jit(solution)/shard_map/reduce_scatter | solution.py:895
  169.1 5.0 copy-start.3
  174.1 148.8 %all-gather.18.cloned.1.call-start = ((), (), s32[]{:S(2)}) async-start(), calls=%async_computation.13 | async-start | bytes 7208960 | tf_op jit(solution)/shard_map/all_gather | solution.py:879
  180.9 19.4 %collective-permute-start.6 = (bf16[128,1408]{1,0:T(8,128)(2,1)}, bf16[128,1408]{1,0:T(8,128)(2,1)}, u32[]{:S(2)}, u32[]{:S(2)}) collective-permute-start(bf16[128,1408]{1,0:T(8,128)(2,1)} %bitcast.233), channel_id=1, source_target_pairs={{0,2},{2,4},{4,6},{6,0},{1,3},{3,5},{5,7},{7,1},{8,10},{10,12},{12... | collective-permute-start | bytes 1081352 | tf_op jit(solution)/shard_map/ppermute | solution.py:863
  183.5 55.2 %collective-permute-start.7 = (bf16[128,1408]{1,0:T(8,128)(2,1)}, bf16[128,1408]{1,0:T(8,128)(2,1)}, u32[]{:S(2)}, u32[]{:S(2)}) collective-permute-start(bf16[128,1408]{1,0:T(8,128)(2,1)} %bitcast.234), channel_id=1, source_target_pairs={{0,4},{2,6},{4,0},{6,2},{1,5},{3,7},{5,1},{7,3},{8,12},{10,14},{12... | collective-permute-start | bytes 1081352 | tf_op jit(solution)/shard_map/ppermute | solution.py:863
  186.5 54.7 %collective-permute-start.8 = (bf16[128,1408]{1,0:T(8,128)(2,1)S(1)}, bf16[128,1408]{1,0:T(8,128)(2,1)}, u32[]{:S(2)}, u32[]{:S(2)}) collective-permute-start(bf16[128,1408]{1,0:T(8,128)(2,1)S(1)} %bitcast.235), channel_id=1, source_target_pairs={{0,6},{2,0},{4,2},{6,4},{1,7},{3,1},{5,3},{7,5},{8,14},{10,8},{12,... | collective-permute-start | bytes 1081352 | tf_op jit(solution)/shard_map/ppermute | solution.py:863
  242.7 10.7 %copy-start.12 = (bf16[1,256,2048]{2,1,0:T(8,128)(2,1)S(1)}, bf16[1,256,2048]{2,1,0:T(8,128)(2,1)}, u32[]{:S(2)}) copy-start(bf16[1,256,2048]{2,1,0:T(8,128)(2,1)} %param.12) | copy-start | bytes 3145732
  242.7 12.0 %copy-start.19 = (f32[2048]{0:T(1024)S(1)}, f32[2048]{0:T(1024)}, u32[]{:S(2)}) copy-start(f32[2048]{0:T(1024)} %param.16) | copy-start | bytes 24580
  244.1 126.5 %all-gather.16.cloned.1.call-start = ((), (), s32[]{:S(2)}) async-start(), calls=%async_computation.12 | async-start | bytes 4718592 | tf_op jit(solution)/shard_map/all_gather | solution.py:891
  256.8 158.3 %all-gather.20.cloned.1.call-start = ((), (), s32[]{:S(2)}) async-start(), calls=%async_computation.14 | async-start | bytes 3604480 | tf_op jit(solution)/shard_map/all_gather | solution.py:879
  258.1 15.9 %collective-permute-start.11 = (bf16[128,704]{0,1:T(8,128)(2,1)S(1)}, bf16[128,704]{0,1:T(8,128)(2,1)S(1)}, u32[]{:S(2)}, u32[]{:S(2)}) collective-permute-start(bf16[128,704]{0,1:T(8,128)(2,1)S(1)} %get-tuple-element.135), channel_id=1, source_target_pairs={{0,6},{2,0},{4,2},{6,4},{1,7},{3,1},{5,3},{7,5},{8,14},{10,8},{12,... | collective-permute-start | bytes 540680 | tf_op jit(solution)/shard_map/ppermute | solution.py:863
  258.2 15.9 %collective-permute-start.10 = (bf16[128,704]{0,1:T(8,128)(2,1)S(1)}, bf16[128,704]{0,1:T(8,128)(2,1)S(1)}, u32[]{:S(2)}, u32[]{:S(2)}) collective-permute-start(bf16[128,704]{0,1:T(8,128)(2,1)S(1)} %get-tuple-element.136), channel_id=1, source_target_pairs={{0,4},{2,6},{4,0},{6,2},{1,5},{3,7},{5,1},{7,3},{8,12},{10,14},{12... | collective-permute-start | bytes 540680 | tf_op jit(solution)/shard_map/ppermute | solution.py:863
  262.5 12.0 %collective-permute-start.9 = (bf16[128,704]{0,1:T(8,128)(2,1)S(1)}, bf16[128,704]{0,1:T(8,128)(2,1)S(1)}, u32[]{:S(2)}, u32[]{:S(2)}) collective-permute-start(bf16[128,704]{0,1:T(8,128)(2,1)S(1)} %get-tuple-element.137), channel_id=1, source_target_pairs={{0,2},{2,4},{4,6},{6,0},{1,3},{3,5},{5,7},{7,1},{8,10},{10,12},{12... | collective-permute-start | bytes 540680 | tf_op jit(solution)/shard_map/ppermute | solution.py:863
  275.7 186.6 %all-gather.24.cloned.1.call-start = ((), (), s32[]{:S(2)}) async-start(), calls=%async_computation.23 | async-start | bytes 4718592 | tf_op jit(solution)/shard_map/all_gather | solution.py:891
  277.7 251.5 %reduce-scatter.13.cloned.1.call-start = ((), (), s32[]{:S(2)}) async-start(), calls=%async_computation.16 | async-start | bytes 4718592 | tf_op jit(solution)/shard_map/reduce_scatter | solution.py:895
  462.3 12.0 %copy-start.23 = (bf16[16,128,1408]{2,1,0:T(8,128)(2,1)S(1)}, bf16[16,128,1408]{2,1,0:T(8,128)(2,1)}, u32[]{:S(2)}) copy-start(bf16[16,128,1408]{2,1,0:T(8,128)(2,1)} %all-gather.18.cloned.1.call-done) | copy-start | bytes 17301508
  472.6 1.7 copy-start.28
  482.6 98.5 %all-gather.22.cloned.1.call-start = ((), (), s32[]{:S(2)}) async-start(), calls=%async_computation.17 | async-start | bytes 4718592 | tf_op jit(solution)/shard_map/all_gather | solution.py:891
  533.5 107.0 %reduce-scatter.23.cloned.1.call-start = ((), (), s32[]{:S(2)}) async-start(), calls=%async_computation.22 | async-start | bytes 3604480 | tf_op jit(solution)/shard_map/reduce_scatter | solution.py:886
  541.2 154.4 %reduce-scatter.21.cloned.1.call-start = ((), (), s32[]{:S(2)}) async-start(), calls=%async_computation.21 | async-start | bytes 7208960 | tf_op jit(solution)/shard_map/reduce_scatter | solution.py:886
  552.9 33.2 %copy-start.2 = (bf16[16,128,256]{2,1,0:T(8,128)(2,1)S(1)}, bf16[16,128,256]{2,1,0:T(8,128)(2,1)}, u32[]{:S(2)}) copy-start(bf16[16,128,256]{2,1,0:T(8,128)(2,1)} %all-gather.14.cloned.1.call-done) | copy-start | bytes 3145732
  552.9 189.3 %reduce-scatter.19.cloned.1.call-start = ((), (), s32[]{:S(2)}) async-start(), calls=%async_computation.20 | async-start | bytes 1310720 | tf_op jit(solution)/shard_map/reduce_scatter | solution.py:886
  585.7 187.6 %reduce-scatter.17.cloned.1.call-start = ((), (), s32[]{:S(2)}) async-start(), calls=%async_computation.19 | async-start | bytes 3932160 | tf_op jit(solution)/shard_map/reduce_scatter | solution.py:886
  586.0 1.2 copy-start.4
  589.5 26.0 %copy-start.14 = (bf16[1024,2048]{1,0:T(8,128)(2,1)S(1)}, bf16[1024,2048]{1,0:T(8,128)(2,1)}, u32[]{:S(2)}) copy-start(bf16[1024,2048]{1,0:T(8,128)(2,1)} %all-gather.10.cloned.1.call-done.n1_ref) | copy-start | bytes 12582916
  622.1 1.4 copy-start.24
  622.2 211.8 %reduce-scatter.15.cloned.1.call-start = ((), (), s32[]{:S(2)}) async-start(), calls=%async_computation.18 | async-start | bytes 4718592 | tf_op jit(solution)/shard_map/reduce_scatter | solution.py:895
  632.2 1.4 copy-start.26
  632.3 253.9 %reduce-scatter.11.cloned.1.call-start = ((), (), s32[]{:S(2)}) async-start(), calls=%async_computation.15 | async-start | bytes 4718592 | tf_op jit(solution)/shard_map/reduce_scatter | solution.py:895
  645.8 54.9 %collective-permute-start.25 = (bf16[128,704]{0,1:T(8,128)(2,1)}, bf16[128,704]{0,1:T(8,128)(2,1)}, u32[]{:S(2)}, u32[]{:S(2)}) collective-permute-start(bf16[128,704]{0,1:T(8,128)(2,1)} %bitcast.203), channel_id=1, source_target_pairs={{0,6},{2,0},{4,2},{6,4},{1,7},{3,1},{5,3},{7,5},{8,14},{10,8},{12,... | collective-permute-start | bytes 540680 | tf_op jit(solution)/shard_map/ppermute | solution.py:863
  647.4 54.8 %collective-permute-start.23 = (bf16[128,704]{0,1:T(8,128)(2,1)}, bf16[128,704]{0,1:T(8,128)(2,1)}, u32[]{:S(2)}, u32[]{:S(2)}) collective-permute-start(bf16[128,704]{0,1:T(8,128)(2,1)} %bitcast.205), channel_id=1, source_target_pairs={{0,2},{2,4},{4,6},{6,0},{1,3},{3,5},{5,7},{7,1},{8,10},{10,12},{12... | collective-permute-start | bytes 540680 | tf_op jit(solution)/shard_map/ppermute | solution.py:863
  648.0 54.1 %collective-permute-start.24 = (bf16[128,704]{0,1:T(8,128)(2,1)}, bf16[128,704]{0,1:T(8,128)(2,1)}, u32[]{:S(2)}, u32[]{:S(2)}) collective-permute-start(bf16[128,704]{0,1:T(8,128)(2,1)} %bitcast.204), channel_id=1, source_target_pairs={{0,4},{2,6},{4,0},{6,2},{1,5},{3,7},{5,1},{7,3},{8,12},{10,14},{12... | collective-permute-start | bytes 540680 | tf_op jit(solution)/shard_map/ppermute | solution.py:863
  697.7 25.8 %collective-permute-start.20 = (bf16[128,1408]{0,1:T(8,128)(2,1)S(1)}, bf16[128,1408]{0,1:T(8,128)(2,1)S(1)}, u32[]{:S(2)}, u32[]{:S(2)}) collective-permute-start(bf16[128,1408]{0,1:T(8,128)(2,1)S(1)} %bitcast.232), channel_id=1, source_target_pairs={{0,2},{2,4},{4,6},{6,0},{1,3},{3,5},{5,7},{7,1},{8,10},{10,12},{12... | collective-permute-start | bytes 1081352 | tf_op jit(solution)/shard_map/ppermute | solution.py:863
  699.2 30.9 %collective-permute-start.21 = (bf16[128,1408]{0,1:T(8,128)(2,1)S(1)}, bf16[128,1408]{0,1:T(8,128)(2,1)S(1)}, u32[]{:S(2)}, u32[]{:S(2)}) collective-permute-start(bf16[128,1408]{0,1:T(8,128)(2,1)S(1)} %bitcast.231), channel_id=1, source_target_pairs={{0,4},{2,6},{4,0},{6,2},{1,5},{3,7},{5,1},{7,3},{8,12},{10,14},{12... | collective-permute-start | bytes 1081352 | tf_op jit(solution)/shard_map/ppermute | solution.py:863
  700.6 31.4 %collective-permute-start.22 = (bf16[128,1408]{0,1:T(8,128)(2,1)S(1)}, bf16[128,1408]{0,1:T(8,128)(2,1)}, u32[]{:S(2)}, u32[]{:S(2)}) collective-permute-start(bf16[128,1408]{0,1:T(8,128)(2,1)S(1)} %bitcast.230), channel_id=1, source_target_pairs={{0,6},{2,0},{4,2},{6,4},{1,7},{3,1},{5,3},{7,5},{8,14},{10,8},{12,... | collective-permute-start | bytes 1081352 | tf_op jit(solution)/shard_map/ppermute | solution.py:863
  743.2 7.0 collective-permute-start.19
  743.2 6.9 collective-permute-start.18
  744.3 6.4 collective-permute-start.17
  775.1 11.4 %collective-permute-start.14 = (bf16[128,768]{0,1:T(8,128)(2,1)S(1)}, bf16[128,768]{0,1:T(8,128)(2,1)S(1)}, u32[]{:S(2)}, u32[]{:S(2)}) collective-permute-start(bf16[128,768]{0,1:T(8,128)(2,1)S(1)} %bitcast.256), channel_id=1, source_target_pairs={{0,2},{2,4},{4,6},{6,0},{1,3},{3,5},{5,7},{7,1},{8,10},{10,12},{12... | collective-permute-start | bytes 589832 | tf_op jit(solution)/shard_map/ppermute | solution.py:863
  776.6 25.9 %collective-permute-start.15 = (bf16[128,768]{0,1:T(8,128)(2,1)S(1)}, bf16[128,768]{0,1:T(8,128)(2,1)S(1)}, u32[]{:S(2)}, u32[]{:S(2)}) collective-permute-start(bf16[128,768]{0,1:T(8,128)(2,1)S(1)} %bitcast.255), channel_id=1, source_target_pairs={{0,4},{2,6},{4,0},{6,2},{1,5},{3,7},{5,1},{7,3},{8,12},{10,14},{12... | collective-permute-start | bytes 589832 | tf_op jit(solution)/shard_map/ppermute | solution.py:863
  778.1 31.4 %collective-permute-start.16 = (bf16[128,768]{0,1:T(8,128)(2,1)S(1)}, bf16[128,768]{0,1:T(8,128)(2,1)S(1)}, u32[]{:S(2)}, u32[]{:S(2)}) collective-permute-start(bf16[128,768]{0,1:T(8,128)(2,1)S(1)} %bitcast.254), channel_id=1, source_target_pairs={{0,6},{2,0},{4,2},{6,4},{1,7},{3,1},{5,3},{7,5},{8,14},{10,8},{12,... | collective-permute-start | bytes 589832 | tf_op jit(solution)/shard_map/ppermute | solution.py:863
  809.8 24.2 %copy-start.13 = (bf16[1,256,2048]{2,1,0:T(8,128)(2,1)S(1)}, bf16[1,256,2048]{2,1,0:T(8,128)(2,1)}, u32[]{:S(2)}) copy-start(bf16[1,256,2048]{2,1,0:T(8,128)(2,1)} %param.12) | copy-start | bytes 3145732
  810.0 76.1 %copy-start.15 = (bf16[128,2048]{1,0:T(8,128)(2,1)S(1)}, bf16[128,2048]{1,0:T(8,128)(2,1)}, u32[]{:S(2)}) copy-start(bf16[128,2048]{1,0:T(8,128)(2,1)} %reduce-scatter.9.cloned.1.call-done) | copy-start | bytes 1572868
  811.6 74.5 %copy-start.16 = (bf16[128,2048]{1,0:T(8,128)(2,1)S(1)}, bf16[128,2048]{1,0:T(8,128)(2,1)}, u32[]{:S(2)}) copy-start(bf16[128,2048]{1,0:T(8,128)(2,1)} %reduce-scatter.13.cloned.1.call-done) | copy-start | bytes 1572868
  811.6 74.5 %copy-start.17 = (bf16[1,256,2048]{2,1,0:T(8,128)(2,1)S(1)}, bf16[1,256,2048]{2,1,0:T(8,128)(2,1)}, u32[]{:S(2)}) copy-start(bf16[1,256,2048]{2,1,0:T(8,128)(2,1)} %param.13) | copy-start | bytes 3145732
  888.2 5.3 collective-permute-start.13
  891.8 3.0 collective-permute-start.12
  893.6 2.3 copy-start.1
  (7 other events, 6.8 us)
Sparse Core Ops, SparseCore 0:
  30.6 44.2 all-gather.11
  77.0 45.7 all-gather.9
  125.2 26.9 all-gather.13
  174.2 79.1 reduce-scatter.8
  255.7 67.1 all-gather.17
  324.9 45.5 all-gather.15
  373.0 42.0 all-gather.19
  416.7 45.5 all-gather.23
  482.8 46.4 reduce-scatter.12
  533.6 47.5 all-gather.21
  584.8 42.0 reduce-scatter.22
  629.7 65.8 reduce-scatter.20
  698.5 27.6 reduce-scatter.18
  729.3 43.9 reduce-scatter.16
  775.5 58.3 reduce-scatter.14
  836.2 49.8 reduce-scatter.10

commit v3 on v2

--- a/solution.py
+++ b/solution.py
@@ -762,7 +762,7 @@
     return jnp.stack(columns, axis=1), chunks.astype(f32)
 
 
-def swap_copy(source, target, send, recv, where):
+def remote(source, target, send, recv, where):
     return pltpu.make_async_remote_copy(
         src_ref=source,
         dst_ref=target,
@@ -775,16 +775,566 @@
 
 def greet(partners):
     barrier = pltpu.get_barrier_semaphore()
-    for partner in partners:
-        pl.semaphore_signal(
-            barrier, inc=1, device_id=partner, device_id_type=pl.DeviceIdType.MESH
-        )
-    pl.semaphore_wait(barrier, len(partners))
+    for partner, there in partners:
+
+        @pl.when(there)
+        def _(partner=partner):
+            pl.semaphore_signal(
+                barrier, inc=1, device_id=partner, device_id_type=pl.DeviceIdType.MESH
+            )
+
+    pl.semaphore_wait(barrier, sum(there.astype(jnp.int32) for _, there in partners))
 
 
 def around(axis):
     count, place = lax.axis_size(axis), lax.axis_index(axis)
     return [lax.rem(place + by, count) for by in range(1, count)]
+
+
+def line_partners():
+    count, place, core = lax.axis_size("seq"), lax.axis_index("seq"), lax.axis_index("tp")
+    return [
+        ({"seq": jnp.minimum(place + 1, count - 1)}, place < count - 1),
+        ({"seq": jnp.maximum(place - 1, 0)}, place > 0),
+        ({"tp": 1 - core}, core >= 0),
+    ]
+
+
+class Line:
+    def __init__(self):
+        self.count, self.place = lax.axis_size("seq"), lax.axis_index("seq")
+        self.core = lax.axis_index("tp")
+        self.other = 1 - self.core
+        self.right = {"seq": jnp.minimum(self.place + 1, self.count - 1)}
+        self.left = {"seq": jnp.maximum(self.place - 1, 0)}
+        self.across = {"tp": self.other}
+
+
+class Gather:
+    sems = 5
+
+    def __init__(self, line, slots, sems):
+        self.line, self.slots, self.sems = line, slots, sems
+
+    def copy(self, kind, seq):
+        line = self.line
+        send = {"right": 0, "left": 1, "across": 2}[kind]
+        recv = 4 if kind == "across" else 3
+        slot = self.slots.at[seq, line.core]
+        where = {"right": line.right, "left": line.left, "across": line.across}[kind]
+        return remote(slot, slot, self.sems.at[send, seq], self.sems.at[recv, seq], where)
+
+    def forward(self, seq, right, left):
+        line = self.line
+        if right:
+
+            @pl.when(line.place < line.count - 1)
+            def _():
+                self.copy("right", seq).start()
+
+        if left:
+
+            @pl.when(line.place > 0)
+            def _():
+                self.copy("left", seq).start()
+
+        self.copy("across", seq).start()
+
+    def phase(self, by):
+        line = self.line
+        if by == 0:
+            self.forward(line.place, True, True)
+            return
+
+        @pl.when(line.place - by >= 0)
+        def _():
+            self.copy("right", line.place - by).wait_recv()
+            self.forward(line.place - by, True, False)
+
+        @pl.when(line.place + by < line.count)
+        def _():
+            self.copy("left", line.place + by).wait_recv()
+            self.forward(line.place + by, False, True)
+
+    def finish(self):
+        line = self.line
+        for seq in range(line.count):
+
+            @pl.when((line.place >= seq) & (line.place < line.count - 1))
+            def _():
+                self.copy("right", seq).wait_send()
+
+            @pl.when((line.place <= seq) & (line.place > 0))
+            def _():
+                self.copy("left", seq).wait_send()
+
+            self.copy("across", seq).wait()
+
+
+class Scatter:
+    sems = 5
+
+    def __init__(self, line, blocks, came, across, sems):
+        self.line, self.blocks, self.came, self.across, self.sems = line, blocks, came, across, sems
+
+    def over(self, seq):
+        line = self.line
+        return remote(
+            self.blocks.at[seq, line.other],
+            self.across.at[seq],
+            self.sems.at[0, seq],
+            self.sems.at[1, seq],
+            line.across,
+        )
+
+    def along(self, kind, seq):
+        line = self.line
+        way = {"right": 0, "left": 1}[kind]
+        return remote(
+            self.blocks.at[seq, line.core],
+            self.came.at[way, seq],
+            self.sems.at[2, seq],
+            self.sems.at[3 + way, seq],
+            line.right if way == 0 else line.left,
+        )
+
+    def offer(self, seq):
+        self.over(seq).start()
+
+    def chip_sum(self, seq):
+        self.over(seq).wait_recv()
+        return self.blocks[seq, self.line.core].astype(jnp.float32) + self.across[seq].astype(
+            jnp.float32
+        )
+
+    def pass_on(self, kind, seq):
+        line = self.line
+        first = line.place == (0 if kind == "right" else line.count - 1)
+        way = {"right": 0, "left": 1}[kind]
+        total = self.chip_sum(seq)
+
+        @pl.when(first)
+        def _():
+            self.blocks[seq, line.core] = total.astype(jnp.bfloat16)
+
+        @pl.when(jnp.logical_not(first))
+        def _():
+            self.along(kind, seq).wait_recv()
+            self.blocks[seq, line.core] = (
+                total + self.came[way, seq].astype(jnp.float32)
+            ).astype(jnp.bfloat16)
+
+        self.along(kind, seq).start()
+
+    def target(self, k):
+        line = self.line
+        return jnp.where(line.place < line.count // 2, line.count - 1 - k, k)
+
+    def near(self, k):
+        line = self.line
+        low = line.place < line.count // 2
+
+        @pl.when(low & (line.count - 1 - k > line.place))
+        def _():
+            self.pass_on("right", line.count - 1 - k)
+
+        @pl.when(jnp.logical_not(low) & (k < line.place))
+        def _():
+            self.pass_on("left", k)
+
+    def far(self, k):
+        line = self.line
+        low = line.place < line.count // 2
+
+        @pl.when(low & (k < line.place))
+        def _():
+            self.pass_on("left", k)
+
+        @pl.when(jnp.logical_not(low) & (line.count - 1 - k > line.place))
+        def _():
+            self.pass_on("right", line.count - 1 - k)
+
+    def wait_own(self):
+        line = self.line
+
+        @pl.when(line.place > 0)
+        def _():
+            self.along("right", line.place).wait_recv()
+
+        @pl.when(line.place < line.count - 1)
+        def _():
+            self.along("left", line.place).wait_recv()
+
+        self.over(line.place).wait_recv()
+
+    def own_rows(self, rows):
+        line = self.line
+        f32 = jnp.float32
+        total = self.blocks[line.place, line.core, rows].astype(f32)
+        total = total + self.across[line.place, rows].astype(f32)
+        from_left = self.came[0, line.place, rows].astype(f32)
+        from_right = self.came[1, line.place, rows].astype(f32)
+        total = total + jnp.where(line.place > 0, from_left, 0.0)
+        return total + jnp.where(line.place < line.count - 1, from_right, 0.0)
+
+    def finish(self):
+        line = self.line
+        for seq in range(line.count):
+            self.over(seq).wait_send()
+
+            @pl.when(line.place != seq)
+            def _():
+                self.along("right", seq).wait_send()
+
+
+def product_rows(left_ref, right_ref, blocks, seq, tile=512):
+    cores, rows, width = blocks.shape[1:]
+    left = left_ref[pl.ds(pl.multiple_of(seq * cores * rows, cores * rows), cores * rows)]
+
+    def columns(t, _):
+        span = pl.ds(pl.multiple_of(t * tile, tile), tile)
+        part = mul(left, right_ref[span], (1, 1)).astype(jnp.bfloat16)
+        for core in range(cores):
+            blocks[seq, core, :, span] = part[core * rows : (core + 1) * rows]
+        return 0
+
+    lax.fori_loop(0, width // tile, columns, 0)
+
+
+STEP = 32
+
+
+def over_rows(count, body):
+    def step(i, _):
+        body(pl.ds(pl.multiple_of(i * STEP, STEP), STEP), i)
+        return 0
+
+    lax.fori_loop(0, count // STEP, step, 0)
+
+
+def own_span(core, rows, inner):
+    return pl.ds(pl.multiple_of(core * rows + inner.start, STEP), inner.size)
+
+
+def resid_kernel(
+    mix_ref, o_ref, x_ref, g_ref, gain_ref, resid_ref, n2_ref, g_full_ref,
+    blocks, came, across, sum_sems, n2_sems, g_sems,
+):
+    line = Line()
+    greet(line_partners())
+    rows = n2_ref.shape[2]
+    total = Scatter(line, blocks, came, across, sum_sems)
+    n2 = Gather(line, n2_ref, n2_sems)
+    grads = Gather(line, g_full_ref, g_sems)
+    g_full_ref[line.place, line.core] = g_ref[
+        pl.ds(pl.multiple_of(line.core * rows, rows), rows)
+    ]
+    for k in range(line.count):
+        seq = total.target(k)
+        product_rows(mix_ref, o_ref, blocks, seq)
+        total.offer(seq)
+    total.near(0)
+    grads.phase(0)
+    for k in range(1, line.count):
+        total.near(k)
+        grads.phase(k)
+    for k in range(line.count):
+        total.far(k)
+    total.wait_own()
+
+    def normed(span, i):
+        x_span = pl.ds(pl.multiple_of(line.core * rows + i * STEP, STEP), STEP)
+        resid = x_ref[x_span].astype(jnp.float32) + total.own_rows(span)
+        resid_ref[span] = resid
+        n2_ref[line.place, line.core, span] = (
+            resid * norm_scale(resid) * gain_ref[...]
+        ).astype(jnp.bfloat16)
+
+    over_rows(rows, normed)
+    for k in range(line.count):
+        n2.phase(k)
+    total.finish()
+    n2.finish()
+    grads.finish()
+
+
+def dma_sems(*shape):
+    return pltpu.SemaphoreType.DMA(shape)
+
+
+def line_call(kernel, collective_id, name, outs, scratch, args, limit=56):
+    return pl.pallas_call(
+        kernel,
+        out_shape=[jax.ShapeDtypeStruct(*out) for out in outs],
+        in_specs=in_vmem(len(args)),
+        out_specs=in_vmem(len(outs)),
+        scratch_shapes=scratch,
+        compiler_params=pltpu.CompilerParams(
+            collective_id=collective_id,
+            has_side_effects=True,
+            vmem_limit_bytes=limit * 1024 * 1024,
+        ),
+        name=name,
+    )(*args)
+
+
+def scatter_scratch(seqs, cores, rows, width):
+    b16 = jnp.bfloat16
+    return [
+        pltpu.VMEM((seqs, cores, rows, width), b16),
+        pltpu.VMEM((2, seqs, rows, width), b16),
+        pltpu.VMEM((seqs, rows, width), b16),
+    ]
+
+
+def run_resid(mix, o_full, x, g, gain):
+    seqs, cores, (piece, width) = lax.axis_size("seq"), lax.axis_size("tp"), x.shape
+    rows, b16 = piece // cores, jnp.bfloat16
+    outs = (
+        ((rows, width), jnp.float32),
+        ((seqs, cores, rows, width), b16),
+        ((seqs, cores, rows, width), b16),
+    )
+    scratch = scatter_scratch(seqs, cores, rows, width) + [dma_sems(5, seqs)] * 3
+    resid, n2, g_full = line_call(
+        resid_kernel, 1, "resid_norm", outs, scratch, (mix, o_full, x, g, gain)
+    )
+    return resid, n2.reshape(-1, width), g_full.reshape(-1, width)
+
+
+def grad_resid_kernel(
+    dgu_ref, gate_up_ref, hidden_ref, down_ref, resid_ref, g_ref, gain_ref,
+    grad_resid_ref, grad_attn_ref, gain_grad_ref, result_ref,
+    blocks, came, across, out_blocks, out_came, out_across,
+    sum_sems, out_sems, attn_sems, swap_sems,
+):
+    line = Line()
+    greet(line_partners())
+    rows = resid_ref.shape[0]
+    total = Scatter(line, blocks, came, across, sum_sems)
+    result = Scatter(line, out_blocks, out_came, out_across, out_sems)
+    attn = Gather(line, grad_attn_ref, attn_sems)
+    for k in range(line.count):
+        seq = total.target(k)
+        product_rows(dgu_ref, gate_up_ref, blocks, seq)
+        total.offer(seq)
+        total.near(k)
+    for k in range(line.count):
+        total.far(k)
+        product_rows(hidden_ref, down_ref, out_blocks, total.target(k))
+    total.wait_own()
+    gain_grad_ref[...] = jnp.zeros_like(gain_grad_ref)
+
+    def back(span, i):
+        own_span = pl.ds(pl.multiple_of(line.core * rows + i * STEP, STEP), STEP)
+        resid = resid_ref[span]
+        grad_two = total.own_rows(span)
+        scale = norm_scale(resid)
+        gain_grad_ref[...] += jnp.sum(grad_two * resid * scale, axis=0, keepdims=True)
+        grad = g_ref[own_span].astype(jnp.float32) + norm_back(
+            resid, scale, gain_ref[...], grad_two
+        )
+        grad_resid_ref[span] = grad
+        grad_attn_ref[line.place, line.core, span] = grad.astype(jnp.bfloat16)
+
+    over_rows(rows, back)
+    attn.phase(0)
+    for k in range(line.count):
+        result.offer(result.target(k))
+    for k in range(1, line.count):
+        result.near(k - 1)
+        attn.phase(k)
+    for k in range(line.count):
+        result.far(k)
+    result.wait_own()
+
+    def finish(span, i):
+        own_span = pl.ds(pl.multiple_of(line.core * rows + i * STEP, STEP), STEP)
+        result_ref[own_span] = (resid_ref[span] + result.own_rows(span)).astype(jnp.bfloat16)
+
+    over_rows(rows, finish)
+    swap = own_swap(line, result_ref, rows, swap_sems)
+    swap.start()
+    total.finish()
+    result.finish()
+    attn.finish()
+    swap.wait()
+
+
+def own_swap(line, ref, rows, sems):
+    own = ref.at[pl.ds(pl.multiple_of(line.core * rows, rows), rows)]
+    return remote(own, own, sems.at[0], sems.at[1], line.across)
+
+
+def run_grad_resid(grad_gate_up, gate_up, hidden, down, resid, g, gain):
+    seqs, cores, (piece, width) = lax.axis_size("seq"), lax.axis_size("tp"), g.shape
+    rows, b16, f32 = piece // cores, jnp.bfloat16, jnp.float32
+    outs = (
+        ((rows, width), f32),
+        ((seqs, cores, rows, width), b16),
+        ((1, width), f32),
+        ((piece, width), b16),
+    )
+    scratch = scatter_scratch(seqs, cores, rows, width) * 2
+    scratch = scratch + [dma_sems(5, seqs)] * 3 + [dma_sems(2)]
+    grad_resid, grad_attn, gain_grad, result = line_call(
+        grad_resid_kernel, 2, "grad_resid", outs, scratch,
+        (grad_gate_up, gate_up, hidden, down, resid, g, gain),
+    )
+    return grad_resid, grad_attn.reshape(-1, width), gain_grad, result
+
+
+def input_grad_kernel(
+    grad_proj_ref, qkv_ref, grad_logit_ref, beta_ref, x_ref, grad_resid_ref, gain_ref,
+    input_grad_ref, gain_grad_ref,
+    blocks, came, across, sum_sems, swap_sems,
+):
+    line = Line()
+    greet(line_partners())
+    rows = grad_resid_ref.shape[0]
+    total = Scatter(line, blocks, came, across, sum_sems)
+
+    def product(seq, tile=512):
+        cores, _, width = blocks.shape[1:]
+        at = pl.ds(pl.multiple_of(seq * cores * rows, cores * rows), cores * rows)
+        left, logit = grad_proj_ref[at], grad_logit_ref[at]
+
+        def columns(t, _):
+            span = pl.ds(pl.multiple_of(t * tile, tile), tile)
+            part = mul(left, qkv_ref[span], (1, 1)) + mul(logit, beta_ref[:, span], (1, 0))
+            part = part.astype(jnp.bfloat16)
+            for core in range(cores):
+                blocks[seq, core, :, span] = part[core * rows : (core + 1) * rows]
+            return 0
+
+        lax.fori_loop(0, width // tile, columns, 0)
+
+    for k in range(line.count):
+        seq = total.target(k)
+        product(seq)
+        total.offer(seq)
+        total.near(k)
+    for k in range(line.count):
+        total.far(k)
+    total.wait_own()
+    gain_grad_ref[...] = jnp.zeros_like(gain_grad_ref)
+
+    def back(span, i):
+        own_span = pl.ds(pl.multiple_of(line.core * rows + i * STEP, STEP), STEP)
+        x = x_ref[own_span].astype(jnp.float32)
+        grad_one = total.own_rows(span)
+        scale = norm_scale(x)
+        gain_grad_ref[...] += jnp.sum(grad_one * x * scale, axis=0, keepdims=True)
+        input_grad_ref[own_span] = (
+            grad_resid_ref[span] + norm_back(x, scale, gain_ref[...], grad_one)
+        ).astype(jnp.bfloat16)
+
+    over_rows(rows, back)
+    swap = own_swap(line, input_grad_ref, rows, swap_sems)
+    swap.start()
+    total.finish()
+    swap.wait()
+
+
+def run_input_grad(grad_proj, qkv, grad_logit, beta, x, grad_resid, gain):
+    seqs, cores, (piece, width) = lax.axis_size("seq"), lax.axis_size("tp"), x.shape
+    rows, b16, f32 = piece // cores, jnp.bfloat16, jnp.float32
+    outs = (((piece, width), b16), ((1, width), f32))
+    scratch = scatter_scratch(seqs, cores, rows, width) + [dma_sems(5, seqs), dma_sems(2)]
+    return line_call(
+        input_grad_kernel, 3, "input_grad", outs, scratch,
+        (grad_proj, qkv, grad_logit, beta, x, grad_resid, gain),
+    )
+
+
+def normed_kernel(
+    x_ref, gain_ref, parts_ref, beta_ref, n1_ref, qkv_ref, beta_full_ref,
+    n1_sems, send_line, recv_line, send_row, recv_row,
+    beta_send_line, beta_recv_line, beta_send_row, beta_recv_row,
+):
+    line = Line()
+    row = lax.axis_index("row")
+    seq_others, row_others = around("seq"), around("row")
+    greet(
+        [({"seq": other}, other >= 0) for other in seq_others]
+        + [({"row": other}, other >= 0) for other in row_others]
+        + [(line.across, line.core >= 0)]
+    )
+    moves = (
+        (parts_ref, qkv_ref, send_line, recv_line, send_row, recv_row),
+        (beta_ref, beta_full_ref, beta_send_line, beta_recv_line, beta_send_row, beta_recv_row),
+    )
+
+    def spread(move, i):
+        source, target, send, recv = move[:4]
+        return remote(
+            source.at[seq_others[i]],
+            target.at[row, line.place],
+            send.at[i],
+            recv.at[i],
+            {"seq": seq_others[i]},
+        )
+
+    def share(move, i, j):
+        target, send, recv = move[1], move[4], move[5]
+        came_from = lax.rem(line.place + line.count - i, line.count)
+        slot = target.at[row, came_from]
+        return remote(slot, slot, send.at[i, j], recv.at[i, j], {"row": row_others[j]})
+
+    for move in moves:
+        for i in range(len(seq_others)):
+            spread(move, i).start()
+    for move in moves:
+        move[1][row, line.place] = move[0][line.place]
+        for j in range(len(row_others)):
+            share(move, 0, j).start()
+    rows = n1_ref.shape[2]
+    n1 = Gather(line, n1_ref, n1_sems)
+
+    def normed(span, i):
+        x_span = pl.ds(pl.multiple_of(line.core * rows + i * STEP, STEP), STEP)
+        x = x_ref[x_span].astype(jnp.float32)
+        n1_ref[line.place, line.core, span] = (x * norm_scale(x) * gain_ref[...]).astype(
+            jnp.bfloat16
+        )
+
+    over_rows(rows, normed)
+    n1.phase(0)
+    for k in range(1, line.count):
+        for move in moves:
+            spread(move, k - 1).wait_recv()
+            for j in range(len(row_others)):
+                share(move, k, j).start()
+        n1.phase(k)
+    for move in moves:
+        for i in range(len(seq_others)):
+            spread(move, i).wait_send()
+        for i in range(line.count):
+            for j in range(len(row_others)):
+                share(move, i, j).wait()
+    n1.finish()
+
+
+def run_normed(x, gain, parts, beta):
+    rows_axis, seqs, cores = (lax.axis_size(axis) for axis in ("row", "seq", "tp"))
+    piece, width = x.shape
+    b16 = jnp.bfloat16
+    outs = (
+        ((seqs, cores, piece // cores, width), b16),
+        ((rows_axis,) + parts.shape, b16),
+        ((rows_axis,) + beta.shape, b16),
+    )
+    moves = [
+        dma_sems(seqs - 1),
+        dma_sems(seqs - 1),
+        dma_sems(seqs, rows_axis - 1),
+        dma_sems(seqs, rows_axis - 1),
+    ]
+    n1, qkv, beta_full = line_call(
+        normed_kernel, 4, "norm_gather", outs, [dma_sems(5, seqs)] + moves * 2,
+        (x, gain, parts, beta),
+    )
+    return n1.reshape(-1, width), qkv.reshape(-1, qkv.shape[-1]), beta_full
 
 
 def small_sums_kernel(
@@ -793,13 +1343,13 @@
     row, seq, tp = (lax.axis_index(axis) for axis in ("row", "seq", "tp"))
     row_others, seq_others, tp_others = around("row"), around("seq"), around("tp")
     greet(
-        [{"row": other} for other in row_others]
-        + [{"seq": other} for other in seq_others]
-        + [{"tp": other} for other in tp_others]
+        [({"row": other}, other >= 0) for other in row_others]
+        + [({"seq": other}, other >= 0) for other in seq_others]
+        + [({"tp": other}, other >= 0) for other in tp_others]
     )
     rows_ref[row] = part_ref[...]
     copies = [
-        swap_copy(part_ref, rows_ref.at[row], send_row.at[i], recv_row.at[i], {"row": other})
+        remote(part_ref, rows_ref.at[row], send_row.at[i], recv_row.at[i], {"row": other})
         for i, other in enumerate(row_others)
     ]
     for copy in copies:
@@ -811,7 +1361,7 @@
         total = total + rows_ref[i]
     all_ref[tp, seq] = total
     copies = [
-        swap_copy(
+        remote(
             all_ref.at[tp, seq], all_ref.at[tp, seq], send_seq.at[i], recv_seq.at[i], {"seq": other}
         )
         for i, other in enumerate(seq_others)
@@ -821,7 +1371,7 @@
     for copy in copies:
         copy.wait()
     copies = [
-        swap_copy(all_ref.at[tp], all_ref.at[tp], send_tp.at[i], recv_tp.at[i], {"tp": other})
+        remote(all_ref.at[tp], all_ref.at[tp], send_tp.at[i], recv_tp.at[i], {"tp": other})
         for i, other in enumerate(tp_others)
     ]
     for copy in copies:
@@ -887,34 +1437,6 @@
     return exchanged(own.reshape(pieces, rows, -1), "seq")
 
 
-def token_gather(own):
-    return lax.all_gather(own, ("seq", "tp"), axis=0, tiled=True)
-
-
-def token_sum(term):
-    return lax.psum_scatter(
-        term.astype(jnp.bfloat16), ("seq", "tp"), scatter_dimension=0, tiled=True
-    ).astype(jnp.float32)
-
-
-def both_cores(own):
-    cores = lax.axis_size("tp")
-    if cores == 1:
-        return own
-    other = lax.ppermute(own, "tp", [(0, 1), (1, 0)])
-    first = lax.axis_index("tp") == 0
-    return jnp.concatenate([jnp.where(first, own, other), jnp.where(first, other, own)], axis=0)
-
-
-def shifted(rows, by):
-    if by == 0:
-        return rows
-    pad = jnp.zeros((abs(by),) + rows.shape[1:], rows.dtype)
-    if by > 0:
-        return jnp.concatenate([pad, rows[:-by]], axis=0)
-    return jnp.concatenate([rows[-by:], pad], axis=0)
-
-
 def local_heads(
     block_input,
     grad_out,
@@ -933,7 +1455,6 @@
     pieces, cores = lax.axis_size("seq"), lax.axis_size("tp")
     piece, core = lax.axis_index("seq"), lax.axis_index("tp")
     row_len = pieces * tok_rows
-    own_rows = tok_rows // cores
     shard_rows = qkv_weight.shape[1]
     half_width = qkv_weight.shape[2]
     width = half_width // pieces
@@ -941,11 +1462,15 @@
     units = gate_up_weight.shape[2] // pieces
     f32, b16 = jnp.float32, jnp.bfloat16
 
-    qkv_parts = qkv_weight.reshape(3, shard_rows, pieces, width).transpose(1, 2, 0, 3)
-    qkv_full = gathered(qkv_parts.reshape(shard_rows, -1))
-    beta_full = lax.all_gather(beta_weight.T, ("row", "seq"), axis=1, tiled=True)
-    beta_full = lax.dynamic_slice_in_dim(beta_full, piece * heads, heads, axis=0)
-    beta_full = jnp.pad(beta_full, ((0, 16 - heads), (0, 0)))
+    x_piece, g_piece = block_input[0], grad_out[0]
+    qkv_parts = qkv_weight.reshape(3, shard_rows, pieces, width).transpose(2, 1, 0, 3)
+    beta_parts = jnp.pad(
+        beta_weight.T.reshape(pieces, heads, shard_rows), ((0, 0), (0, 16 - heads), (0, 0))
+    )
+    normed_one, qkv_full, beta_full = run_normed(
+        x_piece, attn_gain[None], qkv_parts.reshape(pieces, shard_rows, -1), beta_parts
+    )
+    beta_full = beta_full.reshape(-1, 16, shard_rows).transpose(1, 0, 2).reshape(16, -1)
     o_full = gathered(o_weight.T)
     gate_up_parts = gate_up_weight.reshape(2, shard_rows, pieces, units).transpose(1, 2, 0, 3)
     gate_up_full = gathered(gate_up_parts.reshape(shard_rows, -1))
@@ -959,19 +1484,10 @@
     taps = lax.dynamic_slice_in_dim(conv_weight, piece * width, width, axis=2)
     taps = taps.transpose(1, 0, 2).reshape(KW, 3 * width)
 
-    x_rows = lax.dynamic_slice_in_dim(block_input[0], core * own_rows, own_rows, axis=0)
-    x_rows = x_rows.astype(f32)
-    g_rows = lax.dynamic_slice_in_dim(grad_out[0], core * own_rows, own_rows, axis=0)
-    scale_one = norm_scale(x_rows)
-    normed_one = token_gather((x_rows * scale_one * attn_gain).astype(b16))
-    g_full = token_gather(g_rows)
     proj, logit, mixed, normed_mix, inverse, states, written = run_forward(
         normed_one, qkv_full, beta_full, taps, aux, doc_rows, gain_row
     )
-    o_term = jnp.einsum("te,de->td", normed_mix, o_full, preferred_element_type=f32)
-    resid = x_rows + token_sum(o_term)
-    scale_two = norm_scale(resid)
-    normed_two = token_gather((resid * scale_two * mlp_gain).astype(b16))
+    resid, normed_two, g_full = run_resid(normed_mix, o_full, x_piece, g_piece, mlp_gain[None])
     gate_up = jnp.dot(normed_two, gate_up_full, preferred_element_type=f32)
     gate, up = gate_up[:, :units], gate_up[:, units:]
     gate_sig = jax.nn.sigmoid(gate)
@@ -981,13 +1497,9 @@
     grad_gate = grad_hidden * up * gate_sig * (1.0 + gate * (1.0 - gate_sig))
     grad_up = grad_hidden * gate_act
     grad_gate_up = jnp.concatenate([grad_gate, grad_up], axis=1).astype(b16)
-    two_term = jnp.einsum("tf,df->td", grad_gate_up, gate_up_full, preferred_element_type=f32)
-    grad_two = token_sum(two_term)
-    mlp_gain_part = jnp.sum(grad_two * resid * scale_two, axis=0)
-    grad_resid = g_rows.astype(f32) + norm_back(resid, scale_two, mlp_gain, grad_two)
-    grad_attn = token_gather(grad_resid.astype(b16))
-    down_term = jnp.einsum("tf,df->td", hidden, down_full, preferred_element_type=f32)
-    result = both_cores((resid + token_sum(down_term)).astype(b16))
+    grad_resid, grad_attn, mlp_gain_part, result = run_grad_resid(
+        grad_gate_up, gate_up_full, hidden, down_full, resid, g_piece, mlp_gain[None]
+    )
     down_part = jnp.einsum("td,tf->df", g_full, hidden, preferred_element_type=f32)
     gate_up_part = jnp.einsum("td,tf->df", normed_two, grad_gate_up, preferred_element_type=f32)
     o_part = jnp.einsum("td,te->de", grad_attn, normed_mix, preferred_element_type=f32)
@@ -1000,12 +1512,8 @@
         doc_rows,
         gain_row,
     )
-    one_term = jnp.einsum("te,de->td", grad_proj, qkv_full, preferred_element_type=f32)
-    one_term = one_term + jnp.einsum("th,hd->td", grad_logit, beta_full, preferred_element_type=f32)
-    grad_one = token_sum(one_term)
-    attn_gain_part = jnp.sum(grad_one * x_rows * scale_one, axis=0)
-    input_grad = both_cores(
-        (grad_resid + norm_back(x_rows, scale_one, attn_gain, grad_one)).astype(b16)
+    input_grad, attn_gain_part = run_input_grad(
+        grad_proj, qkv_full, grad_logit, beta_full, x_piece, grad_resid, attn_gain[None]
     )
     qkv_part = jnp.einsum("td,te->de", normed_one, grad_proj, preferred_element_type=f32)
     beta_part = jnp.einsum("td,th->hd", normed_one, grad_logit, preferred_element_type=f32)

time: 915 us -> 742 us (0.81)
  waiting for transfers between devices: 552 us -> 97.2 us
  Pallas kernels: 88.7 us -> 470 us
  blocking collectives: 36.9 us -> 0 us
  matrix products: 83.7 us -> 48.4 us
  other arithmetic: 26 us -> 10.8 us
    pallas_call x0 -> x4, Pallas kernels: none -> 384 us  [line_call(): pl.pallas_call(kernel, out_shape=[jax.ShapeDtypeStruct(*out) for out in o...]
    all_gather x4 -> x0, waiting for transfers between devices: 166 us -> none  [token_gather(): return lax.all_gather(own, ('seq', 'tp'), axis=0, tiled=True)]
    reduce_scatter x4 -> x0, waiting for transfers between devices: 105 us -> none  [token_sum(): lax.psum_scatter(term.astype(jnp.bfloat16), ('seq', 'tp'), scatter_dimens...]
    all_gather x4 -> x3, waiting for transfers between devices: 77.5 us -> 0.02 us  [gathered(): whole = lax.all_gather(parts, 'row', axis=0, tiled=True)]
    reduce_scatter x4, waiting for transfers between devices: 67.4 us -> 0.8 us  [returned(): own = lax.psum_scatter(part, 'row', scatter_dimension=0, tiled=True)]
    ppermute x24 -> x21, waiting for transfers between devices: 135 us -> 96.2 us  [exchanged(): lax.ppermute(part, axis, [(i, (i + by) % count) for i in range(count)])]
    all_gather x1 -> x0, blocking collectives: 36.9 us -> none  [local_heads(): lax.all_gather(beta_weight.T, ('row', 'seq'), axis=1, tiled=True)]
    dot_general x5 -> x0, matrix products: 28.7 us -> none  [the longest x1 8.32 us: local_heads(): jnp.einsum('tf,df->td', grad_gate_up, gate_up_full, preferred_element_typ...]
  transfers between devices with their start and end apart: 42 -> 28, of which waited for: 30 -> 17; matrix products, arithmetic and copies ran while one was open for 13% -> 8% of each run, Pallas kernels for 10% -> 45%
where the time goes in v3:
time: 742 us; the launch traced here: 732 us
  Pallas kernels  470 us (63%)
  waiting for transfers between devices  97.2 us (13%)
  matrix products  48.4 us (7%)
  local copies, waits for them, and re-layouts  45.2 us (6%)
  starting transfers between devices  37 us (5%)
  between operations  23.2 us (3%)
  other arithmetic  10.8 us (1%)
    pallas_call x4, Pallas kernels, line_call(): pl.pallas_call(kernel, out_shape=[jax.ShapeDtypeStruct(*out) for out in o...  384 us
    ppermute x21, waiting for transfers between devices, exchanged(): lax.ppermute(part, axis, [(i, (i + by) % count) for i in range(count)])  96.2 us
    pallas_call x1, Pallas kernels, run_forward(): pl.pallas_call(functools.partial(forward_kernel, heads), out_shape=[jax.S...  43.6 us
    ppermute x21, starting transfers between devices, exchanged(): lax.ppermute(part, axis, [(i, (i + by) % count) for i in range(count)])  36.5 us
    pallas_call x1, Pallas kernels, run_backward(): pl.pallas_call(functools.partial(backward_kernel, heads), out_shape=[jax....  25.6 us
    unnamed x73, local copies, waits for them, and re-layouts  20.1 us
    pallas_call x1, Pallas kernels, run_small_sums(): pl.pallas_call(small_sums_kernel, out_shape=jax.ShapeDtypeStruct(shape, p...  16.7 us
  transfers between devices with their start and end apart: 28, of which 17 were waited for; matrix products, arithmetic and copies ran while one was open for 8% of the time, Pallas kernels for 45%

profile of v3, /device:TPU:8, one launch (start us, length us, event | category | flops | bytes accessed | tf_op | source)
XLA Modules:
  0.0 732.1 jit_solution(5615161191873539024)
XLA Ops:
  7.3 1.0 constant_dynamic-slice_fusion.49
  8.6 2.1 collective-permute-start
  10.8 4.5 collective-permute-start.1
  25.4 2.4 collective-permute-start.3
  27.8 11.8 %collective-permute-done.5 = bf16[128,704]{0,1:T(8,128)(2,1)S(1)} collective-permute-done((bf16[128,704]{0,1:T(8,128)(2,1)S(1)}, bf16[128,704]{0,1:T(8,128)(2,1)S(1)}, u32[]{:S(2)}, u32[]{:S(2)}) %collective-permute-start.5) | collective-permute-done | bytes 180256 | tf_op jit(solution)/shard_map/ppermute | solution.py:1413
  42.5 2.5 collective-permute-start.6
  45.2 3.3 collective-permute-start.7
  49.0 20.3 %collective-permute-done.6 = bf16[128,1408]{1,0:T(8,128)(2,1)S(1)} collective-permute-done((bf16[128,1408]{1,0:T(8,128)(2,1)S(1)}, bf16[128,1408]{1,0:T(8,128)(2,1)S(1)}, u32[]{:S(2)}, u32[]{:S(2)}) %collective-permute-start.6) | collective-permute-done | bytes 360480 | tf_op jit(solution)/shard_map/ppermute | solution.py:1413
  69.3 6.0 collective-permute-done.7
  75.3 2.4 collective-permute-done.8
  78.1 1.3 pad_maximum_fusion.2
  81.2 1.2 copy.164.parts_ref
  83.0 68.0 %norm_gather.1 = (bf16[4,2,128,2048]{3,2,1,0:T(8,128)(2,1)}, bf16[4,4,128,768]{3,2,1,0:T(8,128)(2,1)}, bf16[4,4,16,128]{3,2,1,0:T(8,128)(2,1)}) custom-call(bf16[256,2048]{1,0:T(8,128)(2,1)} %bitcast.178, f32[1,2048]{1,0:T(1,128)} %bitcast.247, bf16[4,128,768]{2,1,0:T(8,128)(2,1)} %copy.164.parts_ref, bf16[4,16,128]{2,1,0:T(8,128)(2,1)} %pad.9.beta_ref), custom_call_target="tpu_custom_call" | custom-call | tf_op jit(solution)/shard_map/norm_gather/pallas_call | solution.py:1066
  152.0 43.6 %mixer_forward.1 = (bf16[1024,768]{1,0:T(8,128)(2,1)}, f32[1024,16]{1,0:T(8,128)S(1)}, f32[1024,256]{1,0:T(8,128)S(1)}, bf16[1024,256]{1,0:T(8,128)(2,1)S(1)}, f...) custom-call(bf16[1024,2048]{1,0:T(8,128)(2,1)} %bitcast.170, ...), custom_call_target="tpu_custom_call" | custom-call | tf_op jit(solution)/shard_map/mixer_forward/pallas_call | solution.py:710
  195.6 1.0 copy-done.3
  196.6 1.0 copy-done.7
  198.4 124.2 %resid_norm.1 = (f32[128,2048]{1,0:T(8,128)}, bf16[4,2,128,2048]{3,2,1,0:T(8,128)(2,1)}, bf16[4,2,128,2048]{3,2,1,0:T(8,128)(2,1)}) custom-call(bf16[1024,256]{1,0:T(8,128)(2,1)} %copy-done.11, bf16[2048,256]{1,0:T(8,128)(2,1)} %bitcast.162, bf16[256,2048]{1,0:T(8,128)(2,1)} %bitcast.179, bf16[256,2048]{1,0:T(8,128)(2,1)} %bitcast.189, f32[1,2048]{1,0:T(1,128)} %bitcast.245), custom_call_target="tpu_custom_call" | custom-call | tf_op jit(solution)/shard_map/resid_norm/pallas_call | solution.py:1066
  322.6 4.6 copy.171
  327.3 10.6 %fusion.12 = f32[1024,1408]{1,0:T(8,128)S(1)} fusion(bf16[1024,2048]{1,0:T(8,128)(2,1)} %bitcast.258, bf16[2048,1408]{1,0:T(8,128)(2,1)} %bitcast.182), kind=kOutput, calls=%fused_computation.124 | convolution fusion | flops 5905580032 | bytes 15728640 | tf_op jit(solution)/shard_map/dot_general | solution.py:1491
  337.9 5.2 multiply_convert_fusion.2
  343.1 2.5 pad_maximum_fusion.dgu_ref
  345.6 138.5 %grad_resid.1 = (f32[128,2048]{1,0:T(8,128)}, bf16[4,2,128,2048]{3,2,1,0:T(8,128)(2,1)}, f32[1,2048]{1,0:T(1,128)}, bf16[256,2048]{1,0:T(8,128)(2,1)}) custom-call(bf16[1024,1408]{1,0:T(8,128)(2,1)} %pad_maximum_fusion.dgu_ref, bf16[2048,1408]{1,0:T(8,128)(2,1)} %bitcast.183, bf16[1024,704]{1,0:T(8,128)(2,1)} %get-tuple-element.103.hidden_ref, ...), custom_call_target="tpu_custom_call" | custom-call | tf_op jit(solution)/shard_map/grad_resid/pallas_call | solution.py:1066
  484.1 4.5 convolution_convert_fusion.3
  488.7 7.5 %convolution_convert_fusion.2 = bf16[2048,704]{0,1:T(8,128)(2,1)} fusion(bf16[1024,2048]{1,0:T(8,128)(2,1)} %bitcast.260, bf16[1024,704]{1,0:T(8,128)(2,1)} %get-tuple-element.103.hidden_ref), kind=kOutput, calls=%fused_computation.2 | convolution fusion | flops 2954231808 | bytes 8519680 | tf_op jit(solution)/shard_map/td,tf->df/dot_general | solution.py:1503
  496.2 1.1 copy-done.2
  497.4 1.2 copy-done.4
  498.6 1.2 copy-done.6
  499.9 25.6 %mixer_backward.1 = (bf16[1024,768]{1,0:T(8,128)(2,1)}, bf16[1024,16]{1,0:T(8,128)(2,1)S(1)}, f32[4,768]{1,0:T(4,128)S(1)}, f32[1,128]{1,0:T(1,128)S(1)}) custom-call(bf16[1024,2048]{1,0:T(8,128)(2,1)} %bitcast.188, bf16[2048,256]{1,0:T(8,128)(2,1)S(1)} %bitcast.163, bf16[1024,768]{1,0:T(8,128)(2,1)} %get-tuple-element.43.proj_ref, ...), custom_call_target="tpu_custom_call" | custom-call | tf_op jit(solution)/shard_map/mixer_backward/pallas_call | solution.py:734
  526.2 6.7 convolution_convert_fusion.1
  533.2 1.7 copy-done.16
  534.9 11.0 %convolution_convert_fusion = bf16[2048,1408]{1,0:T(8,128)(2,1)} fusion(bf16[1024,2048]{1,0:T(8,128)(2,1)} %bitcast.259, bf16[1024,1408]{1,0:T(8,128)(2,1)S(1)} %copy-done.16), kind=kOutput, calls=%fused_computation | convolution fusion | flops 5908463616 | bytes 12845056 | tf_op jit(solution)/shard_map/td,tf->df/dot_general | solution.py:1504
  546.0 53.5 %input_grad.1 = (bf16[256,2048]{1,0:T(8,128)(2,1)}, f32[1,2048]{1,0:T(1,128)}) custom-call(bf16[1024,768]{1,0:T(8,128)(2,1)} %get-tuple-element.49.grad_proj_ref, bf16[2048,768]{1,0:T(8,128)(2,1)} %bitcast.176, bf16[1024,16]{1,0:T(8,128)(2,1)} %copy-done.8, bf16[16,2048]{1,0:T(8,128)(2,1)} %bitcast.165, bf16[256,2048]{1,0:T(8,128)(2,1)} %bitcast.180, ...), custom_call_target="tpu_custom_call" | custom-call | tf_op jit(solution)/shard_map/input_grad/pallas_call | solution.py:1066
  599.6 2.9 fusion.1
  603.2 16.7 %small_sums.1 = f32[2,4,96,128]{3,2,1,0:T(8,128)} custom-call(f32[96,128]{1,0:T(8,128)} %copy-done.20), custom_call_target="tpu_custom_call" | custom-call | tf_op jit(solution)/shard_map/small_sums/pallas_call | solution.py:1388
  622.7 1.0 slice_reduce_fusion
  626.3 1.8 collective-permute-start.13
  628.0 3.1 collective-permute-start.12
  631.7 1.3 collective-permute-done.13
  633.0 1.5 collective-permute-done.12
  634.6 1.7 reshape.266
  636.4 1.5 constant_dynamic-slice_fusion.7
  638.0 1.7 collective-permute-start.20
  640.1 3.6 collective-permute-start.19
  643.9 1.0 copy.187
  644.9 1.7 collective-permute-done.20
  646.6 4.2 collective-permute-done.18
  650.8 4.7 collective-permute-done.19
  655.6 1.3 constant_dynamic-slice_fusion.29
  657.6 4.2 collective-permute-start.10
  662.8 1.2 maximum_convert_fusion
  665.2 9.4 %collective-permute-done.10 = bf16[128,768]{0,1:T(8,128)(2,1)S(1)} collective-permute-done((bf16[128,768]{0,1:T(8,128)(2,1)S(1)}, bf16[128,768]{0,1:T(8,128)(2,1)S(1)}, u32[]{:S(2)}, u32[]{:S(2)}) %collective-permute-start.10) | collective-permute-done | bytes 196640 | tf_op jit(solution)/shard_map/ppermute | solution.py:1413
  674.6 3.9 collective-permute-done.11
  679.4 1.4 constant_dynamic-slice_fusion.15
  681.5 1.5 collective-permute-start.15
  683.0 1.4 collective-permute-start.16
  684.4 1.5 collective-permute-start.17
  686.3 1.6 copy.197
  688.2 19.1 %collective-permute-done.15 = bf16[128,1408]{0,1:T(8,128)(2,1)} collective-permute-done((bf16[128,1408]{0,1:T(8,128)(2,1)S(1)}, bf16[128,1408]{0,1:T(8,128)(2,1)}, u32[]{:S(2)}, u32[]{:S(2)}) %collective-permute-start.15) | collective-permute-done | bytes 360480 | tf_op jit(solution)/shard_map/ppermute | solution.py:1413
  707.3 6.6 collective-permute-done.16
  713.9 2.0 collective-permute-done.17
  715.9 1.4 pad_maximum_fusion.3
  718.0 2.2 copy.198
  720.2 2.3 copy.225
  722.5 2.3 copy.226
  (168 shorter events, 24.9 us)
Async XLA Ops:
  7.2 144.8 %copy-start = (f32[3,4,1024]{2,1,0:T(4,128)S(1)}, f32[3,4,1024]{2,1,0:T(4,128)}, u32[]{:S(2)}) copy-start(f32[3,4,1024]{2,1,0:T(4,128)} %param.18) | copy-start | bytes 147460
  7.2 17.5 %copy-start.19 = (bf16[2816,128]{1,0:T(8,128)(2,1)S(1)}, bf16[2816,128]{1,0:T(8,128)(2,1)}, u32[]{:S(2)}) copy-start(bf16[2816,128]{1,0:T(8,128)(2,1)} %param.23) | copy-start | bytes 2162692
  7.2 191.1 %all-gather.4.cloned.1.call-start = ((), (), s32[]{:S(2)}) async-start(), calls=%async_computation.4 | async-start | bytes 1310720 | tf_op jit(solution)/shard_map/all_gather | solution.py:1429
  8.4 15.3 %collective-permute-start.2 = (bf16[128,256]{1,0:T(8,128)(2,1)S(1)}, bf16[128,256]{1,0:T(8,128)(2,1)S(1)}, u32[]{:S(2)}, u32[]{:S(2)}) collective-permute-start(bf16[128,256]{1,0:T(8,128)(2,1)S(1)} %bitcast.235), channel_id=1, source_target_pairs={{0,6},{2,0},{4,2},{6,4},{1,7},{3,1},{5,3},{7,5},{8,14},{10,8},{12,... | collective-permute-start | bytes 196616 | tf_op jit(solution)/shard_map/ppermute | solution.py:1413
  8.6 15.1 %collective-permute-start = (bf16[128,256]{1,0:T(8,128)(2,1)S(1)}, bf16[128,256]{1,0:T(8,128)(2,1)S(1)}, u32[]{:S(2)}, u32[]{:S(2)}) collective-permute-start(bf16[128,256]{1,0:T(8,128)(2,1)S(1)} %bitcast.236), channel_id=1, source_target_pairs={{0,2},{2,4},{4,6},{6,0},{1,3},{3,5},{5,7},{7,1},{8,10},{10,12},{12... | collective-permute-start | bytes 196616 | tf_op jit(solution)/shard_map/ppermute | solution.py:1413
  10.8 13.0 %collective-permute-start.1 = (bf16[128,256]{1,0:T(8,128)(2,1)S(1)}, bf16[128,256]{1,0:T(8,128)(2,1)S(1)}, u32[]{:S(2)}, u32[]{:S(2)}) collective-permute-start(bf16[128,256]{1,0:T(8,128)(2,1)S(1)} %bitcast.237), channel_id=1, source_target_pairs={{0,4},{2,6},{4,0},{6,2},{1,5},{3,7},{5,1},{7,3},{8,12},{10,14},{12... | collective-permute-start | bytes 196616 | tf_op jit(solution)/shard_map/ppermute | solution.py:1413
  24.6 298.0 %all-gather.6.cloned.1.call-start = ((), (), s32[]{:S(2)}) async-start(), calls=%async_computation.5 | async-start | bytes 3604480 | tf_op jit(solution)/shard_map/all_gather | solution.py:1429
  24.8 16.4 %copy-start.17 = (bf16[2,128,2816]{2,1,0:T(8,128)(2,1)S(1)}, bf16[2,128,2816]{2,1,0:T(8,128)(2,1)}, u32[]{:S(2)}) copy-start(bf16[2,128,2816]{2,1,0:T(8,128)(2,1)} %param.22) | copy-start | bytes 4325380
  24.8 14.8 %collective-permute-start.5 = (bf16[128,704]{0,1:T(8,128)(2,1)S(1)}, bf16[128,704]{0,1:T(8,128)(2,1)S(1)}, u32[]{:S(2)}, u32[]{:S(2)}) collective-permute-start(bf16[128,704]{0,1:T(8,128)(2,1)S(1)} %get-tuple-element.141), channel_id=1, source_target_pairs={{0,6},{2,0},{4,2},{6,4},{1,7},{3,1},{5,3},{7,5},{8,14},{10,8},{12,... | collective-permute-start | bytes 540680 | tf_op jit(solution)/shard_map/ppermute | solution.py:1413
  24.9 14.7 %collective-permute-start.4 = (bf16[128,704]{0,1:T(8,128)(2,1)S(1)}, bf16[128,704]{0,1:T(8,128)(2,1)S(1)}, u32[]{:S(2)}, u32[]{:S(2)}) collective-permute-start(bf16[128,704]{0,1:T(8,128)(2,1)S(1)} %get-tuple-element.142), channel_id=1, source_target_pairs={{0,4},{2,6},{4,0},{6,2},{1,5},{3,7},{5,1},{7,3},{8,12},{10,14},{12... | collective-permute-start | bytes 540680 | tf_op jit(solution)/shard_map/ppermute | solution.py:1413
  25.4 14.6 %collective-permute-start.3 = (bf16[128,704]{0,1:T(8,128)(2,1)S(1)}, bf16[128,704]{0,1:T(8,128)(2,1)S(1)}, u32[]{:S(2)}, u32[]{:S(2)}) collective-permute-start(bf16[128,704]{0,1:T(8,128)(2,1)S(1)} %get-tuple-element.143), channel_id=1, source_target_pairs={{0,2},{2,4},{4,6},{6,0},{1,3},{3,5},{5,7},{7,1},{8,10},{10,12},{12... | collective-permute-start | bytes 540680 | tf_op jit(solution)/shard_map/ppermute | solution.py:1413
  41.1 286.1 %all-gather.8.cloned.1.call-start = ((), (), s32[]{:S(2)}) async-start(), calls=%async_computation.6 | async-start | bytes 7208960 | tf_op jit(solution)/shard_map/all_gather | solution.py:1429
  42.5 26.9 %collective-permute-start.6 = (bf16[128,1408]{1,0:T(8,128)(2,1)S(1)}, bf16[128,1408]{1,0:T(8,128)(2,1)S(1)}, u32[]{:S(2)}, u32[]{:S(2)}) collective-permute-start(bf16[128,1408]{1,0:T(8,128)(2,1)S(1)} %bitcast.206), channel_id=1, source_target_pairs={{0,2},{2,4},{4,6},{6,0},{1,3},{3,5},{5,7},{7,1},{8,10},{10,12},{12... | collective-permute-start | bytes 1081352 | tf_op jit(solution)/shard_map/ppermute | solution.py:1413
  45.2 30.1 %collective-permute-start.7 = (bf16[128,1408]{1,0:T(8,128)(2,1)S(1)}, bf16[128,1408]{1,0:T(8,128)(2,1)S(1)}, u32[]{:S(2)}, u32[]{:S(2)}) collective-permute-start(bf16[128,1408]{1,0:T(8,128)(2,1)S(1)} %bitcast.207), channel_id=1, source_target_pairs={{0,4},{2,6},{4,0},{6,2},{1,5},{3,7},{5,1},{7,3},{8,12},{10,14},{12... | collective-permute-start | bytes 1081352 | tf_op jit(solution)/shard_map/ppermute | solution.py:1413
  48.7 29.0 %collective-permute-start.8 = (bf16[128,1408]{1,0:T(8,128)(2,1)S(1)}, bf16[128,1408]{1,0:T(8,128)(2,1)S(1)}, u32[]{:S(2)}, u32[]{:S(2)}) collective-permute-start(bf16[128,1408]{1,0:T(8,128)(2,1)S(1)} %bitcast.208), channel_id=1, source_target_pairs={{0,6},{2,0},{4,2},{6,4},{1,7},{3,1},{5,3},{7,5},{8,14},{10,8},{12,... | collective-permute-start | bytes 1081352 | tf_op jit(solution)/shard_map/ppermute | solution.py:1413
  78.0 1.4 copy-start.25
  78.1 2.7 copy-start.18
  79.4 3.0 copy-start.23
  79.4 545.4 %reduce-scatter.7.cloned.1.call-start = ((), (), s32[]{:S(2)}) async-start(), calls=%async_computation.8 | async-start | bytes 1310720 | tf_op jit(solution)/shard_map/reduce_scatter | solution.py:1436
  81.1 70.8 %copy-start.13 = (f32[128]{0:T(128)S(1)}, f32[128]{0:T(128)}, u32[]{:S(2)}) copy-start(f32[128]{0:T(128)} %param.17) | copy-start | bytes 1540
  151.9 43.7 %copy-start.10 = (bf16[2,8,16,128]{3,1,2,0:T(8,128)(2,1)}, bf16[2,8,16,128]{3,1,2,0:T(8,128)(2,1)S(1)}, u32[]{:S(2)}) copy-start(bf16[2,8,16,128]{3,1,2,0:T(8,128)(2,1)S(1)} %copy.218) | copy-start | bytes 196612
  195.6 1.0 copy-start.3
  196.6 1.0 copy-start.7
  197.6 0.8 copy-start.11
  198.3 128.9 %copy-start.5 = (f32[2,8,128,128]{3,2,1,0:T(8,128)}, f32[2,8,128,128]{3,2,1,0:T(8,128)S(1)}, u32[]{:S(2)}) copy-start(f32[2,8,128,128]{3,2,1,0:T(8,128)S(1)} %get-tuple-element.47.states_ref) | copy-start | bytes 3145732
  327.3 10.6 %copy-start.15 = (bf16[16,128,704]{2,1,0:T(8,128)(2,1)S(1)}, bf16[16,128,704]{2,1,0:T(8,128)(2,1)}, u32[]{:S(2)}) copy-start(bf16[16,128,704]{2,1,0:T(8,128)(2,1)} %copy.171) | copy-start | bytes 8650756
  327.3 10.6 %copy-start.24 = (bf16[4,2,128,2048]{3,2,1,0:T(8,128)(2,1)S(1)}, bf16[4,2,128,2048]{3,2,1,0:T(8,128)(2,1)}, u32[]{:S(2)}) copy-start(bf16[4,2,128,2048]{3,2,1,0:T(8,128)(2,1)} %get-tuple-element.38) | copy-start | bytes 12582916
  345.6 138.5 %copy-start.12 = (bf16[1024,256]{1,0:T(8,128)(2,1)S(1)}, bf16[1024,256]{1,0:T(8,128)(2,1)}, u32[]{:S(2)}) copy-start(bf16[1024,256]{1,0:T(8,128)(2,1)} %copy-done.11) | copy-start | bytes 1572868
  488.7 146.0 %reduce-scatter.11.cloned.1.call-start = ((), (), s32[]{:S(2)}) async-start(), calls=%async_computation.10 | async-start | bytes 3604480 | tf_op jit(solution)/shard_map/reduce_scatter | solution.py:1436
  496.2 1.2 copy-start.2
  496.2 159.4 %reduce-scatter.5.cloned.1.call-start = ((), (), s32[]{:S(2)}) async-start(), calls=%async_computation.7 | async-start | bytes 3932160 | tf_op jit(solution)/shard_map/reduce_scatter | solution.py:1436
  497.4 1.2 copy-start.4
  498.6 1.2 copy-start.6
  499.8 26.4 %copy-start.14 = (bf16[4,2,128,2048]{3,2,1,0:T(8,128)(2,1)S(1)}, bf16[4,2,128,2048]{3,2,1,0:T(8,128)(2,1)}, u32[]{:S(2)}) copy-start(bf16[4,2,128,2048]{3,2,1,0:T(8,128)(2,1)} %get-tuple-element.34) | copy-start | bytes 12582916
  525.5 0.7 copy-start.8
  532.9 2.0 copy-start.16
  532.9 146.5 %reduce-scatter.9.cloned.1.call-start = ((), (), s32[]{:S(2)}) async-start(), calls=%async_computation.9 | async-start | bytes 7208960 | tf_op jit(solution)/shard_map/reduce_scatter | solution.py:1436
  546.0 53.6 %copy-start.9 = (bf16[1024,16]{1,0:T(8,128)(2,1)S(1)}, bf16[1024,16]{1,0:T(8,128)(2,1)}, u32[]{:S(2)}) copy-start(bf16[1024,16]{1,0:T(8,128)(2,1)} %copy-done.8) | copy-start | bytes 98308
  599.5 3.0 copy-start.22
  599.5 3.0 copy-start.21
  602.5 0.6 copy-start.20
  625.8 5.9 collective-permute-start.14
  626.3 6.7 collective-permute-start.13
  628.0 6.5 collective-permute-start.12
  638.0 8.6 %collective-permute-start.20 = (bf16[128,704]{0,1:T(8,128)(2,1)S(1)}, bf16[128,704]{0,1:T(8,128)(2,1)S(1)}, u32[]{:S(2)}, u32[]{:S(2)}) collective-permute-start(bf16[128,704]{0,1:T(8,128)(2,1)S(1)} %bitcast.228), channel_id=1, source_target_pairs={{0,6},{2,0},{4,2},{6,4},{1,7},{3,1},{5,3},{7,5},{8,14},{10,8},{12,... | collective-permute-start | bytes 540680 | tf_op jit(solution)/shard_map/ppermute | solution.py:1413
  639.7 11.1 %collective-permute-start.18 = (bf16[128,704]{0,1:T(8,128)(2,1)S(1)}, bf16[128,704]{0,1:T(8,128)(2,1)S(1)}, u32[]{:S(2)}, u32[]{:S(2)}) collective-permute-start(bf16[128,704]{0,1:T(8,128)(2,1)S(1)} %bitcast.227), channel_id=1, source_target_pairs={{0,2},{2,4},{4,6},{6,0},{1,3},{3,5},{5,7},{7,1},{8,10},{10,12},{12... | collective-permute-start | bytes 540680 | tf_op jit(solution)/shard_map/ppermute | solution.py:1413
  640.1 15.3 %collective-permute-start.19 = (bf16[128,704]{0,1:T(8,128)(2,1)S(1)}, bf16[128,704]{0,1:T(8,128)(2,1)S(1)}, u32[]{:S(2)}, u32[]{:S(2)}) collective-permute-start(bf16[128,704]{0,1:T(8,128)(2,1)S(1)} %bitcast.226), channel_id=1, source_target_pairs={{0,4},{2,6},{4,0},{6,2},{1,5},{3,7},{5,1},{7,3},{8,12},{10,14},{12... | collective-permute-start | bytes 540680 | tf_op jit(solution)/shard_map/ppermute | solution.py:1413
  657.3 7.9 %collective-permute-start.9 = (bf16[128,768]{0,1:T(8,128)(2,1)S(1)}, bf16[128,768]{0,1:T(8,128)(2,1)S(1)}, u32[]{:S(2)}, u32[]{:S(2)}) collective-permute-start(bf16[128,768]{0,1:T(8,128)(2,1)S(1)} %bitcast.225), channel_id=1, source_target_pairs={{0,2},{2,4},{4,6},{6,0},{1,3},{3,5},{5,7},{7,1},{8,10},{10,12},{12... | collective-permute-start | bytes 589832 | tf_op jit(solution)/shard_map/ppermute | solution.py:1413
  657.6 17.0 %collective-permute-start.10 = (bf16[128,768]{0,1:T(8,128)(2,1)S(1)}, bf16[128,768]{0,1:T(8,128)(2,1)S(1)}, u32[]{:S(2)}, u32[]{:S(2)}) collective-permute-start(bf16[128,768]{0,1:T(8,128)(2,1)S(1)} %bitcast.224), channel_id=1, source_target_pairs={{0,4},{2,6},{4,0},{6,2},{1,5},{3,7},{5,1},{7,3},{8,12},{10,14},{12... | collective-permute-start | bytes 589832 | tf_op jit(solution)/shard_map/ppermute | solution.py:1413
  661.9 16.6 %collective-permute-start.11 = (bf16[128,768]{0,1:T(8,128)(2,1)S(1)}, bf16[128,768]{0,1:T(8,128)(2,1)S(1)}, u32[]{:S(2)}, u32[]{:S(2)}) collective-permute-start(bf16[128,768]{0,1:T(8,128)(2,1)S(1)} %bitcast.223), channel_id=1, source_target_pairs={{0,6},{2,0},{4,2},{6,4},{1,7},{3,1},{5,3},{7,5},{8,14},{10,8},{12,... | collective-permute-start | bytes 589832 | tf_op jit(solution)/shard_map/ppermute | solution.py:1413
  681.5 25.8 %collective-permute-start.15 = (bf16[128,1408]{0,1:T(8,128)(2,1)S(1)}, bf16[128,1408]{0,1:T(8,128)(2,1)}, u32[]{:S(2)}, u32[]{:S(2)}) collective-permute-start(bf16[128,1408]{0,1:T(8,128)(2,1)S(1)} %bitcast.205), channel_id=1, source_target_pairs={{0,2},{2,4},{4,6},{6,0},{1,3},{3,5},{5,7},{7,1},{8,10},{10,12},{12... | collective-permute-start | bytes 1081352 | tf_op jit(solution)/shard_map/ppermute | solution.py:1413
  683.0 30.8 %collective-permute-start.16 = (bf16[128,1408]{0,1:T(8,128)(2,1)S(1)}, bf16[128,1408]{0,1:T(8,128)(2,1)}, u32[]{:S(2)}, u32[]{:S(2)}) collective-permute-start(bf16[128,1408]{0,1:T(8,128)(2,1)S(1)} %bitcast.204), channel_id=1, source_target_pairs={{0,4},{2,6},{4,0},{6,2},{1,5},{3,7},{5,1},{7,3},{8,12},{10,14},{12... | collective-permute-start | bytes 1081352 | tf_op jit(solution)/shard_map/ppermute | solution.py:1413
  684.4 31.4 %collective-permute-start.17 = (bf16[128,1408]{0,1:T(8,128)(2,1)S(1)}, bf16[128,1408]{0,1:T(8,128)(2,1)}, u32[]{:S(2)}, u32[]{:S(2)}) collective-permute-start(bf16[128,1408]{0,1:T(8,128)(2,1)S(1)} %bitcast.203), channel_id=1, source_target_pairs={{0,6},{2,0},{4,2},{6,4},{1,7},{3,1},{5,3},{7,5},{8,14},{10,8},{12,... | collective-permute-start | bytes 1081352 | tf_op jit(solution)/shard_map/ppermute | solution.py:1413
  718.0 6.8 copy-start.1
Sparse Core Ops, SparseCore 0:
  24.8 25.7 all-gather.3
  53.0 57.1 all-gather.5
  112.6 75.0 all-gather.7
  488.8 27.9 reduce-scatter.6
  520.0 41.7 reduce-scatter.10
  564.9 43.9 reduce-scatter.4
  612.1 67.2 reduce-scatter.8

commit v4 on v3

--- a/solution.py
+++ b/solution.py
@@ -486,6 +486,10 @@
     aux_ref,
     docs_ref,
     gain_ref,
+    o_weight_ref,
+    gate_ref,
+    up_ref,
+    down_ref,
     proj_ref,
     logit_ref,
     mixed_ref,
@@ -493,17 +497,55 @@
     inverse_ref,
     states_ref,
     written_ref,
+    o_ref,
+    gate_out,
+    up_out,
+    down_out,
     window_ref,
     state_ref,
+    own_sems,
+    *sems,
 ):
     width = heads * DK
+    line = Line()
+    greet(exchange_partners(line))
+    row = lax.axis_index("row")
+
+    def rows_of(ref, count):
+        return lambda seq: ref.at[pl.ds(pl.multiple_of(seq * count, count), count)]
+
+    units = down_out.shape[1]
+    whole = Exchange(line, rows_of(o_weight_ref, width), o_ref, sems[:4])
+    moves = [
+        Exchange(line, lambda seq: gate_ref.at[seq], gate_out, sems[4:6]),
+        Exchange(line, lambda seq: up_ref.at[seq], up_out, sems[6:8]),
+        Exchange(line, rows_of(down_ref, units), down_out, sems[8:10]),
+    ]
+    whole.start()
+    own = [
+        pltpu.make_async_copy(whole.source(line.place), o_ref.at[row, line.place], own_sems.at[0])
+    ]
+    for i, move in enumerate(moves):
+        own.append(
+            pltpu.make_async_copy(
+                move.source(line.place), move.target.at[line.place], own_sems.at[i + 1]
+            )
+        )
+    for copy in own:
+        copy.start()
+    for move in moves:
+        move.start()
+    own[0].wait()
+    whole.share_own()
     window_ref[0:PAD] = jnp.zeros((PAD, 3 * width), jnp.float32)
     state_ref[...] = jnp.zeros_like(state_ref)
 
     def chunk(n, _):
         rows = pl.ds(pl.multiple_of(n * CHUNK, CHUNK), CHUNK)
         n1 = n1_ref[rows]
-        proj = mul(n1, qkv_ref[...], (1, 0)).astype(jnp.bfloat16)
+        proj = jnp.concatenate(
+            [mul(n1, qkv_ref[:, :, c].reshape(-1, width), (1, 0)) for c in range(3)], axis=1
+        ).astype(jnp.bfloat16)
         proj_ref[rows] = proj
         window_ref[PAD : PAD + CHUNK] = proj.astype(jnp.float32)
         logit = mul(n1, beta_ref[...], (1, 1))
@@ -547,7 +589,17 @@
             ).astype(jnp.bfloat16)
         return 0
 
-    lax.fori_loop(0, n1_ref.shape[0] // CHUNK, chunk, 0)
+    chunks = n1_ref.shape[0] // CHUNK
+    middle = chunks // 2
+    lax.fori_loop(0, middle, chunk, 0)
+    for i in range(1, line.count):
+        whole.share_came(i)
+    lax.fori_loop(middle, chunks, chunk, 0)
+    for copy in own[1:]:
+        copy.wait()
+    whole.finish()
+    for move in moves:
+        move.finish()
 
 
 def backward_kernel(
@@ -564,15 +616,36 @@
     aux_ref,
     docs_ref,
     gain_ref,
+    down_sum_ref,
+    gate_sum_ref,
+    up_sum_ref,
+    o_part_ref,
     grad_proj_ref,
     grad_logit_ref,
     conv_grad_ref,
     gain_grad_ref,
+    down_came_ref,
+    gate_came_ref,
+    up_came_ref,
+    o_came_ref,
     window_ref,
     masked_ref,
     state_ref,
+    o_rows,
+    *sems,
 ):
     width = heads * DK
+    greet(along_axis("seq") + along_axis("row"))
+    moves = moves_of(
+        Swap,
+        "seq",
+        (down_sum_ref, gate_sum_ref, up_sum_ref),
+        (down_came_ref, gate_came_ref, up_came_ref),
+        sems[:7],
+    ) + moves_of(Swap, "row", (o_part_ref,), (o_came_ref,), sems[7:])
+    for move in moves:
+        move.start()
+    side_by_side(o_ref, o_rows)
     chunks = grad_ref.shape[0] // CHUNK
     state_ref[...] = jnp.zeros_like(state_ref)
     masked_ref[...] = jnp.zeros_like(masked_ref)
@@ -584,7 +657,7 @@
         rows = pl.ds(pl.multiple_of(n * CHUNK, CHUNK), CHUNK)
         before = jnp.maximum(n - 1, 0)
         aux = aux_ref[rows]
-        grad_normed = mul(grad_ref[rows], o_ref[...], (1, 0))
+        grad_normed = mul(grad_ref[rows], o_rows[...], (1, 1))
         prior = proj_ref[pl.ds(pl.multiple_of(before * CHUNK + CHUNK - 16, 16), 16)]
         window_ref[0:PAD] = prior.astype(jnp.float32)[16 - PAD :]
         window_ref[PAD : PAD + CHUNK] = proj_ref[rows].astype(jnp.float32)
@@ -689,14 +762,17 @@
         return 0
 
     lax.fori_loop(0, chunks, chunk, 0)
+    for move in moves:
+        move.finish()
 
 
 def in_vmem(count):
     return [pl.BlockSpec(memory_space=pltpu.VMEM)] * count
 
 
-def run_forward(n1, qkv, beta, taps, aux, docs, gain):
-    row_len, heads = n1.shape[0], qkv.shape[1] // (3 * DK)
+def run_forward(n1, qkv, beta, taps, aux, docs, gain, o_weight, gate, up, down):
+    row_len, heads = n1.shape[0], qkv.shape[-1] // DK
+    rows_axis, seqs = qkv.shape[:2]
     chunks, width, f32 = row_len // CHUNK, heads * DK, jnp.float32
     shapes = (
         ((row_len, 3 * width), jnp.bfloat16),
@@ -706,23 +782,33 @@
         ((heads, chunks, CHUNK, CHUNK), f32),
         ((heads, chunks, DK, DK), f32),
         ((heads, chunks, CHUNK, DK), f32),
-    )
+        ((rows_axis, seqs, width, o_weight.shape[1]), jnp.bfloat16),
+        (gate.shape, jnp.bfloat16),
+        (up.shape, jnp.bfloat16),
+        ((seqs, down.shape[0] // seqs, down.shape[1]), jnp.bfloat16),
+    )
+    hbm = [pl.BlockSpec(memory_space=pl.ANY)]
     return pl.pallas_call(
         functools.partial(forward_kernel, heads),
         out_shape=[jax.ShapeDtypeStruct(*shape) for shape in shapes],
-        in_specs=in_vmem(7),
-        out_specs=in_vmem(len(shapes)),
+        in_specs=in_vmem(7) + hbm * 4,
+        out_specs=in_vmem(7) + hbm * 4,
         scratch_shapes=[
             pltpu.VMEM((PAD + CHUNK, 3 * width), f32),
             pltpu.VMEM((heads, DK, DK), f32),
-        ],
-        compiler_params=pltpu.CompilerParams(vmem_limit_bytes=48 * 1024 * 1024),
+            dma_sems(4),
+        ]
+        + exchange_sems()
+        + [dma_sems(seqs - 1)] * 6,
+        compiler_params=pltpu.CompilerParams(
+            collective_id=5, has_side_effects=True, vmem_limit_bytes=48 * 1024 * 1024
+        ),
         name="mixer_forward",
-    )(n1, qkv, beta, taps, aux, docs, gain)
-
-
-def run_backward(grad, o_full, saved, taps, aux, docs, gain):
-    row_len, heads = grad.shape[0], o_full.shape[1] // DK
+    )(n1, qkv, beta, taps, aux, docs, gain, o_weight, gate, up, down)
+
+
+def run_backward(grad, o_full, saved, taps, aux, docs, gain, sums, o_part):
+    row_len, heads = grad.shape[0], o_full.shape[2] // DK
     width, f32 = heads * DK, jnp.float32
     logit = saved[1]
     shapes = (
@@ -731,19 +817,26 @@
         ((KW, 3 * width), f32),
         ((1, DK), f32),
     )
+    far = [pl.BlockSpec(memory_space=pl.ANY)] * (len(sums) + 1)
+    far_shapes = tuple((array.shape, array.dtype) for array in (*sums, o_part))
     return pl.pallas_call(
         functools.partial(backward_kernel, heads),
-        out_shape=[jax.ShapeDtypeStruct(*shape) for shape in shapes],
-        in_specs=in_vmem(12),
-        out_specs=in_vmem(len(shapes)),
+        out_shape=[jax.ShapeDtypeStruct(*shape) for shape in shapes + far_shapes],
+        in_specs=in_vmem(12) + far,
+        out_specs=in_vmem(len(shapes)) + far,
         scratch_shapes=[
             pltpu.VMEM((PAD + CHUNK, 3 * width), f32),
             pltpu.VMEM((KW - 1, CHUNK + PAD, 3 * width), f32),
             pltpu.VMEM((heads, DK, DK), f32),
-        ],
-        compiler_params=pltpu.CompilerParams(vmem_limit_bytes=48 * 1024 * 1024),
+            pltpu.VMEM((width, grad.shape[1]), jnp.bfloat16),
+        ]
+        + pair_sems("seq", len(sums))
+        + pair_sems("row", 1),
+        compiler_params=pltpu.CompilerParams(
+            collective_id=6, has_side_effects=True, vmem_limit_bytes=48 * 1024 * 1024
+        ),
         name="mixer_backward",
-    )(grad, o_full, *saved, taps, aux, docs, gain)
+    )(grad, o_full, *saved, taps, aux, docs, gain, *sums, o_part)
 
 
 def row_aux(docs):
@@ -811,161 +904,198 @@
 
 
 class Gather:
-    sems = 5
-
     def __init__(self, line, slots, sems):
         self.line, self.slots, self.sems = line, slots, sems
-
-    def copy(self, kind, seq):
+        self.parts = sems.shape[2]
+        self.rows = slots.shape[2] // self.parts
+
+    def span(self, part):
+        return pl.ds(part * self.rows, self.rows)
+
+    def copy(self, kind, seq, part):
         line = self.line
         send = {"right": 0, "left": 1, "across": 2}[kind]
         recv = 4 if kind == "across" else 3
-        slot = self.slots.at[seq, line.core]
+        slot = self.slots.at[seq, line.core, self.span(part)]
         where = {"right": line.right, "left": line.left, "across": line.across}[kind]
-        return remote(slot, slot, self.sems.at[send, seq], self.sems.at[recv, seq], where)
-
-    def forward(self, seq, right, left):
+        return remote(
+            slot, slot, self.sems.at[send, seq, part], self.sems.at[recv, seq, part], where
+        )
+
+    def forward(self, seq, part, right, left):
         line = self.line
         if right:
 
             @pl.when(line.place < line.count - 1)
             def _():
-                self.copy("right", seq).start()
+                self.copy("right", seq, part).start()
 
         if left:
 
             @pl.when(line.place > 0)
             def _():
-                self.copy("left", seq).start()
-
-        self.copy("across", seq).start()
-
-    def phase(self, by):
+                self.copy("left", seq, part).start()
+
+        self.copy("across", seq, part).start()
+
+    def phase(self, by, part):
         line = self.line
         if by == 0:
-            self.forward(line.place, True, True)
+            self.forward(line.place, part, True, True)
             return
 
         @pl.when(line.place - by >= 0)
         def _():
-            self.copy("right", line.place - by).wait_recv()
-            self.forward(line.place - by, True, False)
+            self.copy("right", line.place - by, part).wait_recv()
+            self.forward(line.place - by, part, True, False)
 
         @pl.when(line.place + by < line.count)
         def _():
-            self.copy("left", line.place + by).wait_recv()
-            self.forward(line.place + by, False, True)
+            self.copy("left", line.place + by, part).wait_recv()
+            self.forward(line.place + by, part, False, True)
+
+    def phases(self, by):
+        for part in range(self.parts):
+            self.phase(by, part)
 
     def finish(self):
         line = self.line
         for seq in range(line.count):
-
-            @pl.when((line.place >= seq) & (line.place < line.count - 1))
-            def _():
-                self.copy("right", seq).wait_send()
-
-            @pl.when((line.place <= seq) & (line.place > 0))
-            def _():
-                self.copy("left", seq).wait_send()
-
-            self.copy("across", seq).wait()
+            for part in range(self.parts):
+
+                @pl.when((line.place >= seq) & (line.place < line.count - 1))
+                def _():
+                    self.copy("right", seq, part).wait_send()
+
+                @pl.when((line.place <= seq) & (line.place > 0))
+                def _():
+                    self.copy("left", seq, part).wait_send()
+
+                self.copy("across", seq, part).wait()
 
 
 class Scatter:
-    sems = 5
-
     def __init__(self, line, blocks, came, across, sems):
         self.line, self.blocks, self.came, self.across, self.sems = line, blocks, came, across, sems
-
-    def over(self, seq):
-        line = self.line
+        self.parts = sems.shape[2]
+        self.rows = blocks.shape[2] // self.parts
+
+    def span(self, part):
+        return pl.ds(part * self.rows, self.rows)
+
+    def over(self, seq, part):
+        line, span = self.line, self.span(part)
         return remote(
-            self.blocks.at[seq, line.other],
-            self.across.at[seq],
-            self.sems.at[0, seq],
-            self.sems.at[1, seq],
+            self.blocks.at[seq, line.other, span],
+            self.across.at[seq, span],
+            self.sems.at[0, seq, part],
+            self.sems.at[1, seq, part],
             line.across,
         )
 
-    def along(self, kind, seq):
-        line = self.line
+    def along(self, kind, seq, part):
+        line, span = self.line, self.span(part)
         way = {"right": 0, "left": 1}[kind]
         return remote(
-            self.blocks.at[seq, line.core],
-            self.came.at[way, seq],
-            self.sems.at[2, seq],
-            self.sems.at[3 + way, seq],
+            self.blocks.at[seq, line.core, span],
+            self.came.at[way, seq, span],
+            self.sems.at[2, seq, part],
+            self.sems.at[3 + way, seq, part],
             line.right if way == 0 else line.left,
         )
 
-    def offer(self, seq):
-        self.over(seq).start()
-
-    def chip_sum(self, seq):
-        self.over(seq).wait_recv()
-        return self.blocks[seq, self.line.core].astype(jnp.float32) + self.across[seq].astype(
-            jnp.float32
-        )
-
-    def pass_on(self, kind, seq):
-        line = self.line
+    def nears(self, k):
+        for part in range(self.parts):
+            self.near(k, part)
+
+    def fars(self, k):
+        for part in range(self.parts):
+            self.far(k, part)
+
+    def product(self, left_ref, right_ref, part, order=1, tile=512, right_tile=None):
+        seqs, cores, _, width = self.blocks.shape
+        span = self.span(part)
+        left = left_ref[:, span].reshape(seqs * cores * self.rows, -1)
+
+        def columns(t, _):
+            across = pl.ds(pl.multiple_of(t * tile, tile), tile)
+            if right_tile is not None:
+                total = right_tile(left, t, across)
+            elif order == 1:
+                total = mul(left, right_ref[across], (1, 1))
+            else:
+                total = mul(left, right_ref[:, across], (1, 0))
+            self.blocks[:, :, span, across] = total.astype(jnp.bfloat16).reshape(
+                seqs, cores, self.rows, tile
+            )
+            return 0
+
+        lax.fori_loop(0, width // tile, columns, 0)
+        for k in range(seqs):
+            self.over(self.target(k), part).start()
+
+    def pass_on(self, kind, seq, part):
+        line, span = self.line, self.span(part)
+        f32 = jnp.float32
         first = line.place == (0 if kind == "right" else line.count - 1)
         way = {"right": 0, "left": 1}[kind]
-        total = self.chip_sum(seq)
+        self.over(seq, part).wait_recv()
+        total = self.blocks[seq, line.core, span].astype(f32)
+        total = total + self.across[seq, span].astype(f32)
 
         @pl.when(first)
         def _():
-            self.blocks[seq, line.core] = total.astype(jnp.bfloat16)
+            self.blocks[seq, line.core, span] = total.astype(jnp.bfloat16)
 
         @pl.when(jnp.logical_not(first))
         def _():
-            self.along(kind, seq).wait_recv()
-            self.blocks[seq, line.core] = (
-                total + self.came[way, seq].astype(jnp.float32)
+            self.along(kind, seq, part).wait_recv()
+            self.blocks[seq, line.core, span] = (
+                total + self.came[way, seq, span].astype(f32)
             ).astype(jnp.bfloat16)
 
-        self.along(kind, seq).start()
+        self.along(kind, seq, part).start()
 
     def target(self, k):
         line = self.line
         return jnp.where(line.place < line.count // 2, line.count - 1 - k, k)
 
-    def near(self, k):
+    def near(self, k, part):
         line = self.line
         low = line.place < line.count // 2
 
         @pl.when(low & (line.count - 1 - k > line.place))
         def _():
-            self.pass_on("right", line.count - 1 - k)
+            self.pass_on("right", line.count - 1 - k, part)
 
         @pl.when(jnp.logical_not(low) & (k < line.place))
         def _():
-            self.pass_on("left", k)
-
-    def far(self, k):
+            self.pass_on("left", k, part)
+
+    def far(self, k, part):
         line = self.line
         low = line.place < line.count // 2
 
         @pl.when(low & (k < line.place))
         def _():
-            self.pass_on("left", k)
+            self.pass_on("left", k, part)
 
         @pl.when(jnp.logical_not(low) & (line.count - 1 - k > line.place))
         def _():
-            self.pass_on("right", line.count - 1 - k)
-
-    def wait_own(self):
+            self.pass_on("right", line.count - 1 - k, part)
+
+    def wait_own(self, part):
         line = self.line
 
         @pl.when(line.place > 0)
         def _():
-            self.along("right", line.place).wait_recv()
+            self.along("right", line.place, part).wait_recv()
 
         @pl.when(line.place < line.count - 1)
         def _():
-            self.along("left", line.place).wait_recv()
-
-        self.over(line.place).wait_recv()
+            self.along("left", line.place, part).wait_recv()
+
+        self.over(line.place, part).wait_recv()
 
     def own_rows(self, rows):
         line = self.line
@@ -980,48 +1110,180 @@
     def finish(self):
         line = self.line
         for seq in range(line.count):
-            self.over(seq).wait_send()
-
-            @pl.when(line.place != seq)
-            def _():
-                self.along("right", seq).wait_send()
-
-
-def product_rows(left_ref, right_ref, blocks, seq, tile=512):
-    cores, rows, width = blocks.shape[1:]
-    left = left_ref[pl.ds(pl.multiple_of(seq * cores * rows, cores * rows), cores * rows)]
-
-    def columns(t, _):
-        span = pl.ds(pl.multiple_of(t * tile, tile), tile)
-        part = mul(left, right_ref[span], (1, 1)).astype(jnp.bfloat16)
-        for core in range(cores):
-            blocks[seq, core, :, span] = part[core * rows : (core + 1) * rows]
+            for part in range(self.parts):
+                self.over(seq, part).wait_send()
+
+                @pl.when(line.place != seq)
+                def _():
+                    self.along("right", seq, part).wait_send()
+
+
+class Exchange:
+    def __init__(self, line, source, target, sems):
+        self.line, self.source, self.target = line, source, target
+        self.send, self.recv = sems[:2]
+        self.shared = len(sems) > 2
+        if self.shared:
+            self.send_row, self.recv_row = sems[2:]
+        self.row = lax.axis_index("row")
+        self.seq_others, self.row_others = around("seq"), around("row")
+
+    def spread(self, i):
+        other = self.seq_others[i]
+        return remote(
+            self.source(other),
+            self.target.at[self.row, self.line.place]
+            if self.shared
+            else self.target.at[self.line.place],
+            self.send.at[i],
+            self.recv.at[i],
+            {"seq": other},
+        )
+
+    def share(self, i, j):
+        line = self.line
+        came_from = lax.rem(line.place + line.count - i, line.count)
+        slot = self.target.at[self.row, came_from]
+        return remote(
+            slot, slot, self.send_row.at[i, j], self.recv_row.at[i, j], {"row": self.row_others[j]}
+        )
+
+    def start(self):
+        for i in range(len(self.seq_others)):
+            self.spread(i).start()
+
+    def share_own(self):
+        for j in range(len(self.row_others)):
+            self.share(0, j).start()
+
+    def share_came(self, i):
+        self.spread(i - 1).wait_recv()
+        for j in range(len(self.row_others)):
+            self.share(i, j).start()
+
+    def finish(self):
+        for i in range(len(self.seq_others)):
+            self.spread(i).wait_send()
+            if not self.shared:
+                self.spread(i).wait_recv()
+        for i in range(len(self.seq_others) + 1 if self.shared else 0):
+            for j in range(len(self.row_others)):
+                self.share(i, j).wait()
+
+
+class Share:
+    def __init__(self, axis, source, target, sems, own_sem):
+        self.axis, self.source, self.target = axis, source, target
+        self.send, self.recv = sems
+        self.others = around(axis)
+        self.own = pltpu.make_async_copy(source, target.at[lax.axis_index(axis)], own_sem)
+
+    def copy(self, i):
+        return remote(
+            self.source,
+            self.target.at[lax.axis_index(self.axis)],
+            self.send.at[i],
+            self.recv.at[i],
+            {self.axis: self.others[i]},
+        )
+
+    def start(self):
+        for i in range(len(self.others)):
+            self.copy(i).start()
+        self.own.start()
+
+    def finish(self):
+        for i in range(len(self.others)):
+            self.copy(i).wait()
+        self.own.wait()
+
+
+class Swap:
+    def __init__(self, axis, source, target, sems, own_sem):
+        self.axis, self.source, self.target = axis, source, target
+        self.send, self.recv = sems
+        self.others = around(axis)
+        place = lax.axis_index(axis)
+        self.own = pltpu.make_async_copy(source.at[place], target.at[place], own_sem)
+
+    def copy(self, i):
+        return remote(
+            self.source.at[self.others[i]],
+            self.target.at[lax.axis_index(self.axis)],
+            self.send.at[i],
+            self.recv.at[i],
+            {self.axis: self.others[i]},
+        )
+
+    def start(self):
+        for i in range(len(self.others)):
+            self.copy(i).start()
+        self.own.start()
+
+    def finish(self):
+        for i in range(len(self.others)):
+            self.copy(i).wait()
+        self.own.wait()
+
+
+def pair_sems(axis, count):
+    return [dma_sems(lax.axis_size(axis) - 1)] * (2 * count) + [dma_sems(count)]
+
+
+def moves_of(kind, axis, sources, targets, sems):
+    return [
+        kind(axis, source, target, sems[2 * i : 2 * i + 2], sems[-1].at[i])
+        for i, (source, target) in enumerate(zip(sources, targets))
+    ]
+
+
+def along_axis(axis):
+    return [({axis: other}, other >= 0) for other in around(axis)]
+
+
+def exchange_sems():
+    seqs, rows = lax.axis_size("seq"), lax.axis_size("row")
+    return [
+        dma_sems(seqs - 1),
+        dma_sems(seqs - 1),
+        dma_sems(seqs, rows - 1),
+        dma_sems(seqs, rows - 1),
+    ]
+
+
+def exchange_partners(line):
+    return [({"seq": other}, other >= 0) for other in around("seq")] + [
+        ({"row": other}, other >= 0) for other in around("row")
+    ]
+
+
+STEP = 32
+
+
+def over_rows(total, part, body):
+    def step(i, _):
+        body(pl.ds(pl.multiple_of(part * total.rows + i * STEP, STEP), STEP))
         return 0
 
-    lax.fori_loop(0, width // tile, columns, 0)
-
-
-STEP = 32
-
-
-def over_rows(count, body):
-    def step(i, _):
-        body(pl.ds(pl.multiple_of(i * STEP, STEP), STEP), i)
-        return 0
-
-    lax.fori_loop(0, count // STEP, step, 0)
-
-
-def own_span(core, rows, inner):
-    return pl.ds(pl.multiple_of(core * rows + inner.start, STEP), inner.size)
+    lax.fori_loop(0, total.rows // STEP, step, 0)
 
 
 def resid_kernel(
-    mix_ref, o_ref, x_ref, g_ref, gain_ref, resid_ref, n2_ref, g_full_ref,
-    blocks, came, across, sum_sems, n2_sems, g_sems,
+    mix_ref, o_ref, x_ref, g_ref, gain_ref, gate_ref, up_ref, down_ref,
+    resid_ref, n2_ref, g_full_ref, gate_full_ref, up_full_ref, down_full_ref,
+    blocks, came, across, o_rows, sum_sems, n2_sems, g_sems, *sems,
 ):
     line = Line()
-    greet(line_partners())
+    greet(line_partners() + along_axis("row"))
+    shares = moves_of(
+        Share,
+        "row",
+        (gate_ref, up_ref, down_ref),
+        (gate_full_ref, up_full_ref, down_full_ref),
+        sems,
+    )
+    for share in shares:
+        share.start()
     rows = n2_ref.shape[2]
     total = Scatter(line, blocks, came, across, sum_sems)
     n2 = Gather(line, n2_ref, n2_sems)
@@ -1029,45 +1291,55 @@
     g_full_ref[line.place, line.core] = g_ref[
         pl.ds(pl.multiple_of(line.core * rows, rows), rows)
     ]
-    for k in range(line.count):
-        seq = total.target(k)
-        product_rows(mix_ref, o_ref, blocks, seq)
-        total.offer(seq)
-    total.near(0)
-    grads.phase(0)
+    grads.phases(0)
+    side_by_side(o_ref, o_rows)
+    for part in range(total.parts):
+        total.product(mix_ref, o_rows, part, order=0)
     for k in range(1, line.count):
-        total.near(k)
-        grads.phase(k)
-    for k in range(line.count):
-        total.far(k)
-    total.wait_own()
-
-    def normed(span, i):
-        x_span = pl.ds(pl.multiple_of(line.core * rows + i * STEP, STEP), STEP)
+        grads.phases(k)
+        total.nears(k - 1)
+    for k in range(line.count - 1):
+        total.fars(k)
+
+    def normed(span):
+        x_span = pl.ds(pl.multiple_of(line.core * rows + span.start, STEP), STEP)
         resid = x_ref[x_span].astype(jnp.float32) + total.own_rows(span)
         resid_ref[span] = resid
         n2_ref[line.place, line.core, span] = (
             resid * norm_scale(resid) * gain_ref[...]
         ).astype(jnp.bfloat16)
 
-    over_rows(rows, normed)
-    for k in range(line.count):
-        n2.phase(k)
+    for part in range(total.parts):
+        total.wait_own(part)
+        over_rows(total, part, normed)
+        n2.phase(0, part)
+    for k in range(1, line.count):
+        n2.phases(k)
     total.finish()
     n2.finish()
     grads.finish()
+    for share in shares:
+        share.finish()
+
+
+def side_by_side(blocks_ref, out_ref):
+    outer, inner, _, width = blocks_ref.shape
+    for i in range(outer):
+        for j in range(inner):
+            out_ref[:, (i * inner + j) * width : (i * inner + j + 1) * width] = blocks_ref[i, j]
 
 
 def dma_sems(*shape):
     return pltpu.SemaphoreType.DMA(shape)
 
 
-def line_call(kernel, collective_id, name, outs, scratch, args, limit=56):
+def line_call(kernel, collective_id, name, outs, scratch, args, limit=56, far_args=(), far_outs=()):
+    far = pl.BlockSpec(memory_space=pl.ANY)
     return pl.pallas_call(
         kernel,
-        out_shape=[jax.ShapeDtypeStruct(*out) for out in outs],
-        in_specs=in_vmem(len(args)),
-        out_specs=in_vmem(len(outs)),
+        out_shape=[jax.ShapeDtypeStruct(*out) for out in (*outs, *far_outs)],
+        in_specs=in_vmem(len(args)) + [far] * len(far_args),
+        out_specs=in_vmem(len(outs)) + [far] * len(far_outs),
         scratch_shapes=scratch,
         compiler_params=pltpu.CompilerParams(
             collective_id=collective_id,
@@ -1075,7 +1347,7 @@
             vmem_limit_bytes=limit * 1024 * 1024,
         ),
         name=name,
-    )(*args)
+    )(*args, *far_args)
 
 
 def scatter_scratch(seqs, cores, rows, width):
@@ -1087,7 +1359,10 @@
     ]
 
 
-def run_resid(mix, o_full, x, g, gain):
+PARTS = 2
+
+
+def run_resid(mix, o_full, x, g, gain, weights):
     seqs, cores, (piece, width) = lax.axis_size("seq"), lax.axis_size("tp"), x.shape
     rows, b16 = piece // cores, jnp.bfloat16
     outs = (
@@ -1095,38 +1370,61 @@
         ((seqs, cores, rows, width), b16),
         ((seqs, cores, rows, width), b16),
     )
-    scratch = scatter_scratch(seqs, cores, rows, width) + [dma_sems(5, seqs)] * 3
-    resid, n2, g_full = line_call(
-        resid_kernel, 1, "resid_norm", outs, scratch, (mix, o_full, x, g, gain)
-    )
-    return resid, n2.reshape(-1, width), g_full.reshape(-1, width)
+    scratch = scatter_scratch(seqs, cores, rows, width)
+    scratch = scratch + [pltpu.VMEM((o_full.shape[2], width), b16)] + [dma_sems(5, seqs, PARTS)] * 3
+    scratch = scratch + pair_sems("row", len(weights))
+    mix = mix.reshape(seqs * cores, rows, -1)
+    resid, n2, g_full, *full = line_call(
+        resid_kernel, 1, "resid_norm", outs, scratch, (mix, o_full, x, g, gain),
+        far_args=weights,
+        far_outs=[((lax.axis_size("row"),) + weight.shape, b16) for weight in weights],
+    )
+    return resid, n2.reshape(-1, width), g_full.reshape(-1, width), full
 
 
 def grad_resid_kernel(
-    dgu_ref, gate_up_ref, hidden_ref, down_ref, resid_ref, g_ref, gain_ref,
+    grad_gate_ref, grad_up_ref, gate_ref, up_ref, hidden_ref, down_ref, resid_ref, g_ref, gain_ref,
+    down_part_ref, gate_part_ref, up_part_ref,
     grad_resid_ref, grad_attn_ref, gain_grad_ref, result_ref,
-    blocks, came, across, out_blocks, out_came, out_across,
-    sum_sems, out_sems, attn_sems, swap_sems,
+    down_came_ref, gate_came_ref, up_came_ref,
+    blocks, came, across, out_blocks, out_came, out_across, down_rows,
+    sum_sems, out_sems, attn_sems, swap_sems, *sems,
 ):
     line = Line()
-    greet(line_partners())
+    greet(line_partners() + along_axis("row"))
+    parts = moves_of(
+        Swap,
+        "row",
+        (down_part_ref, gate_part_ref, up_part_ref),
+        (down_came_ref, gate_came_ref, up_came_ref),
+        sems,
+    )
+    for move in parts:
+        move.start()
     rows = resid_ref.shape[0]
     total = Scatter(line, blocks, came, across, sum_sems)
     result = Scatter(line, out_blocks, out_came, out_across, out_sems)
     attn = Gather(line, grad_attn_ref, attn_sems)
-    for k in range(line.count):
-        seq = total.target(k)
-        product_rows(dgu_ref, gate_up_ref, blocks, seq)
-        total.offer(seq)
-        total.near(k)
-    for k in range(line.count):
-        total.far(k)
-        product_rows(hidden_ref, down_ref, out_blocks, total.target(k))
-    total.wait_own()
+    units = gate_ref.shape[1]
+    for part in range(total.parts):
+        left_up = grad_up_ref[:, total.span(part)].reshape(-1, units)
+
+        def right_tile(left, t, columns, left_up=left_up):
+            return mul(left, gate_ref[columns], (1, 1)) + mul(left_up, up_ref[columns], (1, 1))
+
+        total.product(grad_gate_ref, None, part, right_tile=right_tile)
+    side_by_side(down_ref, down_rows)
+    total.nears(0)
+    for part in range(result.parts):
+        result.product(hidden_ref, down_rows, part, order=0)
+    for k in range(1, line.count - 1):
+        total.nears(k)
+    for k in range(line.count - 1):
+        total.fars(k)
     gain_grad_ref[...] = jnp.zeros_like(gain_grad_ref)
 
-    def back(span, i):
-        own_span = pl.ds(pl.multiple_of(line.core * rows + i * STEP, STEP), STEP)
+    def back(span):
+        own_span = pl.ds(pl.multiple_of(line.core * rows + span.start, STEP), STEP)
         resid = resid_ref[span]
         grad_two = total.own_rows(span)
         scale = norm_scale(resid)
@@ -1137,28 +1435,31 @@
         grad_resid_ref[span] = grad
         grad_attn_ref[line.place, line.core, span] = grad.astype(jnp.bfloat16)
 
-    over_rows(rows, back)
-    attn.phase(0)
-    for k in range(line.count):
-        result.offer(result.target(k))
+    for part in range(total.parts):
+        total.wait_own(part)
+        over_rows(total, part, back)
+        attn.phase(0, part)
     for k in range(1, line.count):
-        result.near(k - 1)
-        attn.phase(k)
-    for k in range(line.count):
-        result.far(k)
-    result.wait_own()
-
-    def finish(span, i):
-        own_span = pl.ds(pl.multiple_of(line.core * rows + i * STEP, STEP), STEP)
+        attn.phases(k)
+        result.nears(k - 1)
+    for k in range(line.count - 1):
+        result.fars(k)
+
+    def finish(span):
+        own_span = pl.ds(pl.multiple_of(line.core * rows + span.start, STEP), STEP)
         result_ref[own_span] = (resid_ref[span] + result.own_rows(span)).astype(jnp.bfloat16)
 
-    over_rows(rows, finish)
+    for part in range(result.parts):
+        result.wait_own(part)
+        over_rows(result, part, finish)
     swap = own_swap(line, result_ref, rows, swap_sems)
     swap.start()
     total.finish()
     result.finish()
     attn.finish()
     swap.wait()
+    for move in parts:
+        move.finish()
 
 
 def own_swap(line, ref, rows, sems):
@@ -1166,7 +1467,7 @@
     return remote(own, own, sems.at[0], sems.at[1], line.across)
 
 
-def run_grad_resid(grad_gate_up, gate_up, hidden, down, resid, g, gain):
+def run_grad_resid(grad_gate, grad_up, gate, up, hidden, down, resid, g, gain, parts):
     seqs, cores, (piece, width) = lax.axis_size("seq"), lax.axis_size("tp"), g.shape
     rows, b16, f32 = piece // cores, jnp.bfloat16, jnp.float32
     outs = (
@@ -1176,51 +1477,69 @@
         ((piece, width), b16),
     )
     scratch = scatter_scratch(seqs, cores, rows, width) * 2
-    scratch = scratch + [dma_sems(5, seqs)] * 3 + [dma_sems(2)]
-    grad_resid, grad_attn, gain_grad, result = line_call(
+    scratch = scratch + [pltpu.VMEM((down.shape[2], width), b16)]
+    scratch = scratch + [dma_sems(5, seqs, PARTS)] * 3 + [dma_sems(2)]
+    scratch = scratch + pair_sems("row", len(parts))
+    grad_gate, grad_up, hidden = (
+        array.reshape(seqs * cores, rows, -1) for array in (grad_gate, grad_up, hidden)
+    )
+    grad_resid, grad_attn, gain_grad, result, *came = line_call(
         grad_resid_kernel, 2, "grad_resid", outs, scratch,
-        (grad_gate_up, gate_up, hidden, down, resid, g, gain),
-    )
-    return grad_resid, grad_attn.reshape(-1, width), gain_grad, result
+        (grad_gate, grad_up, gate, up, hidden, down, resid, g, gain),
+        far_args=parts,
+        far_outs=[(part.shape, b16) for part in parts],
+    )
+    return grad_resid, grad_attn.reshape(-1, width), gain_grad, result, came
 
 
 def input_grad_kernel(
-    grad_proj_ref, qkv_ref, grad_logit_ref, beta_ref, x_ref, grad_resid_ref, gain_ref,
-    input_grad_ref, gain_grad_ref,
-    blocks, came, across, sum_sems, swap_sems,
+    grad_proj_ref, qkv_ref, grad_logit_ref, beta_ref, x_ref, grad_resid_ref, gain_ref, qkv_part_ref,
+    o_sum_ref,
+    input_grad_ref, gain_grad_ref, qkv_came_ref,
+    o_came_ref,
+    blocks, came, across, qkv_rows, qkv_sum, sum_sems, swap_sems, *sems,
 ):
     line = Line()
-    greet(line_partners())
+    greet(along_axis("seq") + along_axis("row") + along_axis("tp"))
+    (o_move,) = moves_of(Swap, "seq", (o_sum_ref,), (o_came_ref,), sems[:3])
+    (rows_move,) = moves_of(Swap, "row", (qkv_part_ref,), (qkv_rows,), sems[3:6])
+    (qkv_move,) = moves_of(Swap, "seq", (qkv_sum,), (qkv_came_ref,), sems[6:9])
+    rows_move.start()
+    o_move.start()
     rows = grad_resid_ref.shape[0]
     total = Scatter(line, blocks, came, across, sum_sems)
 
-    def product(seq, tile=512):
-        cores, _, width = blocks.shape[1:]
-        at = pl.ds(pl.multiple_of(seq * cores * rows, cores * rows), cores * rows)
-        left, logit = grad_proj_ref[at], grad_logit_ref[at]
-
-        def columns(t, _):
-            span = pl.ds(pl.multiple_of(t * tile, tile), tile)
-            part = mul(left, qkv_ref[span], (1, 1)) + mul(logit, beta_ref[:, span], (1, 0))
-            part = part.astype(jnp.bfloat16)
-            for core in range(cores):
-                blocks[seq, core, :, span] = part[core * rows : (core + 1) * rows]
-            return 0
-
-        lax.fori_loop(0, width // tile, columns, 0)
-
-    for k in range(line.count):
-        seq = total.target(k)
-        product(seq)
-        total.offer(seq)
-        total.near(k)
-    for k in range(line.count):
-        total.far(k)
-    total.wait_own()
+    width = qkv_ref.shape[-1]
+
+    for part in range(total.parts):
+        logit = grad_logit_ref[:, total.span(part)].reshape(-1, grad_logit_ref.shape[-1])
+
+        def right_tile(left, t, across, logit=logit):
+            block = qkv_ref[t]
+            out = mul(logit, beta_ref[:, across], (1, 0))
+            for c in range(3):
+                out = out + mul(
+                    left[:, c * width : (c + 1) * width], block[:, c].reshape(-1, width), (1, 1)
+                )
+            return out
+
+        tile = qkv_ref.shape[1] * qkv_ref.shape[3]
+        total.product(grad_proj_ref, None, part, tile=tile, right_tile=right_tile)
+    for k in range(line.count - 1):
+        total.nears(k)
+    for k in range(line.count - 1):
+        total.fars(k)
+    rows_move.finish()
+    for i in range(qkv_rows.shape[1]):
+        piece = qkv_rows[0, i].astype(jnp.float32)
+        for j in range(1, qkv_rows.shape[0]):
+            piece = piece + qkv_rows[j, i].astype(jnp.float32)
+        qkv_sum[i] = piece.astype(jnp.bfloat16)
+    qkv_move.start()
     gain_grad_ref[...] = jnp.zeros_like(gain_grad_ref)
 
-    def back(span, i):
-        own_span = pl.ds(pl.multiple_of(line.core * rows + i * STEP, STEP), STEP)
+    def back(span):
+        own_span = pl.ds(pl.multiple_of(line.core * rows + span.start, STEP), STEP)
         x = x_ref[own_span].astype(jnp.float32)
         grad_one = total.own_rows(span)
         scale = norm_scale(x)
@@ -1229,112 +1548,138 @@
             grad_resid_ref[span] + norm_back(x, scale, gain_ref[...], grad_one)
         ).astype(jnp.bfloat16)
 
-    over_rows(rows, back)
+    for part in range(total.parts):
+        total.wait_own(part)
+        over_rows(total, part, back)
     swap = own_swap(line, input_grad_ref, rows, swap_sems)
     swap.start()
     total.finish()
     swap.wait()
-
-
-def run_input_grad(grad_proj, qkv, grad_logit, beta, x, grad_resid, gain):
+    o_move.finish()
+    qkv_move.finish()
+
+
+def run_input_grad(grad_proj, qkv, grad_logit, beta, x, grad_resid, gain, qkv_part, o_sum):
     seqs, cores, (piece, width) = lax.axis_size("seq"), lax.axis_size("tp"), x.shape
     rows, b16, f32 = piece // cores, jnp.bfloat16, jnp.float32
-    outs = (((piece, width), b16), ((1, width), f32))
-    scratch = scatter_scratch(seqs, cores, rows, width) + [dma_sems(5, seqs), dma_sems(2)]
+    outs = (((piece, width), b16), ((1, width), f32), (qkv_part.shape[1:], b16))
+    scratch = scatter_scratch(seqs, cores, rows, width)
+    scratch = scratch + [pltpu.VMEM(qkv_part.shape, b16), pltpu.VMEM(qkv_part.shape[1:], b16)]
+    scratch = scratch + [dma_sems(5, seqs, PARTS), dma_sems(2)]
+    scratch = scratch + pair_sems("seq", 1) + pair_sems("row", 1) + pair_sems("seq", 1)
+    grad_proj = grad_proj.reshape(seqs * cores, rows, -1)
+    grad_logit = grad_logit.reshape(seqs * cores, rows, -1)
     return line_call(
         input_grad_kernel, 3, "input_grad", outs, scratch,
-        (grad_proj, qkv, grad_logit, beta, x, grad_resid, gain),
+        (grad_proj, qkv, grad_logit, beta, x, grad_resid, gain, qkv_part),
+        far_args=(o_sum,),
+        far_outs=((o_sum.shape, b16),),
     )
 
 
 def normed_kernel(
-    x_ref, gain_ref, parts_ref, beta_ref, n1_ref, qkv_ref, beta_full_ref,
-    n1_sems, send_line, recv_line, send_row, recv_row,
-    beta_send_line, beta_recv_line, beta_send_row, beta_recv_row,
+    x_ref, gain_ref, weight_ref, beta_ref, n1_ref, qkv_ref, beta_full_ref, n1_sems, own_sems, *sems
 ):
     line = Line()
     row = lax.axis_index("row")
-    seq_others, row_others = around("seq"), around("row")
-    greet(
-        [({"seq": other}, other >= 0) for other in seq_others]
-        + [({"row": other}, other >= 0) for other in row_others]
-        + [(line.across, line.core >= 0)]
-    )
-    moves = (
-        (parts_ref, qkv_ref, send_line, recv_line, send_row, recv_row),
-        (beta_ref, beta_full_ref, beta_send_line, beta_recv_line, beta_send_row, beta_recv_row),
-    )
-
-    def spread(move, i):
-        source, target, send, recv = move[:4]
-        return remote(
-            source.at[seq_others[i]],
-            target.at[row, line.place],
-            send.at[i],
-            recv.at[i],
-            {"seq": seq_others[i]},
+    greet(exchange_partners(line) + [(line.across, line.core >= 0)])
+    width = qkv_ref.shape[-1]
+
+    def columns(seq):
+        return weight_ref.at[:, :, pl.ds(pl.multiple_of(seq * width, width), width)]
+
+    moves = [
+        Exchange(line, columns, qkv_ref, sems[:4]),
+        Exchange(line, lambda seq: beta_ref.at[seq], beta_full_ref, sems[4:]),
+    ]
+    for move in moves:
+        move.start()
+    own = [
+        pltpu.make_async_copy(
+            move.source(line.place), move.target.at[row, line.place], own_sems.at[i]
         )
-
-    def share(move, i, j):
-        target, send, recv = move[1], move[4], move[5]
-        came_from = lax.rem(line.place + line.count - i, line.count)
-        slot = target.at[row, came_from]
-        return remote(slot, slot, send.at[i, j], recv.at[i, j], {"row": row_others[j]})
-
-    for move in moves:
-        for i in range(len(seq_others)):
-            spread(move, i).start()
-    for move in moves:
-        move[1][row, line.place] = move[0][line.place]
-        for j in range(len(row_others)):
-            share(move, 0, j).start()
+        for i, move in enumerate(moves)
+    ]
+    for copy in own:
+        copy.start()
     rows = n1_ref.shape[2]
     n1 = Gather(line, n1_ref, n1_sems)
 
-    def normed(span, i):
-        x_span = pl.ds(pl.multiple_of(line.core * rows + i * STEP, STEP), STEP)
+    def normed(span):
+        x_span = pl.ds(pl.multiple_of(line.core * rows + span.start, STEP), STEP)
         x = x_ref[x_span].astype(jnp.float32)
         n1_ref[line.place, line.core, span] = (x * norm_scale(x) * gain_ref[...]).astype(
             jnp.bfloat16
         )
 
-    over_rows(rows, normed)
-    n1.phase(0)
+    for part in range(n1.parts):
+        over_rows(n1, part, normed)
+        n1.phase(0, part)
+    for copy in own:
+        copy.wait()
+    for move in moves:
+        move.share_own()
     for k in range(1, line.count):
         for move in moves:
-            spread(move, k - 1).wait_recv()
-            for j in range(len(row_others)):
-                share(move, k, j).start()
-        n1.phase(k)
+            move.share_came(k)
+        n1.phases(k)
     for move in moves:
-        for i in range(len(seq_others)):
-            spread(move, i).wait_send()
-        for i in range(line.count):
-            for j in range(len(row_others)):
-                share(move, i, j).wait()
+        move.finish()
     n1.finish()
 
 
-def run_normed(x, gain, parts, beta):
+def run_normed(x, gain, weight, beta):
     rows_axis, seqs, cores = (lax.axis_size(axis) for axis in ("row", "seq", "tp"))
     piece, width = x.shape
     b16 = jnp.bfloat16
     outs = (
         ((seqs, cores, piece // cores, width), b16),
-        ((rows_axis,) + parts.shape, b16),
+        ((rows_axis, seqs) + weight.shape[:2] + (weight.shape[2] // seqs,), b16),
         ((rows_axis,) + beta.shape, b16),
     )
-    moves = [
-        dma_sems(seqs - 1),
-        dma_sems(seqs - 1),
-        dma_sems(seqs, rows_axis - 1),
-        dma_sems(seqs, rows_axis - 1),
-    ]
     n1, qkv, beta_full = line_call(
-        normed_kernel, 4, "norm_gather", outs, [dma_sems(5, seqs)] + moves * 2,
-        (x, gain, parts, beta),
-    )
-    return n1.reshape(-1, width), qkv.reshape(-1, qkv.shape[-1]), beta_full
+        normed_kernel, 4, "norm_gather", outs,
+        [dma_sems(5, seqs, PARTS), dma_sems(2)] + exchange_sems() * 2,
+        (x, gain, weight, beta),
+    )
+    return n1.reshape(-1, width), qkv, beta_full
+
+
+def mlp_kernel(
+    n2_ref, g_ref, gate_ref, up_ref, down_ref, hidden_ref, grad_gate_ref, grad_up_ref, down_rows
+):
+    @pl.when(pl.program_id(0) == 0)
+    def _():
+        side_by_side(down_ref, down_rows)
+
+    n2 = n2_ref[...]
+    gate = mul(n2, gate_ref[...], (1, 0))
+    up = mul(n2, up_ref[...], (1, 0))
+    grad_hidden = mul(g_ref[...], down_rows[...], (1, 1))
+    sig = sigmoid(gate)
+    act = gate * sig
+    hidden_ref[...] = (act * up).astype(jnp.bfloat16)
+    grad_up_ref[...] = (grad_hidden * act).astype(jnp.bfloat16)
+    grad_gate_ref[...] = (grad_hidden * up * sig * (1.0 + gate * (1.0 - sig))).astype(jnp.bfloat16)
+
+
+def run_mlp(n2, g, gate, up, down, block=128):
+    row_len, width = n2.shape
+    units = gate.shape[1]
+    tokens = pl.BlockSpec((block, width), lambda i: (i, 0))
+    out = pl.BlockSpec((block, units), lambda i: (i, 0))
+    whole = pl.BlockSpec(memory_space=pltpu.VMEM)
+    shape = jax.ShapeDtypeStruct((row_len, units), jnp.bfloat16)
+    return pl.pallas_call(
+        mlp_kernel,
+        grid=(row_len // block,),
+        out_shape=[shape] * 3,
+        in_specs=[tokens, tokens, whole, whole, whole],
+        out_specs=[out] * 3,
+        scratch_shapes=[pltpu.VMEM((units, width), jnp.bfloat16)],
+        compiler_params=pltpu.CompilerParams(vmem_limit_bytes=48 * 1024 * 1024),
+        name="mlp",
+    )(n2, g, gate, up, down)
 
 
 def small_sums_kernel(
@@ -1405,38 +1750,6 @@
     )(part)
 
 
-def exchanged(parts, axis):
-    count, place = lax.axis_size(axis), lax.axis_index(axis)
-    came = [lax.dynamic_index_in_dim(parts, place, 0, keepdims=False)]
-    for by in range(1, count):
-        part = lax.dynamic_index_in_dim(parts, (place + by) % count, 0, keepdims=False)
-        came.append(lax.ppermute(part, axis, [(i, (i + by) % count) for i in range(count)]))
-    came = jnp.stack(came)
-    order = (place - jnp.arange(count)) % count
-    return jnp.concatenate(
-        [lax.dynamic_slice_in_dim(came, order[j], 1, axis=0) for j in range(count)], axis=0
-    )
-
-
-def spread(shard, pieces, axis):
-    rows, width = shard.shape
-    return exchanged(shard.reshape(rows, pieces, width // pieces).transpose(1, 0, 2), axis)
-
-
-def gathered(shard):
-    pieces = lax.axis_size("seq")
-    parts = spread(shard, pieces, "seq")
-    whole = lax.all_gather(parts, "row", axis=0, tiled=True)
-    return whole.reshape(-1, whole.shape[-1])
-
-
-def returned(part):
-    pieces = lax.axis_size("seq")
-    rows = part.shape[0] // (pieces * lax.axis_size("row"))
-    own = lax.psum_scatter(part, "row", scatter_dimension=0, tiled=True)
-    return exchanged(own.reshape(pieces, rows, -1), "seq")
-
-
 def local_heads(
     block_input,
     grad_out,
@@ -1463,18 +1776,14 @@
     f32, b16 = jnp.float32, jnp.bfloat16
 
     x_piece, g_piece = block_input[0], grad_out[0]
-    qkv_parts = qkv_weight.reshape(3, shard_rows, pieces, width).transpose(2, 1, 0, 3)
     beta_parts = jnp.pad(
         beta_weight.T.reshape(pieces, heads, shard_rows), ((0, 0), (0, 16 - heads), (0, 0))
     )
     normed_one, qkv_full, beta_full = run_normed(
-        x_piece, attn_gain[None], qkv_parts.reshape(pieces, shard_rows, -1), beta_parts
+        x_piece, attn_gain[None], qkv_weight, beta_parts
     )
     beta_full = beta_full.reshape(-1, 16, shard_rows).transpose(1, 0, 2).reshape(16, -1)
-    o_full = gathered(o_weight.T)
-    gate_up_parts = gate_up_weight.reshape(2, shard_rows, pieces, units).transpose(1, 2, 0, 3)
-    gate_up_full = gathered(gate_up_parts.reshape(shard_rows, -1))
-    down_full = gathered(down_weight.T)
+    gate_up_parts = gate_up_weight.reshape(2, shard_rows, pieces, units).transpose(0, 2, 1, 3)
 
     ends = jnp.cumsum(doc_lengths[0])
     places = jnp.arange(row_len, dtype=jnp.int32)
@@ -1484,26 +1793,38 @@
     taps = lax.dynamic_slice_in_dim(conv_weight, piece * width, width, axis=2)
     taps = taps.transpose(1, 0, 2).reshape(KW, 3 * width)
 
-    proj, logit, mixed, normed_mix, inverse, states, written = run_forward(
-        normed_one, qkv_full, beta_full, taps, aux, doc_rows, gain_row
-    )
-    resid, normed_two, g_full = run_resid(normed_mix, o_full, x_piece, g_piece, mlp_gain[None])
-    gate_up = jnp.dot(normed_two, gate_up_full, preferred_element_type=f32)
-    gate, up = gate_up[:, :units], gate_up[:, units:]
-    gate_sig = jax.nn.sigmoid(gate)
-    gate_act = gate * gate_sig
-    hidden = (gate_act * up).astype(b16)
-    grad_hidden = jnp.dot(g_full, down_full, preferred_element_type=f32)
-    grad_gate = grad_hidden * up * gate_sig * (1.0 + gate * (1.0 - gate_sig))
-    grad_up = grad_hidden * gate_act
-    grad_gate_up = jnp.concatenate([grad_gate, grad_up], axis=1).astype(b16)
-    grad_resid, grad_attn, mlp_gain_part, result = run_grad_resid(
-        grad_gate_up, gate_up_full, hidden, down_full, resid, g_piece, mlp_gain[None]
-    )
-    down_part = jnp.einsum("td,tf->df", g_full, hidden, preferred_element_type=f32)
-    gate_up_part = jnp.einsum("td,tf->df", normed_two, grad_gate_up, preferred_element_type=f32)
+    (
+        proj, logit, mixed, normed_mix, inverse, states, written,
+        o_full, gate_came, up_came, down_came,
+    ) = run_forward(
+        normed_one, qkv_full, beta_full, taps, aux, doc_rows, gain_row,
+        o_weight, gate_up_parts[0], gate_up_parts[1], down_weight,
+    )
+    resid, normed_two, g_full, (gate_full, up_full, down_full) = run_resid(
+        normed_mix, o_full, x_piece, g_piece, mlp_gain[None], (gate_came, up_came, down_came)
+    )
+    gate_full = gate_full.reshape(model_width, units)
+    up_full = up_full.reshape(model_width, units)
+    hidden, grad_gate, grad_up = run_mlp(normed_two, g_full, gate_full, up_full, down_full)
+    down_part = jnp.einsum("td,tf->df", g_full, hidden, preferred_element_type=f32).astype(b16)
+    gate_part = jnp.einsum("td,tf->df", normed_two, grad_gate, preferred_element_type=f32).astype(b16)
+    up_part = jnp.einsum("td,tf->df", normed_two, grad_up, preferred_element_type=f32).astype(b16)
+    rows_axis = lax.axis_size("row")
+
+    def by_row(part):
+        return part.reshape(rows_axis, pieces, shard_rows, -1)
+
+    def summed(came):
+        return jnp.sum(came.astype(f32), axis=0).astype(b16)
+
+    grad_resid, grad_attn, mlp_gain_part, result, came = run_grad_resid(
+        grad_gate, grad_up, gate_full, up_full, hidden, down_full, resid, g_piece, mlp_gain[None],
+        (by_row(down_part), by_row(gate_part), by_row(up_part)),
+    )
     o_part = jnp.einsum("td,te->de", grad_attn, normed_mix, preferred_element_type=f32)
-    grad_proj, grad_logit, conv_part, out_gain_part = run_backward(
+    (
+        grad_proj, grad_logit, conv_part, out_gain_part, down_sum, gate_sum, up_sum, o_came,
+    ) = run_backward(
         grad_attn,
         o_full,
         (proj, logit, mixed, inverse, states, written),
@@ -1511,11 +1832,14 @@
         aux,
         doc_rows,
         gain_row,
-    )
-    input_grad, attn_gain_part = run_input_grad(
-        grad_proj, qkv_full, grad_logit, beta_full, x_piece, grad_resid, attn_gain[None]
+        [summed(array) for array in came],
+        by_row(o_part.astype(b16)),
     )
     qkv_part = jnp.einsum("td,te->de", normed_one, grad_proj, preferred_element_type=f32)
+    input_grad, attn_gain_part, qkv_sum, o_sum = run_input_grad(
+        grad_proj, qkv_full, grad_logit, beta_full, x_piece, grad_resid, attn_gain[None],
+        by_row(qkv_part.astype(b16)), summed(o_came),
+    )
     beta_part = jnp.einsum("td,th->hd", normed_one, grad_logit, preferred_element_type=f32)
     packed = jnp.concatenate(
         [
@@ -1542,10 +1866,7 @@
     beta_sum = lax.dynamic_slice_in_dim(
         beta_sum, (lax.axis_index("row") * pieces + piece) * shard_rows, shard_rows, axis=1
     ).T
-    down_sum = returned(down_part.astype(b16))
-    gate_up_sum = returned(gate_up_part.astype(b16)).reshape(pieces, shard_rows, 2, units)
-    o_sum = returned(o_part.astype(b16))
-    qkv_sum = returned(qkv_part.astype(b16)).reshape(pieces, shard_rows, 3, width)
+    qkv_sum = qkv_sum.reshape(pieces, shard_rows, 3, width)
     return (
         result[None],
         input_grad[None],
@@ -1556,7 +1877,7 @@
         qkv_sum.transpose(2, 1, 0, 3).reshape(3, shard_rows, -1).astype(f32),
         beta_sum,
         o_sum.transpose(0, 2, 1).reshape(-1, shard_rows).astype(f32),
-        gate_up_sum.transpose(2, 1, 0, 3).reshape(2, shard_rows, -1).astype(f32),
+        jnp.stack([gate_sum, up_sum]).transpose(0, 2, 1, 3).reshape(2, shard_rows, -1).astype(f32),
         down_sum.transpose(0, 2, 1).reshape(-1, shard_rows).astype(f32),
     )
 

time: 742 us -> 609 us (0.82)
  waiting for transfers between devices: 97.2 us -> 0 us
  starting transfers between devices: 37 us -> 0 us
  Pallas kernels: 470 us -> 499 us
  between operations: 23.2 us -> 1.52 us
  matrix products: 48.4 us -> 28.6 us
    ppermute x21 -> x0, waiting for transfers between devices: 96.2 us -> none  [exchanged(): lax.ppermute(part, axis, [(i, (i + by) % count) for i in range(count)])]
    ppermute x21 -> x0, starting transfers between devices: 36.5 us -> none  [exchanged(): lax.ppermute(part, axis, [(i, (i + by) % count) for i in range(count)])]
    pallas_call x1, Pallas kernels: 25.6 us -> 59.7 us  [run_backward(): pl.pallas_call(functools.partial(backward_kernel, heads), out_shape=[jax....]
    pallas_call x4 -> x5, Pallas kernels: 384 us -> 364 us  [the longest x4 343 us: line_call(): pl.pallas_call(kernel, out_shape=[jax.ShapeDtypeStruct(*out) for out in (...]
    pallas_call x1, Pallas kernels: 43.6 us -> 62.2 us  [run_forward(): pl.pallas_call(functools.partial(forward_kernel, heads), out_shape=[jax.S...]
    convert_element_type x1 -> x5, local copies, waits for them, and re-layouts: 0.2 us -> 17.8 us  [the longest x1 4.85 us: local_heads(): jnp.einsum('td,tf->df', normed_two, grad_up, preferred_element_type=f32)]
    dot_general x3 -> x2, matrix products: 26.9 us -> 11.7 us  [the longest x1 7.12 us: local_heads(): jnp.einsum('td,tf->df', normed_two, grad_gate, preferred_element_type=f32)]
    reduce_sum x0 -> x4, other arithmetic: none -> 9.79 us  [summed(): return jnp.sum(came.astype(f32), axis=0).astype(b16)]
  transfers between devices with their start and end apart: 28 -> 0, of which waited for: 17 -> 0; matrix products, arithmetic and copies ran while one was open for 8% -> 0% of each run, Pallas kernels for 45% -> 0%
where the time goes in v4:
time: 609 us; the launch traced here: 598 us
  Pallas kernels  499 us (82%)
  local copies, waits for them, and re-layouts  52.6 us (9%)
  matrix products  28.6 us (5%)
  other arithmetic  16 us (3%)
    pallas_call x4, Pallas kernels, line_call(): pl.pallas_call(kernel, out_shape=[jax.ShapeDtypeStruct(*out) for out in (...  343 us
    pallas_call x1, Pallas kernels, run_forward(): pl.pallas_call(functools.partial(forward_kernel, heads), out_shape=[jax.S...  62.2 us
    pallas_call x1, Pallas kernels, run_backward(): pl.pallas_call(functools.partial(backward_kernel, heads), out_shape=[jax....  59.7 us
    unnamed x76, local copies, waits for them, and re-layouts  22.2 us
    pallas_call x1, Pallas kernels, run_mlp(): pl.pallas_call(mlp_kernel, grid=(row_len // block,), out_shape=[shape] *...  20.4 us
    pallas_call x1, Pallas kernels, run_small_sums(): pl.pallas_call(small_sums_kernel, out_shape=jax.ShapeDtypeStruct(shape, p...  13.4 us

profile of v4, /device:TPU:8, one launch (start us, length us, event | category | flops | bytes accessed | tf_op | source)
XLA Modules:
  0.0 597.8 jit_solution(1514372125891792620)
XLA Ops:
  0.7 0.8 reduce-window.8
  1.5 0.1 convert_reduce_fusion
  1.6 0.2 slice_reduce_fusion.1
  1.8 0.2 slice_reduce_fusion.2
  2.0 0.1 pad_add_fusion
  2.2 0.1 fusion.5
  2.4 1.3 pad.9.beta_ref
  3.7 0.2 copy.91.aux_ref
  3.9 2.5 copy.89
  6.4 1.7 copy.90
  8.1 1.0 slice_bitcast_fusion
  9.1 60.2 %norm_gather.1 = (bf16[4,2,128,2048]{3,2,1,0:T(8,128)(2,1)}, bf16[4,4,3,128,256]{4,3,2,1,0:T(8,128)(2,1)}, bf16[4,4,16,128]{3,2,1,0:T(8,128)(2,1)}) custom-call(bf16[256,2048]{1,0:T(8,128)(2,1)} %bitcast.117, f32[1,2048]{1,0:T(1,128)} %bitcast.149, bf16[3,128,1024]{2,1,0:T(8,128)(2,1)} %weight_ref.1, bf16[4,16,128]{2,1,0:T(8,128)(2,1)} %pad.9.beta_ref), custom_call_target="tpu_custom_call" | custom-call | tf_op jit(solution)/shard_map/norm_gather/pallas_call | solution.py:1338
  69.3 0.9 copy.88
  70.3 62.2 %mixer_forward.1 = (bf16[1024,768]{1,0:T(8,128)(2,1)}, f32[1024,16]{1,0:T(8,128)S(1)}, f32[1024,256]{1,0:T(8,128)}, bf16[1024,256]{1,0:T(8,128)(2,1)S(1)}, f32[2...) custom-call(bf16[1024,2048]{1,0:T(8,128)(2,1)} %bitcast.106, ...), custom_call_target="tpu_custom_call" | custom-call | tf_op jit(solution)/shard_map/mixer_forward/pallas_call | solution.py:791
  132.5 0.9 copy-done.14
  133.4 0.9 copy-done.15
  134.3 0.9 copy-done.16
  135.1 0.8 copy-done.19
  135.9 0.8 copy-done.21
  136.7 107.9 %resid_norm.1 = (f32[128,2048]{1,0:T(8,128)}, bf16[4,2,128,2048]{3,2,1,0:T(8,128)(2,1)}, bf16[4,2,128,2048]{3,2,1,0:T(8,128)(2,1)}, bf16[4,4,128,704]{3,2,1,0:T(...) custom-call(bf16[8,128,256]{2,1,0:T(8,128)(2,1)} %bitcast.101, ...), custom_call_target="tpu_custom_call" | custom-call | tf_op jit(solution)/shard_map/resid_norm/pallas_call | solution.py:1338
  244.7 20.4 %mlp.1 = (bf16[1024,704]{1,0:T(8,128)(2,1)S(1)}, bf16[1024,704]{1,0:T(8,128)(2,1)S(1)}, bf16[1024,704]{1,0:T(8,128)(2,1)S(1)}) custom-call(bf16[1024,2048]{1,0:T(8,128)(2,1)} %bitcast.128, bf16[1024,2048]{1,0:T(8,128)(2,1)} %bitcast.131, bf16[2048,704]{1,0:T(8,128)(2,1)} %bitcast.112, bf16[2048,704]{1,0:T(8,128)(2,1)} %bitcast.114, ...), custom_call_target="tpu_custom_call" | custom-call | tf_op jit(solution)/shard_map/mlp/pallas_call | solution.py:1673
  265.1 4.5 convolution_convert_fusion.3
  269.7 4.8 copy.92
  274.5 7.1 %convolution_convert_fusion.2 = bf16[2048,704]{0,1:T(8,128)(2,1)} fusion(bf16[1024,2048]{1,0:T(8,128)(2,1)} %bitcast.129, bf16[1024,704]{1,0:T(8,128)(2,1)S(1)} %copy-done.4), kind=kOutput, calls=%fused_computation.2 | convolution fusion | flops 2954231808 | bytes 8519680 | tf_op jit(solution)/shard_map/td,tf->df/dot_general | solution.py:1810
  281.6 4.6 convolution_convert_fusion.1
  286.2 4.8 copy.94
  291.0 2.9 copy.93
  293.9 114.0 %grad_resid.1 = (f32[128,2048]{1,0:T(8,128)}, bf16[4,2,128,2048]{3,2,1,0:T(8,128)(2,1)}, f32[1,2048]{1,0:T(1,128)}, bf16[256,2048]{1,0:T(8,128)(2,1)}, bf16[4,4,...) custom-call(bf16[8,128,704]{2,1,0:T(8,128)(2,1)} %bitcast.94, ...), custom_call_target="tpu_custom_call" | custom-call | tf_op jit(solution)/shard_map/grad_resid/pallas_call | solution.py:1338
  407.9 4.5 convolution_convert_fusion.4
  412.4 2.5 reduce_sum.70.down_sum_ref
  414.9 2.5 reduce_sum.71.gate_sum_ref
  417.4 2.5 reduce_sum.72.up_sum_ref
  419.9 1.0 copy-done.20
  421.0 59.7 %mixer_backward.1 = (bf16[1024,768]{1,0:T(8,128)(2,1)}, bf16[1024,16]{1,0:T(8,128)(2,1)S(1)}, f32[4,768]{1,0:T(4,128)S(1)}, f32[1,128]{1,0:T(1,128)S(1)}, bf16[4...) custom-call(bf16[1024,2048]{1,0:T(8,128)(2,1)} %bitcast.127, ...), custom_call_target="tpu_custom_call" | custom-call | tf_op jit(solution)/shard_map/mixer_backward/pallas_call | solution.py:822
  480.6 0.9 copy-done.8
  481.5 0.9 copy-done.10
  482.4 0.9 copy-done.12
  483.3 2.3 reduce_sum.73.o_sum_ref
  485.6 3.0 fusion
  488.6 0.4 copy-done.25
  489.0 4.9 convolution_convert_fusion
  493.9 61.3 %input_grad.1 = (bf16[256,2048]{1,0:T(8,128)(2,1)}, f32[1,2048]{1,0:T(1,128)}, bf16[4,128,768]{2,1,0:T(8,128)(2,1)}, bf16[4,128,256]{2,1,0:T(8,128)(2,1)}) custom-call(bf16[8,128,768]{2,1,0:T(8,128)(2,1)} %bitcast.134, bf16[4,4,3,128,256]{4,3,2,1,0:T(8,128)(2,1)} %get-tuple-element.54.qkv_ref, bf16[8,128,16]{2,1,0:T(8,128)(2,1)} %bitcast.96, ...), custom_call_target="tpu_custom_call" | custom-call | tf_op jit(solution)/shard_map/input_grad/pallas_call | solution.py:1338
  555.2 0.8 constant_dynamic-update-slice_fusion.3
  556.0 0.6 copy-done.31
  556.6 13.4 %small_sums.1 = f32[2,4,96,128]{3,2,1,0:T(8,128)} custom-call(f32[96,128]{1,0:T(8,128)} %copy-done.31), custom_call_target="tpu_custom_call" | custom-call | tf_op jit(solution)/shard_map/small_sums/pallas_call | solution.py:1733
  570.0 1.0 slice_reduce_fusion
  571.0 0.5 slice_bitcast_fusion.4
  571.5 0.6 slice_bitcast_fusion.2
  572.1 0.9 slice.54
  573.0 0.9 dynamic-slice_bitcast_fusion
  574.0 0.6 dynamic-slice_bitcast_fusion.1
  574.7 0.7 reshape.245
  575.4 1.0 convert_bitcast_fusion.2
  576.4 1.0 copy.99
  577.4 0.3 copy.97
  577.7 1.3 copy.98
  578.9 3.0 copy.102
  582.0 1.3 convert_bitcast_fusion.1
  583.2 3.0 copy.101
  586.2 1.9 convert_bitcast_fusion
  588.1 2.4 copy.100
  590.5 2.2 copy.103
  592.7 2.3 copy.113
  595.0 2.3 copy.114
  (74 shorter events, 0.6 us)
Async XLA Ops:
  0.6 1.6 copy-start
  8.1 62.1 %copy-start.17 = (bf16[2816,128]{1,0:T(8,128)(2,1)S(1)}, bf16[2816,128]{1,0:T(8,128)(2,1)}, u32[]{:S(2)}) copy-start(bf16[2816,128]{1,0:T(8,128)(2,1)} %down_ref.1) | copy-start | bytes 2162692
  8.1 62.1 %copy-start.23 = (bf16[1024,128]{1,0:T(8,128)(2,1)S(1)}, bf16[1024,128]{1,0:T(8,128)(2,1)}, u32[]{:S(2)}) copy-start(bf16[1024,128]{1,0:T(8,128)(2,1)} %o_weight_ref.1) | copy-start | bytes 786436
  8.1 62.1 %copy-start.24 = (f32[128]{0:T(128)S(1)}, f32[128]{0:T(128)}, u32[]{:S(2)}) copy-start(f32[128]{0:T(128)} %param.17) | copy-start | bytes 1540
  70.2 62.3 %copy-start.18 = (bf16[2,8,16,128]{3,1,2,0:T(8,128)(2,1)}, bf16[2,8,16,128]{3,1,2,0:T(8,128)(2,1)S(1)}, u32[]{:S(2)}) copy-start(bf16[2,8,16,128]{3,1,2,0:T(8,128)(2,1)S(1)} %copy.106) | copy-start | bytes 196612
  132.5 0.9 copy-start.14
  133.4 0.9 copy-start.15
  134.3 0.9 copy-start.16
  135.1 0.8 copy-start.19
  135.9 0.8 copy-start.21
  244.6 20.4 %copy-start.27 = (bf16[4,2,128,2048]{3,2,1,0:T(8,128)(2,1)S(1)}, bf16[4,2,128,2048]{3,2,1,0:T(8,128)(2,1)}, u32[]{:S(2)}) copy-start(bf16[4,2,128,2048]{3,2,1,0:T(8,128)(2,1)} %get-tuple-element.62) | copy-start | bytes 12582916
  265.1 4.6 copy-start.2
  265.1 4.6 copy-start.3
  265.1 4.6 copy-start.5
  269.6 4.8 copy-start.4
  274.5 7.1 %copy-start.6 = (bf16[1024,704]{1,0:T(8,128)(2,1)S(1)}, bf16[1024,704]{1,0:T(8,128)(2,1)}, u32[]{:S(2)}) copy-start(bf16[1024,704]{1,0:T(8,128)(2,1)} %copy-done.5) | copy-start | bytes 4325380
  274.5 7.1 %copy-start.26 = (bf16[4,2,128,2048]{3,2,1,0:T(8,128)(2,1)S(1)}, bf16[4,2,128,2048]{3,2,1,0:T(8,128)(2,1)}, u32[]{:S(2)}) copy-start(bf16[4,2,128,2048]{3,2,1,0:T(8,128)(2,1)} %get-tuple-element.61) | copy-start | bytes 12582916
  286.2 4.9 copy-start.28
  293.9 114.0 %copy-start.22 = (bf16[1024,256]{1,0:T(8,128)(2,1)S(1)}, bf16[1024,256]{1,0:T(8,128)(2,1)}, u32[]{:S(2)}) copy-start(bf16[1024,256]{1,0:T(8,128)(2,1)} %copy-done.21) | copy-start | bytes 1572868
  419.9 1.0 copy-start.20
  480.6 0.9 copy-start.8
  481.5 0.9 copy-start.10
  482.4 0.9 copy-start.12
  483.3 5.3 copy-start.7
  483.3 5.3 copy-start.29
  485.6 3.4 copy-start.25
  493.9 62.1 %copy-start.32 = (f32[1,2048]{1,0:T(1,128)S(1)}, f32[1,2048]{1,0:T(1,128)}, u32[]{:S(2)}) copy-start(f32[1,2048]{1,0:T(1,128)} %get-tuple-element.88) | copy-start | bytes 24580
  555.1 22.3 %copy-start.30 = (bf16[4,128,768]{2,1,0:T(8,128)(2,1)S(1)}, bf16[4,128,768]{2,1,0:T(8,128)(2,1)}, u32[]{:S(2)}) copy-start(bf16[4,128,768]{2,1,0:T(8,128)(2,1)} %get-tuple-element.90) | copy-start | bytes 2359300
  556.0 0.6 copy-start.31
  577.7 4.3 copy-start.13
  582.0 4.3 copy-start.9
  582.0 4.3 copy-start.11
  590.5 6.8 %copy-start.1 = (f32[3,4,1024]{2,1,0:T(4,128)S(1)}, f32[3,4,1024]{2,1,0:T(4,128)}, u32[]{:S(2)}) copy-start(f32[3,4,1024]{2,1,0:T(4,128)} %param.18) | copy-start | bytes 147460

commit v5 on v4

--- a/solution.py
+++ b/solution.py
@@ -516,27 +516,25 @@
 
     units = down_out.shape[1]
     whole = Exchange(line, rows_of(o_weight_ref, width), o_ref, sems[:4])
+    gates = Exchange(line, lambda seq: gate_ref.at[seq], gate_out, sems[4:8])
     moves = [
-        Exchange(line, lambda seq: gate_ref.at[seq], gate_out, sems[4:6]),
-        Exchange(line, lambda seq: up_ref.at[seq], up_out, sems[6:8]),
-        Exchange(line, rows_of(down_ref, units), down_out, sems[8:10]),
+        Exchange(line, lambda seq: up_ref.at[seq], up_out, sems[8:10]),
+        Exchange(line, rows_of(down_ref, units), down_out, sems[10:12]),
     ]
-    whole.start()
-    own = [
-        pltpu.make_async_copy(whole.source(line.place), o_ref.at[row, line.place], own_sems.at[0])
-    ]
+    own = []
+    for i, move in enumerate((whole, gates)):
+        target = move.target.at[row, line.place]
+        own.append(pltpu.make_async_copy(move.source(line.place), target, own_sems.at[i]))
     for i, move in enumerate(moves):
-        own.append(
-            pltpu.make_async_copy(
-                move.source(line.place), move.target.at[line.place], own_sems.at[i + 1]
-            )
-        )
+        target = move.target.at[line.place]
+        own.append(pltpu.make_async_copy(move.source(line.place), target, own_sems.at[i + 2]))
+    for move in (whole, gates, *moves):
+        move.start()
     for copy in own:
         copy.start()
-    for move in moves:
-        move.start()
-    own[0].wait()
-    whole.share_own()
+    for i, move in enumerate((whole, gates)):
+        own[i].wait()
+        move.share_own()
     window_ref[0:PAD] = jnp.zeros((PAD, 3 * width), jnp.float32)
     state_ref[...] = jnp.zeros_like(state_ref)
 
@@ -590,15 +588,17 @@
         return 0
 
     chunks = n1_ref.shape[0] // CHUNK
-    middle = chunks // 2
-    lax.fori_loop(0, middle, chunk, 0)
+    early, late = chunks // 4, 3 * chunks // 4
+    lax.fori_loop(0, early, chunk, 0)
     for i in range(1, line.count):
         whole.share_came(i)
-    lax.fori_loop(middle, chunks, chunk, 0)
-    for copy in own[1:]:
+    lax.fori_loop(early, late, chunk, 0)
+    for i in range(1, line.count):
+        gates.share_came(i)
+    lax.fori_loop(late, chunks, chunk, 0)
+    for copy in own[2:]:
         copy.wait()
-    whole.finish()
-    for move in moves:
+    for move in (whole, gates, *moves):
         move.finish()
 
 
@@ -616,14 +616,17 @@
     aux_ref,
     docs_ref,
     gain_ref,
-    down_sum_ref,
-    gate_sum_ref,
-    up_sum_ref,
-    o_part_ref,
+    normed_mix_ref,
+    n1_ref,
+    qkv_ref,
+    beta_ref,
+    attn_gain_ref,
+    mlp_grad_ref,
+    sum_ref,
     grad_proj_ref,
     grad_logit_ref,
-    conv_grad_ref,
-    gain_grad_ref,
+    small_ref,
+    qkv_part_ref,
     down_came_ref,
     gate_came_ref,
     up_came_ref,
@@ -632,6 +635,9 @@
     masked_ref,
     state_ref,
     o_rows,
+    o_part_ref,
+    conv_grad_ref,
+    gain_grad_ref,
     *sems,
 ):
     width = heads * DK
@@ -639,11 +645,24 @@
     moves = moves_of(
         Swap,
         "seq",
-        (down_sum_ref, gate_sum_ref, up_sum_ref),
+        [sum_ref.at[m] for m in range(3)],
         (down_came_ref, gate_came_ref, up_came_ref),
         sems[:7],
-    ) + moves_of(Swap, "row", (o_part_ref,), (o_came_ref,), sems[7:])
+    )
     for move in moves:
+        move.start()
+    rows_axis, seqs, shard, _ = o_part_ref.shape
+    span = seqs * shard
+
+    def o_rows_of(r, _):
+        columns = pl.ds(pl.multiple_of(r * span, span), span)
+        part = mul(grad_ref[:, columns], normed_mix_ref[...], (0, 0))
+        o_part_ref[r] = part.astype(jnp.bfloat16).reshape(seqs, shard, -1)
+        return 0
+
+    lax.fori_loop(0, rows_axis, o_rows_of, 0)
+    o_moves = moves_of(Swap, "row", (o_part_ref,), (o_came_ref,), sems[7:])
+    for move in o_moves:
         move.start()
     side_by_side(o_ref, o_rows)
     chunks = grad_ref.shape[0] // CHUNK
@@ -762,7 +781,34 @@
         return 0
 
     lax.fori_loop(0, chunks, chunk, 0)
-    for move in moves:
+
+    def qkv_rows_of(r, _):
+        columns = pl.ds(pl.multiple_of(r * span, span), span)
+        n1 = n1_ref[:, columns]
+        part = mul(n1, grad_proj_ref[...], (0, 0))
+        qkv_part_ref[r] = part.astype(jnp.bfloat16).reshape(seqs, shard, -1)
+        weights = qkv_ref[r]
+        total = 0.0
+        for c in range(3):
+            weight = weights[:, c].reshape(span, width).astype(jnp.float32)
+            total = total + weight * part[:, c * width : (c + 1) * width]
+        total = fine(jnp.ones((8, width), jnp.float32), total, (1, 1))[0:1]
+        beta_part = mul(grad_logit_ref[...], n1, (0, 0))
+        total = total + jnp.sum(
+            beta_part * beta_ref[:, columns].astype(jnp.float32), axis=0, keepdims=True
+        )
+        small_ref[0:1, columns] = total / attn_gain_ref[:, columns]
+        small_ref[2 : 2 + heads, columns] = beta_part[:heads]
+        return 0
+
+    lax.fori_loop(0, rows_axis, qkv_rows_of, 0)
+    small_ref[1:2] = mlp_grad_ref[...]
+    at = 2 + heads
+    for tap in range(KW):
+        lanes = pl.ds((tap % 2) * 3 * width, 3 * width)
+        small_ref[at + tap // 2 : at + tap // 2 + 1, lanes] = conv_grad_ref[tap : tap + 1]
+    small_ref[at : at + 1, 6 * width : 6 * width + DK] = gain_grad_ref[...]
+    for move in moves + o_moves:
         move.finish()
 
 
@@ -783,7 +829,7 @@
         ((heads, chunks, DK, DK), f32),
         ((heads, chunks, CHUNK, DK), f32),
         ((rows_axis, seqs, width, o_weight.shape[1]), jnp.bfloat16),
-        (gate.shape, jnp.bfloat16),
+        ((rows_axis,) + gate.shape, jnp.bfloat16),
         (up.shape, jnp.bfloat16),
         ((seqs, down.shape[0] // seqs, down.shape[1]), jnp.bfloat16),
     )
@@ -798,8 +844,8 @@
             pltpu.VMEM((heads, DK, DK), f32),
             dma_sems(4),
         ]
-        + exchange_sems()
-        + [dma_sems(seqs - 1)] * 6,
+        + exchange_sems() * 2
+        + [dma_sems(seqs - 1)] * 4,
         compiler_params=pltpu.CompilerParams(
             collective_id=5, has_side_effects=True, vmem_limit_bytes=48 * 1024 * 1024
         ),
@@ -807,36 +853,43 @@
     )(n1, qkv, beta, taps, aux, docs, gain, o_weight, gate, up, down)
 
 
-def run_backward(grad, o_full, saved, taps, aux, docs, gain, sums, o_part):
+def run_backward(grad, o_full, saved, taps, aux, docs, gain, extra, sums):
     row_len, heads = grad.shape[0], o_full.shape[2] // DK
+    model_width = grad.shape[1]
+    rows_axis, seqs, _, shard = o_full.shape
+    b16 = jnp.bfloat16
     width, f32 = heads * DK, jnp.float32
     logit = saved[1]
     shapes = (
         ((row_len, 3 * width), jnp.bfloat16),
         (logit.shape, jnp.bfloat16),
-        ((KW, 3 * width), f32),
-        ((1, DK), f32),
-    )
-    far = [pl.BlockSpec(memory_space=pl.ANY)] * (len(sums) + 1)
-    far_shapes = tuple((array.shape, array.dtype) for array in (*sums, o_part))
+        ((4 + heads, model_width), f32),
+        ((rows_axis, seqs, shard, 3 * width), b16),
+    )
+    o_shape = (rows_axis, seqs, shard, width)
+    far = [pl.BlockSpec(memory_space=pl.ANY)]
+    far_shapes = ((sums.shape[1:], b16),) * 3 + ((o_shape, b16),)
     return pl.pallas_call(
         functools.partial(backward_kernel, heads),
         out_shape=[jax.ShapeDtypeStruct(*shape) for shape in shapes + far_shapes],
-        in_specs=in_vmem(12) + far,
-        out_specs=in_vmem(len(shapes)) + far,
+        in_specs=in_vmem(12 + len(extra)) + far,
+        out_specs=in_vmem(len(shapes)) + far * len(far_shapes),
         scratch_shapes=[
             pltpu.VMEM((PAD + CHUNK, 3 * width), f32),
             pltpu.VMEM((KW - 1, CHUNK + PAD, 3 * width), f32),
             pltpu.VMEM((heads, DK, DK), f32),
-            pltpu.VMEM((width, grad.shape[1]), jnp.bfloat16),
+            pltpu.VMEM((width, model_width), b16),
+            pltpu.VMEM(o_shape, b16),
+            pltpu.VMEM((KW, 3 * width), f32),
+            pltpu.VMEM((1, DK), f32),
         ]
-        + pair_sems("seq", len(sums))
+        + pair_sems("seq", 3)
         + pair_sems("row", 1),
         compiler_params=pltpu.CompilerParams(
             collective_id=6, has_side_effects=True, vmem_limit_bytes=48 * 1024 * 1024
         ),
         name="mixer_backward",
-    )(grad, o_full, *saved, taps, aux, docs, gain, *sums, o_part)
+    )(grad, o_full, *saved, taps, aux, docs, gain, *extra, sums)
 
 
 def row_aux(docs):
@@ -996,9 +1049,10 @@
     def along(self, kind, seq, part):
         line, span = self.line, self.span(part)
         way = {"right": 0, "left": 1}[kind]
+        slot = seq if way == 0 else jnp.where(seq == line.place - 1, line.count, seq)
         return remote(
             self.blocks.at[seq, line.core, span],
-            self.came.at[way, seq, span],
+            self.came.at[slot, span],
             self.sems.at[2, seq, part],
             self.sems.at[3 + way, seq, part],
             line.right if way == 0 else line.left,
@@ -1031,7 +1085,10 @@
             return 0
 
         lax.fori_loop(0, width // tile, columns, 0)
-        for k in range(seqs):
+        self.offer(part)
+
+    def offer(self, part):
+        for k in range(self.blocks.shape[0]):
             self.over(self.target(k), part).start()
 
     def pass_on(self, kind, seq, part):
@@ -1051,7 +1108,7 @@
         def _():
             self.along(kind, seq, part).wait_recv()
             self.blocks[seq, line.core, span] = (
-                total + self.came[way, seq, span].astype(f32)
+                total + self.came[seq, span].astype(f32)
             ).astype(jnp.bfloat16)
 
         self.along(kind, seq, part).start()
@@ -1060,6 +1117,9 @@
         line = self.line
         return jnp.where(line.place < line.count // 2, line.count - 1 - k, k)
 
+    def edge(self):
+        return (self.line.place == 0) | (self.line.place == self.line.count - 1)
+
     def near(self, k, part):
         line = self.line
         low = line.place < line.count // 2
@@ -1083,6 +1143,23 @@
         @pl.when(jnp.logical_not(low) & (line.count - 1 - k > line.place))
         def _():
             self.pass_on("right", line.count - 1 - k, part)
+
+    def start_edges(self, part):
+        @pl.when(self.edge())
+        def _():
+            for k in range(self.line.count - 1):
+                self.near(k, part)
+
+    def relay(self, k, part):
+        @pl.when(jnp.logical_not(self.edge()))
+        def _():
+            self.near(k, part)
+
+    def relay_back(self, part):
+        @pl.when(jnp.logical_not(self.edge()))
+        def _():
+            for k in range(self.line.count - 1):
+                self.far(k, part)
 
     def wait_own(self, part):
         line = self.line
@@ -1102,8 +1179,8 @@
         f32 = jnp.float32
         total = self.blocks[line.place, line.core, rows].astype(f32)
         total = total + self.across[line.place, rows].astype(f32)
-        from_left = self.came[0, line.place, rows].astype(f32)
-        from_right = self.came[1, line.place, rows].astype(f32)
+        from_left = self.came[line.place, rows].astype(f32)
+        from_right = self.came[line.count, rows].astype(f32)
         total = total + jnp.where(line.place > 0, from_left, 0.0)
         return total + jnp.where(line.place < line.count - 1, from_right, 0.0)
 
@@ -1226,6 +1303,81 @@
         self.own.wait()
 
 
+class RowSum:
+    def __init__(self, blocks, halves, came, sems):
+        self.blocks, self.halves, self.came = blocks, halves, came
+        self.row = lax.axis_index("row")
+        even_x, even_y = lax.rem(self.row, 2) == 0, self.row < 2
+        x_step, y_step = jnp.where(even_x, 1, -1), jnp.where(even_y, 2, -2)
+        self.near = (self.row + x_step, self.row + y_step)
+        self.far = self.row + x_step + y_step
+        self.half = blocks.shape[2] // 2
+        self.send_half, self.recv_half, self.send, self.recv = sems
+
+    def rows(self, i):
+        return pl.ds(i * self.half, self.half)
+
+    def half_copy(self, i, m):
+        return remote(
+            self.blocks.at[self.far, m, self.rows(i)],
+            self.halves.at[i, m],
+            self.send_half.at[i, m],
+            self.recv_half.at[i, m],
+            {"row": self.near[i]},
+        )
+
+    def copy(self, i, j, m):
+        return remote(
+            self.blocks.at[self.near[i], m, self.rows(j)],
+            self.came.at[i, m, self.rows(j)],
+            self.send.at[i, j, m],
+            self.recv.at[i, j, m],
+            {"row": self.near[i]},
+        )
+
+    def start_far(self, m):
+        for i in range(2):
+            self.half_copy(i, m).start()
+
+    def start_near(self, i, m):
+        self.copy(i, i, m).start()
+
+    def add_half(self, i, m):
+        j = 1 - i
+        self.half_copy(j, m).wait_recv()
+        rows = self.rows(j)
+        total = self.blocks[self.near[i], m, rows].astype(jnp.float32)
+        total = total + self.halves[j, m].astype(jnp.float32)
+        self.blocks[self.near[i], m, rows] = total.astype(jnp.bfloat16)
+        self.copy(i, j, m).start()
+
+    def total(self, m):
+        for i in range(2):
+            for j in range(2):
+                self.copy(i, j, m).wait_recv()
+        total = self.blocks[self.row, m].astype(jnp.float32)
+        for i in range(2):
+            total = total + self.came[i, m].astype(jnp.float32)
+        return total
+
+    def finish(self):
+        for m in range(self.blocks.shape[1]):
+            for i in range(2):
+                self.half_copy(i, m).wait_send()
+                for j in range(2):
+                    self.copy(i, j, m).wait_send()
+
+
+def row_sum_scratch(shape):
+    b16 = jnp.bfloat16
+    _, count, rows, width = shape
+    return [
+        pltpu.VMEM(shape, b16),
+        pltpu.VMEM((2, count, rows // 2, width), b16),
+        pltpu.VMEM((2, count, rows, width), b16),
+    ], [dma_sems(2, count), dma_sems(2, count), dma_sems(2, 2, count), dma_sems(2, 2, count)]
+
+
 def pair_sems(axis, count):
     return [dma_sems(lax.axis_size(axis) - 1)] * (2 * count) + [dma_sems(count)]
 
@@ -1269,8 +1421,8 @@
 
 
 def resid_kernel(
-    mix_ref, o_ref, x_ref, g_ref, gain_ref, gate_ref, up_ref, down_ref,
-    resid_ref, n2_ref, g_full_ref, gate_full_ref, up_full_ref, down_full_ref,
+    mix_ref, o_ref, x_ref, g_ref, gain_ref, up_ref, down_ref,
+    resid_ref, n2_ref, g_full_ref, up_full_ref, down_full_ref,
     blocks, came, across, o_rows, sum_sems, n2_sems, g_sems, *sems,
 ):
     line = Line()
@@ -1278,8 +1430,8 @@
     shares = moves_of(
         Share,
         "row",
-        (gate_ref, up_ref, down_ref),
-        (gate_full_ref, up_full_ref, down_full_ref),
+        (up_ref, down_ref),
+        (up_full_ref, down_full_ref),
         sems,
     )
     for share in shares:
@@ -1354,7 +1506,7 @@
     b16 = jnp.bfloat16
     return [
         pltpu.VMEM((seqs, cores, rows, width), b16),
-        pltpu.VMEM((2, seqs, rows, width), b16),
+        pltpu.VMEM((seqs + 1, rows, width), b16),
         pltpu.VMEM((seqs, rows, width), b16),
     ]
 
@@ -1383,44 +1535,92 @@
 
 
 def grad_resid_kernel(
-    grad_gate_ref, grad_up_ref, gate_ref, up_ref, hidden_ref, down_ref, resid_ref, g_ref, gain_ref,
-    down_part_ref, gate_part_ref, up_part_ref,
+    grad_gate_ref, grad_up_ref, hidden_ref, down_ref, resid_ref, g_ref, gain_ref,
+    gate_ref, up_ref, n2_ref, g_full_ref,
     grad_resid_ref, grad_attn_ref, gain_grad_ref, result_ref,
-    down_came_ref, gate_came_ref, up_came_ref,
-    blocks, came, across, out_blocks, out_came, out_across, down_rows,
-    sum_sems, out_sems, attn_sems, swap_sems, *sems,
+    sum_ref,
+    blocks, came, across, out_blocks, out_came, out_across, weights, tokens, parts, halves, parts_came,
+    sum_sems, out_sems, attn_sems, swap_sems, weight_sems, token_sems, own_sems, *sems,
 ):
     line = Line()
     greet(line_partners() + along_axis("row"))
-    parts = moves_of(
-        Swap,
-        "row",
-        (down_part_ref, gate_part_ref, up_part_ref),
-        (down_came_ref, gate_came_ref, up_came_ref),
-        sems,
-    )
-    for move in parts:
-        move.start()
     rows = resid_ref.shape[0]
     total = Scatter(line, blocks, came, across, sum_sems)
     result = Scatter(line, out_blocks, out_came, out_across, out_sems)
     attn = Gather(line, grad_attn_ref, attn_sems)
-    units = gate_ref.shape[1]
+    sums = RowSum(parts, halves, parts_came, sems)
+    units = hidden_ref.shape[2]
+    tile = weights.shape[2]
+    tiles = blocks.shape[3] // tile
+    steps = total.parts * tiles
+
+    def weight_copies(step):
+        slot = step % 2
+        span = pl.ds((step % tiles) * tile, tile)
+        return [
+            pltpu.make_async_copy(ref.at[span], weights.at[slot, i], weight_sems.at[slot, i])
+            for i, ref in enumerate((gate_ref, up_ref))
+        ]
+
+    orders = (sums.far, sums.near[0], sums.near[1], sums.row)
+    block_width = tokens.shape[3]
+
+    def token_copies(step):
+        slot = step % 2
+        columns = pl.ds(pl.multiple_of(orders[step] * block_width, block_width), block_width)
+        return [
+            pltpu.make_async_copy(ref.at[:, columns], tokens.at[slot, i], token_sems.at[slot, i])
+            for i, ref in enumerate((g_full_ref, n2_ref))
+        ]
+
+    for copy in weight_copies(0) + token_copies(0):
+        copy.start()
+
+    def product(part):
+        span = total.span(part)
+        left_gate = grad_gate_ref[:, span].reshape(-1, units)
+        left_up = grad_up_ref[:, span].reshape(-1, units)
+        for t in range(tiles):
+            step = part * tiles + t
+            if step + 1 < steps:
+                for copy in weight_copies(step + 1):
+                    copy.start()
+            for copy in weight_copies(step):
+                copy.wait()
+            slot = step % 2
+            out = mul(left_gate, weights[slot, 0], (1, 1)) + mul(left_up, weights[slot, 1], (1, 1))
+            out = out.astype(jnp.bfloat16).reshape(blocks.shape[:2] + (total.rows, tile))
+            blocks[:, :, span, t * tile : (t + 1) * tile] = out
+        total.offer(part)
+        total.start_edges(part)
+
+    def weight_grads(step):
+        if step + 1 < len(orders):
+            for copy in token_copies(step + 1):
+                copy.start()
+        for copy in token_copies(step):
+            copy.wait()
+        slot, to = step % 2, orders[step]
+        for m, (i, ref) in enumerate(((0, hidden_ref), (1, grad_gate_ref), (1, grad_up_ref))):
+            part = mul(tokens[slot, i], ref[...].reshape(-1, units), (0, 0))
+            parts[to, m] = part.astype(jnp.bfloat16)
+            if step == 0:
+                sums.start_far(m)
+            elif step < 3:
+                sums.start_near(step - 1, m)
+
     for part in range(total.parts):
-        left_up = grad_up_ref[:, total.span(part)].reshape(-1, units)
-
-        def right_tile(left, t, columns, left_up=left_up):
-            return mul(left, gate_ref[columns], (1, 1)) + mul(left_up, up_ref[columns], (1, 1))
-
-        total.product(grad_gate_ref, None, part, right_tile=right_tile)
-    side_by_side(down_ref, down_rows)
-    total.nears(0)
-    for part in range(result.parts):
-        result.product(hidden_ref, down_rows, part, order=0)
-    for k in range(1, line.count - 1):
-        total.nears(k)
-    for k in range(line.count - 1):
-        total.fars(k)
+        product(part)
+    weight_grads(0)
+    total.relay(0, 0)
+    total.relay(1, 0)
+    weight_grads(1)
+    total.relay_back(0)
+    weight_grads(2)
+    total.relay(0, 1)
+    total.relay(1, 1)
+    weight_grads(3)
+    total.relay_back(1)
     gain_grad_ref[...] = jnp.zeros_like(gain_grad_ref)
 
     def back(span):
@@ -1439,6 +1639,11 @@
         total.wait_own(part)
         over_rows(total, part, back)
         attn.phase(0, part)
+    for part in range(result.parts):
+        result.product(hidden_ref, down_ref, part, order=0)
+    for m in range(parts.shape[1]):
+        for i in range(2):
+            sums.add_half(i, m)
     for k in range(1, line.count):
         attn.phases(k)
         result.nears(k - 1)
@@ -1454,12 +1659,20 @@
         over_rows(result, part, finish)
     swap = own_swap(line, result_ref, rows, swap_sems)
     swap.start()
+    own = []
+    for m in range(parts.shape[1]):
+        parts[sums.row, m] = sums.total(m).astype(jnp.bfloat16)
+        own.append(
+            pltpu.make_async_copy(parts.at[sums.row, m], sum_ref.at[m], own_sems.at[m])
+        )
+        own[m].start()
     total.finish()
     result.finish()
     attn.finish()
     swap.wait()
-    for move in parts:
-        move.finish()
+    sums.finish()
+    for copy in own:
+        copy.wait()
 
 
 def own_swap(line, ref, rows, sems):
@@ -1467,43 +1680,59 @@
     return remote(own, own, sems.at[0], sems.at[1], line.across)
 
 
-def run_grad_resid(grad_gate, grad_up, gate, up, hidden, down, resid, g, gain, parts):
+def run_grad_resid(grad_gate, grad_up, gate, up, hidden, down, resid, g, gain, n2, g_full):
     seqs, cores, (piece, width) = lax.axis_size("seq"), lax.axis_size("tp"), g.shape
+    rows_axis = lax.axis_size("row")
     rows, b16, f32 = piece // cores, jnp.bfloat16, jnp.float32
+    units, span = gate.shape[1], width // rows_axis
     outs = (
         ((rows, width), f32),
         ((seqs, cores, rows, width), b16),
         ((1, width), f32),
         ((piece, width), b16),
     )
+    sum_buffers, sum_sems = row_sum_scratch((rows_axis, 3, span, units))
     scratch = scatter_scratch(seqs, cores, rows, width) * 2
-    scratch = scratch + [pltpu.VMEM((down.shape[2], width), b16)]
-    scratch = scratch + [dma_sems(5, seqs, PARTS)] * 3 + [dma_sems(2)]
-    scratch = scratch + pair_sems("row", len(parts))
+    scratch = scratch + [
+        pltpu.VMEM((2, 2, span, units), b16),
+        pltpu.VMEM((2, 2, n2.shape[0], span), b16),
+    ]
+    scratch = scratch + sum_buffers + [dma_sems(5, seqs, PARTS)] * 3
+    scratch = scratch + [dma_sems(2), dma_sems(2, 2), dma_sems(2, 2), dma_sems(3)] + sum_sems
     grad_gate, grad_up, hidden = (
         array.reshape(seqs * cores, rows, -1) for array in (grad_gate, grad_up, hidden)
     )
-    grad_resid, grad_attn, gain_grad, result, *came = line_call(
+    grad_resid, grad_attn, gain_grad, result, sums = line_call(
         grad_resid_kernel, 2, "grad_resid", outs, scratch,
-        (grad_gate, grad_up, gate, up, hidden, down, resid, g, gain),
-        far_args=parts,
-        far_outs=[(part.shape, b16) for part in parts],
-    )
-    return grad_resid, grad_attn.reshape(-1, width), gain_grad, result, came
+        (grad_gate, grad_up, hidden, down, resid, g, gain),
+        limit=60,
+        far_args=(gate, up, n2, g_full),
+        far_outs=(((3, span, units), b16),),
+    )
+    return grad_resid, grad_attn.reshape(-1, width), gain_grad, result, sums
 
 
 def input_grad_kernel(
     grad_proj_ref, qkv_ref, grad_logit_ref, beta_ref, x_ref, grad_resid_ref, gain_ref, qkv_part_ref,
-    o_sum_ref,
-    input_grad_ref, gain_grad_ref, qkv_came_ref,
+    small_ref, o_sum_ref,
+    input_grad_ref, qkv_came_ref, small_all_ref,
     o_came_ref,
-    blocks, came, across, qkv_rows, qkv_sum, sum_sems, swap_sems, *sems,
+    blocks, came, across, qkv_rows, qkv_sum, small_rows, sum_sems, swap_sems, *sems,
 ):
     line = Line()
     greet(along_axis("seq") + along_axis("row") + along_axis("tp"))
     (o_move,) = moves_of(Swap, "seq", (o_sum_ref,), (o_came_ref,), sems[:3])
     (rows_move,) = moves_of(Swap, "row", (qkv_part_ref,), (qkv_rows,), sems[3:6])
     (qkv_move,) = moves_of(Swap, "seq", (qkv_sum,), (qkv_came_ref,), sems[6:9])
+    (small_row,) = moves_of(Share, "row", (small_ref,), (small_rows,), sems[9:12])
+    own_small = small_all_ref.at[line.core, line.place]
+    small_seq = [
+        remote(own_small, own_small, sems[12].at[i], sems[13].at[i], {"seq": other})
+        for i, other in enumerate(around("seq"))
+    ]
+    core_small = small_all_ref.at[line.core]
+    small_core = remote(core_small, core_small, sems[14].at[0], sems[14].at[1], line.across)
+    small_row.start()
     rows_move.start()
     o_move.start()
     rows = grad_resid_ref.shape[0]
@@ -1525,8 +1754,18 @@
 
         tile = qkv_ref.shape[1] * qkv_ref.shape[3]
         total.product(grad_proj_ref, None, part, tile=tile, right_tile=right_tile)
+    small_row.finish()
+    small = small_rows[0]
+    for i in range(1, small_rows.shape[0]):
+        small = small + small_rows[i]
+    small_all_ref[line.core, line.place] = small
+    for copy in small_seq:
+        copy.start()
     for k in range(line.count - 1):
         total.nears(k)
+    for copy in small_seq:
+        copy.wait()
+    small_core.start()
     for k in range(line.count - 1):
         total.fars(k)
     rows_move.finish()
@@ -1536,14 +1775,12 @@
             piece = piece + qkv_rows[j, i].astype(jnp.float32)
         qkv_sum[i] = piece.astype(jnp.bfloat16)
     qkv_move.start()
-    gain_grad_ref[...] = jnp.zeros_like(gain_grad_ref)
 
     def back(span):
         own_span = pl.ds(pl.multiple_of(line.core * rows + span.start, STEP), STEP)
         x = x_ref[own_span].astype(jnp.float32)
         grad_one = total.own_rows(span)
         scale = norm_scale(x)
-        gain_grad_ref[...] += jnp.sum(grad_one * x * scale, axis=0, keepdims=True)
         input_grad_ref[own_span] = (
             grad_resid_ref[span] + norm_back(x, scale, gain_ref[...], grad_one)
         ).astype(jnp.bfloat16)
@@ -1555,23 +1792,30 @@
     swap.start()
     total.finish()
     swap.wait()
+    small_core.wait()
     o_move.finish()
     qkv_move.finish()
 
 
-def run_input_grad(grad_proj, qkv, grad_logit, beta, x, grad_resid, gain, qkv_part, o_sum):
+def run_input_grad(grad_proj, qkv, grad_logit, beta, x, grad_resid, gain, qkv_part, small, o_sum):
     seqs, cores, (piece, width) = lax.axis_size("seq"), lax.axis_size("tp"), x.shape
     rows, b16, f32 = piece // cores, jnp.bfloat16, jnp.float32
-    outs = (((piece, width), b16), ((1, width), f32), (qkv_part.shape[1:], b16))
+    outs = (
+        ((piece, width), b16),
+        (qkv_part.shape[1:], b16),
+        ((cores, seqs) + small.shape, f32),
+    )
     scratch = scatter_scratch(seqs, cores, rows, width)
     scratch = scratch + [pltpu.VMEM(qkv_part.shape, b16), pltpu.VMEM(qkv_part.shape[1:], b16)]
+    scratch = scratch + [pltpu.VMEM((lax.axis_size("row"),) + small.shape, f32)]
     scratch = scratch + [dma_sems(5, seqs, PARTS), dma_sems(2)]
     scratch = scratch + pair_sems("seq", 1) + pair_sems("row", 1) + pair_sems("seq", 1)
+    scratch = scratch + pair_sems("row", 1) + [dma_sems(seqs - 1)] * 2 + [dma_sems(2)]
     grad_proj = grad_proj.reshape(seqs * cores, rows, -1)
     grad_logit = grad_logit.reshape(seqs * cores, rows, -1)
     return line_call(
         input_grad_kernel, 3, "input_grad", outs, scratch,
-        (grad_proj, qkv, grad_logit, beta, x, grad_resid, gain, qkv_part),
+        (grad_proj, qkv, grad_logit, beta, x, grad_resid, gain, qkv_part, small),
         far_args=(o_sum,),
         far_outs=((o_sum.shape, b16),),
     )
@@ -1663,7 +1907,7 @@
     grad_gate_ref[...] = (grad_hidden * up * sig * (1.0 + gate * (1.0 - sig))).astype(jnp.bfloat16)
 
 
-def run_mlp(n2, g, gate, up, down, block=128):
+def run_mlp(n2, g, gate, up, down, block=256):
     row_len, width = n2.shape
     units = gate.shape[1]
     tokens = pl.BlockSpec((block, width), lambda i: (i, 0))
@@ -1673,81 +1917,78 @@
     return pl.pallas_call(
         mlp_kernel,
         grid=(row_len // block,),
-        out_shape=[shape] * 3,
+        out_shape=[shape] * 3 + [jax.ShapeDtypeStruct((units, width), jnp.bfloat16)],
         in_specs=[tokens, tokens, whole, whole, whole],
-        out_specs=[out] * 3,
-        scratch_shapes=[pltpu.VMEM((units, width), jnp.bfloat16)],
+        out_specs=[out] * 3 + [whole],
         compiler_params=pltpu.CompilerParams(vmem_limit_bytes=48 * 1024 * 1024),
         name="mlp",
     )(n2, g, gate, up, down)
 
 
-def small_sums_kernel(
-    part_ref, out_ref, rows_ref, all_ref, send_row, recv_row, send_seq, recv_seq, send_tp, recv_tp
+def finish_kernel(
+    small_ref, qkv_ref, o_ref, gate_ref, up_ref, down_ref,
+    attn_gain_ref, mlp_gain_ref, out_gain_ref, conv_ref, qkv_out, o_out, gate_up_out, down_out,
 ):
-    row, seq, tp = (lax.axis_index(axis) for axis in ("row", "seq", "tp"))
-    row_others, seq_others, tp_others = around("row"), around("seq"), around("tp")
-    greet(
-        [({"row": other}, other >= 0) for other in row_others]
-        + [({"seq": other}, other >= 0) for other in seq_others]
-        + [({"tp": other}, other >= 0) for other in tp_others]
-    )
-    rows_ref[row] = part_ref[...]
-    copies = [
-        remote(part_ref, rows_ref.at[row], send_row.at[i], recv_row.at[i], {"row": other})
-        for i, other in enumerate(row_others)
-    ]
-    for copy in copies:
-        copy.start()
-    for copy in copies:
-        copy.wait()
-    total = rows_ref[0]
-    for i in range(1, rows_ref.shape[0]):
-        total = total + rows_ref[i]
-    all_ref[tp, seq] = total
-    copies = [
-        remote(
-            all_ref.at[tp, seq], all_ref.at[tp, seq], send_seq.at[i], recv_seq.at[i], {"seq": other}
-        )
-        for i, other in enumerate(seq_others)
-    ]
-    for copy in copies:
-        copy.start()
-    for copy in copies:
-        copy.wait()
-    copies = [
-        remote(all_ref.at[tp], all_ref.at[tp], send_tp.at[i], recv_tp.at[i], {"tp": other})
-        for i, other in enumerate(tp_others)
-    ]
-    for copy in copies:
-        copy.start()
-    for copy in copies:
-        copy.wait()
-    out_ref[...] = all_ref[...]
-
-
-def run_small_sums(part):
-    rows, seqs, tps = (lax.axis_size(axis) for axis in ("row", "seq", "tp"))
-    dma = pltpu.SemaphoreType.DMA
-    shape = (tps, seqs) + part.shape
+    f32 = jnp.float32
+    cores, seqs, _, _ = small_ref.shape
+    _, shard, width3 = qkv_ref.shape
+    width, units = width3 // 3, gate_ref.shape[2]
+    at = 2 + width // DK
+    for ref, rows, lanes in (
+        (attn_gain_ref, slice(0, 1), slice(None)),
+        (mlp_gain_ref, slice(1, 2), slice(None)),
+        (out_gain_ref, slice(at, at + 1), slice(2 * width3, 2 * width3 + DK)),
+    ):
+        total = small_ref[0, 0, rows, lanes]
+        for i in range(1, cores * seqs):
+            total = total + small_ref[i // seqs, i % seqs, rows, lanes]
+        ref[...] = total
+    down = lax.broadcasted_iota(jnp.int32, (shard, shard), 0)
+    along = lax.broadcasted_iota(jnp.int32, (shard, shard), 1)
+    unit = jnp.where(down == along, 1.0, 0.0).astype(jnp.bfloat16)
+    for core in range(cores):
+        for seq in range(seqs):
+            for c in range(3):
+                for tap in range(KW):
+                    row, lane = at + tap // 2, (tap % 2) * width3 + c * width
+                    to = (core * seqs + seq) * width
+                    conv_ref[c, tap : tap + 1, to : to + width] = small_ref[
+                        core, seq, row : row + 1, lane : lane + width
+                    ]
+    for seq in range(seqs):
+        for c in range(3):
+            qkv_out[c, :, seq * width : (seq + 1) * width] = qkv_ref[
+                seq, :, c * width : (c + 1) * width
+            ].astype(f32)
+        o_out[seq * width : (seq + 1) * width] = mul(o_ref[seq], unit, (0, 0))
+        down_out[seq * units : (seq + 1) * units] = mul(down_ref[seq], unit, (0, 0))
+    for i, ref in enumerate((gate_ref, up_ref)):
+        gate_up_out[i] = jnp.concatenate([ref[seq].astype(f32) for seq in range(seqs)], axis=1)
+
+
+def run_finish(small, qkv, o, gate, up, down):
+    f32 = jnp.float32
+    cores, seqs, _, model_width = small.shape
+    _, shard, width3 = qkv.shape
+    units = gate.shape[2]
+    shapes = (
+        (1, model_width),
+        (1, model_width),
+        (1, DK),
+        (3, KW, model_width),
+        (3, shard, seqs * width3 // 3),
+        (seqs * width3 // 3, shard),
+        (2, shard, seqs * units),
+        (seqs * units, shard),
+    )
     return pl.pallas_call(
-        small_sums_kernel,
-        out_shape=jax.ShapeDtypeStruct(shape, part.dtype),
-        in_specs=in_vmem(1),
-        out_specs=pl.BlockSpec(memory_space=pltpu.VMEM),
-        scratch_shapes=[
-            pltpu.VMEM((rows,) + part.shape, part.dtype),
-            pltpu.VMEM(shape, part.dtype),
-            dma((rows - 1,)),
-            dma((rows - 1,)),
-            dma((seqs - 1,)),
-            dma((seqs - 1,)),
-            dma((tps - 1,)),
-            dma((tps - 1,)),
-        ],
-        compiler_params=pltpu.CompilerParams(collective_id=0, has_side_effects=True),
-        name="small_sums",
-    )(part)
+        finish_kernel,
+        out_shape=[jax.ShapeDtypeStruct(shape, f32) for shape in shapes],
+        in_specs=in_vmem(6),
+        out_specs=in_vmem(len(shapes)),
+        compiler_params=pltpu.CompilerParams(vmem_limit_bytes=48 * 1024 * 1024),
+        name="finish",
+    )(small, qkv, o, gate, up, down)
 
 
 def local_heads(
@@ -1769,8 +2010,7 @@
     piece, core = lax.axis_index("seq"), lax.axis_index("tp")
     row_len = pieces * tok_rows
     shard_rows = qkv_weight.shape[1]
-    half_width = qkv_weight.shape[2]
-    width = half_width // pieces
+    width = qkv_weight.shape[2] // pieces
     heads = width // DK
     units = gate_up_weight.shape[2] // pieces
     f32, b16 = jnp.float32, jnp.bfloat16
@@ -1795,36 +2035,28 @@
 
     (
         proj, logit, mixed, normed_mix, inverse, states, written,
-        o_full, gate_came, up_came, down_came,
+        o_full, gate_full, up_came, down_came,
     ) = run_forward(
         normed_one, qkv_full, beta_full, taps, aux, doc_rows, gain_row,
         o_weight, gate_up_parts[0], gate_up_parts[1], down_weight,
     )
-    resid, normed_two, g_full, (gate_full, up_full, down_full) = run_resid(
-        normed_mix, o_full, x_piece, g_piece, mlp_gain[None], (gate_came, up_came, down_came)
+    resid, normed_two, g_full, (up_full, down_full) = run_resid(
+        normed_mix, o_full, x_piece, g_piece, mlp_gain[None], (up_came, down_came)
     )
     gate_full = gate_full.reshape(model_width, units)
     up_full = up_full.reshape(model_width, units)
-    hidden, grad_gate, grad_up = run_mlp(normed_two, g_full, gate_full, up_full, down_full)
-    down_part = jnp.einsum("td,tf->df", g_full, hidden, preferred_element_type=f32).astype(b16)
-    gate_part = jnp.einsum("td,tf->df", normed_two, grad_gate, preferred_element_type=f32).astype(b16)
-    up_part = jnp.einsum("td,tf->df", normed_two, grad_up, preferred_element_type=f32).astype(b16)
-    rows_axis = lax.axis_size("row")
-
-    def by_row(part):
-        return part.reshape(rows_axis, pieces, shard_rows, -1)
+    hidden, grad_gate, grad_up, down_rows = run_mlp(
+        normed_two, g_full, gate_full, up_full, down_full
+    )
 
     def summed(came):
         return jnp.sum(came.astype(f32), axis=0).astype(b16)
 
-    grad_resid, grad_attn, mlp_gain_part, result, came = run_grad_resid(
-        grad_gate, grad_up, gate_full, up_full, hidden, down_full, resid, g_piece, mlp_gain[None],
-        (by_row(down_part), by_row(gate_part), by_row(up_part)),
-    )
-    o_part = jnp.einsum("td,te->de", grad_attn, normed_mix, preferred_element_type=f32)
-    (
-        grad_proj, grad_logit, conv_part, out_gain_part, down_sum, gate_sum, up_sum, o_came,
-    ) = run_backward(
+    grad_resid, grad_attn, mlp_gain_part, result, sums = run_grad_resid(
+        grad_gate, grad_up, gate_full, up_full, hidden, down_rows, resid, g_piece, mlp_gain[None],
+        normed_two, g_full,
+    )
+    grad_proj, grad_logit, small, qkv_part, down_sum, gate_sum, up_sum, o_came = run_backward(
         grad_attn,
         o_full,
         (proj, logit, mixed, inverse, states, written),
@@ -1832,53 +2064,35 @@
         aux,
         doc_rows,
         gain_row,
-        [summed(array) for array in came],
-        by_row(o_part.astype(b16)),
-    )
-    qkv_part = jnp.einsum("td,te->de", normed_one, grad_proj, preferred_element_type=f32)
-    input_grad, attn_gain_part, qkv_sum, o_sum = run_input_grad(
+        (normed_mix, normed_one, qkv_full, beta_full, attn_gain[None], mlp_gain_part),
+        sums.reshape(3, pieces, shard_rows, units),
+    )
+    input_grad, qkv_sum, small, o_sum = run_input_grad(
         grad_proj, qkv_full, grad_logit, beta_full, x_piece, grad_resid, attn_gain[None],
-        by_row(qkv_part.astype(b16)), summed(o_came),
-    )
-    beta_part = jnp.einsum("td,th->hd", normed_one, grad_logit, preferred_element_type=f32)
-    packed = jnp.concatenate(
-        [
-            conv_part.reshape(-1, 128),
-            attn_gain_part.reshape(-1, 128),
-            mlp_gain_part.reshape(-1, 128),
-            beta_part[:heads].reshape(-1, 128),
-            jnp.pad(out_gain_part, ((0, 7), (0, 0))),
-        ],
-        axis=0,
-    )
-    small = run_small_sums(packed)
-    at = KW * 3 * width // 128
-    span = model_width // 128
-    conv_grad = small[:, :, :at].reshape(cores, pieces, KW, 3, width)
-    conv_grad = conv_grad.transpose(3, 2, 0, 1, 4).reshape(3, KW, model_width)
-    sums = jnp.sum(small[:, :, at:], axis=(0, 1))
-    attn_gain_grad = sums[:span].reshape(-1)
-    mlp_gain_grad = sums[span : 2 * span].reshape(-1)
-    out_gain_grad = sums[(2 + heads) * span]
-    beta_sum = lax.dynamic_index_in_dim(small, core, 0, keepdims=False)
-    beta_sum = beta_sum[:, at + 2 * span : at + (2 + heads) * span]
-    beta_sum = beta_sum.reshape(pieces * heads, model_width)
+        qkv_part, small, summed(o_came),
+    )
+    attn_gain_grad, mlp_gain_grad, out_gain_grad, conv_grad, qkv_grad, o_grad, gate_up_grad, down_grad = (
+        run_finish(small, qkv_sum, o_sum, gate_sum, up_sum, down_sum)
+    )
+    beta_sum = lax.dynamic_index_in_dim(small[:, :, 2 : 2 + heads], core, 0, keepdims=False)
     beta_sum = lax.dynamic_slice_in_dim(
-        beta_sum, (lax.axis_index("row") * pieces + piece) * shard_rows, shard_rows, axis=1
+        beta_sum.reshape(pieces * heads, model_width),
+        (lax.axis_index("row") * pieces + piece) * shard_rows,
+        shard_rows,
+        axis=1,
     ).T
-    qkv_sum = qkv_sum.reshape(pieces, shard_rows, 3, width)
     return (
         result[None],
         input_grad[None],
-        attn_gain_grad,
-        mlp_gain_grad,
-        out_gain_grad,
+        attn_gain_grad[0],
+        mlp_gain_grad[0],
+        out_gain_grad[0],
         conv_grad,
-        qkv_sum.transpose(2, 1, 0, 3).reshape(3, shard_rows, -1).astype(f32),
+        qkv_grad,
         beta_sum,
-        o_sum.transpose(0, 2, 1).reshape(-1, shard_rows).astype(f32),
-        jnp.stack([gate_sum, up_sum]).transpose(0, 2, 1, 3).reshape(2, shard_rows, -1).astype(f32),
-        down_sum.transpose(0, 2, 1).reshape(-1, shard_rows).astype(f32),
+        o_grad,
+        gate_up_grad,
+        down_grad,
     )
 
 

time: 609 us -> 502 us (0.82); the launches traced: 598 us -> 499 us
  matrix products: 28.6 us -> 0 us
  Pallas kernels: 499 us -> 471 us
  local copies, waits for them, and re-layouts: 52.6 us -> 24.9 us
  other arithmetic: 16 us -> 1.99 us
    dot_general x6 -> x0, matrix products: 28.6 us -> none  [the longest x1 7.12 us: local_heads(): jnp.einsum('td,tf->df', normed_two, grad_gate, preferred_element_type=f32)]
    convert_element_type x8 -> x0, local copies, waits for them, and re-layouts: 20.4 us -> none  [the longest x1 4.85 us: local_heads(): jnp.einsum('td,tf->df', normed_two, grad_up, preferred_element_type=f32)]
    pallas_call x4, Pallas kernels: 343 us -> 324 us  [line_call(): pl.pallas_call(kernel, out_shape=[jax.ShapeDtypeStruct(*out) for out in (...]
    pallas_call x1, Pallas kernels: 13.4 us -> 3.31 us  [run_finish(): pl.pallas_call(finish_kernel, out_shape=[jax.ShapeDtypeStruct(shape, f32)...]
    reduce_sum x4 -> x1, other arithmetic: 9.79 us -> 0.9 us  [summed(): return jnp.sum(came.astype(f32), axis=0).astype(b16)]
    unnamed x76 -> x56, local copies, waits for them, and re-layouts: 22.2 us -> 18.4 us
where the time goes in v5:
time: 502 us; the launch traced here: 499 us
  Pallas kernels  471 us (94%)
  local copies, waits for them, and re-layouts  24.9 us (5%)
    pallas_call x4, Pallas kernels, line_call(): pl.pallas_call(kernel, out_shape=[jax.ShapeDtypeStruct(*out) for out in (...  324 us
    pallas_call x1, Pallas kernels, run_forward(): pl.pallas_call(functools.partial(forward_kernel, heads), out_shape=[jax.S...  64.2 us
    pallas_call x1, Pallas kernels, run_backward(): pl.pallas_call(functools.partial(backward_kernel, heads), out_shape=[jax....  63.3 us
    unnamed x56, local copies, waits for them, and re-layouts  18.4 us
    pallas_call x1, Pallas kernels, run_mlp(): pl.pallas_call(mlp_kernel, grid=(row_len // block,), out_shape=[shape] *...  16.1 us

profile of v5, /device:TPU:8, one launch (start us, length us, event | category | flops | bytes accessed | tf_op | source)
XLA Modules:
  0.0 498.9 jit_solution(17526037222491308249)
XLA Ops:
  0.6 0.0 copy-start
  0.7 0.8 reduce-window.8
  1.5 0.1 convert_reduce_fusion
  1.6 0.2 slice_reduce_fusion
  1.8 0.2 slice_reduce_fusion.1
  2.0 0.1 pad_add_fusion
  2.0 0.1 eq.47
  2.1 0.1 eq.51
  2.2 0.0 copy-done
  2.2 0.1 fusion.3
  2.3 0.1 stack.31
  2.4 1.3 pad.5.beta_ref
  3.7 0.2 copy.44.aux_ref
  3.9 2.5 copy.42
  6.4 1.7 copy.43
  8.1 0.0 copy-start.14
  8.1 0.0 copy-start.19
  8.1 0.0 copy-start.23
  8.1 0.1 slice_bitcast_fusion
  8.2 60.3 %norm_gather.1 = (bf16[4,2,128,2048]{3,2,1,0:T(8,128)(2,1)}, bf16[4,4,3,128,256]{4,3,2,1,0:T(8,128)(2,1)}, bf16[4,4,16,128]{3,2,1,0:T(8,128)(2,1)}) custom-call(bf16[256,2048]{1,0:T(8,128)(2,1)} %bitcast.78, f32[1,2048]{1,0:T(1,128)} %bitcast.63, bf16[3,128,1024]{2,1,0:T(8,128)(2,1)} %weight_ref.1, bf16[4,16,128]{2,1,0:T(8,128)(2,1)} %pad.5.beta_ref), custom_call_target="tpu_custom_call" | custom-call | tf_op jit(solution)/shard_map/norm_gather/pallas_call | solution.py:1490
  68.6 0.9 copy.41
  69.5 0.0 copy-start.7
  69.5 0.0 copy-done.14
  69.5 0.0 copy-done.19
  69.5 0.0 copy-done.23
  69.5 64.2 %mixer_forward.1 = (bf16[1024,768]{1,0:T(8,128)(2,1)}, f32[1024,16]{1,0:T(8,128)S(1)}, f32[1024,256]{1,0:T(8,128)}, bf16[1024,256]{1,0:T(8,128)(2,1)S(1)}, f32[2...) custom-call(bf16[1024,2048]{1,0:T(8,128)(2,1)} %bitcast.68, ...), custom_call_target="tpu_custom_call" | custom-call | tf_op jit(solution)/shard_map/mixer_forward/pallas_call | solution.py:837
  133.7 0.0 copy-start.2
  133.7 0.8 copy-done.2
  134.5 0.0 copy-start.9
  134.5 0.9 copy-done.9
  135.4 0.9 copy-done.13
  136.3 0.8 copy-done.15
  137.1 86.6 %resid_norm.1 = (f32[128,2048]{1,0:T(8,128)}, bf16[4,2,128,2048]{3,2,1,0:T(8,128)(2,1)}, bf16[4,2,128,2048]{3,2,1,0:T(8,128)(2,1)}, bf16[4,4,128,704]{3,2,1,0:T(8,128)(2,1)}, bf16[4,4,704,128]{3,2,1,0:T(8,128)(2,1)}) custom-call(bf16[8,128,256]{2,1,0:T(8,128)(2,1)} %bitcast.53, bf16[4,4,256,128]{3,2,1,0:T(8,128)(2,1)} %get-tuple-element.63.o_ref, ...), custom_call_target="tpu_custom_call" | custom-call | tf_op jit(solution)/shard_map/resid_norm/pallas_call | solution.py:1490
  223.7 16.1 %mlp.1 = (bf16[1024,704]{1,0:T(8,128)(2,1)S(1)}, bf16[1024,704]{1,0:T(8,128)(2,1)S(1)}, bf16[1024,704]{1,0:T(8,128)(2,1)S(1)}, bf16[704,2048]{1,0:T(8,128)(2,1)}) custom-call(bf16[1024,2048]{1,0:T(8,128)(2,1)} %bitcast.70, bf16[1024,2048]{1,0:T(8,128)(2,1)} %bitcast.72, bf16[2048,704]{1,0:T(8,128)(2,1)} %bitcast.74, bf16[2048,704]{1,0:T(8,128)(2,1)} %bitcast.76, ...), custom_call_target="tpu_custom_call" | custom-call | tf_op jit(solution)/shard_map/mlp/pallas_call | solution.py:1917
  239.8 0.0 copy-start.4
  239.8 1.1 copy-done.4
  241.0 1.1 copy-done.5
  242.1 1.2 copy-done.6
  243.3 107.4 %grad_resid.1 = (f32[128,2048]{1,0:T(8,128)}, bf16[4,2,128,2048]{3,2,1,0:T(8,128)(2,1)}, f32[1,2048]{1,0:T(1,128)}, bf16[256,2048]{1,0:T(8,128)(2,1)}, bf16[3,512,704]{2,1,0:T(8,128)(2,1)}) custom-call(bf16[8,128,704]{2,1,0:T(8,128)(2,1)} %bitcast.55, bf16[8,128,704]{2,1,0:T(8,128)(2,1)} %bitcast.56, bf16[8,128,704]{2,1,0:T(8,128)(2,1)} %bitcast.54, ...), custom_call_target="tpu_custom_call" | custom-call | tf_op jit(solution)/shard_map/grad_resid/pallas_call | solution.py:1490
  350.6 0.0 copy-done.7
  350.7 0.0 copy-done.3
  350.7 0.0 copy-done.20
  350.7 0.0 copy-start.16
  350.7 1.0 copy-done.16
  351.7 0.7 copy-done.22
  352.4 63.3 %mixer_backward.1 = (bf16[1024,768]{1,0:T(8,128)(2,1)}, bf16[1024,16]{1,0:T(8,128)(2,1)S(1)}, f32[6,2048]{1,0:T(8,128)S(1)}, bf16[4,4,128,768]{3,2,1,0:T(8,128)(...) custom-call(bf16[1024,2048]{1,0:T(8,128)(2,1)} %bitcast.83, ...), custom_call_target="tpu_custom_call" | custom-call | tf_op jit(solution)/shard_map/mixer_backward/pallas_call | solution.py:872
  415.7 0.0 copy-start.10
  415.7 0.9 copy-done.10
  416.6 0.7 copy-done.17
  417.3 0.6 copy-done.21
  417.9 0.9 reduce_sum.25.o_sum_ref
  418.8 69.7 %input_grad.1 = (bf16[256,2048]{1,0:T(8,128)(2,1)}, bf16[4,128,768]{2,1,0:T(8,128)(2,1)}, f32[2,4,6,2048]{3,2,1,0:T(8,128)}, bf16[4,128,256]{2,1,0:T(8,128)(2,1)}) custom-call(bf16[8,128,768]{2,1,0:T(8,128)(2,1)} %bitcast.87, bf16[4,4,3,128,256]{4,3,2,1,0:T(8,128)(2,1)} %get-tuple-element.60.qkv_ref, bf16[8,128,16]{2,1,0:T(8,128)(2,1)} %bitcast.60, ...), custom_call_target="tpu_custom_call" | custom-call | tf_op jit(solution)/shard_map/input_grad/pallas_call | solution.py:1490
  488.5 1.1 slice.31
  489.7 0.6 dynamic-slice_bitcast_fusion
  490.3 0.0 copy-done.11
  490.3 1.0 copy-done.8
  491.4 1.1 copy-done.12
  492.5 0.9 copy-done.18
  493.5 3.3 finish.1
  496.8 0.0 copy-done.24
  496.8 1.0 copy.51
  497.7 0.0 copy-done.25
  497.8 1.0 copy.52
  498.7 0.0 copy-done.1
  (24 shorter events, 0.1 us)
Async XLA Ops:
  0.6 1.6 copy-start
  8.1 61.4 %copy-start.14 = (bf16[2816,128]{1,0:T(8,128)(2,1)S(1)}, bf16[2816,128]{1,0:T(8,128)(2,1)}, u32[]{:S(2)}) copy-start(bf16[2816,128]{1,0:T(8,128)(2,1)} %down_ref.1) | copy-start | bytes 2162692
  8.1 61.4 %copy-start.19 = (bf16[1024,128]{1,0:T(8,128)(2,1)S(1)}, bf16[1024,128]{1,0:T(8,128)(2,1)}, u32[]{:S(2)}) copy-start(bf16[1024,128]{1,0:T(8,128)(2,1)} %o_weight_ref.1) | copy-start | bytes 786436
  8.1 61.4 %copy-start.23 = (f32[128]{0:T(128)S(1)}, f32[128]{0:T(128)}, u32[]{:S(2)}) copy-start(f32[128]{0:T(128)} %param.17) | copy-start | bytes 1540
  69.5 281.2 %copy-start.7 = (bf16[2,8,16,128]{3,1,2,0:T(8,128)(2,1)}, bf16[2,8,16,128]{3,1,2,0:T(8,128)(2,1)S(1)}, u32[]{:S(2)}) copy-start(bf16[2,8,16,128]{3,1,2,0:T(8,128)(2,1)S(1)} %copy.48) | copy-start | bytes 196612
  133.7 0.8 copy-start.2
  134.5 0.9 copy-start.9
  135.4 0.9 copy-start.13
  136.3 0.8 copy-start.15
  239.8 1.1 copy-start.4
  241.0 1.1 copy-start.5
  242.1 1.2 copy-start.6
  243.3 107.4 %copy-start.3 = (bf16[1024,256]{1,0:T(8,128)(2,1)S(1)}, bf16[1024,256]{1,0:T(8,128)(2,1)}, u32[]{:S(2)}) copy-start(bf16[1024,256]{1,0:T(8,128)(2,1)} %copy-done.2) | copy-start | bytes 1572868
  243.3 107.4 %copy-start.20 = (f32[2048]{0:T(1024)S(1)}, f32[2048]{0:T(1024)}, u32[]{:S(2)}) copy-start(f32[2048]{0:T(1024)} %param.15) | copy-start | bytes 24580
  350.7 1.0 copy-start.16
  351.7 0.7 copy-start.22
  415.7 0.9 copy-start.10
  416.6 0.7 copy-start.17
  417.3 0.6 copy-start.21
  418.8 71.5 %copy-start.11 = (bf16[4,128,704]{2,1,0:T(8,128)(2,1)S(1)}, bf16[4,128,704]{2,1,0:T(8,128)(2,1)}, u32[]{:S(2)}) copy-start(bf16[4,128,704]{2,1,0:T(8,128)(2,1)} %copy-done.10) | copy-start | bytes 2162692
  490.3 1.0 copy-start.8
  491.4 1.1 copy-start.12
  492.5 0.9 copy-start.18
  493.5 3.3 copy-start.24
  493.5 4.3 copy-start.25
  493.5 5.3 %copy-start.1 = (f32[3,4,1024]{2,1,0:T(4,128)S(1)}, f32[3,4,1024]{2,1,0:T(4,128)}, u32[]{:S(2)}) copy-start(f32[3,4,1024]{2,1,0:T(4,128)} %param.18) | copy-start | bytes 147460

commit v6 on v5

--- a/solution.py
+++ b/solution.py
@@ -410,14 +410,18 @@
 PAD = 8
 
 
-def mul(left, right, dims, precision=None):
+def mul(left, right, dims):
     return lax.dot_general(
-        left, right, ((dims[:1], dims[1:]), ((), ())), precision=precision, preferred_element_type=jnp.float32
+        left, right, ((dims[:1], dims[1:]), ((), ())), preferred_element_type=jnp.float32
     )
 
 
 def fine(left, right, dims=(1, 0)):
-    return mul(left, right, dims, precise)
+    left_high, right_high = left.astype(jnp.bfloat16), right.astype(jnp.bfloat16)
+    left_rest = (left - left_high.astype(jnp.float32)).astype(jnp.bfloat16)
+    right_rest = (right - right_high.astype(jnp.float32)).astype(jnp.bfloat16)
+    rest = mul(left_high, right_rest, dims) + mul(left_rest, right_high, dims)
+    return mul(left_high, right_high, dims) + rest
 
 
 def plain(left, right, dims=(1, 0)):
@@ -479,6 +483,7 @@
 
 def forward_kernel(
     heads,
+    staged,
     n1_ref,
     qkv_ref,
     beta_ref,
@@ -486,6 +491,9 @@
     aux_ref,
     docs_ref,
     gain_ref,
+    x_ref,
+    mlp_gain_ref,
+    g_ref,
     o_weight_ref,
     gate_ref,
     up_ref,
@@ -498,47 +506,59 @@
     states_ref,
     written_ref,
     o_ref,
+    resid_ref,
+    n2_ref,
+    g_full_ref,
     gate_out,
     up_out,
     down_out,
     window_ref,
     state_ref,
+    o_rows,
+    n2_own,
+    blocks,
+    came,
+    across,
     own_sems,
+    sum_sems,
+    n2_sems,
+    g_sems,
     *sems,
 ):
     width = heads * DK
     line = Line()
-    greet(exchange_partners(line))
+    greet(exchange_partners(line) + along_axis("tp"))
     row = lax.axis_index("row")
+    rows = n2_ref.shape[2]
+    units = down_out.shape[2]
 
     def rows_of(ref, count):
         return lambda seq: ref.at[pl.ds(pl.multiple_of(seq * count, count), count)]
 
-    units = down_out.shape[1]
-    whole = Exchange(line, rows_of(o_weight_ref, width), o_ref, sems[:4])
-    gates = Exchange(line, lambda seq: gate_ref.at[seq], gate_out, sems[4:8])
-    moves = [
-        Exchange(line, lambda seq: up_ref.at[seq], up_out, sems[8:10]),
-        Exchange(line, rows_of(down_ref, units), down_out, sems[10:12]),
-    ]
+    o_move = Exchange(line, rows_of(o_weight_ref, width), o_ref, sems[:4])
+    gate_move = Exchange(line, lambda seq: gate_ref.at[seq], gate_out, sems[4:8])
+    up_move = Exchange(line, lambda seq: up_ref.at[seq], up_out, sems[8:12])
+    down_move = Exchange(line, rows_of(down_ref, units), down_out, sems[12:16])
+    moves = (o_move, gate_move, up_move, down_move)
+    total = Scatter(line, blocks, came, across, sum_sems)
+    n2 = Gather(line, n2_ref, n2_own, n2_sems)
+    g_own = g_ref.at[pl.ds(pl.multiple_of(line.core * rows, rows), rows)]
+    grads = Gather(line, g_full_ref, g_own, g_sems)
     own = []
-    for i, move in enumerate((whole, gates)):
+    for i, move in enumerate(moves):
         target = move.target.at[row, line.place]
         own.append(pltpu.make_async_copy(move.source(line.place), target, own_sems.at[i]))
+        own[i].start()
+    o_move.start()
+    gate_move.start()
+    grads.phases(0)
     for i, move in enumerate(moves):
-        target = move.target.at[line.place]
-        own.append(pltpu.make_async_copy(move.source(line.place), target, own_sems.at[i + 2]))
-    for move in (whole, gates, *moves):
-        move.start()
-    for copy in own:
-        copy.start()
-    for i, move in enumerate((whole, gates)):
         own[i].wait()
         move.share_own()
     window_ref[0:PAD] = jnp.zeros((PAD, 3 * width), jnp.float32)
     state_ref[...] = jnp.zeros_like(state_ref)
 
-    def chunk(n, _):
+    def prepare(n):
         rows = pl.ds(pl.multiple_of(n * CHUNK, CHUNK), CHUNK)
         n1 = n1_ref[rows]
         proj = jnp.concatenate(
@@ -553,7 +573,6 @@
         act = conv * sigmoid(conv)
         window_ref[0:PAD] = window_ref[CHUNK : CHUNK + PAD]
         valid, carry, tail = aux[:, 1:2], aux[:, 2:3], aux[:, 3:4]
-        carry_last = carry[CHUNK - 1 :]
         lower, strict, down, along = chunk_masks(aux[:, 0:1], docs_ref[pl.ds(n, 1)])
         rate_all = sigmoid(logit) * valid
         parts = []
@@ -564,18 +583,18 @@
             query = query * unit_scale(query)[0]
             key = key * unit_scale(key)[0]
             rate = rate_all[:, h : h + 1]
+            scores = plain(query, key, (1, 1)) * lower
             system = rate * fine(key, key, (1, 1)) * strict
-            parts.append((query, key, value, rate, system))
-        inverses = lower_inverse([part[4] for part in parts], down, along)
-        for h, (query, key, value, rate, _) in enumerate(parts):
+            parts.append((query, key, value, rate, scores, system))
+        return rows, valid, carry, tail, parts, down, along
+
+    def advance(n, rows, valid, carry, tail, parts, inverses):
+        carry_last = carry[CHUNK - 1 :]
+        for h, (query, key, value, rate, scores, _) in enumerate(parts):
             inverse = inverses[h]
             state = state_ref[h]
-            carried_key = carry * key
-            right = rate * (value - fine(carried_key, state))
-            written = fine(inverse, right)
-            scores = plain(query, key, (1, 1)) * lower
-            mixed = carry * plain(query, state) + plain(scores, written)
-            mixed = mixed * valid
+            written = fine(inverse, rate * (value - fine(carry * key, state)))
+            mixed = (carry * plain(query, state) + plain(scores, written)) * valid
             states_ref[h, n] = state
             written_ref[h, n] = written
             inverse_ref[h, n] = inverse
@@ -585,25 +604,82 @@
             normed_ref[rows, columns] = (
                 mixed * mix_norm(mixed)[0] * gain_ref[...]
             ).astype(jnp.bfloat16)
+
+    chunks = n1_ref.shape[0] // CHUNK
+    together = 4 if chunks % 4 == 0 else 1
+
+    def several(m, _):
+        ready = [prepare(together * m + i) for i in range(together)]
+        down, along = ready[0][5:]
+        inverses = lower_inverse([part[5] for one in ready for part in one[4]], down, along)
+        for i, one in enumerate(ready):
+            advance(together * m + i, *one[:5], inverses[i * heads : (i + 1) * heads])
         return 0
 
-    chunks = n1_ref.shape[0] // CHUNK
-    early, late = chunks // 4, 3 * chunks // 4
-    lax.fori_loop(0, early, chunk, 0)
-    for i in range(1, line.count):
-        whole.share_came(i)
-    lax.fori_loop(early, late, chunk, 0)
-    for i in range(1, line.count):
-        gates.share_came(i)
-    lax.fori_loop(late, chunks, chunk, 0)
-    for copy in own[2:]:
-        copy.wait()
-    for move in (whole, gates, *moves):
+    def share_came(move):
+        for i in range(1, line.count):
+            move.share_came(i)
+
+    half = chunks // together // 2
+    staged.need(n1_ref, qkv_ref, beta_ref, taps_ref, aux_ref, docs_ref, gain_ref)
+    lax.fori_loop(0, half, several, 0)
+    share_came(o_move)
+    grads.phases(1)
+    up_move.start()
+    lax.fori_loop(half, chunks // together, several, 0)
+    staged.store(
+        proj_ref, logit_ref, mixed_ref, normed_ref, inverse_ref, states_ref, written_ref
+    )
+    share_came(gate_move)
+    down_move.start()
+    o_move.finish()
+    staged.store(o_ref)
+    side_by_side(o_ref, o_rows)
+    for part in range(total.parts):
+        total.product(part_rows(normed_ref, total, part), o_rows, part, order=0)
+        total.start_edges(part)
+    grads.phases(2)
+    total.relay(0, 0)
+    total.relay(1, 0)
+    share_came(up_move)
+    total.relay_back(0)
+    grads.phases(3)
+    total.relay(0, 1)
+    total.relay(1, 1)
+    share_came(down_move)
+    total.relay_back(1)
+    staged.need(x_ref, mlp_gain_ref)
+
+    def normed(span):
+        x_span = pl.ds(pl.multiple_of(line.core * rows + span.start, STEP), STEP)
+        resid = x_ref[x_span].astype(jnp.float32) + total.own_rows(span)
+        resid_ref[span] = resid
+        n2_own[span] = (resid * norm_scale(resid) * mlp_gain_ref[...]).astype(jnp.bfloat16)
+
+    for part in range(total.parts):
+        total.wait_own(part)
+        over_rows(total, part, normed)
+        n2.phase(0, part)
+    staged.store(resid_ref)
+    for k in range(1, line.count):
+        n2.phases(k)
+    total.finish()
+    n2.finish()
+    grads.finish()
+    for move in moves[1:]:
         move.finish()
+
+
+def part_rows(ref, total, part):
+    seqs, cores, rows, _ = total.blocks.shape
+    return jnp.concatenate(
+        [ref[pl.ds(i * rows + part * total.rows, total.rows)] for i in range(seqs * cores)], axis=0
+    )
 
 
 def backward_kernel(
     heads,
+    staged,
     grad_ref,
     o_ref,
     proj_ref,
@@ -622,26 +698,44 @@
     beta_ref,
     attn_gain_ref,
     mlp_grad_ref,
+    x_ref,
+    grad_resid_ref,
     sum_ref,
-    grad_proj_ref,
-    grad_logit_ref,
-    small_ref,
-    qkv_part_ref,
+    input_grad_ref,
+    small_all_ref,
+    qkv_came_ref,
+    o_came_ref,
     down_came_ref,
     gate_came_ref,
     up_came_ref,
-    o_came_ref,
     window_ref,
     masked_ref,
     state_ref,
     o_rows,
-    o_part_ref,
     conv_grad_ref,
     gain_grad_ref,
+    grad_proj_ref,
+    grad_logit_ref,
+    small_ref,
+    small_rows,
+    qkv_sum,
+    o_sum,
+    blocks,
+    came,
+    across,
+    qkv_parts,
+    qkv_halves,
+    qkv_rows_came,
+    o_parts,
+    o_halves,
+    o_rows_came,
+    sum_sems,
+    swap_sems,
     *sems,
 ):
     width = heads * DK
-    greet(along_axis("seq") + along_axis("row"))
+    line = Line()
+    greet(along_axis("seq") + along_axis("row") + along_axis("tp"))
     moves = moves_of(
         Swap,
         "seq",
@@ -651,21 +745,35 @@
     )
     for move in moves:
         move.start()
-    rows_axis, seqs, shard, _ = o_part_ref.shape
-    span = seqs * shard
-
-    def o_rows_of(r, _):
-        columns = pl.ds(pl.multiple_of(r * span, span), span)
-        part = mul(grad_ref[:, columns], normed_mix_ref[...], (0, 0))
-        o_part_ref[r] = part.astype(jnp.bfloat16).reshape(seqs, shard, -1)
-        return 0
-
-    lax.fori_loop(0, rows_axis, o_rows_of, 0)
-    o_moves = moves_of(Swap, "row", (o_part_ref,), (o_came_ref,), sems[7:])
-    for move in o_moves:
-        move.start()
+    (o_move,) = moves_of(Swap, "seq", (o_sum,), (o_came_ref,), sems[7:10])
+    (qkv_move,) = moves_of(Swap, "seq", (qkv_sum,), (qkv_came_ref,), sems[10:13])
+    (small_row,) = moves_of(Share, "row", (small_ref,), (small_rows,), sems[13:16])
+    own_small = small_all_ref.at[line.core, line.place]
+    small_seq = [
+        remote(own_small, own_small, sems[16].at[i], sems[17].at[i], {"seq": other})
+        for i, other in enumerate(around("seq"))
+    ]
+    core_small = small_all_ref.at[line.core]
+    small_core = remote(core_small, core_small, sems[18].at[0], sems[18].at[1], line.across)
+    o_sums = RowSum(o_parts, o_halves, o_rows_came, sems[19:23])
+    qkv_sums = RowSum(qkv_parts, qkv_halves, qkv_rows_came, sems[23:27])
+    total = Scatter(line, blocks, came, across, sum_sems)
+    span = o_parts.shape[2]
+
+    def own_columns(index):
+        return pl.ds(pl.multiple_of(index * span, span), span)
+
+    staged.need(grad_ref, normed_mix_ref)
+    for step, index in enumerate(o_sums.order()):
+        part = mul(grad_ref[:, own_columns(index)], normed_mix_ref[...], (0, 0))
+        o_parts[index, 0] = part.astype(jnp.bfloat16)
+        o_sums.start(step, 0)
+    chunks = grad_ref.shape[0] // CHUNK
+    staged.need(
+        o_ref, proj_ref, logit_ref, mixed_ref, inverse_ref, states_ref, written_ref, taps_ref,
+        aux_ref, docs_ref, gain_ref,
+    )
     side_by_side(o_ref, o_rows)
-    chunks = grad_ref.shape[0] // CHUNK
     state_ref[...] = jnp.zeros_like(state_ref)
     masked_ref[...] = jnp.zeros_like(masked_ref)
     conv_grad_ref[...] = jnp.zeros_like(conv_grad_ref)
@@ -780,116 +888,192 @@
         )
         return 0
 
-    lax.fori_loop(0, chunks, chunk, 0)
-
-    def qkv_rows_of(r, _):
-        columns = pl.ds(pl.multiple_of(r * span, span), span)
+    early, late = chunks // 4, chunks // 2
+    lax.fori_loop(0, early, chunk, 0)
+    o_sums.add_halves(0)
+    lax.fori_loop(early, late, chunk, 0)
+    o_sum[...] = o_sums.total(0).astype(jnp.bfloat16).reshape(o_sum.shape)
+    o_move.start()
+    lax.fori_loop(late, chunks, chunk, 0)
+    staged.need(
+        n1_ref, qkv_ref, beta_ref, attn_gain_ref, mlp_grad_ref, x_ref, grad_resid_ref
+    )
+
+    def product(part):
+        left = part_rows(grad_proj_ref, total, part)
+        logit = part_rows(grad_logit_ref, total, part)
+
+        def right_tile(left, t, across):
+            weights = qkv_ref[t]
+            out = mul(logit, beta_ref[:, across], (1, 0))
+            for c in range(3):
+                out = out + mul(
+                    left[:, c * width : (c + 1) * width], weights[:, c].reshape(-1, width), (1, 1)
+                )
+            return out
+
+        total.product(left, None, part, tile=span, right_tile=right_tile)
+        total.start_edges(part)
+
+    def qkv_grads(step):
+        index = qkv_sums.order()[step]
+        columns = own_columns(index)
         n1 = n1_ref[:, columns]
         part = mul(n1, grad_proj_ref[...], (0, 0))
-        qkv_part_ref[r] = part.astype(jnp.bfloat16).reshape(seqs, shard, -1)
-        weights = qkv_ref[r]
-        total = 0.0
+        qkv_parts[index, 0] = part.astype(jnp.bfloat16)
+        qkv_sums.start(step, 0)
+        weights = qkv_ref[index]
+        terms = 0.0
         for c in range(3):
             weight = weights[:, c].reshape(span, width).astype(jnp.float32)
-            total = total + weight * part[:, c * width : (c + 1) * width]
-        total = fine(jnp.ones((8, width), jnp.float32), total, (1, 1))[0:1]
+            terms = terms + weight * part[:, c * width : (c + 1) * width]
+        terms = fine(jnp.ones((8, width), jnp.float32), terms, (1, 1))[0:1]
         beta_part = mul(grad_logit_ref[...], n1, (0, 0))
-        total = total + jnp.sum(
+        terms = terms + jnp.sum(
             beta_part * beta_ref[:, columns].astype(jnp.float32), axis=0, keepdims=True
         )
-        small_ref[0:1, columns] = total / attn_gain_ref[:, columns]
+        small_ref[0:1, columns] = terms / attn_gain_ref[:, columns]
         small_ref[2 : 2 + heads, columns] = beta_part[:heads]
-        return 0
-
-    lax.fori_loop(0, rows_axis, qkv_rows_of, 0)
+
+    product(0)
+    qkv_grads(0)
+    product(1)
+    qkv_grads(1)
+    total.relay(0, 0)
+    total.relay(1, 0)
+    qkv_grads(2)
+    qkv_grads(3)
     small_ref[1:2] = mlp_grad_ref[...]
     at = 2 + heads
     for tap in range(KW):
         lanes = pl.ds((tap % 2) * 3 * width, 3 * width)
         small_ref[at + tap // 2 : at + tap // 2 + 1, lanes] = conv_grad_ref[tap : tap + 1]
     small_ref[at : at + 1, 6 * width : 6 * width + DK] = gain_grad_ref[...]
-    for move in moves + o_moves:
+    small_row.start()
+    total.relay_back(0)
+    qkv_sums.add_halves(0)
+    total.relay(0, 1)
+    total.relay(1, 1)
+    small_row.finish()
+    small = small_rows[0]
+    for i in range(1, small_rows.shape[0]):
+        small = small + small_rows[i]
+    small_all_ref[line.core, line.place] = small
+    for copy in small_seq:
+        copy.start()
+    total.relay_back(1)
+    qkv_sum[...] = qkv_sums.total(0).astype(jnp.bfloat16).reshape(qkv_sum.shape)
+    qkv_move.start()
+    rows = grad_resid_ref.shape[0]
+
+    def back(inner):
+        own_span = pl.ds(pl.multiple_of(line.core * rows + inner.start, STEP), STEP)
+        x = x_ref[own_span].astype(jnp.float32)
+        input_grad_ref[own_span] = (
+            grad_resid_ref[inner]
+            + norm_back(x, norm_scale(x), attn_gain_ref[...], total.own_rows(inner))
+        ).astype(jnp.bfloat16)
+
+    for part in range(total.parts):
+        total.wait_own(part)
+        over_rows(total, part, back)
+    swap = own_swap(line, input_grad_ref, rows, swap_sems)
+    swap.start()
+    for copy in small_seq:
+        copy.wait()
+    small_core.start()
+    total.finish()
+    o_sums.finish()
+    qkv_sums.finish()
+    for move in moves + [o_move, qkv_move]:
         move.finish()
+    swap.wait()
+    small_core.wait()
 
 
 def in_vmem(count):
     return [pl.BlockSpec(memory_space=pltpu.VMEM)] * count
 
 
-def run_forward(n1, qkv, beta, taps, aux, docs, gain, o_weight, gate, up, down):
+def run_forward(n1, qkv, beta, taps, aux, docs, gain, x, g, mlp_gain, weights):
     row_len, heads = n1.shape[0], qkv.shape[-1] // DK
-    rows_axis, seqs = qkv.shape[:2]
-    chunks, width, f32 = row_len // CHUNK, heads * DK, jnp.float32
-    shapes = (
-        ((row_len, 3 * width), jnp.bfloat16),
+    rows_axis, seqs, _, shard, _ = qkv.shape
+    cores, (piece, model_width) = lax.axis_size("tp"), x.shape
+    rows = piece // cores
+    chunks, width, f32, b16 = row_len // CHUNK, heads * DK, jnp.float32, jnp.bfloat16
+    units = weights[3].shape[0] // seqs
+    outs = (
+        ((row_len, 3 * width), b16),
         ((row_len, beta.shape[0]), f32),
         ((row_len, width), f32),
-        ((row_len, width), jnp.bfloat16),
+        ((row_len, width), b16),
         ((heads, chunks, CHUNK, CHUNK), f32),
         ((heads, chunks, DK, DK), f32),
         ((heads, chunks, CHUNK, DK), f32),
-        ((rows_axis, seqs, width, o_weight.shape[1]), jnp.bfloat16),
-        ((rows_axis,) + gate.shape, jnp.bfloat16),
-        (up.shape, jnp.bfloat16),
-        ((seqs, down.shape[0] // seqs, down.shape[1]), jnp.bfloat16),
-    )
-    hbm = [pl.BlockSpec(memory_space=pl.ANY)]
-    return pl.pallas_call(
-        functools.partial(forward_kernel, heads),
-        out_shape=[jax.ShapeDtypeStruct(*shape) for shape in shapes],
-        in_specs=in_vmem(7) + hbm * 4,
-        out_specs=in_vmem(7) + hbm * 4,
-        scratch_shapes=[
-            pltpu.VMEM((PAD + CHUNK, 3 * width), f32),
-            pltpu.VMEM((heads, DK, DK), f32),
-            dma_sems(4),
-        ]
-        + exchange_sems() * 2
-        + [dma_sems(seqs - 1)] * 4,
-        compiler_params=pltpu.CompilerParams(
-            collective_id=5, has_side_effects=True, vmem_limit_bytes=48 * 1024 * 1024
+        ((rows_axis, seqs, width, shard), b16),
+        ((rows, model_width), f32),
+    )
+    scratch = [
+        pltpu.VMEM((PAD + CHUNK, 3 * width), f32),
+        pltpu.VMEM((heads, DK, DK), f32),
+        pltpu.VMEM((width, model_width), b16),
+        pltpu.VMEM((rows, model_width), b16),
+    ]
+    scratch = scratch + scatter_scratch(seqs, cores, rows, model_width) + [dma_sems(4)]
+    scratch = scratch + [dma_sems(6, seqs, PARTS)] * 3 + exchange_sems() * 4
+    *saved, o_full, resid, n2, g_full, gate, up, down = line_call(
+        functools.partial(forward_kernel, heads), 5, "mixer_forward", outs, scratch,
+        (n1, qkv, beta, taps, aux, docs, gain, x, mlp_gain),
+        far_args=(g, *weights),
+        far_outs=(
+            ((seqs, cores, rows, model_width), b16),
+            ((seqs, cores, rows, model_width), b16),
+            ((rows_axis,) + weights[1].shape, b16),
+            ((rows_axis,) + weights[2].shape, b16),
+            ((rows_axis, seqs, units, shard), b16),
         ),
-        name="mixer_forward",
-    )(n1, qkv, beta, taps, aux, docs, gain, o_weight, gate, up, down)
+    )
+    n2, g_full = n2.reshape(-1, model_width), g_full.reshape(-1, model_width)
+    gate, up = gate.reshape(model_width, units), up.reshape(model_width, units)
+    return saved, o_full, resid, n2, g_full, gate, up, down
 
 
 def run_backward(grad, o_full, saved, taps, aux, docs, gain, extra, sums):
     row_len, heads = grad.shape[0], o_full.shape[2] // DK
     model_width = grad.shape[1]
     rows_axis, seqs, _, shard = o_full.shape
-    b16 = jnp.bfloat16
-    width, f32 = heads * DK, jnp.float32
-    logit = saved[1]
-    shapes = (
-        ((row_len, 3 * width), jnp.bfloat16),
-        (logit.shape, jnp.bfloat16),
-        ((4 + heads, model_width), f32),
-        ((rows_axis, seqs, shard, 3 * width), b16),
-    )
-    o_shape = (rows_axis, seqs, shard, width)
-    far = [pl.BlockSpec(memory_space=pl.ANY)]
-    far_shapes = ((sums.shape[1:], b16),) * 3 + ((o_shape, b16),)
-    return pl.pallas_call(
-        functools.partial(backward_kernel, heads),
-        out_shape=[jax.ShapeDtypeStruct(*shape) for shape in shapes + far_shapes],
-        in_specs=in_vmem(12 + len(extra)) + far,
-        out_specs=in_vmem(len(shapes)) + far * len(far_shapes),
-        scratch_shapes=[
-            pltpu.VMEM((PAD + CHUNK, 3 * width), f32),
-            pltpu.VMEM((KW - 1, CHUNK + PAD, 3 * width), f32),
-            pltpu.VMEM((heads, DK, DK), f32),
-            pltpu.VMEM((width, model_width), b16),
-            pltpu.VMEM(o_shape, b16),
-            pltpu.VMEM((KW, 3 * width), f32),
-            pltpu.VMEM((1, DK), f32),
-        ]
-        + pair_sems("seq", 3)
-        + pair_sems("row", 1),
-        compiler_params=pltpu.CompilerParams(
-            collective_id=6, has_side_effects=True, vmem_limit_bytes=48 * 1024 * 1024
-        ),
-        name="mixer_backward",
-    )(grad, o_full, *saved, taps, aux, docs, gain, *extra, sums)
+    cores = lax.axis_size("tp")
+    width, f32, b16 = heads * DK, jnp.float32, jnp.bfloat16
+    rows, span = row_len // (seqs * cores), model_width // rows_axis
+    small = (4 + heads, model_width)
+    outs = (((cores * rows, model_width), b16), ((cores, seqs) + small, f32))
+    far_outs = (((seqs, shard, 3 * width), b16), ((seqs, shard, width), b16))
+    qkv_buffers, qkv_sems = row_sum_scratch((rows_axis, 1, span, 3 * width))
+    o_buffers, o_sems = row_sum_scratch((rows_axis, 1, span, width))
+    scratch = [
+        pltpu.VMEM((PAD + CHUNK, 3 * width), f32),
+        pltpu.VMEM((KW - 1, CHUNK + PAD, 3 * width), f32),
+        pltpu.VMEM((heads, DK, DK), f32),
+        pltpu.VMEM((width, model_width), b16),
+        pltpu.VMEM((KW, 3 * width), f32),
+        pltpu.VMEM((1, DK), f32),
+        pltpu.VMEM((row_len, 3 * width), b16),
+        pltpu.VMEM(saved[1].shape, b16),
+        pltpu.VMEM(small, f32),
+        pltpu.VMEM((rows_axis,) + small, f32),
+        pltpu.VMEM((seqs, shard, 3 * width), b16),
+        pltpu.VMEM((seqs, shard, width), b16),
+    ]
+    scratch = scratch + scatter_scratch(seqs, cores, rows, model_width) + qkv_buffers + o_buffers
+    scratch = scratch + [dma_sems(6, seqs, PARTS), dma_sems(2)]
+    scratch = scratch + pair_sems("seq", 3) + pair_sems("seq", 1) * 2 + pair_sems("row", 1)
+    scratch = scratch + [dma_sems(seqs - 1)] * 2 + [dma_sems(2)] + o_sems + qkv_sems
+    return line_call(
+        functools.partial(backward_kernel, heads), 6, "mixer_backward", outs, scratch,
+        (grad, o_full, *saved, taps, aux, docs, gain, *extra),
+        far_args=(sums,),
+        far_outs=far_outs + ((sums.shape[1:], b16),) * 3,
+    )
 
 
 def row_aux(docs):
@@ -957,44 +1141,54 @@
 
 
 class Gather:
-    def __init__(self, line, slots, sems):
-        self.line, self.slots, self.sems = line, slots, sems
+    def __init__(self, line, slots, own, sems):
+        self.line, self.slots, self.own, self.sems = line, slots, own, sems
         self.parts = sems.shape[2]
         self.rows = slots.shape[2] // self.parts
 
     def span(self, part):
         return pl.ds(part * self.rows, self.rows)
 
-    def copy(self, kind, seq, part):
+    def copy(self, kind, seq, part, own=False):
         line = self.line
         send = {"right": 0, "left": 1, "across": 2}[kind]
         recv = 4 if kind == "across" else 3
         slot = self.slots.at[seq, line.core, self.span(part)]
         where = {"right": line.right, "left": line.left, "across": line.across}[kind]
+        source = self.own.at[self.span(part)] if own else slot
         return remote(
-            slot, slot, self.sems.at[send, seq, part], self.sems.at[recv, seq, part], where
+            source, slot, self.sems.at[send, seq, part], self.sems.at[recv, seq, part], where
         )
 
-    def forward(self, seq, part, right, left):
+    def own_copy(self, part):
+        line = self.line
+        return pltpu.make_async_copy(
+            self.own.at[self.span(part)],
+            self.slots.at[line.place, line.core, self.span(part)],
+            self.sems.at[5, 0, part],
+        )
+
+    def forward(self, seq, part, right, left, own=False):
         line = self.line
         if right:
 
             @pl.when(line.place < line.count - 1)
             def _():
-                self.copy("right", seq, part).start()
+                self.copy("right", seq, part, own).start()
 
         if left:
 
             @pl.when(line.place > 0)
             def _():
-                self.copy("left", seq, part).start()
-
-        self.copy("across", seq, part).start()
+                self.copy("left", seq, part, own).start()
+
+        self.copy("across", seq, part, own).start()
 
     def phase(self, by, part):
         line = self.line
         if by == 0:
-            self.forward(line.place, part, True, True)
+            self.forward(line.place, part, True, True, own=True)
+            self.own_copy(part).start()
             return
 
         @pl.when(line.place - by >= 0)
@@ -1013,6 +1207,8 @@
 
     def finish(self):
         line = self.line
+        for part in range(self.parts):
+            self.own_copy(part).wait()
         for seq in range(line.count):
             for part in range(self.parts):
 
@@ -1069,7 +1265,9 @@
     def product(self, left_ref, right_ref, part, order=1, tile=512, right_tile=None):
         seqs, cores, _, width = self.blocks.shape
         span = self.span(part)
-        left = left_ref[:, span].reshape(seqs * cores * self.rows, -1)
+        left = left_ref
+        if len(left_ref.shape) == 3:
+            left = left_ref[:, span].reshape(seqs * cores * self.rows, -1)
 
         def columns(t, _):
             across = pl.ds(pl.multiple_of(t * tile, tile), tile)
@@ -1198,10 +1396,7 @@
 class Exchange:
     def __init__(self, line, source, target, sems):
         self.line, self.source, self.target = line, source, target
-        self.send, self.recv = sems[:2]
-        self.shared = len(sems) > 2
-        if self.shared:
-            self.send_row, self.recv_row = sems[2:]
+        self.send, self.recv, self.send_row, self.recv_row = sems
         self.row = lax.axis_index("row")
         self.seq_others, self.row_others = around("seq"), around("row")
 
@@ -1209,9 +1404,7 @@
         other = self.seq_others[i]
         return remote(
             self.source(other),
-            self.target.at[self.row, self.line.place]
-            if self.shared
-            else self.target.at[self.line.place],
+            self.target.at[self.row, self.line.place],
             self.send.at[i],
             self.recv.at[i],
             {"seq": other},
@@ -1241,9 +1434,7 @@
     def finish(self):
         for i in range(len(self.seq_others)):
             self.spread(i).wait_send()
-            if not self.shared:
-                self.spread(i).wait_recv()
-        for i in range(len(self.seq_others) + 1 if self.shared else 0):
+        for i in range(len(self.seq_others) + 1):
             for j in range(len(self.row_others)):
                 self.share(i, j).wait()
 
@@ -1351,6 +1542,19 @@
         self.blocks[self.near[i], m, rows] = total.astype(jnp.bfloat16)
         self.copy(i, j, m).start()
 
+    def start(self, step, m):
+        if step == 0:
+            self.start_far(m)
+        elif step < 3:
+            self.start_near(step - 1, m)
+
+    def order(self):
+        return (self.far, self.near[0], self.near[1], self.row)
+
+    def add_halves(self, m):
+        for i in range(2):
+            self.add_half(i, m)
+
     def total(self, m):
         for i in range(2):
             for j in range(2):
@@ -1420,60 +1624,6 @@
     lax.fori_loop(0, total.rows // STEP, step, 0)
 
 
-def resid_kernel(
-    mix_ref, o_ref, x_ref, g_ref, gain_ref, up_ref, down_ref,
-    resid_ref, n2_ref, g_full_ref, up_full_ref, down_full_ref,
-    blocks, came, across, o_rows, sum_sems, n2_sems, g_sems, *sems,
-):
-    line = Line()
-    greet(line_partners() + along_axis("row"))
-    shares = moves_of(
-        Share,
-        "row",
-        (up_ref, down_ref),
-        (up_full_ref, down_full_ref),
-        sems,
-    )
-    for share in shares:
-        share.start()
-    rows = n2_ref.shape[2]
-    total = Scatter(line, blocks, came, across, sum_sems)
-    n2 = Gather(line, n2_ref, n2_sems)
-    grads = Gather(line, g_full_ref, g_sems)
-    g_full_ref[line.place, line.core] = g_ref[
-        pl.ds(pl.multiple_of(line.core * rows, rows), rows)
-    ]
-    grads.phases(0)
-    side_by_side(o_ref, o_rows)
-    for part in range(total.parts):
-        total.product(mix_ref, o_rows, part, order=0)
-    for k in range(1, line.count):
-        grads.phases(k)
-        total.nears(k - 1)
-    for k in range(line.count - 1):
-        total.fars(k)
-
-    def normed(span):
-        x_span = pl.ds(pl.multiple_of(line.core * rows + span.start, STEP), STEP)
-        resid = x_ref[x_span].astype(jnp.float32) + total.own_rows(span)
-        resid_ref[span] = resid
-        n2_ref[line.place, line.core, span] = (
-            resid * norm_scale(resid) * gain_ref[...]
-        ).astype(jnp.bfloat16)
-
-    for part in range(total.parts):
-        total.wait_own(part)
-        over_rows(total, part, normed)
-        n2.phase(0, part)
-    for k in range(1, line.count):
-        n2.phases(k)
-    total.finish()
-    n2.finish()
-    grads.finish()
-    for share in shares:
-        share.finish()
-
-
 def side_by_side(blocks_ref, out_ref):
     outer, inner, _, width = blocks_ref.shape
     for i in range(outer):
@@ -1485,17 +1635,67 @@
     return pltpu.SemaphoreType.DMA(shape)
 
 
-def line_call(kernel, collective_id, name, outs, scratch, args, limit=56, far_args=(), far_outs=()):
+class Staged:
+    def __init__(self, inputs, outputs, in_sems, out_sems):
+        self.loads = [
+            (near, pltpu.make_async_copy(far, near, in_sems.at[i]))
+            for i, (far, near) in enumerate(inputs)
+        ]
+        self.stores = [
+            (near, pltpu.make_async_copy(near, far, out_sems.at[i]))
+            for i, (far, near) in enumerate(outputs)
+        ]
+        self.stored = []
+        for _, copy in self.loads:
+            copy.start()
+
+    def need(self, *refs):
+        for ref in refs:
+            (at,) = [i for i, (near, _) in enumerate(self.loads) if near is ref]
+            self.loads.pop(at)[1].wait()
+
+    def store(self, *refs):
+        for ref in refs:
+            (at,) = [i for i, (near, _) in enumerate(self.stores) if near is ref]
+            copy = self.stores.pop(at)[1]
+            copy.start()
+            self.stored.append(copy)
+
+    def finish(self):
+        self.need(*[near for near, _ in self.loads])
+        self.store(*[near for near, _ in self.stores])
+        for copy in self.stored:
+            copy.wait()
+
+
+def line_call(kernel, collective_id, name, outs, scratch, args, limit=60, far_args=(), far_outs=()):
+    counts = [len(args), len(far_args), len(outs), len(far_outs), len(args), len(outs)]
+
+    def body(*refs):
+        groups, at = [], 0
+        for count in counts:
+            groups.append(refs[at : at + count])
+            at += count
+        near_in, near_out, in_sems, out_sems, *rest = *groups[4:], *refs[at:]
+        staged = Staged(
+            list(zip(groups[0], near_in)), list(zip(groups[2], near_out)), in_sems, out_sems
+        )
+        kernel(staged, *near_in, *groups[1], *near_out, *groups[3], *rest)
+        staged.finish()
+
     far = pl.BlockSpec(memory_space=pl.ANY)
+    stages = [pltpu.VMEM(arg.shape, arg.dtype) for arg in args]
+    stages += [pltpu.VMEM(*out) for out in outs]
+    stages += [dma_sems(max(len(args), 1)), dma_sems(max(len(outs), 1))]
     return pl.pallas_call(
-        kernel,
+        body,
         out_shape=[jax.ShapeDtypeStruct(*out) for out in (*outs, *far_outs)],
-        in_specs=in_vmem(len(args)) + [far] * len(far_args),
-        out_specs=in_vmem(len(outs)) + [far] * len(far_outs),
-        scratch_shapes=scratch,
+        in_specs=[far] * (len(args) + len(far_args)),
+        out_specs=[far] * (len(outs) + len(far_outs)),
+        scratch_shapes=stages + scratch,
         compiler_params=pltpu.CompilerParams(
             collective_id=collective_id,
-            has_side_effects=True,
+            has_side_effects=collective_id is not None,
             vmem_limit_bytes=limit * 1024 * 1024,
         ),
         name=name,
@@ -1514,32 +1714,12 @@
 PARTS = 2
 
 
-def run_resid(mix, o_full, x, g, gain, weights):
-    seqs, cores, (piece, width) = lax.axis_size("seq"), lax.axis_size("tp"), x.shape
-    rows, b16 = piece // cores, jnp.bfloat16
-    outs = (
-        ((rows, width), jnp.float32),
-        ((seqs, cores, rows, width), b16),
-        ((seqs, cores, rows, width), b16),
-    )
-    scratch = scatter_scratch(seqs, cores, rows, width)
-    scratch = scratch + [pltpu.VMEM((o_full.shape[2], width), b16)] + [dma_sems(5, seqs, PARTS)] * 3
-    scratch = scratch + pair_sems("row", len(weights))
-    mix = mix.reshape(seqs * cores, rows, -1)
-    resid, n2, g_full, *full = line_call(
-        resid_kernel, 1, "resid_norm", outs, scratch, (mix, o_full, x, g, gain),
-        far_args=weights,
-        far_outs=[((lax.axis_size("row"),) + weight.shape, b16) for weight in weights],
-    )
-    return resid, n2.reshape(-1, width), g_full.reshape(-1, width), full
-
-
 def grad_resid_kernel(
-    grad_gate_ref, grad_up_ref, hidden_ref, down_ref, resid_ref, g_ref, gain_ref,
+    staged, grad_gate_ref, grad_up_ref, hidden_ref, down_ref, resid_ref, g_ref, gain_ref,
     gate_ref, up_ref, n2_ref, g_full_ref,
-    grad_resid_ref, grad_attn_ref, gain_grad_ref, result_ref,
-    sum_ref,
-    blocks, came, across, out_blocks, out_came, out_across, weights, tokens, parts, halves, parts_came,
+    grad_resid_ref, gain_grad_ref, result_ref,
+    grad_attn_ref, sum_ref,
+    attn_own, blocks, came, across, out_blocks, out_came, out_across, weights, tokens, parts, halves, parts_came,
     sum_sems, out_sems, attn_sems, swap_sems, weight_sems, token_sems, own_sems, *sems,
 ):
     line = Line()
@@ -1547,7 +1727,7 @@
     rows = resid_ref.shape[0]
     total = Scatter(line, blocks, came, across, sum_sems)
     result = Scatter(line, out_blocks, out_came, out_across, out_sems)
-    attn = Gather(line, grad_attn_ref, attn_sems)
+    attn = Gather(line, grad_attn_ref, attn_own, attn_sems)
     sums = RowSum(parts, halves, parts_came, sems)
     units = hidden_ref.shape[2]
     tile = weights.shape[2]
@@ -1562,7 +1742,7 @@
             for i, ref in enumerate((gate_ref, up_ref))
         ]
 
-    orders = (sums.far, sums.near[0], sums.near[1], sums.row)
+    orders = sums.order()
     block_width = tokens.shape[3]
 
     def token_copies(step):
@@ -1604,13 +1784,12 @@
         for m, (i, ref) in enumerate(((0, hidden_ref), (1, grad_gate_ref), (1, grad_up_ref))):
             part = mul(tokens[slot, i], ref[...].reshape(-1, units), (0, 0))
             parts[to, m] = part.astype(jnp.bfloat16)
-            if step == 0:
-                sums.start_far(m)
-            elif step < 3:
-                sums.start_near(step - 1, m)
-
+            sums.start(step, m)
+
+    staged.need(grad_gate_ref, grad_up_ref)
     for part in range(total.parts):
         product(part)
+    staged.need(hidden_ref)
     weight_grads(0)
     total.relay(0, 0)
     total.relay(1, 0)
@@ -1621,6 +1800,7 @@
     total.relay(1, 1)
     weight_grads(3)
     total.relay_back(1)
+    staged.need(resid_ref, g_ref, gain_ref, down_ref)
     gain_grad_ref[...] = jnp.zeros_like(gain_grad_ref)
 
     def back(span):
@@ -1633,17 +1813,17 @@
             resid, scale, gain_ref[...], grad_two
         )
         grad_resid_ref[span] = grad
-        grad_attn_ref[line.place, line.core, span] = grad.astype(jnp.bfloat16)
+        attn_own[span] = grad.astype(jnp.bfloat16)
 
     for part in range(total.parts):
         total.wait_own(part)
         over_rows(total, part, back)
         attn.phase(0, part)
+    staged.store(grad_resid_ref, gain_grad_ref)
     for part in range(result.parts):
         result.product(hidden_ref, down_ref, part, order=0)
     for m in range(parts.shape[1]):
-        for i in range(2):
-            sums.add_half(i, m)
+        sums.add_halves(m)
     for k in range(1, line.count):
         attn.phases(k)
         result.nears(k - 1)
@@ -1687,142 +1867,32 @@
     units, span = gate.shape[1], width // rows_axis
     outs = (
         ((rows, width), f32),
-        ((seqs, cores, rows, width), b16),
         ((1, width), f32),
         ((piece, width), b16),
     )
     sum_buffers, sum_sems = row_sum_scratch((rows_axis, 3, span, units))
-    scratch = scatter_scratch(seqs, cores, rows, width) * 2
+    scratch = [pltpu.VMEM((rows, width), b16)] + scatter_scratch(seqs, cores, rows, width) * 2
     scratch = scratch + [
         pltpu.VMEM((2, 2, span, units), b16),
         pltpu.VMEM((2, 2, n2.shape[0], span), b16),
     ]
-    scratch = scratch + sum_buffers + [dma_sems(5, seqs, PARTS)] * 3
+    scratch = scratch + sum_buffers + [dma_sems(6, seqs, PARTS)] * 3
     scratch = scratch + [dma_sems(2), dma_sems(2, 2), dma_sems(2, 2), dma_sems(3)] + sum_sems
     grad_gate, grad_up, hidden = (
         array.reshape(seqs * cores, rows, -1) for array in (grad_gate, grad_up, hidden)
     )
-    grad_resid, grad_attn, gain_grad, result, sums = line_call(
+    grad_resid, gain_grad, result, grad_attn, sums = line_call(
         grad_resid_kernel, 2, "grad_resid", outs, scratch,
         (grad_gate, grad_up, hidden, down, resid, g, gain),
-        limit=60,
         far_args=(gate, up, n2, g_full),
-        far_outs=(((3, span, units), b16),),
+        far_outs=(((seqs, cores, rows, width), b16), ((3, span, units), b16)),
     )
     return grad_resid, grad_attn.reshape(-1, width), gain_grad, result, sums
 
 
-def input_grad_kernel(
-    grad_proj_ref, qkv_ref, grad_logit_ref, beta_ref, x_ref, grad_resid_ref, gain_ref, qkv_part_ref,
-    small_ref, o_sum_ref,
-    input_grad_ref, qkv_came_ref, small_all_ref,
-    o_came_ref,
-    blocks, came, across, qkv_rows, qkv_sum, small_rows, sum_sems, swap_sems, *sems,
-):
-    line = Line()
-    greet(along_axis("seq") + along_axis("row") + along_axis("tp"))
-    (o_move,) = moves_of(Swap, "seq", (o_sum_ref,), (o_came_ref,), sems[:3])
-    (rows_move,) = moves_of(Swap, "row", (qkv_part_ref,), (qkv_rows,), sems[3:6])
-    (qkv_move,) = moves_of(Swap, "seq", (qkv_sum,), (qkv_came_ref,), sems[6:9])
-    (small_row,) = moves_of(Share, "row", (small_ref,), (small_rows,), sems[9:12])
-    own_small = small_all_ref.at[line.core, line.place]
-    small_seq = [
-        remote(own_small, own_small, sems[12].at[i], sems[13].at[i], {"seq": other})
-        for i, other in enumerate(around("seq"))
-    ]
-    core_small = small_all_ref.at[line.core]
-    small_core = remote(core_small, core_small, sems[14].at[0], sems[14].at[1], line.across)
-    small_row.start()
-    rows_move.start()
-    o_move.start()
-    rows = grad_resid_ref.shape[0]
-    total = Scatter(line, blocks, came, across, sum_sems)
-
-    width = qkv_ref.shape[-1]
-
-    for part in range(total.parts):
-        logit = grad_logit_ref[:, total.span(part)].reshape(-1, grad_logit_ref.shape[-1])
-
-        def right_tile(left, t, across, logit=logit):
-            block = qkv_ref[t]
-            out = mul(logit, beta_ref[:, across], (1, 0))
-            for c in range(3):
-                out = out + mul(
-                    left[:, c * width : (c + 1) * width], block[:, c].reshape(-1, width), (1, 1)
-                )
-            return out
-
-        tile = qkv_ref.shape[1] * qkv_ref.shape[3]
-        total.product(grad_proj_ref, None, part, tile=tile, right_tile=right_tile)
-    small_row.finish()
-    small = small_rows[0]
-    for i in range(1, small_rows.shape[0]):
-        small = small + small_rows[i]
-    small_all_ref[line.core, line.place] = small
-    for copy in small_seq:
-        copy.start()
-    for k in range(line.count - 1):
-        total.nears(k)
-    for copy in small_seq:
-        copy.wait()
-    small_core.start()
-    for k in range(line.count - 1):
-        total.fars(k)
-    rows_move.finish()
-    for i in range(qkv_rows.shape[1]):
-        piece = qkv_rows[0, i].astype(jnp.float32)
-        for j in range(1, qkv_rows.shape[0]):
-            piece = piece + qkv_rows[j, i].astype(jnp.float32)
-        qkv_sum[i] = piece.astype(jnp.bfloat16)
-    qkv_move.start()
-
-    def back(span):
-        own_span = pl.ds(pl.multiple_of(line.core * rows + span.start, STEP), STEP)
-        x = x_ref[own_span].astype(jnp.float32)
-        grad_one = total.own_rows(span)
-        scale = norm_scale(x)
-        input_grad_ref[own_span] = (
-            grad_resid_ref[span] + norm_back(x, scale, gain_ref[...], grad_one)
-        ).astype(jnp.bfloat16)
-
-    for part in range(total.parts):
-        total.wait_own(part)
-        over_rows(total, part, back)
-    swap = own_swap(line, input_grad_ref, rows, swap_sems)
-    swap.start()
-    total.finish()
-    swap.wait()
-    small_core.wait()
-    o_move.finish()
-    qkv_move.finish()
-
-
-def run_input_grad(grad_proj, qkv, grad_logit, beta, x, grad_resid, gain, qkv_part, small, o_sum):
-    seqs, cores, (piece, width) = lax.axis_size("seq"), lax.axis_size("tp"), x.shape
-    rows, b16, f32 = piece // cores, jnp.bfloat16, jnp.float32
-    outs = (
-        ((piece, width), b16),
-        (qkv_part.shape[1:], b16),
-        ((cores, seqs) + small.shape, f32),
-    )
-    scratch = scatter_scratch(seqs, cores, rows, width)
-    scratch = scratch + [pltpu.VMEM(qkv_part.shape, b16), pltpu.VMEM(qkv_part.shape[1:], b16)]
-    scratch = scratch + [pltpu.VMEM((lax.axis_size("row"),) + small.shape, f32)]
-    scratch = scratch + [dma_sems(5, seqs, PARTS), dma_sems(2)]
-    scratch = scratch + pair_sems("seq", 1) + pair_sems("row", 1) + pair_sems("seq", 1)
-    scratch = scratch + pair_sems("row", 1) + [dma_sems(seqs - 1)] * 2 + [dma_sems(2)]
-    grad_proj = grad_proj.reshape(seqs * cores, rows, -1)
-    grad_logit = grad_logit.reshape(seqs * cores, rows, -1)
-    return line_call(
-        input_grad_kernel, 3, "input_grad", outs, scratch,
-        (grad_proj, qkv, grad_logit, beta, x, grad_resid, gain, qkv_part, small),
-        far_args=(o_sum,),
-        far_outs=((o_sum.shape, b16),),
-    )
-
-
 def normed_kernel(
-    x_ref, gain_ref, weight_ref, beta_ref, n1_ref, qkv_ref, beta_full_ref, n1_sems, own_sems, *sems
+    staged, x_ref, gain_ref, weight_ref, beta_ref, n1_ref, qkv_ref, beta_full_ref, n1_own, n1_sems,
+    own_sems, *sems,
 ):
     line = Line()
     row = lax.axis_index("row")
@@ -1847,14 +1917,13 @@
     for copy in own:
         copy.start()
     rows = n1_ref.shape[2]
-    n1 = Gather(line, n1_ref, n1_sems)
+    n1 = Gather(line, n1_ref, n1_own, n1_sems)
+    staged.need(x_ref, gain_ref)
 
     def normed(span):
         x_span = pl.ds(pl.multiple_of(line.core * rows + span.start, STEP), STEP)
         x = x_ref[x_span].astype(jnp.float32)
-        n1_ref[line.place, line.core, span] = (x * norm_scale(x) * gain_ref[...]).astype(
-            jnp.bfloat16
-        )
+        n1_own[span] = (x * norm_scale(x) * gain_ref[...]).astype(jnp.bfloat16)
 
     for part in range(n1.parts):
         over_rows(n1, part, normed)
@@ -1882,9 +1951,12 @@
         ((rows_axis,) + beta.shape, b16),
     )
     n1, qkv, beta_full = line_call(
-        normed_kernel, 4, "norm_gather", outs,
-        [dma_sems(5, seqs, PARTS), dma_sems(2)] + exchange_sems() * 2,
-        (x, gain, weight, beta),
+        normed_kernel, 4, "norm_gather", (),
+        [pltpu.VMEM((piece // cores, width), b16), dma_sems(6, seqs, PARTS), dma_sems(2)]
+        + exchange_sems() * 2,
+        (x, gain),
+        far_args=(weight, beta),
+        far_outs=outs,
     )
     return n1.reshape(-1, width), qkv, beta_full
 
@@ -1926,10 +1998,11 @@
 
 
 def finish_kernel(
-    small_ref, qkv_ref, o_ref, gate_ref, up_ref, down_ref,
+    staged, small_ref, qkv_ref, o_ref, gate_ref, up_ref, down_ref,
     attn_gain_ref, mlp_gain_ref, out_gain_ref, conv_ref, qkv_out, o_out, gate_up_out, down_out,
 ):
     f32 = jnp.float32
+    staged.need(small_ref, qkv_ref, o_ref, gate_ref, up_ref, down_ref)
     cores, seqs, _, _ = small_ref.shape
     _, shard, width3 = qkv_ref.shape
     width, units = width3 // 3, gate_ref.shape[2]
@@ -1981,14 +2054,10 @@
         (2, shard, seqs * units),
         (seqs * units, shard),
     )
-    return pl.pallas_call(
-        finish_kernel,
-        out_shape=[jax.ShapeDtypeStruct(shape, f32) for shape in shapes],
-        in_specs=in_vmem(6),
-        out_specs=in_vmem(len(shapes)),
-        compiler_params=pltpu.CompilerParams(vmem_limit_bytes=48 * 1024 * 1024),
-        name="finish",
-    )(small, qkv, o, gate, up, down)
+    return line_call(
+        finish_kernel, None, "finish", [(shape, f32) for shape in shapes], [],
+        (small, qkv, o, gate, up, down),
+    )
 
 
 def local_heads(
@@ -2033,30 +2102,21 @@
     taps = lax.dynamic_slice_in_dim(conv_weight, piece * width, width, axis=2)
     taps = taps.transpose(1, 0, 2).reshape(KW, 3 * width)
 
-    (
-        proj, logit, mixed, normed_mix, inverse, states, written,
-        o_full, gate_full, up_came, down_came,
-    ) = run_forward(
+    saved, o_full, resid, normed_two, g_full, gate_full, up_full, down_full = run_forward(
         normed_one, qkv_full, beta_full, taps, aux, doc_rows, gain_row,
-        o_weight, gate_up_parts[0], gate_up_parts[1], down_weight,
-    )
-    resid, normed_two, g_full, (up_full, down_full) = run_resid(
-        normed_mix, o_full, x_piece, g_piece, mlp_gain[None], (up_came, down_came)
-    )
-    gate_full = gate_full.reshape(model_width, units)
-    up_full = up_full.reshape(model_width, units)
+        x_piece, g_piece, mlp_gain[None],
+        (o_weight, gate_up_parts[0], gate_up_parts[1], down_weight),
+    )
+    proj, logit, mixed, normed_mix, inverse, states, written = saved
     hidden, grad_gate, grad_up, down_rows = run_mlp(
         normed_two, g_full, gate_full, up_full, down_full
     )
-
-    def summed(came):
-        return jnp.sum(came.astype(f32), axis=0).astype(b16)
 
     grad_resid, grad_attn, mlp_gain_part, result, sums = run_grad_resid(
         grad_gate, grad_up, gate_full, up_full, hidden, down_rows, resid, g_piece, mlp_gain[None],
         normed_two, g_full,
     )
-    grad_proj, grad_logit, small, qkv_part, down_sum, gate_sum, up_sum, o_came = run_backward(
+    input_grad, small, qkv_sum, o_sum, down_sum, gate_sum, up_sum = run_backward(
         grad_attn,
         o_full,
         (proj, logit, mixed, inverse, states, written),
@@ -2064,12 +2124,11 @@
         aux,
         doc_rows,
         gain_row,
-        (normed_mix, normed_one, qkv_full, beta_full, attn_gain[None], mlp_gain_part),
+        (
+            normed_mix, normed_one, qkv_full, beta_full, attn_gain[None], mlp_gain_part,
+            x_piece, grad_resid,
+        ),
         sums.reshape(3, pieces, shard_rows, units),
-    )
-    input_grad, qkv_sum, small, o_sum = run_input_grad(
-        grad_proj, qkv_full, grad_logit, beta_full, x_piece, grad_resid, attn_gain[None],
-        qkv_part, small, summed(o_came),
     )
     attn_gain_grad, mlp_gain_grad, out_gain_grad, conv_grad, qkv_grad, o_grad, gate_up_grad, down_grad = (
         run_finish(small, qkv_sum, o_sum, gate_sum, up_sum, down_sum)

time: 502 us -> 451 us (0.90)
  Pallas kernels: 471 us -> 429 us
  local copies, waits for them, and re-layouts: 24.9 us -> 16 us
    pallas_call x7 -> x5, Pallas kernels: 455 us -> 413 us  [line_call(): pl.pallas_call(body, out_shape=[jax.ShapeDtypeStruct(*out) for out in (*o...]
    unnamed x56 -> x18, local copies, waits for them, and re-layouts: 18.4 us -> 7.86 us
where the time goes in v6:
time: 451 us; the launch traced here: 448 us
  Pallas kernels  429 us (95%)
  local copies, waits for them, and re-layouts  16 us (4%)
    pallas_call x5, Pallas kernels, line_call(): pl.pallas_call(body, out_shape=[jax.ShapeDtypeStruct(*out) for out in (*o...  413 us
    pallas_call x1, Pallas kernels, run_mlp(): pl.pallas_call(mlp_kernel, grid=(row_len // block,), out_shape=[shape] *...  16.1 us

profile of v6, /device:TPU:8, one launch (start us, length us, event | category | flops | bytes accessed | tf_op | source)
XLA Modules:
  0.0 447.8 jit_solution(3466390276887728897)
XLA Ops:
  0.6 0.0 copy-start
  0.7 0.8 reduce-window.8
  1.5 0.1 convert_reduce_fusion
  1.6 0.2 slice_reduce_fusion
  1.8 0.2 slice_reduce_fusion.1
  2.0 0.1 pad_add_fusion
  2.0 0.1 eq.47
  2.1 0.1 eq.51
  2.2 0.6 bitcast_convert_fusion.refs_5_.refs_10_
  2.8 0.0 copy-done
  2.8 0.6 constant_dynamic-slice_fusion.1
  3.4 0.1 fusion.3
  3.5 0.1 stack.31
  3.6 1.3 pad.5.refs_3_
  4.9 1.0 copy.44.refs_4_.refs_9_
  5.8 1.8 copy.42
  7.7 0.7 copy.43
  8.4 1.2 slice_bitcast_fusion
  9.6 56.5 %norm_gather.1 = (bf16[4,2,128,2048]{3,2,1,0:T(8,128)(2,1)}, bf16[4,4,3,128,256]{4,3,2,1,0:T(8,128)(2,1)}, bf16[4,4,16,128]{3,2,1,0:T(8,128)(2,1)}) custom-call(bf16[256,2048]{1,0:T(8,128)(2,1)} %bitcast.63, f32[1,2048]{1,0:T(1,128)} %bitcast.84, bf16[3,128,1024]{2,1,0:T(8,128)(2,1)} %refs_2_.1, bf16[4,16,128]{2,1,0:T(8,128)(2,1)} %pad.5.refs_3_), custom_call_target="tpu_custom_call" | custom-call | tf_op jit(solution)/shard_map/norm_gather/pallas_call | solution.py:1690
  66.2 0.9 copy.41
  67.0 0.6 copy.48
  67.7 139.3 %mixer_forward.1 = (bf16[1024,768]{1,0:T(8,128)(2,1)}, f32[1024,16]{1,0:T(8,128)}, f32[1024,256]{1,0:T(8,128)}, bf16[1024,256]{1,0:T(8,128)(2,1)}, f32[2,8,128,1...) custom-call(bf16[1024,2048]{1,0:T(8,128)(2,1)} %bitcast.53, ...), custom_call_target="tpu_custom_call" | custom-call | tf_op jit(solution)/shard_map/mixer_forward/pallas_call | solution.py:1690
  207.0 16.1 %mlp.1 = (bf16[1024,704]{1,0:T(8,128)(2,1)S(1)}, bf16[1024,704]{1,0:T(8,128)(2,1)S(1)}, bf16[1024,704]{1,0:T(8,128)(2,1)S(1)}, bf16[704,2048]{1,0:T(8,128)(2,1)}) custom-call(bf16[1024,2048]{1,0:T(8,128)(2,1)} %bitcast.55, bf16[1024,2048]{1,0:T(8,128)(2,1)} %bitcast.57, bf16[2048,704]{1,0:T(8,128)(2,1)} %bitcast.59, bf16[2048,704]{1,0:T(8,128)(2,1)} %bitcast.61, ...), custom_call_target="tpu_custom_call" | custom-call | tf_op jit(solution)/shard_map/mlp/pallas_call | solution.py:1989
  223.1 0.0 copy-start.2
  223.1 1.1 copy-done.2
  224.2 0.0 copy-start.3
  224.2 1.1 copy-done.3
  225.4 0.0 copy-start.4
  225.4 1.1 copy-done.4
  226.5 104.1 %grad_resid.1 = (f32[128,2048]{1,0:T(8,128)}, f32[1,2048]{1,0:T(1,128)}, bf16[256,2048]{1,0:T(8,128)(2,1)}, bf16[4,2,128,2048]{3,2,1,0:T(8,128)(2,1)}, bf16[3,512,704]{2,1,0:T(8,128)(2,1)}) custom-call(bf16[8,128,704]{2,1,0:T(8,128)(2,1)} %bitcast.51, bf16[8,128,704]{2,1,0:T(8,128)(2,1)} %bitcast.52, bf16[8,128,704]{2,1,0:T(8,128)(2,1)} %bitcast.50, ...), custom_call_target="tpu_custom_call" | custom-call | tf_op jit(solution)/shard_map/grad_resid/pallas_call | solution.py:1690
  330.7 107.3 %mixer_backward.1 = (bf16[256,2048]{1,0:T(8,128)(2,1)}, f32[2,4,6,2048]{3,2,1,0:T(8,128)}, bf16[4,128,768]{2,1,0:T(8,128)(2,1)}, bf16[4,128,256]{2,1,0:T(8,128)(...) custom-call(bf16[1024,2048]{1,0:T(8,128)(2,1)} %bitcast.68, ...), custom_call_target="tpu_custom_call" | custom-call | tf_op jit(solution)/shard_map/mixer_backward/pallas_call | solution.py:1690
  437.9 0.0 copy-start.5
  437.9 1.2 slice.31
  439.2 0.6 dynamic-slice_bitcast_fusion
  439.8 0.0 copy-start.6
  439.8 0.0 copy-start.1
  439.8 5.7 %finish.1 = (f32[1,2048]{1,0:T(1,128)}, f32[1,2048]{1,0:T(1,128)}, f32[1,128]{1,0:T(1,128)}, f32[3,4,2048]{2,1,0:T(4,128)}, f32[3,128,1024]{2,1,0:T(8,128)}, /*i...) custom-call(f32[2,4,6,2048]{3,2,1,0:T(8,128)} %get-tuple-element.79.refs_0_, ...), custom_call_target="tpu_custom_call" | custom-call | tf_op jit(solution)/shard_map/finish/pallas_call | solution.py:1690
  445.5 0.0 copy-done.5
  445.6 1.0 copy.51
  446.5 0.0 copy-done.6
  446.5 1.0 copy.52
  447.5 0.0 copy-done.1
  (5 shorter events, 0.1 us)
Async XLA Ops:
  0.6 2.2 copy-start
  223.1 1.1 copy-start.2
  224.2 1.1 copy-start.3
  225.4 1.1 copy-start.4
  437.9 7.6 %copy-start.5 = (bf16[256,2048]{1,0:T(8,128)(2,1)S(1)}, bf16[256,2048]{1,0:T(8,128)(2,1)}, u32[]{:S(2)}) copy-start(bf16[256,2048]{1,0:T(8,128)(2,1)} %get-tuple-element.65) | copy-start | bytes 3145732
  439.8 6.7 %copy-start.6 = (bf16[256,2048]{1,0:T(8,128)(2,1)S(1)}, bf16[256,2048]{1,0:T(8,128)(2,1)}, u32[]{:S(2)}) copy-start(bf16[256,2048]{1,0:T(8,128)(2,1)} %get-tuple-element.78) | copy-start | bytes 3145732
  439.8 7.7 %copy-start.1 = (f32[3,4,1024]{2,1,0:T(4,128)S(1)}, f32[3,4,1024]{2,1,0:T(4,128)}, u32[]{:S(2)}) copy-start(f32[3,4,1024]{2,1,0:T(4,128)} %param.18) | copy-start | bytes 147460
